TPU v7x, 32 devices: a whole 2x2x4 slice. The times are simulated.
32 devices in a mesh: ctx: 8 (over y, x, core), fsdp: 4 (over z).
Axes of the slice: x: 2, y: 2, z: 4, core: 2. Of those that a mesh axis runs over, the one named last changes fastest.
Arguments:
- inputs: bfloat16 [4, 1024, 512], P('fsdp', 'ctx'), may hold values from -6 to 6
- block_order: int32 [16], replicated, may hold values from 0 to 15, each once
- ln1_gain: bfloat16 [512], P('fsdp'), may hold values from 0.5 to 1.5
- ln1_bias: bfloat16 [512], P('fsdp'), may hold values from -3 to 3
- w_qkv: bfloat16 [512, 1536], P('fsdp'), may hold values from -0.25 to 0.25
- b_qkv: bfloat16 [1536], P('fsdp'), may hold values from -3 to 3
- w_attn_out: bfloat16 [512, 512], P('fsdp'), may hold values from -3 to 3
- b_attn_out: bfloat16 [512], P('fsdp'), may hold values from -3 to 3
- ln2_gain: bfloat16 [512], P('fsdp'), may hold values from 0.5 to 1.5
- ln2_bias: bfloat16 [512], P('fsdp'), may hold values from -3 to 3
- w_up: bfloat16 [512, 2048], P('fsdp'), may hold values from -0.25 to 0.25
- b_up: bfloat16 [2048], P('fsdp'), may hold values from -3 to 3
- w_down: bfloat16 [2048, 512], P('fsdp'), may hold values from -0.125 to 0.125
- b_down: bfloat16 [512], P('fsdp'), may hold values from -3 to 3
- cotangent: bfloat16 [4, 1024, 512], P('fsdp', 'ctx'), may hold values from -6 to 6
Outputs:
- output: bfloat16 [4, 1024, 512], P('fsdp', 'ctx')
- grad_inputs: float32 [4, 1024, 512], P('fsdp', 'ctx')
- grad_ln1_gain: float32 [512], P('fsdp')
- grad_ln1_bias: float32 [512], P('fsdp')
- grad_w_qkv: float32 [512, 1536], P('fsdp')
- grad_b_qkv: float32 [1536], P('fsdp')
- grad_w_attn_out: float32 [512, 512], P('fsdp')
- grad_b_attn_out: float32 [512], P('fsdp')
- grad_ln2_gain: float32 [512], P('fsdp')
- grad_ln2_bias: float32 [512], P('fsdp')
- grad_w_up: float32 [512, 2048], P('fsdp')
- grad_b_up: float32 [2048], P('fsdp')
- grad_w_down: float32 [2048, 512], P('fsdp')
- grad_b_down: float32 [512], P('fsdp')
Inputs may be any that keep to these rules, and one draw needn't show every extreme that they name: Each number appears once; storage block j of a sequence (rows j * 64 to (j + 1) * 64 - 1) holds position block block_order[j].
All inputs are finite; a program needn't handle non-finite values.
Results may differ from a plain program's by a relative error of at most 0.018.
Values may be sent and summed in bfloat16 or wider, within the bound.
No kernel may reach another device: no remote copies, remote signals or barrier semaphores. Data moves between devices by JAX's collectives and lax.ppermute only.
A program may use at most 128 MiB of HBM per device.

v0:
```python
import jax
import jax.numpy as jnp
from jax import lax
from jax.sharding import PartitionSpec as P

HEADS = 8
HEAD_DIM = 64
TOK_CTX = 128
D = 512
ROT = 16
HALF = 64


def layer_norm(values, scale_vec, shift_vec):
    center = values - jnp.mean(values, axis=-1, keepdims=True)
    spread = jnp.mean(center * center, axis=-1, keepdims=True)
    return center * lax.rsqrt(spread + 1e-05) * scale_vec + shift_vec


def rotate(tensor, cosine, sine_val):
    half_rot = cosine.shape[-1]
    cos_b = cosine[:, None, :]
    sin_b = sine_val[:, None, :]
    front_half = tensor[..., :half_rot]
    back_half = tensor[..., half_rot : 2 * half_rot]
    return jnp.concatenate(
        [
            front_half * cos_b - back_half * sin_b,
            back_half * cos_b + front_half * sin_b,
            tensor[..., 2 * half_rot :],
        ],
        axis=-1,
    )


def exact_gelu(tensor):
    return jax.nn.gelu(tensor, approximate=False)


def row_term(left_side, right_side):
    return lax.dot_general(
        left_side, right_side, (((0,), (0,)), ((), ())), preferred_element_type=jnp.float32
    )


def contract_last(left_side, right_side):
    return lax.dot_general(
        left_side, right_side, (((1,), (1,)), ((), ())), preferred_element_type=jnp.float32
    )


def per_device(
    inputs,
    block_order,
    ln1_gain,
    ln1_bias,
    w_qkv,
    b_qkv,
    w_attn_out,
    b_attn_out,
    ln2_gain,
    ln2_bias,
    w_up,
    b_up,
    w_down,
    b_down,
    cotangent,
):
    ctx_count = lax.axis_size("ctx")
    seq_len = TOK_CTX * ctx_count
    place_ctx = lax.axis_index("ctx")
    rows_all = jnp.arange(seq_len, dtype=jnp.int32)
    one_hot = (rows_all // HALF)[:, None] == jnp.arange(2 * ctx_count, dtype=jnp.int32)[None, :]
    block_of = jnp.sum(jnp.where(one_hot, block_order[None, :], 0), axis=1)
    pos_all = block_of * HALF + rows_all % HALF
    pos_here = lax.dynamic_slice_in_dim(pos_all, place_ctx * TOK_CTX, TOK_CTX)
    inverse = 10000.0 ** (-jnp.arange(ROT // 2, dtype=jnp.float32) * 2.0 / ROT)
    angles = pos_here.astype(jnp.float32)[:, None] * inverse[None, :]
    cosine = jnp.cos(angles)
    sine_val = jnp.sin(angles)
    gathered = (
        lax.all_gather(ln1_gain, "fsdp", axis=0, tiled=True),
        lax.all_gather(ln1_bias, "fsdp", axis=0, tiled=True),
        lax.all_gather(w_qkv, "fsdp", axis=0, tiled=True),
        lax.all_gather(b_qkv, "fsdp", axis=0, tiled=True),
        lax.all_gather(w_attn_out, "fsdp", axis=0, tiled=True),
        lax.all_gather(b_attn_out, "fsdp", axis=0, tiled=True),
        lax.all_gather(ln2_gain, "fsdp", axis=0, tiled=True),
        lax.all_gather(ln2_bias, "fsdp", axis=0, tiled=True),
        lax.all_gather(w_up, "fsdp", axis=0, tiled=True),
        lax.all_gather(b_up, "fsdp", axis=0, tiled=True),
        lax.all_gather(w_down, "fsdp", axis=0, tiled=True),
        lax.all_gather(b_down, "fsdp", axis=0, tiled=True),
    )
    (
        ln1_scale,
        ln1_shift,
        qkv_weight,
        qkv_bias,
        out_weight,
        out_bias,
        ln2_scale,
        ln2_shift,
        up_weight,
        up_bias,
        down_weight,
        down_bias,
    ) = gathered
    source = inputs[0].astype(jnp.float32)
    first_bf = layer_norm(
        source, ln1_scale.astype(jnp.float32), ln1_shift.astype(jnp.float32)
    ).astype(jnp.bfloat16)
    project = jnp.dot(first_bf, qkv_weight, preferred_element_type=jnp.float32) + qkv_bias.astype(
        jnp.float32
    )
    query_raw = project[:, :D].reshape(TOK_CTX, HEADS, HEAD_DIM)
    key_raw = project[:, D : 2 * D].reshape(TOK_CTX, HEADS, HEAD_DIM)
    query_bf = rotate(query_raw, cosine, sine_val).astype(jnp.bfloat16)
    key_bf = rotate(key_raw, cosine, sine_val).reshape(TOK_CTX, D).astype(jnp.bfloat16)
    value_bf = project[:, 2 * D :].astype(jnp.bfloat16)
    pieces = (
        lax.all_gather(key_bf, "ctx", axis=0, tiled=True),
        lax.all_gather(value_bf, "ctx", axis=0, tiled=True),
    )
    run_max = jnp.full((HEADS, TOK_CTX), -1e30, jnp.float32)
    rows_count = pieces[0].shape[0]
    key_piece = pieces[0].reshape(rows_count, HEADS, HEAD_DIM)
    value_piece = pieces[1].reshape(rows_count, HEADS, HEAD_DIM)
    key_pos = pos_all
    logits = (
        jnp.einsum("qhd,khd->hqk", query_bf, key_piece, preferred_element_type=jnp.float32) * 0.125
    )
    allowed = (pos_here[:, None] >= key_pos[None, :])[None]
    logits = jnp.where(allowed, logits, -1e30)
    new_max = jnp.maximum(run_max, jnp.max(logits, axis=-1))
    exp_weights = jnp.where(allowed, jnp.exp(logits - new_max[..., None]), 0.0)
    run_sum = jnp.sum(exp_weights, axis=-1)
    run_acc = jnp.einsum(
        "hqk,khd->hqd",
        exp_weights.astype(jnp.bfloat16),
        value_piece,
        preferred_element_type=jnp.float32,
    )
    run_max, run_sum, run_acc = (new_max, run_sum, run_acc)
    log_total = run_max + jnp.log(run_sum)
    mix_full = (run_acc / run_sum[..., None]).transpose(1, 0, 2)
    mix_bf = mix_full.reshape(TOK_CTX, D).astype(jnp.bfloat16)
    attn_out = jnp.dot(mix_bf, out_weight, preferred_element_type=jnp.float32) + out_bias.astype(
        jnp.float32
    )
    second_bf = layer_norm(
        source, ln2_scale.astype(jnp.float32), ln2_shift.astype(jnp.float32)
    ).astype(jnp.bfloat16)
    pre_act = jnp.dot(second_bf, up_weight, preferred_element_type=jnp.float32) + up_bias.astype(
        jnp.float32
    )
    hidden_bf = exact_gelu(pre_act).astype(jnp.bfloat16)
    result = (
        source
        + attn_out
        + jnp.dot(hidden_bf, down_weight, preferred_element_type=jnp.float32)
        + down_bias.astype(jnp.float32)
    )
    output = result.astype(jnp.bfloat16)[None]
    back_ln1, back_qkv, back_out, back_ln2, back_up, back_down = (
        ln1_scale,
        qkv_weight,
        out_weight,
        ln2_scale,
        up_weight,
        down_weight,
    )
    grad_out = cotangent[0]
    grad_out_f = grad_out.astype(jnp.float32)
    grad_hidden = contract_last(grad_out, back_down)
    unused_gelu, gelu_back = jax.vjp(exact_gelu, pre_act)
    grad_pre_bf = gelu_back(grad_hidden)[0].astype(jnp.bfloat16)
    grad_second = contract_last(grad_pre_bf, back_up)
    grad_mix_bf = (
        contract_last(grad_out, back_out).astype(jnp.bfloat16).reshape(TOK_CTX, HEADS, HEAD_DIM)
    )
    delta_rows = jnp.sum(grad_mix_bf.astype(jnp.float32) * mix_full, axis=-1).T
    pieces = (
        lax.all_gather(key_bf, "ctx", axis=0, tiled=True),
        lax.all_gather(value_bf, "ctx", axis=0, tiled=True),
    )
    rows_count = pieces[0].shape[0]
    key_piece = pieces[0].reshape(rows_count, HEADS, HEAD_DIM)
    value_piece = pieces[1].reshape(rows_count, HEADS, HEAD_DIM)
    key_pos = pos_all
    logits = (
        jnp.einsum("qhd,khd->hqk", query_bf, key_piece, preferred_element_type=jnp.float32) * 0.125
    )
    allowed = (pos_here[:, None] >= key_pos[None, :])[None]
    logits = jnp.where(allowed, logits, -1e30)
    attn_probs = jnp.where(allowed, jnp.exp(logits - log_total[..., None]), 0.0)
    probs_bf = attn_probs.astype(jnp.bfloat16)
    grad_probs = jnp.einsum(
        "qhd,khd->hqk", grad_mix_bf, value_piece, preferred_element_type=jnp.float32
    )
    grad_logits = (attn_probs * (grad_probs - delta_rows[..., None])).astype(jnp.bfloat16)
    probs_bf, grad_logits = (probs_bf, grad_logits)
    grad_query = 0.125 * jnp.einsum(
        "hqk,khd->qhd", grad_logits, key_piece, preferred_element_type=jnp.float32
    )
    key_grad = 0.125 * jnp.einsum(
        "hqk,qhd->khd", grad_logits, query_bf, preferred_element_type=jnp.float32
    ).reshape(rows_count, D)
    value_grad = jnp.einsum(
        "hqk,qhd->khd", probs_bf, grad_mix_bf, preferred_element_type=jnp.float32
    ).reshape(rows_count, D)
    key_terms = key_grad
    value_terms = value_grad
    grad_query, key_terms, value_terms = (grad_query, key_terms, value_terms)
    grad_key, grad_value = (
        lax.psum_scatter(
            key_terms.astype(jnp.bfloat16), "ctx", scatter_dimension=0, tiled=True
        ).astype(jnp.float32),
        lax.psum_scatter(
            value_terms.astype(jnp.bfloat16), "ctx", scatter_dimension=0, tiled=True
        ).astype(jnp.float32),
    )

    def turn_fn(tensor):
        return rotate(tensor, cosine, sine_val)

    unused_turn, turn_back = jax.vjp(turn_fn, query_raw)
    grad_query_raw = turn_back(grad_query)[0].reshape(TOK_CTX, D)
    grad_key_raw = turn_back(grad_key.reshape(TOK_CTX, HEADS, HEAD_DIM))[0].reshape(TOK_CTX, D)
    grad_project_bf = jnp.concatenate([grad_query_raw, grad_key_raw, grad_value], axis=1).astype(
        jnp.bfloat16
    )
    grad_first = contract_last(grad_project_bf, back_qkv)
    unused_one, norm_one_back = jax.vjp(
        layer_norm, source, back_ln1.astype(jnp.float32), ln1_shift.astype(jnp.float32)
    )
    grad_src_one, grad_scale_one, grad_shift_one = norm_one_back(grad_first)
    unused_two, norm_two_back = jax.vjp(
        layer_norm, source, back_ln2.astype(jnp.float32), ln2_shift.astype(jnp.float32)
    )
    grad_src_two, grad_scale_two, grad_shift_two = norm_two_back(grad_second)
    grad_inputs = (grad_out_f + grad_src_one + grad_src_two)[None]
    grad_qkv_bias = jnp.sum(grad_project_bf.astype(jnp.float32), axis=0)
    grad_out_bias = jnp.sum(grad_out_f, axis=0)
    grad_up_bias = jnp.sum(grad_pre_bf.astype(jnp.float32), axis=0)
    part_qkv = lax.psum_scatter(
        row_term(first_bf, grad_project_bf).astype(jnp.bfloat16),
        "fsdp",
        scatter_dimension=0,
        tiled=True,
    )
    part_attn = lax.psum_scatter(
        row_term(mix_bf, grad_out).astype(jnp.bfloat16), "fsdp", scatter_dimension=0, tiled=True
    )
    part_up = lax.psum_scatter(
        row_term(second_bf, grad_pre_bf).astype(jnp.bfloat16),
        "fsdp",
        scatter_dimension=0,
        tiled=True,
    )
    part_down = lax.psum_scatter(
        row_term(hidden_bf, grad_out).astype(jnp.bfloat16), "fsdp", scatter_dimension=0, tiled=True
    )
    small_parts = (
        lax.psum_scatter(grad_scale_one, "fsdp", scatter_dimension=0, tiled=True),
        lax.psum_scatter(grad_shift_one, "fsdp", scatter_dimension=0, tiled=True),
        lax.psum_scatter(grad_qkv_bias, "fsdp", scatter_dimension=0, tiled=True),
        lax.psum_scatter(grad_out_bias, "fsdp", scatter_dimension=0, tiled=True),
        lax.psum_scatter(grad_scale_two, "fsdp", scatter_dimension=0, tiled=True),
        lax.psum_scatter(grad_shift_two, "fsdp", scatter_dimension=0, tiled=True),
        lax.psum_scatter(grad_up_bias, "fsdp", scatter_dimension=0, tiled=True),
        lax.psum_scatter(grad_out_bias, "fsdp", scatter_dimension=0, tiled=True),
    )
    totals = (
        lax.psum(small_parts[0].astype(jnp.bfloat16), "ctx").astype(jnp.float32),
        lax.psum(small_parts[1].astype(jnp.bfloat16), "ctx").astype(jnp.float32),
        lax.psum(part_qkv, "ctx").astype(jnp.float32),
        lax.psum(small_parts[2].astype(jnp.bfloat16), "ctx").astype(jnp.float32),
        lax.psum(part_attn, "ctx").astype(jnp.float32),
        lax.psum(small_parts[3].astype(jnp.bfloat16), "ctx").astype(jnp.float32),
        lax.psum(small_parts[4].astype(jnp.bfloat16), "ctx").astype(jnp.float32),
        lax.psum(small_parts[5].astype(jnp.bfloat16), "ctx").astype(jnp.float32),
        lax.psum(part_up, "ctx").astype(jnp.float32),
        lax.psum(small_parts[6].astype(jnp.bfloat16), "ctx").astype(jnp.float32),
        lax.psum(part_down, "ctx").astype(jnp.float32),
        lax.psum(small_parts[7].astype(jnp.bfloat16), "ctx").astype(jnp.float32),
    )
    return (
        output,
        grad_inputs,
        totals[0],
        totals[1],
        totals[2],
        totals[3],
        totals[4],
        totals[5],
        totals[6],
        totals[7],
        totals[8],
        totals[9],
        totals[10],
        totals[11],
    )


def solution(mesh):
    placed = (
        P("fsdp", "ctx", None),
        P(),
        P("fsdp"),
        P("fsdp"),
        P("fsdp", None),
        P("fsdp"),
        P("fsdp", None),
        P("fsdp"),
        P("fsdp"),
        P("fsdp"),
        P("fsdp", None),
        P("fsdp"),
        P("fsdp", None),
        P("fsdp"),
        P("fsdp", "ctx", None),
    )
    return jax.shard_map(
        per_device,
        mesh=mesh,
        in_specs=placed,
        out_specs=(
            P("fsdp", "ctx", None),
            P("fsdp", "ctx", None),
            P("fsdp"),
            P("fsdp"),
            P("fsdp", None),
            P("fsdp"),
            P("fsdp", None),
            P("fsdp"),
            P("fsdp"),
            P("fsdp"),
            P("fsdp", None),
            P("fsdp"),
            P("fsdp", None),
            P("fsdp"),
        ),
        check_vma=False,
    )
```

profile of v0, /device:TPU:0, one launch (start us, length us, event | category | flops | bytes accessed | tf_op | source)
XLA Modules:
  0.0 498.5 jit_solution(901221746316520825)
XLA Ops:
  8.0 12.7 %all-gather = bf16[4,1,128]{2,1,0:T(2,128)(2,1)S(1)} all-gather(bf16[1,1,128]{2,1,0:T(2,128)(2,1)} %bitcast.186), channel_id=1, replica_groups=mesh['ctx'=8,'fsdp'=4] {'fsdp'}, dimensions={0}, use_global_device_ids=true | all-gather | bytes 1280 | tf_op jit(solution)/shard_map/all_gather | solution.py:82
  20.7 7.9 %all-gather.1 = bf16[4,1,128]{2,1,0:T(2,128)(2,1)S(1)} all-gather(bf16[1,1,128]{2,1,0:T(2,128)(2,1)} %bitcast.187), channel_id=1, replica_groups=mesh['ctx'=8,'fsdp'=4] {'fsdp'}, dimensions={0}, use_global_device_ids=true | all-gather | bytes 1280 | tf_op jit(solution)/shard_map/all_gather | solution.py:83
  29.3 12.0 %all-gather.2 = bf16[4,1,384]{2,1,0:T(2,128)(2,1)S(1)} all-gather(bf16[1,1,384]{2,1,0:T(2,128)(2,1)S(1)} %reshape.255), channel_id=1, replica_groups=mesh['ctx'=8,'fsdp'=4] {'fsdp'}, dimensions={0}, use_global_device_ids=true | all-gather | bytes 3840 | tf_op jit(solution)/shard_map/all_gather | solution.py:85
  42.4 1.1 fusion.51
  43.5 6.0 %all-gather.14.cloned.1.call-done = bf16[512,1536]{1,0:T(8,128)(2,1)} async-done(((bf16[128,1536]{1,0:T(8,128)(2,1)}), bf16[512,1536]{1,0:T(8,128)(2,1)}) %all-gather.14.cloned.1.call-update) | async-done | bytes 1572880 | tf_op jit(solution)/shard_map/all_gather | solution.py:84
  49.5 1.9 convolution_add_fusion
  55.5 15.7 %all_gather.50 = bf16[512,512]{1,0:T(8,128)(2,1)S(1)} all-gather(bf16[128,512]{1,0:T(8,128)(2,1)S(1)} %copy-done.18), channel_id=1, replica_groups=mesh['ctx'=8,'fsdp'=4] {'fsdp'}, dimensions={0}, use_global_device_ids=true | all-gather | bytes 655360 | tf_op jit(solution)/shard_map/all_gather | solution.py:86
  71.8 3.0 all-gather.18.cloned.1.call-done
  74.8 1.5 copy.50
  76.3 24.4 %all-gather.16.cloned.1.call-done = bf16[1024,512]{0,1:T(8,128)(2,1)} async-done(((bf16[128,512]{0,1:T(8,128)(2,1)}), bf16[1024,512]{0,1:T(8,128)(2,1)}) %all-gather.16.cloned.1.call-update) | async-done | bytes 1048592 | tf_op jit(solution)/shard_map/all_gather | solution.py:122
  100.7 2.2 fusion.3
  103.0 1.3 fusion
  104.2 1.3 multiply_reduce_fusion
  105.6 3.0 multiply_convert_fusion
  108.6 1.4 multiply_convert_fusion.1
  110.0 2.3 copy.52
  112.4 4.6 fusion.14
  117.0 2.3 copy.54
  119.4 11.0 %all-gather.4 = bf16[4,1,128]{2,1,0:T(2,128)(2,1)S(1)} all-gather(bf16[1,1,128]{2,1,0:T(2,128)(2,1)S(1)} %bitcast.188), channel_id=1, replica_groups=mesh['ctx'=8,'fsdp'=4] {'fsdp'}, dimensions={0}, use_global_device_ids=true | all-gather | bytes 1280 | tf_op jit(solution)/shard_map/all_gather | solution.py:88
  130.4 7.6 %all-gather.5 = bf16[4,1,128]{2,1,0:T(2,128)(2,1)S(1)} all-gather(bf16[1,1,128]{2,1,0:T(2,128)(2,1)S(1)} %bitcast.189), channel_id=1, replica_groups=mesh['ctx'=8,'fsdp'=4] {'fsdp'}, dimensions={0}, use_global_device_ids=true | all-gather | bytes 1280 | tf_op jit(solution)/shard_map/all_gather | solution.py:89
  138.0 12.0 %all-gather.6 = bf16[4,1,512]{2,1,0:T(2,128)(2,1)S(1)} all-gather(bf16[1,1,512]{2,1,0:T(2,128)(2,1)S(1)} %reshape.263), channel_id=1, replica_groups=mesh['ctx'=8,'fsdp'=4] {'fsdp'}, dimensions={0}, use_global_device_ids=true | all-gather | bytes 5120 | tf_op jit(solution)/shard_map/all_gather | solution.py:91
  150.0 1.1 convolution_convert_fusion.3
  151.3 5.6 %multiply_convert_fusion.2 = (bf16[128,2048]{1,0:T(8,128)(2,1)S(1)}, f32[128,2048]{1,0:T(8,128)}, f32[128,2048]{1,0:T(8,128)}) fusion(f32[2048]{0:T(1024)S(1)} %bitcast.185, bf16[512,2048]{1,0:T(8,128)(2,1)} %all-gather.20.cloned.1.call-done, bf16[1,128,512]{2,1,0:T(8,128)(2,1)S(1)} %copy-done.1, f32[512]{0:T(512)S(1)} %bitcast.181, f32[512]{0:T(512)S(1)} %bitcast.173, ...), kind=kOutput, calls=%fused_computation.39 | convolution fusion | flops 286130176 | bytes 4862976 | tf_op jit(solution)/shard_map/dot_general | solution.py:154
  157.0 37.4 %all-gather.22.cloned.1.call-done = bf16[2048,512]{1,0:T(8,128)(2,1)} async-done(((bf16[512,512]{1,0:T(8,128)(2,1)}), bf16[2048,512]{1,0:T(8,128)(2,1)}) %all-gather.22.cloned.1.call-update) | async-done | bytes 2097168 | tf_op jit(solution)/shard_map/all_gather | solution.py:92
  194.4 3.7 convert_reduce_fusion
  198.9 2.2 convolution_convert_fusion.1
  201.1 2.0 convolution_convert_fusion
  203.2 2.1 fusion.22
  206.0 26.2 %reduce-scatter.19.cloned.1.call-done = bf16[128,512]{1,0:T(8,128)(2,1)} async-done(((bf16[1024,512]{1,0:T(8,128)(2,1)}), bf16[128,512]{1,0:T(8,128)(2,1)}) %reduce-scatter.19.cloned.1.call-update) | async-done | bytes 131088
  232.2 1.0 copy.53
  234.0 37.5 %reduce-scatter.21.cloned.1.call-done = bf16[128,512]{1,0:T(8,128)(2,1)} async-done(((bf16[1024,512]{1,0:T(8,128)(2,1)}), bf16[128,512]{1,0:T(8,128)(2,1)}) %reduce-scatter.21.cloned.1.call-update) | async-done | bytes 131088
  272.5 1.2 add_convert_fusion.1
  274.4 2.5 convolution_convert_fusion.2
  277.0 1.2 dynamic-slice
  280.2 11.1 %all-gather.3 = bf16[4,1,128]{2,1,0:T(2,128)(2,1)S(1)} all-gather(bf16[1,1,128]{2,1,0:T(2,128)(2,1)} %bitcast.190), channel_id=1, replica_groups=mesh['ctx'=8,'fsdp'=4] {'fsdp'}, dimensions={0}, use_global_device_ids=true | all-gather | bytes 1280 | tf_op jit(solution)/shard_map/all_gather | solution.py:87
  291.3 7.7 %all-gather.7 = bf16[4,1,128]{2,1,0:T(2,128)(2,1)S(1)} all-gather(bf16[1,1,128]{2,1,0:T(2,128)(2,1)} %bitcast.191), channel_id=1, replica_groups=mesh['ctx'=8,'fsdp'=4] {'fsdp'}, dimensions={0}, use_global_device_ids=true | all-gather | bytes 1280 | tf_op jit(solution)/shard_map/all_gather | solution.py:93
  299.1 2.6 fusion.93
  301.8 1.2 fusion.18
  303.0 1.1 fusion.24
  305.0 34.9 %reduce-scatter.15.cloned.1.call-done = bf16[128,2048]{1,0:T(8,128)(2,1)} async-done(((bf16[512,2048]{1,0:T(8,128)(2,1)}), bf16[128,2048]{1,0:T(8,128)(2,1)}) %reduce-scatter.15.cloned.1.call-update) | async-done | bytes 524304 | tf_op jit(solution)/shard_map/reduce_scatter | solution.py:255
  339.9 45.4 %reduce-scatter.17.cloned.1.call-done = bf16[512,512]{1,0:T(8,128)(2,1)} async-done(((bf16[2048,512]{1,0:T(8,128)(2,1)}), bf16[512,512]{1,0:T(8,128)(2,1)}) %reduce-scatter.17.cloned.1.call-update) | async-done | bytes 524304 | tf_op jit(solution)/shard_map/reduce_scatter | solution.py:261
  385.4 36.9 %reduce-scatter.11.cloned.1.call-done = bf16[128,1536]{1,0:T(8,128)(2,1)} async-done(((bf16[512,1536]{1,0:T(8,128)(2,1)}), bf16[128,1536]{1,0:T(8,128)(2,1)}) %reduce-scatter.11.cloned.1.call-update) | async-done | bytes 393232 | tf_op jit(solution)/shard_map/reduce_scatter | solution.py:246
  424.5 17.0 %all-reduce.13 = (bf16[512]{0:T(512)(128)(2,1)S(1)}, bf16[512]{0:T(512)(128)(2,1)S(1)}, bf16[1536]{0:T(1024)(128)(2,1)S(1)}, bf16[512]{0:T(512)(128)(2,1)S(1)}, ...) all-reduce(f32[512]{0:T(512)S(1)} %get-tuple-element.23, ...), channel_id=4, replica_groups=mesh['ctx'=8,'fsdp'=4] {'fsdp'}, use_global_device_ids=true, to_apply=%region_13.14.clone | all-reduce | flops 6144 | bytes 36864
  442.1 12.1 %all-reduce.14 = (bf16[128]{0:T(256)(128)(2,1)S(1)}, bf16[128]{0:T(256)(128)(2,1)S(1)}, bf16[384]{0:T(512)(128)(2,1)S(1)}, bf16[128]{0:T(256)(128)(2,1)S(1)}, bf...) all-reduce(bf16[128]{0:T(256)(128)(2,1)S(1)} %dynamic-slice.27, ...), channel_id=1, replica_groups=mesh['ctx'=8,'fsdp'=4] {'ctx'}, use_global_device_ids=true, to_apply=%region_14.15 | all-reduce | flops 1536 | bytes 6144 | tf_op jit(solution)/shard_map/psum | solution.py:275
  457.4 26.7 %all-reduce.18.cloned.1.call-done = (bf16[128,1536]{1,0:T(8,128)(2,1)}, bf16[128,512]{1,0:T(8,128)(2,1)}, bf16[128,2048]{1,0:T(8,128)(2,1)}, bf16[512,512]{1,0:T(8,128)(2,1)}) async-done(((bf16[128,1536]{1,0:T(8,128)(2,1)}, bf16[128,512]{1,0:T(8,128)(2,1)}, bf16[128,2048]{1,0:T(8,128)(2,1)}, bf16[512,512]{1,0:T(8,128)(2,1)}), (bf16[128,1536]{1,0:T(8,128)(2,1)}, bf16[128,512]{1,0:T(8,128)(2,1)}, ...) | async-done | bytes 1572880 | tf_op jit(solution)/shard_map/psum | solution.py:277
  484.2 2.2 convert_element_type.225
  486.3 2.1 convert_element_type.230
  488.5 2.0 convert_element_type.212
  (158 shorter events, 19.5 us)
Async XLA Ops:
  7.2 48.3 %copy-start.18 = (bf16[128,512]{1,0:T(8,128)(2,1)S(1)}, bf16[128,512]{1,0:T(8,128)(2,1)}, u32[]{:S(2)}) copy-start(bf16[128,512]{1,0:T(8,128)(2,1)} %param.21) | copy-start | bytes 393220
  7.2 64.0 %copy-start.4 = (bf16[1,128,512]{2,1,0:T(8,128)(2,1)S(1)}, bf16[1,128,512]{2,1,0:T(8,128)(2,1)}, u32[]{:S(2)}) copy-start(bf16[1,128,512]{2,1,0:T(8,128)(2,1)} %param.29) | copy-start | bytes 393220
  7.2 42.3 %all-gather.14.cloned.1.call-start = ((), (), s32[]{:S(2)}) async-start(), calls=%async_computation.6 | async-start | bytes 1966080 | tf_op jit(solution)/shard_map/all_gather | solution.py:84
  7.9 66.9 %all-gather.18.cloned.1.call-start = ((), (), s32[]{:S(2)}) async-start(), calls=%async_computation.8 | async-start | bytes 1179648 | tf_op jit(solution)/shard_map/all_gather | solution.py:123
  28.6 24.9 %copy-start.20 = (f32[4,1,128]{2,1,0:T(1,128)}, f32[4,1,128]{2,1,0:T(1,128)S(1)}, u32[]{:S(2)}) copy-start(f32[4,1,128]{2,1,0:T(1,128)S(1)} %convert_element_type.232) | copy-start | bytes 6148
  42.4 11.2 %copy-start.21 = (f32[128]{0:T(128)}, f32[128]{0:T(128)S(1)}, u32[]{:S(2)}) copy-start(f32[128]{0:T(128)S(1)} %broadcast_multiply_fusion) | copy-start | bytes 1540
  43.5 10.1 %copy-start.29 = (f32[128]{0:T(128)}, f32[128]{0:T(128)S(1)}, u32[]{:S(2)}) copy-start(f32[128]{0:T(128)S(1)} %fusion.51) | copy-start | bytes 1540
  43.5 8.8 %copy-start.25 = (f32[128]{0:T(128)}, f32[128]{0:T(128)S(1)}, u32[]{:S(2)}) copy-start(f32[128]{0:T(128)S(1)} %fusion.72) | copy-start | bytes 1540
  52.2 48.6 %all-gather.16.cloned.1.call-start = ((), (), s32[]{:S(2)}) async-start(), calls=%async_computation.7 | async-start | bytes 1179648 | tf_op jit(solution)/shard_map/all_gather | solution.py:122
  54.3 97.0 %all-gather.20.cloned.1.call-start = ((), (), s32[]{:S(2)}) async-start(), calls=%async_computation.9 | async-start | bytes 2621440 | tf_op jit(solution)/shard_map/all_gather | solution.py:90
  54.9 139.5 %all-gather.22.cloned.1.call-start = ((), (), s32[]{:S(2)}) async-start(), calls=%async_computation.10 | async-start | bytes 2621440 | tf_op jit(solution)/shard_map/all_gather | solution.py:92
  55.5 176.8 %reduce-scatter.19.cloned.1.call-start = ((), (), s32[]{:S(2)}) async-start(), calls=%async_computation.15 | async-start | bytes 1179648
  76.3 27.9 %copy-start.16 = (bf16[1024,512]{0,1:T(8,128)(2,1)}, bf16[1024,512]{0,1:T(8,128)(2,1)S(1)}, u32[]{:S(2)}) copy-start(bf16[1024,512]{0,1:T(8,128)(2,1)S(1)} %copy.50) | copy-start | bytes 3145732
  102.9 2.6 copy-start
  105.5 44.5 %copy-start.17 = (bf16[128,8,64]{0,2,1:T(8,128)(2,1)}, bf16[128,8,64]{0,2,1:T(8,128)(2,1)S(1)}, u32[]{:S(2)}) copy-start(bf16[128,8,64]{0,2,1:T(8,128)(2,1)S(1)} %get-tuple-element.59) | copy-start | bytes 393220
  112.3 7.1 %copy-start.32 = (bf16[128]{0:T(256)(128)(2,1)S(1)}, bf16[128]{0:T(256)(128)(2,1)}, u32[]{:S(2)}) copy-start(bf16[128]{0:T(256)(128)(2,1)} %param.23) | copy-start | bytes 772
  112.3 18.0 %copy-start.33 = (bf16[128]{0:T(256)(128)(2,1)S(1)}, bf16[128]{0:T(256)(128)(2,1)}, u32[]{:S(2)}) copy-start(bf16[128]{0:T(256)(128)(2,1)} %param.24) | copy-start | bytes 772
  112.4 25.6 %copy-start.31 = (bf16[512]{0:T(512)(128)(2,1)S(1)}, bf16[512]{0:T(512)(128)(2,1)}, u32[]{:S(2)}) copy-start(bf16[512]{0:T(512)(128)(2,1)} %param.26) | copy-start | bytes 3076
  112.4 39.0 %copy-start.1 = (bf16[1,128,512]{2,1,0:T(8,128)(2,1)S(1)}, bf16[1,128,512]{2,1,0:T(8,128)(2,1)}, u32[]{:S(2)}) copy-start(bf16[1,128,512]{2,1,0:T(8,128)(2,1)} %param.15) | copy-start | bytes 393220
  112.4 159.1 %reduce-scatter.21.cloned.1.call-start = ((), (), s32[]{:S(2)}) async-start(), calls=%async_computation.16 | async-start | bytes 1179648
  119.3 185.7 %reduce-scatter.13.cloned.1.call-start = ((), (), s32[]{:S(2)}) async-start(), calls=%async_computation.12 | async-start | bytes 655360 | tf_op jit(solution)/shard_map/reduce_scatter | solution.py:252
  151.1 188.8 %reduce-scatter.15.cloned.1.call-start = ((), (), s32[]{:S(2)}) async-start(), calls=%async_computation.13 | async-start | bytes 2621440 | tf_op jit(solution)/shard_map/reduce_scatter | solution.py:255
  157.0 41.9 %copy-start.22 = (f32[128]{0:T(128)S(1)}, f32[128]{0:T(128)}, u32[]{:S(2)}) copy-start(f32[128]{0:T(128)} %copy-done.21) | copy-start | bytes 1540
  157.0 41.9 %copy-start.26 = (f32[128]{0:T(128)S(1)}, f32[128]{0:T(128)}, u32[]{:S(2)}) copy-start(f32[128]{0:T(128)} %copy-done.25) | copy-start | bytes 1540
  198.1 0.8 copy-start.3
  201.1 184.3 %reduce-scatter.17.cloned.1.call-start = ((), (), s32[]{:S(2)}) async-start(), calls=%async_computation.14 | async-start | bytes 2621440 | tf_op jit(solution)/shard_map/reduce_scatter | solution.py:261
  203.2 219.1 %reduce-scatter.11.cloned.1.call-start = ((), (), s32[]{:S(2)}) async-start(), calls=%async_computation.11 | async-start | bytes 1966080 | tf_op jit(solution)/shard_map/reduce_scatter | solution.py:246
  272.5 26.6 %copy-start.7 = (bf16[128,512]{0,1:T(8,128)(2,1)}, bf16[128,512]{0,1:T(8,128)(2,1)S(1)}, u32[]{:S(2)}) copy-start(bf16[128,512]{0,1:T(8,128)(2,1)S(1)} %copy.55) | copy-start | bytes 393220
  272.5 30.5 %copy-start.2 = (bf16[2048,512]{1,0:T(8,128)(2,1)S(1)}, bf16[2048,512]{1,0:T(8,128)(2,1)}, u32[]{:S(2)}) copy-start(bf16[2048,512]{1,0:T(8,128)(2,1)} %all-gather.22.cloned.1.call-done) | copy-start | bytes 6291460
  273.7 0.7 copy-start.13
  273.8 25.3 %copy-start.10 = (bf16[128,8,64]{0,2,1:T(8,128)(2,1)}, bf16[128,8,64]{0,2,1:T(8,128)(2,1)S(1)}, u32[]{:S(2)}) copy-start(bf16[128,8,64]{0,2,1:T(8,128)(2,1)S(1)} %get-tuple-element.77) | copy-start | bytes 393220
  276.9 27.2 %copy-start.23 = (f32[128]{0:T(128)S(1)}, f32[128]{0:T(128)}, u32[]{:S(2)}) copy-start(f32[128]{0:T(128)} %copy-done.21) | copy-start | bytes 1540
  277.0 207.2 %all-reduce.18.cloned.1.call-start = ((), (), s32[]{:S(2)}) async-start(), calls=%async_computation.17 | async-start | bytes 3145728 | tf_op jit(solution)/shard_map/psum | solution.py:277
  280.2 23.9 %copy-start.6 = (bf16[512,1536]{1,0:T(8,128)(2,1)S(1)}, bf16[512,1536]{1,0:T(8,128)(2,1)}, u32[]{:S(2)}) copy-start(bf16[512,1536]{1,0:T(8,128)(2,1)} %all-gather.14.cloned.1.call-done) | copy-start | bytes 4718596
  280.2 23.9 %copy-start.14 = (bf16[128,8,64]{0,2,1:T(8,128)(2,1)S(1)}, bf16[128,8,64]{0,2,1:T(8,128)(2,1)}, u32[]{:S(2)}) copy-start(bf16[128,8,64]{0,2,1:T(8,128)(2,1)} %copy-done.13) | copy-start | bytes 393220
  299.1 5.1 %copy-start.8 = (bf16[128,512]{0,1:T(8,128)(2,1)S(1)}, bf16[128,512]{0,1:T(8,128)(2,1)}, u32[]{:S(2)}) copy-start(bf16[128,512]{0,1:T(8,128)(2,1)} %copy-done.7) | copy-start | bytes 393220
  299.1 5.1 %copy-start.11 = (bf16[128,8,64]{0,2,1:T(8,128)(2,1)S(1)}, bf16[128,8,64]{0,2,1:T(8,128)(2,1)}, u32[]{:S(2)}) copy-start(bf16[128,8,64]{0,2,1:T(8,128)(2,1)} %copy-done.10) | copy-start | bytes 393220
  301.8 3.2 copy-start.30
  303.0 119.3 %copy-start.9 = (bf16[128,512]{0,1:T(8,128)(2,1)S(1)}, bf16[128,512]{0,1:T(8,128)(2,1)}, u32[]{:S(2)}) copy-start(bf16[128,512]{0,1:T(8,128)(2,1)} %copy-done.7) | copy-start | bytes 393220
  303.0 119.3 %copy-start.12 = (bf16[128,8,64]{0,2,1:T(8,128)(2,1)S(1)}, bf16[128,8,64]{0,2,1:T(8,128)(2,1)}, u32[]{:S(2)}) copy-start(bf16[128,8,64]{0,2,1:T(8,128)(2,1)} %copy-done.10) | copy-start | bytes 393220
  303.0 119.3 %copy-start.15 = (bf16[128,8,64]{0,2,1:T(8,128)(2,1)S(1)}, bf16[128,8,64]{0,2,1:T(8,128)(2,1)}, u32[]{:S(2)}) copy-start(bf16[128,8,64]{0,2,1:T(8,128)(2,1)} %copy-done.13) | copy-start | bytes 393220
  303.0 120.5 %copy-start.5 = (bf16[1,128,512]{2,1,0:T(8,128)(2,1)S(1)}, bf16[1,128,512]{2,1,0:T(8,128)(2,1)}, u32[]{:S(2)}) copy-start(bf16[1,128,512]{2,1,0:T(8,128)(2,1)} %param.29) | copy-start | bytes 393220
  304.2 119.4 %copy-start.24 = (f32[128]{0:T(128)S(1)}, f32[128]{0:T(128)}, u32[]{:S(2)}) copy-start(f32[128]{0:T(128)} %copy-done.21) | copy-start | bytes 1540
  304.2 119.4 %copy-start.27 = (f32[128]{0:T(128)S(1)}, f32[128]{0:T(128)}, u32[]{:S(2)}) copy-start(f32[128]{0:T(128)} %copy-done.25) | copy-start | bytes 1540
  304.2 120.3 %copy-start.28 = (f32[2048]{0:T(1024)S(1)}, f32[2048]{0:T(1024)}, u32[]{:S(2)}) copy-start(f32[2048]{0:T(1024)} %get-tuple-element.75) | copy-start | bytes 24580
  455.4 36.3 %copy-start.34 = (f32[128]{0:T(128)}, f32[128]{0:T(128)S(1)}, u32[]{:S(2)}) copy-start(f32[128]{0:T(128)S(1)} %convert_element_type.219) | copy-start | bytes 1540
  484.2 6.3 %copy-start.19 = (bf16[128,512]{1,0:T(8,128)(2,1)S(1)}, bf16[128,512]{1,0:T(8,128)(2,1)}, u32[]{:S(2)}) copy-start(bf16[128,512]{1,0:T(8,128)(2,1)} %get-tuple-element.39) | copy-start | bytes 393220
Sparse Core Ops, SparseCore 0:
  9.6 39.8 all-gather.13
  52.3 22.4 all-gather.17
  77.3 23.4 all-gather.15
  102.2 46.1 all-gather.19
  149.7 44.6 all-gather.21
  197.4 34.7 reduce-scatter.18
  235.4 35.9 reduce-scatter.20
  273.7 21.6 reduce-scatter.12
  297.7 42.1 reduce-scatter.14
  342.2 43.1 reduce-scatter.16
  387.7 34.5 reduce-scatter.10
  425.7 58.3 all-reduce.17
where the time goes:
time: 499 us
  waiting for transfers between devices  281 us (56%)
  blocking collectives  127 us (25%)
  matrix products  39.6 us (8%)
  other arithmetic  18.8 us (4%)
  between operations  16.9 us (3%)
  local copies, waits for them, and re-layouts  15.2 us (3%)
    unnamed x14, waiting for transfers between devices  65.6 us
    reduce_scatter x1, waiting for transfers between devices, per_device(): lax.psum_scatter(row_term(hidden_bf, grad_out).astype(jnp.bfloat16), 'fsd...  45.4 us
    all_gather x1, waiting for transfers between devices, per_device(): lax.all_gather(w_down, 'fsdp', axis=0, tiled=True)  37.4 us
    reduce_scatter x1, waiting for transfers between devices, per_device(): lax.psum_scatter(row_term(first_bf, grad_project_bf).astype(jnp.bfloat16)...  36.9 us
    reduce_scatter x1, waiting for transfers between devices, per_device(): lax.psum_scatter(row_term(second_bf, grad_pre_bf).astype(jnp.bfloat16), '...  34.9 us
    psum x1, waiting for transfers between devices, per_device(): lax.psum(part_qkv, 'ctx').astype(jnp.float32)  26.7 us
    all_gather x1, waiting for transfers between devices, per_device(): lax.all_gather(key_bf, 'ctx', axis=0, tiled=True)  24.4 us
    unnamed x1, blocking collectives  17 us
  transfers between devices with their start and end apart: 12, of which 10 were waited for; matrix products, arithmetic and copies ran while one was open for 12% of the time, Pallas kernels for 0%

commit v1 on v0

v1 whole, which is shorter than its diff:
```python
import functools

import jax
import jax.numpy as jnp
import numpy as np
from jax import lax
from jax.experimental import pallas as pl
from jax.experimental.pallas import tpu as pltpu
from jax.sharding import PartitionSpec as P

HEADS = 8
HEAD_DIM = 64
D = 512
FF = 2048
ROT = 16
HALF = 64
TOK = 128
EPS = 1e-05
F32 = jnp.float32
BF16 = jnp.bfloat16
VMEM_LIMIT = 48 * 1024 * 1024


def mm(left, right, dims):
    return lax.dot_general(left, right, (dims, ((), ())), preferred_element_type=F32)


def mm_nn(left, right):
    return mm(left, right, ((1,), (0,)))


def mm_nt(left, right):
    return mm(left, right, ((1,), (1,)))


def mm_tn(left, right):
    return mm(left, right, ((0,), (0,)))


def vmem_call(body, out_shape, scratch=(), n_smem=0, n_in=0, cost=None, name=None):
    smem = pl.BlockSpec(memory_space=pltpu.SMEM)
    vmem = pl.BlockSpec(memory_space=pltpu.VMEM)
    return pl.pallas_call(
        body,
        out_shape=out_shape,
        in_specs=[smem] * n_smem + [vmem] * n_in,
        out_specs=jax.tree.map(lambda _: vmem, out_shape),
        scratch_shapes=list(scratch),
        compiler_params=pltpu.CompilerParams(vmem_limit_bytes=VMEM_LIMIT),
        cost_estimate=cost,
        name=name,
    )


def half_pick(block, odd, to_upper):
    moved = pltpu.roll(block, 64, 1)
    return jnp.where(odd, block if to_upper else moved, moved if to_upper else block)


def low_lanes(shape):
    return lax.broadcasted_iota(jnp.int32, shape, len(shape) - 1) % 128 < 64


def pack_body(nz, place, w_qkv, w_up, w_down, w_out, out_a, out_b, out_w):
    me = place[0]
    pair = me // 2
    odd = (me % 2) == 1
    lane = pl.multiple_of(pair * 128, 128)

    def take(ref, start):
        return ref[:, pl.ds(pl.multiple_of(start + lane, 128), 128)].astype(F32)

    rows = w_qkv.shape[0]
    low = low_lanes((rows, 128))
    q = half_pick(take(w_qkv, 0), odd, False)
    k = half_pick(take(w_qkv, D), odd, True)
    v = half_pick(take(w_qkv, 2 * D), odd, False)
    out_a[:, 0:128] = jnp.where(low, q, k).astype(BF16)
    out_a[:, 128:256] = jnp.where(low, v, 0.0).astype(BF16)
    span = FF // nz
    for z in range(0, nz, 2):
        even = half_pick(take(w_up, z * span), odd, False)
        later = half_pick(take(w_up, (z + 1) * span), odd, True)
        out_b[:, z * 64 : z * 64 + 128] = jnp.where(low, even, later).astype(BF16)
    down = w_down[pl.ds(pl.multiple_of(me * 64, 64), 64), :]
    out_b[0:64, 256:512] = down[:, 0:256]
    out_b[64:128, 256:512] = down[:, 256:512]
    out_w[...] = w_out[pl.ds(pl.multiple_of((me % 2) * 64, 64), 64), :]


def small_body(nz, place, *refs):
    pieces, out, held = refs[:nz], refs[nz], refs[nz + 1]
    me, zed = place[0], place[1]
    pair = me // 2
    odd = (me % 2) == 1
    for k in range(nz):
        held[zed ^ k] = pieces[k][...].astype(F32)
    out[...] = jnp.zeros_like(out)
    for z in range(nz):
        lanes = slice(z * 128, (z + 1) * 128)
        out[0:4, lanes] = held[z, 0:4, :]
        out[4:5, lanes] = held[z, 4:5, :] + held[z, 5:6, :]
    low = low_lanes((1, 128))

    def qkv_row(group):
        index = group * 4 + pair
        z = index // 3
        return held[z, pl.ds(6 + index - 3 * z, 1), :]

    q = half_pick(qkv_row(0), odd, False)
    k = half_pick(qkv_row(1), odd, True)
    v = half_pick(qkv_row(2), odd, False)
    out[5:6, 0:128] = jnp.where(low, q, k)
    out[5:6, 128:256] = jnp.where(low, v, 0.0)
    for z in range(0, nz, 2):
        even = half_pick(held[z, pl.ds(9 + pair, 1), :], odd, False)
        later = half_pick(held[z + 1, pl.ds(9 + pair, 1), :], odd, True)
        out[6:7, z * 64 : z * 64 + 128] = jnp.where(low, even, later)


def normalized(x):
    center = x - jnp.mean(x, axis=-1, keepdims=True)
    spread = jnp.mean(center * center, axis=-1, keepdims=True)
    inv = lax.rsqrt(spread + EPS)
    return center * inv, inv


def ff_body(n, nz, fast, place, *refs):
    pieces = refs[:n]
    n_w = nz if fast else 2
    weights = refs[n : n + n_w]
    params = refs[n + n_w]
    outs = refs[n + n_w + 1 :]
    n_pay = nz if fast else 2
    acc_o, acc_d, vec = outs[:3]
    pays = outs[3 : 3 + n_pay]
    w_up, w_down, norms, hiddens, dpres, gs, grad_up, grad_down = outs[3 + n_pay :]
    width = w_up.shape[1]
    zed = place[1]
    if fast:
        for k in range(nz):
            z = zed ^ k
            w_up[pl.ds(pl.multiple_of(z * 128, 128), 128), :] = weights[k][:, 0:256]
            rows = pl.ds(pl.multiple_of(z * 64, 64), 64)
            w_down[rows, 0:256] = weights[k][0:64, 256:512]
            w_down[rows, 256:512] = weights[k][64:128, 256:512]
    else:
        w_up[...] = weights[0][...]
        w_down[...] = weights[1][...]
    gain, shift = params[2:3, :], params[3:4, :]
    b_up = params[6:7, 0:width]
    g_gain = jnp.zeros((8, D), F32)
    g_shift = jnp.zeros((8, D), F32)
    g_sum = jnp.zeros((8, D), F32)
    g_bup = jnp.zeros((8, width), F32)

    def fold(values):
        return jnp.sum(values.reshape(values.shape[0] // 8, 8, values.shape[1]), axis=0)

    for p in range(n):
        rows = slice(p * TOK, (p + 1) * TOK)
        x = pieces[p][0:TOK, :].astype(F32)
        g = pieces[p][TOK : 2 * TOK, :]
        nhat, _ = normalized(x)
        norm = (nhat * gain + shift).astype(BF16)
        pre = mm_nn(norm, w_up[...]) + b_up
        cdf = 0.5 * (1.0 + lax.erf(pre * 0.7071067811865476))
        hidden = (pre * cdf).astype(BF16)
        slope = cdf + pre * (0.3989422804014327 * jnp.exp(-0.5 * pre * pre))
        dpre_f = mm_nt(g, w_down[...]) * slope
        dpre = dpre_f.astype(BF16)
        acc_o[rows, :] = mm_nn(hidden, w_down[...]).astype(acc_o.dtype)
        dnorm = mm_nt(dpre, w_up[...])
        acc_d[rows, :] = (dnorm * gain).astype(acc_d.dtype)
        g_gain += fold(dnorm * nhat)
        g_shift += fold(dnorm)
        g_sum += fold(g.astype(F32))
        g_bup += fold(dpre.astype(F32))
        norms[rows, :] = norm
        hiddens[rows, :] = hidden
        dpres[rows, :] = dpre
        gs[rows, :] = g
    vec[...] = jnp.zeros_like(vec)
    vec[2:3, :] = jnp.sum(g_gain, axis=0, keepdims=True)
    vec[3:4, :] = jnp.sum(g_shift, axis=0, keepdims=True)
    vec[4:5, :] = jnp.sum(g_sum, axis=0, keepdims=True)
    vec[6:7, 0:width] = jnp.sum(g_bup, axis=0, keepdims=True)
    up_t = mm_tn(dpres[...], norms[...])
    grad_up[...] = up_t.T.astype(BF16)
    grad_down[...] = mm_tn(hiddens[...], gs[...]).astype(BF16)
    if fast:
        for k in range(nz):
            z = zed ^ k
            pays[k][:, 0:256] = grad_up[pl.ds(pl.multiple_of(z * 128, 128), 128), :]
            rows = pl.ds(pl.multiple_of(z * 64, 64), 64)
            pays[k][0:64, 256:512] = grad_down[rows, 0:256]
            pays[k][64:128, 256:512] = grad_down[rows, 256:512]
    else:
        pays[0][...] = grad_up[...]
        pays[1][...] = grad_down[...]


def attn_body(n, nz, fast, order_list, place, order, *refs):
    seq = n * TOK
    qblk = min(256, seq)
    pieces = refs[:n]
    n_w = nz if fast else 1
    weights = refs[n : n + n_w]
    w_out, params, acc_o, acc_d, vec_in, cos_t, sin_t = refs[n + n_w : n + n_w + 7]
    outs = refs[n + n_w + 7 :]
    n_pay = nz if fast else 2
    keep_pay, send_pay, g_out = outs[:3]
    pays = outs[3 : 3 + n_pay]
    (w_all, norms, nhats, raw, qs, ks, vs, dms, mixs, dks, dvs, dqs, dqkvs, mixn, dqkvn, gs, grad_w, vec) = outs[3 + n_pay :]
    zed = place[1]
    if fast:
        for k in range(nz):
            w_all[pl.ds(pl.multiple_of((zed ^ k) * 128, 128), 128), :] = weights[k][...]
    else:
        w_all[...] = weights[0][...]
    gain, shift = params[0:1, :], params[1:2, :]
    bias = params[5:6, 0:256]

    def sorted_rows(block):
        return pl.ds(pl.multiple_of(order[block] * HALF, HALF), HALF)

    for p in range(n):
        rows = slice(p * TOK, (p + 1) * TOK)
        nhat, _ = normalized(pieces[p][0:TOK, :].astype(F32))
        g = pieces[p][TOK : 2 * TOK, :]
        norm = (nhat * gain + shift).astype(BF16)
        nhats[rows, :] = nhat
        norms[rows, :] = norm
        gs[rows, :] = g
        qkv = mm_nn(norm, w_all[...]) + bias
        dmix = mm_nt(g, w_out[...]).astype(BF16)
        for h in range(TOK // HALF):
            here = slice(h * HALF, (h + 1) * HALF)
            where = sorted_rows(p * (TOK // HALF) + h)
            raw[where, :] = qkv[here, :]
            dms[where, :] = dmix[here, :]

    lanes = lax.broadcasted_iota(jnp.int32, (qblk, 128), 1) % 64

    def swapped(t):
        return jnp.where(lanes < ROT // 2, pltpu.roll(t, 128 - ROT // 2, 1), pltpu.roll(t, ROT // 2, 1))

    for i in range(seq // qblk):
        rows = slice(i * qblk, (i + 1) * qblk)
        qk = raw[rows, 0:128]
        turned = (qk * cos_t[rows, :] + swapped(qk) * sin_t[rows, :]).astype(BF16)
        qs[rows, :] = turned[:, 0:64]
        ks[rows, :] = turned[:, 64:128]
        vs[rows, :] = raw[rows, 128:192].astype(BF16)

    dks[...] = jnp.zeros_like(dks)
    dvs[...] = jnp.zeros_like(dvs)
    for i in range(seq // qblk):
        rows = slice(i * qblk, (i + 1) * qblk)
        span = (i + 1) * qblk
        q = qs[rows, :]
        keys = ks[0:span, :]
        values = vs[0:span, :]
        s = mm_nt(q, keys) * 0.125
        q_at = lax.broadcasted_iota(jnp.int32, (qblk, span), 0) + i * qblk
        k_at = lax.broadcasted_iota(jnp.int32, (qblk, span), 1)
        s = jnp.where(q_at >= k_at, s, -1e30)
        top = jnp.max(s, axis=1, keepdims=True)
        e = jnp.exp(s - top)
        prob = e * (1.0 / jnp.sum(e, axis=1, keepdims=True))
        prob_b = prob.astype(BF16)
        mix = mm_nn(prob_b, values)
        mixs[rows, :] = mix.astype(BF16)
        dmix = dms[rows, :]
        delta = jnp.sum(dmix.astype(F32) * mix, axis=1, keepdims=True)
        dprob = mm_nt(dmix, values)
        ds = (prob * (dprob - delta)).astype(BF16)
        dqs[rows, 0:64] = mm_nn(ds, keys) * 0.125
        dks[:, 0:span] += mm_tn(q, ds)
        dvs[:, 0:span] += mm_tn(dmix, prob_b)
    dqs[:, 64:128] = dks[...].T * 0.125
    dqkvs[:, 128:192] = dvs[...].T.astype(BF16)
    dqkvs[:, 192:256] = jnp.zeros((seq, 64), BF16)
    for i in range(seq // qblk):
        rows = slice(i * qblk, (i + 1) * qblk)
        dqk = dqs[rows, :]
        dqkvs[rows, 0:128] = (dqk * cos_t[rows, :] - swapped(dqk) * sin_t[rows, :]).astype(BF16)

    scale = None
    if n > HEADS:
        scale = jnp.where(place[0] % (n // HEADS) == 0, 1.0, 0.0).astype(BF16)
    for b in range(seq // HALF):
        here = slice(b * HALF, (b + 1) * HALF)
        where = sorted_rows(b)
        mix, dqkv = mixs[where, :], dqkvs[where, :]
        if scale is not None:
            mix, dqkv = mix * scale, dqkv * scale
        mixn[here, :] = mix
        dqkvn[here, :] = dqkv

    g_gain = jnp.zeros((8, D), F32)
    g_shift = jnp.zeros((8, D), F32)
    g_bias = jnp.zeros((8, 256), F32)

    def fold(values):
        return jnp.sum(values.reshape(values.shape[0] // 8, 8, values.shape[1]), axis=0)

    for at, rel in enumerate(order_list):
        rows = slice(at * TOK, (at + 1) * TOK)
        dqkv = dqkvn[rows, :]
        part_o = mm_nn(mixn[rows, :], w_out[...]) + acc_o[rows, :].astype(F32)
        dnorm = mm_nt(dqkv, w_all[...])
        part_d = dnorm * gain + acc_d[rows, :].astype(F32)
        g_gain += fold(dnorm * nhats[rows, :])
        g_shift += fold(dnorm)
        g_bias += fold(dqkv.astype(F32))
        target = send_pay if rel % 2 else keep_pay
        target[rel // 2, :, 0:512] = part_o.astype(BF16)
        target[rel // 2, :, 512:1024] = part_d.astype(BF16)
    vec[...] = vec_in[...]
    vec[0:1, :] = jnp.sum(g_gain, axis=0, keepdims=True)
    vec[1:2, :] = jnp.sum(g_shift, axis=0, keepdims=True)
    vec[5:6, 0:256] = jnp.sum(g_bias, axis=0, keepdims=True)
    grad_w[...] = mm_tn(dqkvn[...], norms[...]).T.astype(BF16)
    g_out[...] = mm_tn(mixn[...], gs[...]).astype(BF16)
    if fast:
        tail = jnp.concatenate([vec[...], jnp.zeros((8, D), F32)], axis=0).astype(BF16)
        for k in range(nz):
            rows = pl.ds(pl.multiple_of((zed ^ k) * 128, 128), 128)
            pays[k][0:128, :] = grad_w[rows, :]
            pays[k][128:144, :] = tail[:, 0:256]
            pays[k][144:160, :] = tail[:, 256:512]
    else:
        pays[0][...] = grad_w[...]
        pays[1][...] = vec[...]


def close_body(place, x_ref, g_ref, params, *refs):
    parts, out, grad = refs[:-2], refs[-2], refs[-1]
    x = x_ref[...].astype(F32)
    nhat, inv = normalized(x)
    total = parts[0][...].astype(F32)
    for part in parts[1:]:
        total = total + part[...].astype(F32)
    out[...] = (x + total[:, 0:512] + params[4:5, :]).astype(BF16)
    dn = total[:, 512:1024]
    lead = jnp.mean(dn, axis=-1, keepdims=True)
    along = jnp.mean(dn * nhat, axis=-1, keepdims=True)
    grad[...] = g_ref[...].astype(F32) + inv * (dn - lead - nhat * along)


def sum_body(n_parts, *refs):
    out = refs[n_parts]
    total = refs[0][...].astype(F32)
    for ref in refs[1:n_parts]:
        total = total + ref[...].astype(F32)
    out[...] = total.astype(BF16)


def finish_body(n, nz, place, *refs):
    ffs, atts, wos = refs[:n], refs[n : 2 * n], refs[2 * n : 3 * n]
    (ln1g, ln1b, gqkv, bqkv, gout, bout, ln2g, ln2b, gup, bup, gdown, bdown) = refs[3 * n : 3 * n + 12]
    held_u, held_d, held_a, held_v, flat = refs[3 * n + 12 :]
    me, zed = place[0], place[1]
    span = FF // nz
    total = jnp.zeros((8, D), F32)
    for k in range(n):
        who = me ^ k
        held_u[who] = ffs[k][:, 0:256].astype(F32)
        rows = pl.ds(pl.multiple_of(who * 64, 64), 64)
        gdown[rows, 0:256] = ffs[k][0:64, 256:512].astype(F32)
        gdown[rows, 256:512] = ffs[k][64:128, 256:512].astype(F32)
        held_a[who] = atts[k][0:128, :].astype(F32)
        small = jnp.concatenate([atts[k][128:144, :].astype(F32)[0:8], atts[k][144:160, :].astype(F32)[0:8]], axis=1)
        held_v[who] = small
        total = total + small
    for h in range(0, n, 2):
        even, later = held_a[h], held_a[h + 1]
        low = low_lanes((128, 128))
        at = h * 64
        gqkv[:, at : at + 128] = jnp.where(low, even[:, 0:128], pltpu.roll(later[:, 0:128], 64, 1))
        gqkv[:, D + at : D + at + 128] = jnp.where(low, pltpu.roll(even[:, 0:128], 64, 1), later[:, 0:128])
        gqkv[:, 2 * D + at : 2 * D + at + 128] = jnp.where(low, even[:, 128:256], pltpu.roll(later[:, 128:256], 64, 1))
        for z in range(0, nz, 2):
            lanes = slice(z * 64, z * 64 + 128)
            e, l = held_u[h][:, lanes], held_u[h + 1][:, lanes]
            gup[:, z * span + at : z * span + at + 128] = jnp.where(low, e, pltpu.roll(l, 64, 1))
            gup[:, (z + 1) * span + at : (z + 1) * span + at + 128] = jnp.where(low, pltpu.roll(e, 64, 1), l)
        low = low_lanes((1, 128))
        e, l = held_v[h], held_v[h + 1]
        flat[h // 2 : h // 2 + 1, :] = jnp.where(low, e[5:6, 0:128], pltpu.roll(l[5:6, 0:128], 64, 1))
        flat[4 + h // 2 : 5 + h // 2, :] = jnp.where(low, pltpu.roll(e[5:6, 0:128], 64, 1), l[5:6, 0:128])
        flat[8 + h // 2 : 9 + h // 2, :] = jnp.where(low, e[5:6, 128:256], pltpu.roll(l[5:6, 128:256], 64, 1))
        lane = pl.ds(pl.multiple_of((zed // 2) * 128, 128), 128)
        odd = (zed % 2) == 1
        e = half_pick(held_v[h, 6:7, lane], odd, False)
        l = half_pick(held_v[h + 1, 6:7, lane], odd, True)
        bup[:, at : at + 128] = jnp.where(low, e, l)
    mine = pl.multiple_of((me % 2) * 64, 64)
    other = pl.multiple_of((1 - me % 2) * 64, 64)
    for parity, start in ((0, mine), (1, other)):
        acc = wos[parity][...].astype(F32)
        for k in range(parity + 2, n, 2):
            acc = acc + wos[k][...].astype(F32)
        gout[pl.ds(start, 64), :] = acc
    flat[12:20, :] = jnp.zeros((8, 128), F32)
    for r in range(3):
        bqkv[:, r * 128 : (r + 1) * 128] = flat[pl.ds(zed * 3 + r, 1), :]
    held_v[0] = total
    lane = pl.ds(pl.multiple_of(zed * 128, 128), 128)
    ln1g[...] = held_v[0, 0:1, lane]
    ln1b[...] = held_v[0, 1:2, lane]
    ln2g[...] = held_v[0, 2:3, lane]
    ln2b[...] = held_v[0, 3:4, lane]
    held_v[1] = total * (1.0 / n)
    bout[...] = held_v[1, 4:5, lane]
    bdown[...] = held_v[1, 4:5, lane]


def xor_pairs(size, k):
    return [(i, i ^ k) for i in range(size)]


def gather_ctx(value, n):
    got = {0: value}
    for k in range(2, n, 2):
        got[k] = lax.ppermute(value, "ctx", xor_pairs(n, k))
    for k in range(0, n, 2):
        got[k + 1] = lax.ppermute(got[k], "ctx", xor_pairs(n, 1))
    return [got[k] for k in range(n)]


def gather_fsdp(value, nz):
    return [value] + [lax.ppermute(value, "fsdp", xor_pairs(nz, k)) for k in range(1, nz)]


def swap_fsdp(values, nz):
    return [values[0]] + [lax.ppermute(values[k], "fsdp", xor_pairs(nz, k)) for k in range(1, nz)]


def rotary_tables(seq):
    pos = np.arange(seq, dtype=np.float32)
    inverse = (np.float32(10000.0) ** (-np.arange(ROT // 2, dtype=np.float32) * np.float32(2.0) / np.float32(ROT))).astype(np.float32)
    angles = (pos[:, None] * inverse[None, :]).astype(np.float32).astype(np.float64)
    cos_t = np.ones((seq, 64), np.float32)
    sin_t = np.zeros((seq, 64), np.float32)
    half = ROT // 2
    cos_t[:, 0:half] = np.cos(angles)
    cos_t[:, half:ROT] = np.cos(angles)
    sin_t[:, 0:half] = -np.sin(angles)
    sin_t[:, half:ROT] = np.sin(angles)
    return np.concatenate([cos_t, cos_t], axis=1), np.concatenate([sin_t, sin_t], axis=1)


def shape(dims, dtype=F32):
    return jax.ShapeDtypeStruct(dims, dtype)


def per_device(
    n,
    nz,
    inputs,
    block_order,
    ln1_gain,
    ln1_bias,
    w_qkv,
    b_qkv,
    w_attn_out,
    b_attn_out,
    ln2_gain,
    ln2_bias,
    w_up,
    b_up,
    w_down,
    b_down,
    cotangent,
):
    fast = n == HEADS and nz * 2 == HEADS
    seq = n * TOK
    width = FF // n
    me = lax.axis_index("ctx").astype(jnp.int32)
    zed = lax.axis_index("fsdp").astype(jnp.int32)
    place = jnp.stack([me, zed])
    x, g = inputs[0], cotangent[0]
    piece = jnp.concatenate([x, g], axis=0)
    order_list = list(range(n))
    blocks = TOK // HALF
    chunk_at = (jnp.arange(n, dtype=jnp.int32) ^ me)[:, None] * blocks + jnp.arange(blocks, dtype=jnp.int32)[None, :]
    pick = chunk_at.reshape(-1)[:, None] == jnp.arange(n * blocks, dtype=jnp.int32)[None, :]
    order = jnp.sum(jnp.where(pick, block_order[None, :], 0), axis=1).astype(jnp.int32)
    cos_t, sin_t = rotary_tables(seq)

    pieces = gather_ctx(piece, n)
    if fast:
        pack_a, pack_b, pack_w = vmem_call(
            functools.partial(pack_body, nz),
            (shape((D // nz, 256), BF16), shape((D // nz, 512), BF16), shape((HEAD_DIM, D), BF16)),
            n_smem=1,
            n_in=4,
            name="pack",
        )(place, w_qkv, w_up, w_down, w_attn_out)
        flat = jnp.concatenate([ln1_gain, ln1_bias, ln2_gain, ln2_bias, b_attn_out, b_down, b_qkv, b_up])
        rows = flat.shape[0] // 128
        flat = jnp.pad(flat.reshape(rows, 128), ((0, 16 - rows), (0, 0)))
        small = gather_fsdp(flat, nz)
        ff_w = gather_fsdp(pack_b, nz)
        attn_w = gather_fsdp(pack_a, nz)
        pairs = []
        for c in range(n):
            for z in range(nz):
                pairs.append((c * nz + z, (2 * z + c % 2) * nz + c // 2))
        head_w = lax.ppermute(pack_w, ("ctx", "fsdp"), pairs)
        params = vmem_call(
            functools.partial(small_body, nz),
            shape((8, D)),
            scratch=[pltpu.VMEM((nz, 16, 128), F32)],
            n_smem=1,
            n_in=nz,
            name="small",
        )(place, *small)
    else:
        whole = [
            lax.all_gather(v, "fsdp", axis=0, tiled=True)
            for v in (ln1_gain, ln1_bias, ln2_gain, ln2_bias, b_attn_out, b_down, b_qkv, b_up)
        ]
        whole = [v.astype(F32) for v in whole]
        head = me // (n // HEADS)
        bq = lax.dynamic_index_in_dim(whole[6].reshape(3, HEADS, HEAD_DIM), head, 1, False).reshape(-1)
        bu = lax.dynamic_index_in_dim(whole[7].reshape(n, width), me, 0, False)
        params = jnp.stack(
            [whole[0], whole[1], whole[2], whole[3], whole[4] + whole[5]]
            + [jnp.pad(bq, (0, D - 3 * HEAD_DIM)), jnp.pad(bu, (0, D - width)), jnp.zeros((D,), F32)]
        )
        wq = lax.dynamic_index_in_dim(w_qkv.reshape(-1, 3, HEADS, HEAD_DIM), head, 2, False).reshape(-1, 3 * HEAD_DIM)
        attn_w = [jnp.pad(lax.all_gather(wq, "fsdp", axis=0, tiled=True), ((0, 0), (0, 64)))]
        wu = lax.dynamic_slice_in_dim(w_up, me * width, width, 1)
        wd = lax.all_gather(w_down, "fsdp", axis=0, tiled=True)
        ff_w = [lax.all_gather(wu, "fsdp", axis=0, tiled=True), lax.dynamic_slice_in_dim(wd, me * width, width, 0)]
        wo = lax.all_gather(w_attn_out, "fsdp", axis=0, tiled=True)
        head_w = lax.dynamic_slice_in_dim(wo, head * HEAD_DIM, HEAD_DIM, 0)

    ff_pays = [shape((D // nz, 512), BF16)] * nz if fast else [shape((D, width), BF16), shape((width, D), BF16)]
    ff_out = vmem_call(
        functools.partial(ff_body, n, nz, fast),
        [shape((seq, D), BF16), shape((seq, D), BF16), shape((8, D))] + ff_pays,
        scratch=[
            pltpu.VMEM((D, width), BF16),
            pltpu.VMEM((width, D), BF16),
            pltpu.VMEM((seq, D), BF16),
            pltpu.VMEM((seq, width), BF16),
            pltpu.VMEM((seq, width), BF16),
            pltpu.VMEM((seq, D), BF16),
            pltpu.VMEM((D, width), BF16),
            pltpu.VMEM((width, D), BF16),
        ],
        n_smem=1,
        n_in=n + len(ff_w) + 1,
        cost=pl.CostEstimate(flops=12 * seq * D * width, bytes_accessed=8 * seq * D, transcendentals=2 * seq * width),
        name="feed_forward",
    )(place, *pieces, *ff_w, params)
    acc_o, acc_d, vec_ff = ff_out[:3]
    ff_pay = ff_out[3:]
    if fast:
        ff_got = swap_fsdp(ff_pay, nz)

    attn_pays = [shape((D // nz + 32, 256), BF16)] * nz if fast else [shape((D, 256), BF16), shape((8, D))]
    half = (n // 2, TOK, 2 * D)
    attn_out = vmem_call(
        functools.partial(attn_body, n, nz, fast, order_list),
        [shape(half, BF16), shape(half, BF16), shape((HEAD_DIM, D), BF16)] + attn_pays,
        scratch=[
            pltpu.VMEM((D, 256), BF16),
            pltpu.VMEM((seq, D), BF16),
            pltpu.VMEM((seq, D), F32),
            pltpu.VMEM((seq, 256), F32),
            pltpu.VMEM((seq, 64), BF16),
            pltpu.VMEM((seq, 64), BF16),
            pltpu.VMEM((seq, 64), BF16),
            pltpu.VMEM((seq, 64), BF16),
            pltpu.VMEM((seq, 64), BF16),
            pltpu.VMEM((64, seq), F32),
            pltpu.VMEM((64, seq), F32),
            pltpu.VMEM((seq, 128), F32),
            pltpu.VMEM((seq, 256), BF16),
            pltpu.VMEM((seq, 64), BF16),
            pltpu.VMEM((seq, 256), BF16),
            pltpu.VMEM((seq, D), BF16),
            pltpu.VMEM((D, 256), BF16),
            pltpu.VMEM((8, D), F32),
        ],
        n_smem=2,
        n_in=n + len(attn_w) + 7,
        cost=pl.CostEstimate(flops=14 * seq * seq * 64, bytes_accessed=12 * seq * D, transcendentals=seq * seq),
        name="attention",
    )(place, order, *pieces, *attn_w, head_w, params, acc_o, acc_d, vec_ff, cos_t, sin_t)
    keep_pay, send_pay, g_out = attn_out[:3]
    attn_pay = attn_out[3:]

    came = lax.ppermute(send_pay, "ctx", xor_pairs(n, 1))
    chip_sum = (keep_pay.astype(F32) + came.astype(F32)).astype(BF16)
    parts = [chip_sum[0]] + [lax.ppermute(chip_sum[k // 2], "ctx", xor_pairs(n, k)) for k in range(2, n, 2)]
    output, grad_inputs = vmem_call(
        close_body,
        (shape((TOK, D), BF16), shape((TOK, D))),
        n_smem=1,
        n_in=3 + len(parts),
        name="close",
    )(place, x, g, params, *parts)

    if fast:
        back = []
        for c in range(n):
            for z in range(nz):
                back.append(((2 * z + c % 2) * nz + c // 2, c * nz + z))
        out_got = lax.ppermute(g_out, ("ctx", "fsdp"), back)
        attn_got = swap_fsdp(attn_pay, nz)
        ff_sum = vmem_call(functools.partial(sum_body, nz), shape(ff_pay[0].shape, BF16), n_in=nz, name="sum_ff")(*ff_got)
        attn_sum = vmem_call(functools.partial(sum_body, nz), shape(attn_pay[0].shape, BF16), n_in=nz, name="sum_attn")(
            *attn_got
        )
        ff_all = gather_ctx(ff_sum, n)
        out_all = gather_ctx(out_got, n)
        attn_all = gather_ctx(attn_sum, n)
        dz = D // nz
        outs = vmem_call(
            functools.partial(finish_body, n, nz),
            [
                shape((1, dz)),
                shape((1, dz)),
                shape((dz, 3 * D)),
                shape((1, 3 * dz)),
                shape((dz, D)),
                shape((1, dz)),
                shape((1, dz)),
                shape((1, dz)),
                shape((dz, FF)),
                shape((1, FF // nz)),
                shape((FF // nz, D)),
                shape((1, dz)),
            ],
            scratch=[
                pltpu.VMEM((n, 128, 256), F32),
                pltpu.VMEM((8, 128), F32),
                pltpu.VMEM((n, 128, 256), F32),
                pltpu.VMEM((n, 8, D), F32),
                pltpu.VMEM((24, 128), F32),
            ],
            n_smem=1,
            n_in=3 * n,
            name="finish",
        )(place, *ff_all, *attn_all, *out_all)
        outs = [o.reshape(-1) if o.shape[0] == 1 else o for o in outs]
    else:
        everyone = ("ctx", "fsdp")
        head = me // (n // HEADS)
        g_up, g_down = ff_pay
        g_qkv, vec = attn_pay

        def own(full, axis=0):
            size = full.shape[axis] // nz
            return lax.dynamic_slice_in_dim(full, zed * size, size, axis)

        def spread(part, dims, index, axis):
            full = jnp.zeros(dims, part.dtype)
            return lax.psum(lax.dynamic_update_index_in_dim(full, part, index, axis), everyone).astype(F32)

        qkv_full = spread(g_qkv[:, 0:192].reshape(D, 3, HEAD_DIM), (D, 3, HEADS, HEAD_DIM), head, 2).reshape(D, 3 * D)
        out_full = spread(g_out, (HEADS, HEAD_DIM, D), head, 0).reshape(D, D)
        up_full = spread(g_up, (D, n, width), me, 1).reshape(D, FF)
        down_full = spread(g_down, (n, width, D), me, 0).reshape(FF, D)
        bq_full = spread(vec[5, 0:192].reshape(3, HEAD_DIM), (3, HEADS, HEAD_DIM), head, 1).reshape(3 * D)
        bu_full = spread(vec[6, 0:width], (n, width), me, 0).reshape(FF)
        flat = lax.psum(vec, everyone)
        b_full = flat[4] * (1.0 / n)
        outs = [own(v) for v in (flat[0], flat[1], qkv_full, bq_full, out_full, b_full)]
        outs += [own(v) for v in (flat[2], flat[3], up_full, bu_full, down_full, b_full)]
    return (output[None], grad_inputs[None], *outs)


def solution(mesh):
    rows, flat, tokens = P("fsdp", None), P("fsdp"), P("fsdp", "ctx", None)
    weights = (flat, flat, rows, flat, rows, flat, flat, flat, rows, flat, rows, flat)
    return jax.shard_map(
        functools.partial(per_device, mesh.shape["ctx"], mesh.shape["fsdp"]),
        mesh=mesh,
        in_specs=(tokens, P(), *weights, tokens),
        out_specs=(tokens, tokens, *weights),
        check_vma=False,
    )
```

time: 499 us -> 123 us (0.25)
  waiting for transfers between devices: 281 us -> 32.4 us
  blocking collectives: 127 us -> 0 us
  starting transfers between devices: 0.67 us -> 55.3 us
  matrix products: 39.6 us -> 0 us
  Pallas kernels: 0 us -> 19.3 us
  other arithmetic: 18.8 us -> 2.34 us
  between operations: 16.9 us -> 0.87 us
    reduce_scatter x4 -> x0, waiting for transfers between devices: 117 us -> none  [the longest x1 45.4 us: per_device(): lax.psum_scatter(row_term(hidden_bf, grad_out).astype(jnp.bfloat16), 'fsd...]
    all_gather x9 -> x0, blocking collectives: 97.7 us -> none  [the longest x1 15.7 us: per_device(): lax.all_gather(w_attn_out, 'fsdp', axis=0, tiled=True)]
    all_gather x5 -> x0, waiting for transfers between devices: 70.9 us -> none  [the longest x1 37.4 us: per_device(): lax.all_gather(w_down, 'fsdp', axis=0, tiled=True)]
    unnamed x14 -> x0, waiting for transfers between devices: 65.6 us -> none
    ppermute x0 -> x49, starting transfers between devices: none -> 55.3 us  [the longest x9 17.8 us: gather_fsdp(): lax.ppermute(value, 'fsdp', xor_pairs(nz, k))]
    dot_general x18 -> x0, matrix products: 39.6 us -> none  [the longest x4 7.79 us: row_term(): lax.dot_general(left_side, right_side, (((0,), (0,)), ((), ())), preferre...]
    ppermute x0 -> x49, waiting for transfers between devices: none -> 32.4 us  [the longest x12 10.8 us: gather_ctx(): got[k] = lax.ppermute(value, 'ctx', xor_pairs(n, k))]
    psum x1 -> x0, waiting for transfers between devices: 26.7 us -> none  [per_device(): lax.psum(part_qkv, 'ctx').astype(jnp.float32)]
  transfers between devices with their start and end apart: 12 -> 49, of which waited for: 10 -> 19; matrix products, arithmetic and copies ran while one was open for 12% -> 7% of each run, Pallas kernels for 0% -> 7%
where the time goes in v1:
time: 123 us
  starting transfers between devices  55.3 us (45%)
  waiting for transfers between devices  32.4 us (26%)
  Pallas kernels  19.3 us (16%)
  local copies, waits for them, and re-layouts  12.8 us (10%)
  other arithmetic  2.34 us (2%)
    ppermute x9, starting transfers between devices, gather_fsdp(): lax.ppermute(value, 'fsdp', xor_pairs(nz, k))  17.8 us
    ppermute x6, starting transfers between devices, swap_fsdp(): lax.ppermute(values[k], 'fsdp', xor_pairs(nz, k))  16.4 us
    ppermute x12, starting transfers between devices, gather_ctx(): got[k] = lax.ppermute(value, 'ctx', xor_pairs(n, k))  13.5 us
    unnamed x29, local copies, waits for them, and re-layouts  11.8 us
    ppermute x12, waiting for transfers between devices, gather_ctx(): got[k] = lax.ppermute(value, 'ctx', xor_pairs(n, k))  10.8 us
    pallas_call x1, Pallas kernels, per_device(): vmem_call(functools.partial(attn_body, n, nz, fast, order_list), [shape(h...  8.99 us
    ppermute x3, waiting for transfers between devices, per_device(): lax.ppermute(chip_sum[k // 2], 'ctx', xor_pairs(n, k))  6.75 us
    ppermute x9, waiting for transfers between devices, gather_fsdp(): lax.ppermute(value, 'fsdp', xor_pairs(nz, k))  6.27 us
  transfers between devices with their start and end apart: 49, of which 19 were waited for; matrix products, arithmetic and copies ran while one was open for 7% of the time, Pallas kernels for 7%

profile of v1, /device:TPU:0, one launch (start us, length us, event | category | flops | bytes accessed | tf_op | source)
XLA Modules:
  0.0 122.9 jit_solution(45818131512017220)
XLA Ops:
  0.7 1.0 pad_maximum_fusion.refs_0_
  1.6 4.0 %collective-permute-start.8 = (bf16[256,512]{1,0:T(8,128)(2,1)S(1)}, bf16[256,512]{1,0:T(8,128)(2,1)S(1)}, u32[]{:S(2)}, u32[]{:S(2)}) collective-permute-start(bf16[256,512]{1,0:T(8,128)(2,1)S(1)} %pad_maximum_fusion.refs_0_), channel_id=1, source_target_pairs={{0,24},{4,28},{8,16},{12,20},{16,8},{20,12},{24,0},{28,4},{1,25},{... | collective-permute-start | bytes 786440 | tf_op jit(solution)/shard_map/ppermute | solution.py:427
  6.3 0.8 dynamic-update-slice
  7.1 0.8 dynamic-update-slice.1
  7.9 0.8 dynamic-update-slice.2
  8.8 0.8 dynamic-update-slice.3
  9.6 0.8 dynamic-update-slice.4
  10.4 0.8 dynamic-update-slice.5
  11.3 0.9 dynamic-update-slice.6
  12.1 0.9 dynamic-update-slice.7
  13.0 4.1 %collective-permute-start.2 = (bf16[16,128]{1,0:T(8,128)(2,1)S(1)}, bf16[16,128]{1,0:T(8,128)(2,1)S(1)}, u32[]{:S(2)}, u32[]{:S(2)}) collective-permute-start(bf16[16,128]{1,0:T(8,128)(2,1)S(1)} %pad.4.refs_0_), channel_id=1, source_target_pairs={{0,3},{1,2},{2,1},{3,0},{4,7},{5,6},{6,5},{7,4},{8,11},{9,10},{10,... | collective-permute-start | bytes 12296 | tf_op jit(solution)/shard_map/ppermute | solution.py:434
  17.0 1.6 %collective-permute-done.2.refs_3_ = bf16[16,128]{1,0:T(8,128)(2,1)S(1)} collective-permute-done((bf16[16,128]{1,0:T(8,128)(2,1)S(1)}, bf16[16,128]{1,0:T(8,128)(2,1)S(1)}, u32[]{:S(2)}, u32[]{:S(2)}) %collective-permute-start.2) | collective-permute-done | bytes 4128 | tf_op jit(solution)/shard_map/ppermute | solution.py:434
  18.7 1.0 copy-done.4
  19.7 1.0 copy-done.5
  20.8 1.0 copy-done.8
  21.8 0.9 copy-done.9
  23.4 3.9 %collective-permute-start.16 = (bf16[128,512]{1,0:T(8,128)(2,1)S(1)}, bf16[128,512]{1,0:T(8,128)(2,1)S(1)}, u32[]{:S(2)}, u32[]{:S(2)}) collective-permute-start(bf16[128,512]{1,0:T(8,128)(2,1)S(1)} %get-tuple-element.47.refs_8_), channel_id=1, source_target_pairs={{0,3},{1,2},{2,1},{3,0},{4,7},{5,6},{6,5},{7,4},{8,11},{9,10},{10,... | collective-permute-start | bytes 393224 | tf_op jit(solution)/shard_map/ppermute | solution.py:434
  27.9 3.6 %collective-permute-done.16.refs_11_ = bf16[128,512]{1,0:T(8,128)(2,1)S(1)} collective-permute-done((bf16[128,512]{1,0:T(8,128)(2,1)S(1)}, bf16[128,512]{1,0:T(8,128)(2,1)S(1)}, u32[]{:S(2)}, u32[]{:S(2)}) %collective-permute-start.16) | collective-permute-done | bytes 131104 | tf_op jit(solution)/shard_map/ppermute | solution.py:434
  31.5 4.8 %collective-permute-start.14 = (bf16[128,512]{1,0:T(8,128)(2,1)S(1)}, bf16[128,512]{1,0:T(8,128)(2,1)S(1)}, u32[]{:S(2)}, u32[]{:S(2)}) collective-permute-start(bf16[128,512]{1,0:T(8,128)(2,1)S(1)} %get-tuple-element.47.refs_8_), channel_id=1, source_target_pairs={{0,1},{1,0},{2,3},{3,2},{4,5},{5,4},{6,7},{7,6},{8,9},{9,8},{10,11... | collective-permute-start | bytes 393224 | tf_op jit(solution)/shard_map/ppermute | solution.py:434
  36.4 0.9 collective-permute-done.15.refs_10_
  39.5 3.5 %collective-permute-start.12 = (bf16[128,256]{1,0:T(8,128)(2,1)S(1)}, bf16[128,256]{1,0:T(8,128)(2,1)S(1)}, u32[]{:S(2)}, u32[]{:S(2)}) collective-permute-start(bf16[128,256]{1,0:T(8,128)(2,1)S(1)} %get-tuple-element.45.refs_8_), channel_id=1, source_target_pairs={{0,3},{1,2},{2,1},{3,0},{4,7},{5,6},{6,5},{7,4},{8,11},{9,10},{10,... | collective-permute-start | bytes 196616 | tf_op jit(solution)/shard_map/ppermute | solution.py:434
  42.9 0.9 collective-permute-start.10
  43.9 1.0 collective-permute-start.13
  44.9 4.4 %feed_forward.1 = (bf16[1024,512]{1,0:T(8,128)(2,1)S(1)}, bf16[1024,512]{1,0:T(8,128)(2,1)S(1)}, f32[8,512]{1,0:T(8,128)S(1)}, bf16[128,512]{1,0:T(8,128)(2,1)S(...) custom-call(s32[2]{0:T(128)S(1)} %pad_add_fusion.place, ...), custom_call_target="tpu_custom_call" | custom-call | flops 1610612736 | bytes 4194304 | tf_op jit(solution)/shard_map/feed_forward/pallas_call | solution.py:543
  49.2 1.0 copy-done
  50.2 1.0 copy-done.1
  51.2 9.0 %attention.1 = (bf16[4,128,1024]{2,1,0:T(8,128)(2,1)S(1)}, bf16[4,128,1024]{2,1,0:T(8,128)(2,1)S(1)}, bf16[64,512]{1,0:T(8,128)(2,1)S(1)}, bf16[160,256]{1,0:T(8...) custom-call(s32[2]{0:T(128)S(1)} %pad_add_fusion.place, ...), custom_call_target="tpu_custom_call" | custom-call | flops 939524096 | bytes 6291456 | tf_op jit(solution)/shard_map/attention/pallas_call | solution.py:568
  60.3 0.9 collective-permute-start.41
  61.2 6.7 %collective-permute-start.31 = (bf16[160,256]{1,0:T(8,128)(2,1)S(1)}, bf16[160,256]{1,0:T(8,128)(2,1)S(1)}, u32[]{:S(2)}, u32[]{:S(2)}) collective-permute-start(bf16[160,256]{1,0:T(8,128)(2,1)S(1)} %get-tuple-element.60), channel_id=1, source_target_pairs={{0,1},{1,0},{2,3},{3,2},{4,5},{5,4},{6,7},{7,6},{8,9},{9,8},{10,11... | collective-permute-start | bytes 245768 | tf_op jit(solution)/shard_map/ppermute | solution.py:438
  67.8 5.5 %collective-permute-start.32 = (bf16[160,256]{1,0:T(8,128)(2,1)S(1)}, bf16[160,256]{1,0:T(8,128)(2,1)S(1)}, u32[]{:S(2)}, u32[]{:S(2)}) collective-permute-start(bf16[160,256]{1,0:T(8,128)(2,1)S(1)} %get-tuple-element.61), channel_id=1, source_target_pairs={{0,2},{1,3},{2,0},{3,1},{4,6},{5,7},{6,4},{7,5},{8,10},{9,11},{10,... | collective-permute-start | bytes 245768 | tf_op jit(solution)/shard_map/ppermute | solution.py:438
  73.4 4.3 %collective-permute-start.47 = (bf16[64,512]{1,0:T(8,128)(2,1)S(1)}, bf16[64,512]{1,0:T(8,128)(2,1)S(1)}, u32[]{:S(2)}, u32[]{:S(2)}) collective-permute-start(bf16[64,512]{1,0:T(8,128)(2,1)S(1)} %collective-permute-done.41.refs_16_), channel_id=1, source_target_pairs={{0,24},{4,28},{8,16},{12,20},{16,8},{20,12},{24,0},{28,4},{1,25},{... | collective-permute-start | bytes 196616 | tf_op jit(solution)/shard_map/ppermute | solution.py:427
  77.7 2.4 %collective-permute-done.32.refs_2_ = bf16[160,256]{1,0:T(8,128)(2,1)S(1)} collective-permute-done((bf16[160,256]{1,0:T(8,128)(2,1)S(1)}, bf16[160,256]{1,0:T(8,128)(2,1)S(1)}, u32[]{:S(2)}, u32[]{:S(2)}) %collective-permute-start.32) | collective-permute-done | bytes 81952 | tf_op jit(solution)/shard_map/ppermute | solution.py:438
  80.7 2.5 %collective-permute-start.22 = (bf16[128,512]{1,0:T(8,128)(2,1)S(1)}, bf16[128,512]{1,0:T(8,128)(2,1)S(1)}, u32[]{:S(2)}, u32[]{:S(2)}) collective-permute-start(bf16[128,512]{1,0:T(8,128)(2,1)S(1)} %get-tuple-element.57), channel_id=1, source_target_pairs={{0,2},{1,3},{2,0},{3,1},{4,6},{5,7},{6,4},{7,5},{8,10},{9,11},{10,... | collective-permute-start | bytes 393224 | tf_op jit(solution)/shard_map/ppermute | solution.py:438
  83.2 1.7 %collective-permute-start.23 = (bf16[128,512]{1,0:T(8,128)(2,1)S(1)}, bf16[128,512]{1,0:T(8,128)(2,1)S(1)}, u32[]{:S(2)}, u32[]{:S(2)}) collective-permute-start(bf16[128,512]{1,0:T(8,128)(2,1)S(1)} %get-tuple-element.58), channel_id=1, source_target_pairs={{0,3},{1,2},{2,1},{3,0},{4,7},{5,6},{6,5},{7,4},{8,11},{9,10},{10,... | collective-permute-start | bytes 393224 | tf_op jit(solution)/shard_map/ppermute | solution.py:438
  85.0 4.7 %collective-permute-done.43.refs_18_ = bf16[64,512]{1,0:T(8,128)(2,1)S(1)} collective-permute-done((bf16[64,512]{1,0:T(8,128)(2,1)S(1)}, bf16[64,512]{1,0:T(8,128)(2,1)S(1)}, u32[]{:S(2)}, u32[]{:S(2)}) %collective-permute-start.43) | collective-permute-done | bytes 65568 | tf_op jit(solution)/shard_map/ppermute | solution.py:427
  90.7 2.6 %collective-permute-done.22.refs_2_ = bf16[128,512]{1,0:T(8,128)(2,1)S(1)} collective-permute-done((bf16[128,512]{1,0:T(8,128)(2,1)S(1)}, bf16[128,512]{1,0:T(8,128)(2,1)S(1)}, u32[]{:S(2)}, u32[]{:S(2)}) %collective-permute-start.22) | collective-permute-done | bytes 131104 | tf_op jit(solution)/shard_map/ppermute | solution.py:438
  93.4 1.2 collective-permute-done.42.refs_17_
  95.6 2.1 %collective-permute-done.35.refs_10_ = bf16[160,256]{1,0:T(8,128)(2,1)S(1)} collective-permute-done((bf16[160,256]{1,0:T(8,128)(2,1)S(1)}, bf16[160,256]{1,0:T(8,128)(2,1)S(1)}, u32[]{:S(2)}, u32[]{:S(2)}) %collective-permute-start.35) | collective-permute-done | bytes 81952 | tf_op jit(solution)/shard_map/ppermute | solution.py:427
  98.7 1.0 collective-permute-start.29
  100.2 2.0 %collective-permute-start.25 = (bf16[128,512]{1,0:T(8,128)(2,1)S(1)}, bf16[128,512]{1,0:T(8,128)(2,1)S(1)}, u32[]{:S(2)}, u32[]{:S(2)}) collective-permute-start(bf16[128,512]{1,0:T(8,128)(2,1)S(1)} %sum_ff.1.refs_0_), channel_id=1, source_target_pairs={{0,8},{4,12},{8,0},{12,4},{16,24},{20,28},{24,16},{28,20},{1,9},{5... | collective-permute-start | bytes 393224 | tf_op jit(solution)/shard_map/ppermute | solution.py:427
  103.7 2.4 %collective-permute-done.29.refs_6_ = bf16[128,512]{1,0:T(8,128)(2,1)S(1)} collective-permute-done((bf16[128,512]{1,0:T(8,128)(2,1)S(1)}, bf16[128,512]{1,0:T(8,128)(2,1)S(1)}, u32[]{:S(2)}, u32[]{:S(2)}) %collective-permute-start.29) | collective-permute-done | bytes 131104 | tf_op jit(solution)/shard_map/ppermute | solution.py:427
  106.1 0.8 collective-permute-start.20
  107.7 1.9 %collective-permute-start.18 = (bf16[128,1024]{1,0:T(8,128)(2,1)S(1)}, bf16[128,1024]{1,0:T(8,128)(2,1)S(1)}, u32[]{:S(2)}, u32[]{:S(2)}) collective-permute-start(bf16[128,1024]{1,0:T(8,128)(2,1)S(1)} %get-tuple-element.78), channel_id=1, source_target_pairs={{0,8},{4,12},{8,0},{12,4},{16,24},{20,28},{24,16},{28,20},{1,9},{5... | collective-permute-start | bytes 786440 | tf_op jit(solution)/shard_map/ppermute | solution.py:601
  110.1 0.8 collective-permute-done.28.refs_5_
  111.1 2.8 %finish.1 = (f32[1,128]{1,0:T(1,128)}, f32[1,128]{1,0:T(1,128)}, f32[128,1536]{1,0:T(8,128)}, f32[1,384]{1,0:T(1,128)S(1)}, f32[128,512]{1,0:T(8,128)}, /*index=...) custom-call(s32[2]{0:T(128)S(1)} %pad_add_fusion.place, ...), custom_call_target="tpu_custom_call" | custom-call | tf_op jit(solution)/shard_map/finish/pallas_call | solution.py:625
  114.6 1.6 %collective-permute-done.20.refs_3_ = bf16[128,1024]{1,0:T(8,128)(2,1)S(1)} collective-permute-done((bf16[128,1024]{1,0:T(8,128)(2,1)S(1)}, bf16[128,1024]{1,0:T(8,128)(2,1)S(1)}, u32[]{:S(2)}, u32[]{:S(2)}) %collective-permute-start.20) | collective-permute-done | bytes 262176 | tf_op jit(solution)/shard_map/ppermute | solution.py:601
  116.1 5.2 %collective-permute-done.19.refs_2_ = bf16[128,1024]{1,0:T(8,128)(2,1)S(1)} collective-permute-done((bf16[128,1024]{1,0:T(8,128)(2,1)S(1)}, bf16[128,1024]{1,0:T(8,128)(2,1)S(1)}, u32[]{:S(2)}, u32[]{:S(2)}) %collective-permute-start.19) | collective-permute-done | bytes 262176 | tf_op jit(solution)/shard_map/ppermute | solution.py:601
  121.3 1.6 %close.1 = (bf16[128,512]{1,0:T(8,128)(2,1)}, f32[128,512]{1,0:T(8,128)}) custom-call(s32[2]{0:T(128)S(1)} %pad_add_fusion.place, bf16[128,512]{1,0:T(8,128)(2,1)S(1)} %bitcast.23, bf16[128,512]{1,0:T(8,128)(2,1)S(1)} %bitcast.25, f32[8,512]{1,0:T(8,128)S(1)} %small.1.refs_12_.refs_13_.params, bf16[128,1024]{1,0:T(8,128)(2,1)S(1)} %get-tuple-element.79.refs_0_, ...), custom_call_target="tpu_custom_call" | custom-call | tf_op jit(solution)/shard_map/close/pallas_call | solution.py:602
  (99 shorter events, 12.0 us)
Async XLA Ops:
  1.6 35.7 %collective-permute-start.8 = (bf16[256,512]{1,0:T(8,128)(2,1)S(1)}, bf16[256,512]{1,0:T(8,128)(2,1)S(1)}, u32[]{:S(2)}, u32[]{:S(2)}) collective-permute-start(bf16[256,512]{1,0:T(8,128)(2,1)S(1)} %pad_maximum_fusion.refs_0_), channel_id=1, source_target_pairs={{0,24},{4,28},{8,16},{12,20},{16,8},{20,12},{24,0},{28,4},{1,25},{... | collective-permute-start | bytes 786440 | tf_op jit(solution)/shard_map/ppermute | solution.py:427
  5.6 32.2 %collective-permute-start.6 = (bf16[256,512]{1,0:T(8,128)(2,1)S(1)}, bf16[256,512]{1,0:T(8,128)(2,1)S(1)}, u32[]{:S(2)}, u32[]{:S(2)}) collective-permute-start(bf16[256,512]{1,0:T(8,128)(2,1)S(1)} %pad_maximum_fusion.refs_0_), channel_id=1, source_target_pairs={{0,16},{4,20},{8,24},{12,28},{16,0},{20,4},{24,8},{28,12},{1,17},{... | collective-permute-start | bytes 786440 | tf_op jit(solution)/shard_map/ppermute | solution.py:427
  6.1 31.8 %collective-permute-start.4 = (bf16[256,512]{1,0:T(8,128)(2,1)S(1)}, bf16[256,512]{1,0:T(8,128)(2,1)S(1)}, u32[]{:S(2)}, u32[]{:S(2)}) collective-permute-start(bf16[256,512]{1,0:T(8,128)(2,1)S(1)} %pad_maximum_fusion.refs_0_), channel_id=1, source_target_pairs={{0,8},{4,12},{8,0},{12,4},{16,24},{20,28},{24,16},{28,20},{1,9},{5... | collective-permute-start | bytes 786440 | tf_op jit(solution)/shard_map/ppermute | solution.py:427
  13.0 5.7 %collective-permute-start.2 = (bf16[16,128]{1,0:T(8,128)(2,1)S(1)}, bf16[16,128]{1,0:T(8,128)(2,1)S(1)}, u32[]{:S(2)}, u32[]{:S(2)}) collective-permute-start(bf16[16,128]{1,0:T(8,128)(2,1)S(1)} %pad.4.refs_0_), channel_id=1, source_target_pairs={{0,3},{1,2},{2,1},{3,0},{4,7},{5,6},{6,5},{7,4},{8,11},{9,10},{10,... | collective-permute-start | bytes 12296 | tf_op jit(solution)/shard_map/ppermute | solution.py:434
  17.0 6.3 %collective-permute-start.1 = (bf16[16,128]{1,0:T(8,128)(2,1)S(1)}, bf16[16,128]{1,0:T(8,128)(2,1)S(1)}, u32[]{:S(2)}, u32[]{:S(2)}) collective-permute-start(bf16[16,128]{1,0:T(8,128)(2,1)S(1)} %pad.4.refs_0_), channel_id=1, source_target_pairs={{0,2},{1,3},{2,0},{3,1},{4,6},{5,7},{6,4},{7,5},{8,10},{9,11},{10,... | collective-permute-start | bytes 12296 | tf_op jit(solution)/shard_map/ppermute | solution.py:434
  18.6 8.7 %collective-permute-start = (bf16[16,128]{1,0:T(8,128)(2,1)S(1)}, bf16[16,128]{1,0:T(8,128)(2,1)S(1)}, u32[]{:S(2)}, u32[]{:S(2)}) collective-permute-start(bf16[16,128]{1,0:T(8,128)(2,1)S(1)} %pad.4.refs_0_), channel_id=1, source_target_pairs={{0,1},{1,0},{2,3},{3,2},{4,5},{5,4},{6,7},{7,6},{8,9},{9,8},{10,11... | collective-permute-start | bytes 12296 | tf_op jit(solution)/shard_map/ppermute | solution.py:434
  23.4 8.1 %collective-permute-start.16 = (bf16[128,512]{1,0:T(8,128)(2,1)S(1)}, bf16[128,512]{1,0:T(8,128)(2,1)S(1)}, u32[]{:S(2)}, u32[]{:S(2)}) collective-permute-start(bf16[128,512]{1,0:T(8,128)(2,1)S(1)} %get-tuple-element.47.refs_8_), channel_id=1, source_target_pairs={{0,3},{1,2},{2,1},{3,0},{4,7},{5,6},{6,5},{7,4},{8,11},{9,10},{10,... | collective-permute-start | bytes 393224 | tf_op jit(solution)/shard_map/ppermute | solution.py:434
  27.3 10.0 %collective-permute-start.15 = (bf16[128,512]{1,0:T(8,128)(2,1)S(1)}, bf16[128,512]{1,0:T(8,128)(2,1)S(1)}, u32[]{:S(2)}, u32[]{:S(2)}) collective-permute-start(bf16[128,512]{1,0:T(8,128)(2,1)S(1)} %get-tuple-element.47.refs_8_), channel_id=1, source_target_pairs={{0,2},{1,3},{2,0},{3,1},{4,6},{5,7},{6,4},{7,5},{8,10},{9,11},{10,... | collective-permute-start | bytes 393224 | tf_op jit(solution)/shard_map/ppermute | solution.py:434
  31.5 7.9 %collective-permute-start.14 = (bf16[128,512]{1,0:T(8,128)(2,1)S(1)}, bf16[128,512]{1,0:T(8,128)(2,1)S(1)}, u32[]{:S(2)}, u32[]{:S(2)}) collective-permute-start(bf16[128,512]{1,0:T(8,128)(2,1)S(1)} %get-tuple-element.47.refs_8_), channel_id=1, source_target_pairs={{0,1},{1,0},{2,3},{3,2},{4,5},{5,4},{6,7},{7,6},{8,9},{9,8},{10,11... | collective-permute-start | bytes 393224 | tf_op jit(solution)/shard_map/ppermute | solution.py:434
  37.3 5.6 %collective-permute-start.3 = (bf16[256,512]{1,0:T(8,128)(2,1)S(1)}, bf16[256,512]{1,0:T(8,128)(2,1)S(1)}, u32[]{:S(2)}, u32[]{:S(2)}) collective-permute-start(bf16[256,512]{1,0:T(8,128)(2,1)S(1)} %pad_maximum_fusion.refs_0_), channel_id=1, source_target_pairs={{0,4},{4,0},{8,12},{12,8},{16,20},{20,16},{24,28},{28,24},{1,5},{5... | collective-permute-start | bytes 786440 | tf_op jit(solution)/shard_map/ppermute | solution.py:429
  37.3 5.6 %collective-permute-start.9 = (bf16[256,512]{1,0:T(8,128)(2,1)S(1)}, bf16[256,512]{1,0:T(8,128)(2,1)S(1)}, u32[]{:S(2)}, u32[]{:S(2)}) collective-permute-start(bf16[256,512]{1,0:T(8,128)(2,1)S(1)} %collective-permute-done.8.refs_6_), channel_id=1, source_target_pairs={{0,4},{4,0},{8,12},{12,8},{16,20},{20,16},{24,28},{28,24},{1,5},{5... | collective-permute-start | bytes 786440 | tf_op jit(solution)/shard_map/ppermute | solution.py:429
  37.8 6.0 %collective-permute-start.7 = (bf16[256,512]{1,0:T(8,128)(2,1)S(1)}, bf16[256,512]{1,0:T(8,128)(2,1)S(1)}, u32[]{:S(2)}, u32[]{:S(2)}) collective-permute-start(bf16[256,512]{1,0:T(8,128)(2,1)S(1)} %collective-permute-done.6.refs_4_), channel_id=1, source_target_pairs={{0,4},{4,0},{8,12},{12,8},{16,20},{20,16},{24,28},{28,24},{1,5},{5... | collective-permute-start | bytes 786440 | tf_op jit(solution)/shard_map/ppermute | solution.py:429
  37.9 6.9 %collective-permute-start.5 = (bf16[256,512]{1,0:T(8,128)(2,1)S(1)}, bf16[256,512]{1,0:T(8,128)(2,1)S(1)}, u32[]{:S(2)}, u32[]{:S(2)}) collective-permute-start(bf16[256,512]{1,0:T(8,128)(2,1)S(1)} %collective-permute-done.4.refs_2_), channel_id=1, source_target_pairs={{0,4},{4,0},{8,12},{12,8},{16,20},{20,16},{24,28},{28,24},{1,5},{5... | collective-permute-start | bytes 786440 | tf_op jit(solution)/shard_map/ppermute | solution.py:429
  39.5 11.7 %collective-permute-start.12 = (bf16[128,256]{1,0:T(8,128)(2,1)S(1)}, bf16[128,256]{1,0:T(8,128)(2,1)S(1)}, u32[]{:S(2)}, u32[]{:S(2)}) collective-permute-start(bf16[128,256]{1,0:T(8,128)(2,1)S(1)} %get-tuple-element.45.refs_8_), channel_id=1, source_target_pairs={{0,3},{1,2},{2,1},{3,0},{4,7},{5,6},{6,5},{7,4},{8,11},{9,10},{10,... | collective-permute-start | bytes 196616 | tf_op jit(solution)/shard_map/ppermute | solution.py:434
  42.9 8.3 %collective-permute-start.11 = (bf16[128,256]{1,0:T(8,128)(2,1)S(1)}, bf16[128,256]{1,0:T(8,128)(2,1)S(1)}, u32[]{:S(2)}, u32[]{:S(2)}) collective-permute-start(bf16[128,256]{1,0:T(8,128)(2,1)S(1)} %get-tuple-element.45.refs_8_), channel_id=1, source_target_pairs={{0,2},{1,3},{2,0},{3,1},{4,6},{5,7},{6,4},{7,5},{8,10},{9,11},{10,... | collective-permute-start | bytes 196616 | tf_op jit(solution)/shard_map/ppermute | solution.py:434
  42.9 8.3 %collective-permute-start.10 = (bf16[128,256]{1,0:T(8,128)(2,1)S(1)}, bf16[128,256]{1,0:T(8,128)(2,1)S(1)}, u32[]{:S(2)}, u32[]{:S(2)}) collective-permute-start(bf16[128,256]{1,0:T(8,128)(2,1)S(1)} %get-tuple-element.45.refs_8_), channel_id=1, source_target_pairs={{0,1},{1,0},{2,3},{3,2},{4,5},{5,4},{6,7},{7,6},{8,9},{9,8},{10,11... | collective-permute-start | bytes 196616 | tf_op jit(solution)/shard_map/ppermute | solution.py:434
  43.9 7.3 %collective-permute-start.13 = (bf16[64,512]{1,0:T(8,128)(2,1)S(1)}, bf16[64,512]{1,0:T(8,128)(2,1)S(1)}, u32[]{:S(2)}, u32[]{:S(2)}) collective-permute-start(bf16[64,512]{1,0:T(8,128)(2,1)S(1)} %get-tuple-element.46), channel_id=1, source_target_pairs={{0,0},{1,8},{2,16},{3,24},{4,4},{5,12},{6,20},{7,28},{8,1},{9,9},{... | collective-permute-start | bytes 196616 | tf_op jit(solution)/shard_map/ppermute | solution.py:512
  60.2 37.5 %collective-permute-start.17 = (bf16[4,128,1024]{2,1,0:T(8,128)(2,1)S(1)}, bf16[4,128,1024]{2,1,0:T(8,128)(2,1)S(1)}, u32[]{:S(2)}, u32[]{:S(2)}) collective-permute-start(bf16[4,128,1024]{2,1,0:T(8,128)(2,1)S(1)} %get-tuple-element.52), channel_id=1, source_target_pairs={{0,4},{4,0},{8,12},{12,8},{16,20},{20,16},{24,28},{28,24},{1,5},{5... | collective-permute-start | bytes 3145736 | tf_op jit(solution)/shard_map/ppermute | solution.py:599
  60.3 13.1 %collective-permute-start.41 = (bf16[64,512]{1,0:T(8,128)(2,1)S(1)}, bf16[64,512]{1,0:T(8,128)(2,1)S(1)}, u32[]{:S(2)}, u32[]{:S(2)}) collective-permute-start(bf16[64,512]{1,0:T(8,128)(2,1)S(1)} %get-tuple-element.63), channel_id=1, source_target_pairs={{0,0},{8,1},{16,2},{24,3},{4,4},{12,5},{20,6},{28,7},{1,8},{9,9},{... | collective-permute-start | bytes 196616 | tf_op jit(solution)/shard_map/ppermute | solution.py:615
  61.2 16.6 %collective-permute-start.31 = (bf16[160,256]{1,0:T(8,128)(2,1)S(1)}, bf16[160,256]{1,0:T(8,128)(2,1)S(1)}, u32[]{:S(2)}, u32[]{:S(2)}) collective-permute-start(bf16[160,256]{1,0:T(8,128)(2,1)S(1)} %get-tuple-element.60), channel_id=1, source_target_pairs={{0,1},{1,0},{2,3},{3,2},{4,5},{5,4},{6,7},{7,6},{8,9},{9,8},{10,11... | collective-permute-start | bytes 245768 | tf_op jit(solution)/shard_map/ppermute | solution.py:438
  67.8 12.3 %collective-permute-start.32 = (bf16[160,256]{1,0:T(8,128)(2,1)S(1)}, bf16[160,256]{1,0:T(8,128)(2,1)S(1)}, u32[]{:S(2)}, u32[]{:S(2)}) collective-permute-start(bf16[160,256]{1,0:T(8,128)(2,1)S(1)} %get-tuple-element.61), channel_id=1, source_target_pairs={{0,2},{1,3},{2,0},{3,1},{4,6},{5,7},{6,4},{7,5},{8,10},{9,11},{10,... | collective-permute-start | bytes 245768 | tf_op jit(solution)/shard_map/ppermute | solution.py:438
  73.4 7.3 %collective-permute-start.33 = (bf16[160,256]{1,0:T(8,128)(2,1)S(1)}, bf16[160,256]{1,0:T(8,128)(2,1)S(1)}, u32[]{:S(2)}, u32[]{:S(2)}) collective-permute-start(bf16[160,256]{1,0:T(8,128)(2,1)S(1)} %get-tuple-element.62), channel_id=1, source_target_pairs={{0,3},{1,2},{2,1},{3,0},{4,7},{5,6},{6,5},{7,4},{8,11},{9,10},{10,... | collective-permute-start | bytes 245768 | tf_op jit(solution)/shard_map/ppermute | solution.py:438
  73.4 9.8 %collective-permute-start.47 = (bf16[64,512]{1,0:T(8,128)(2,1)S(1)}, bf16[64,512]{1,0:T(8,128)(2,1)S(1)}, u32[]{:S(2)}, u32[]{:S(2)}) collective-permute-start(bf16[64,512]{1,0:T(8,128)(2,1)S(1)} %collective-permute-done.41.refs_16_), channel_id=1, source_target_pairs={{0,24},{4,28},{8,16},{12,20},{16,8},{20,12},{24,0},{28,4},{1,25},{... | collective-permute-start | bytes 196616 | tf_op jit(solution)/shard_map/ppermute | solution.py:427
  77.7 7.2 %collective-permute-start.45 = (bf16[64,512]{1,0:T(8,128)(2,1)S(1)}, bf16[64,512]{1,0:T(8,128)(2,1)S(1)}, u32[]{:S(2)}, u32[]{:S(2)}) collective-permute-start(bf16[64,512]{1,0:T(8,128)(2,1)S(1)} %collective-permute-done.41.refs_16_), channel_id=1, source_target_pairs={{0,16},{4,20},{8,24},{12,28},{16,0},{20,4},{24,8},{28,12},{1,17},{... | collective-permute-start | bytes 196616 | tf_op jit(solution)/shard_map/ppermute | solution.py:427
  80.1 10.2 %collective-permute-start.21 = (bf16[128,512]{1,0:T(8,128)(2,1)S(1)}, bf16[128,512]{1,0:T(8,128)(2,1)S(1)}, u32[]{:S(2)}, u32[]{:S(2)}) collective-permute-start(bf16[128,512]{1,0:T(8,128)(2,1)S(1)} %get-tuple-element.56), channel_id=1, source_target_pairs={{0,1},{1,0},{2,3},{3,2},{4,5},{5,4},{6,7},{7,6},{8,9},{9,8},{10,11... | collective-permute-start | bytes 393224 | tf_op jit(solution)/shard_map/ppermute | solution.py:438
  80.7 12.6 %collective-permute-start.22 = (bf16[128,512]{1,0:T(8,128)(2,1)S(1)}, bf16[128,512]{1,0:T(8,128)(2,1)S(1)}, u32[]{:S(2)}, u32[]{:S(2)}) collective-permute-start(bf16[128,512]{1,0:T(8,128)(2,1)S(1)} %get-tuple-element.57), channel_id=1, source_target_pairs={{0,2},{1,3},{2,0},{3,1},{4,6},{5,7},{6,4},{7,5},{8,10},{9,11},{10,... | collective-permute-start | bytes 393224 | tf_op jit(solution)/shard_map/ppermute | solution.py:438
  83.2 10.1 %collective-permute-start.23 = (bf16[128,512]{1,0:T(8,128)(2,1)S(1)}, bf16[128,512]{1,0:T(8,128)(2,1)S(1)}, u32[]{:S(2)}, u32[]{:S(2)}) collective-permute-start(bf16[128,512]{1,0:T(8,128)(2,1)S(1)} %get-tuple-element.58), channel_id=1, source_target_pairs={{0,3},{1,2},{2,1},{3,0},{4,7},{5,6},{6,5},{7,4},{8,11},{9,10},{10,... | collective-permute-start | bytes 393224 | tf_op jit(solution)/shard_map/ppermute | solution.py:438
  84.9 4.7 %collective-permute-start.43 = (bf16[64,512]{1,0:T(8,128)(2,1)S(1)}, bf16[64,512]{1,0:T(8,128)(2,1)S(1)}, u32[]{:S(2)}, u32[]{:S(2)}) collective-permute-start(bf16[64,512]{1,0:T(8,128)(2,1)S(1)} %collective-permute-done.41.refs_16_), channel_id=1, source_target_pairs={{0,8},{4,12},{8,0},{12,4},{16,24},{20,28},{24,16},{28,20},{1,9},{5... | collective-permute-start | bytes 196616 | tf_op jit(solution)/shard_map/ppermute | solution.py:427
  89.6 5.4 %collective-permute-start.39 = (bf16[160,256]{1,0:T(8,128)(2,1)S(1)}, bf16[160,256]{1,0:T(8,128)(2,1)S(1)}, u32[]{:S(2)}, u32[]{:S(2)}) collective-permute-start(bf16[160,256]{1,0:T(8,128)(2,1)S(1)} %sum_attn.1.refs_8_), channel_id=1, source_target_pairs={{0,24},{4,28},{8,16},{12,20},{16,8},{20,12},{24,0},{28,4},{1,25},{... | collective-permute-start | bytes 245768 | tf_op jit(solution)/shard_map/ppermute | solution.py:427
  90.3 5.3 %collective-permute-start.37 = (bf16[160,256]{1,0:T(8,128)(2,1)S(1)}, bf16[160,256]{1,0:T(8,128)(2,1)S(1)}, u32[]{:S(2)}, u32[]{:S(2)}) collective-permute-start(bf16[160,256]{1,0:T(8,128)(2,1)S(1)} %sum_attn.1.refs_8_), channel_id=1, source_target_pairs={{0,16},{4,20},{8,24},{12,28},{16,0},{20,4},{24,8},{28,12},{1,17},{... | collective-permute-start | bytes 245768 | tf_op jit(solution)/shard_map/ppermute | solution.py:427
  93.3 4.4 %collective-permute-start.35 = (bf16[160,256]{1,0:T(8,128)(2,1)S(1)}, bf16[160,256]{1,0:T(8,128)(2,1)S(1)}, u32[]{:S(2)}, u32[]{:S(2)}) collective-permute-start(bf16[160,256]{1,0:T(8,128)(2,1)S(1)} %sum_attn.1.refs_8_), channel_id=1, source_target_pairs={{0,8},{4,12},{8,0},{12,4},{16,24},{20,28},{24,16},{28,20},{1,9},{5... | collective-permute-start | bytes 245768 | tf_op jit(solution)/shard_map/ppermute | solution.py:427
  94.6 4.1 %collective-permute-start.34 = (bf16[160,256]{1,0:T(8,128)(2,1)S(1)}, bf16[160,256]{1,0:T(8,128)(2,1)S(1)}, u32[]{:S(2)}, u32[]{:S(2)}) collective-permute-start(bf16[160,256]{1,0:T(8,128)(2,1)S(1)} %sum_attn.1.refs_8_), channel_id=1, source_target_pairs={{0,4},{4,0},{8,12},{12,8},{16,20},{20,16},{24,28},{28,24},{1,5},{5... | collective-permute-start | bytes 245768 | tf_op jit(solution)/shard_map/ppermute | solution.py:429
  95.1 4.7 %collective-permute-start.48 = (bf16[64,512]{1,0:T(8,128)(2,1)S(1)}, bf16[64,512]{1,0:T(8,128)(2,1)S(1)}, u32[]{:S(2)}, u32[]{:S(2)}) collective-permute-start(bf16[64,512]{1,0:T(8,128)(2,1)S(1)} %collective-permute-done.47.refs_22_), channel_id=1, source_target_pairs={{0,4},{4,0},{8,12},{12,8},{16,20},{20,16},{24,28},{28,24},{1,5},{5... | collective-permute-start | bytes 196616 | tf_op jit(solution)/shard_map/ppermute | solution.py:429
  95.6 4.6 %collective-permute-start.46 = (bf16[64,512]{1,0:T(8,128)(2,1)S(1)}, bf16[64,512]{1,0:T(8,128)(2,1)S(1)}, u32[]{:S(2)}, u32[]{:S(2)}) collective-permute-start(bf16[64,512]{1,0:T(8,128)(2,1)S(1)} %collective-permute-done.45.refs_20_), channel_id=1, source_target_pairs={{0,4},{4,0},{8,12},{12,8},{16,20},{20,16},{24,28},{28,24},{1,5},{5... | collective-permute-start | bytes 196616 | tf_op jit(solution)/shard_map/ppermute | solution.py:429
  97.8 4.5 %collective-permute-start.44 = (bf16[64,512]{1,0:T(8,128)(2,1)S(1)}, bf16[64,512]{1,0:T(8,128)(2,1)S(1)}, u32[]{:S(2)}, u32[]{:S(2)}) collective-permute-start(bf16[64,512]{1,0:T(8,128)(2,1)S(1)} %collective-permute-done.43.refs_18_), channel_id=1, source_target_pairs={{0,4},{4,0},{8,12},{12,8},{16,20},{20,16},{24,28},{28,24},{1,5},{5... | collective-permute-start | bytes 196616 | tf_op jit(solution)/shard_map/ppermute | solution.py:429
  97.8 4.5 %collective-permute-start.40 = (bf16[160,256]{1,0:T(8,128)(2,1)S(1)}, bf16[160,256]{1,0:T(8,128)(2,1)S(1)}, u32[]{:S(2)}, u32[]{:S(2)}) collective-permute-start(bf16[160,256]{1,0:T(8,128)(2,1)S(1)} %collective-permute-done.39.refs_14_), channel_id=1, source_target_pairs={{0,4},{4,0},{8,12},{12,8},{16,20},{20,16},{24,28},{28,24},{1,5},{5... | collective-permute-start | bytes 245768 | tf_op jit(solution)/shard_map/ppermute | solution.py:429
  98.7 7.4 %collective-permute-start.29 = (bf16[128,512]{1,0:T(8,128)(2,1)S(1)}, bf16[128,512]{1,0:T(8,128)(2,1)S(1)}, u32[]{:S(2)}, u32[]{:S(2)}) collective-permute-start(bf16[128,512]{1,0:T(8,128)(2,1)S(1)} %sum_ff.1.refs_0_), channel_id=1, source_target_pairs={{0,24},{4,28},{8,16},{12,20},{16,8},{20,12},{24,0},{28,4},{1,25},{... | collective-permute-start | bytes 393224 | tf_op jit(solution)/shard_map/ppermute | solution.py:427
  99.8 7.9 %collective-permute-start.27 = (bf16[128,512]{1,0:T(8,128)(2,1)S(1)}, bf16[128,512]{1,0:T(8,128)(2,1)S(1)}, u32[]{:S(2)}, u32[]{:S(2)}) collective-permute-start(bf16[128,512]{1,0:T(8,128)(2,1)S(1)} %sum_ff.1.refs_0_), channel_id=1, source_target_pairs={{0,16},{4,20},{8,24},{12,28},{16,0},{20,4},{24,8},{28,12},{1,17},{... | collective-permute-start | bytes 393224 | tf_op jit(solution)/shard_map/ppermute | solution.py:427
  100.2 7.5 %collective-permute-start.25 = (bf16[128,512]{1,0:T(8,128)(2,1)S(1)}, bf16[128,512]{1,0:T(8,128)(2,1)S(1)}, u32[]{:S(2)}, u32[]{:S(2)}) collective-permute-start(bf16[128,512]{1,0:T(8,128)(2,1)S(1)} %sum_ff.1.refs_0_), channel_id=1, source_target_pairs={{0,8},{4,12},{8,0},{12,4},{16,24},{20,28},{24,16},{28,20},{1,9},{5... | collective-permute-start | bytes 393224 | tf_op jit(solution)/shard_map/ppermute | solution.py:427
  102.3 1.3 %collective-permute-start.38 = (bf16[160,256]{1,0:T(8,128)(2,1)S(1)}, bf16[160,256]{1,0:T(8,128)(2,1)S(1)}, u32[]{:S(2)}, u32[]{:S(2)}) collective-permute-start(bf16[160,256]{1,0:T(8,128)(2,1)S(1)} %collective-permute-done.37.refs_12_), channel_id=1, source_target_pairs={{0,4},{4,0},{8,12},{12,8},{16,20},{20,16},{24,28},{28,24},{1,5},{5... | collective-permute-start | bytes 245768 | tf_op jit(solution)/shard_map/ppermute | solution.py:429
  102.3 3.8 %collective-permute-start.36 = (bf16[160,256]{1,0:T(8,128)(2,1)S(1)}, bf16[160,256]{1,0:T(8,128)(2,1)S(1)}, u32[]{:S(2)}, u32[]{:S(2)}) collective-permute-start(bf16[160,256]{1,0:T(8,128)(2,1)S(1)} %collective-permute-done.35.refs_10_), channel_id=1, source_target_pairs={{0,4},{4,0},{8,12},{12,8},{16,20},{20,16},{24,28},{28,24},{1,5},{5... | collective-permute-start | bytes 245768 | tf_op jit(solution)/shard_map/ppermute | solution.py:429
  103.6 6.0 %collective-permute-start.24 = (bf16[128,512]{1,0:T(8,128)(2,1)S(1)}, bf16[128,512]{1,0:T(8,128)(2,1)S(1)}, u32[]{:S(2)}, u32[]{:S(2)}) collective-permute-start(bf16[128,512]{1,0:T(8,128)(2,1)S(1)} %sum_ff.1.refs_0_), channel_id=1, source_target_pairs={{0,4},{4,0},{8,12},{12,8},{16,20},{20,16},{24,28},{28,24},{1,5},{5... | collective-permute-start | bytes 393224 | tf_op jit(solution)/shard_map/ppermute | solution.py:429
  106.1 3.5 %collective-permute-start.30 = (bf16[128,512]{1,0:T(8,128)(2,1)S(1)}, bf16[128,512]{1,0:T(8,128)(2,1)S(1)}, u32[]{:S(2)}, u32[]{:S(2)}) collective-permute-start(bf16[128,512]{1,0:T(8,128)(2,1)S(1)} %collective-permute-done.29.refs_6_), channel_id=1, source_target_pairs={{0,4},{4,0},{8,12},{12,8},{16,20},{20,16},{24,28},{28,24},{1,5},{5... | collective-permute-start | bytes 393224 | tf_op jit(solution)/shard_map/ppermute | solution.py:429
  106.1 10.0 %collective-permute-start.20 = (bf16[128,1024]{1,0:T(8,128)(2,1)S(1)}, bf16[128,1024]{1,0:T(8,128)(2,1)S(1)}, u32[]{:S(2)}, u32[]{:S(2)}) collective-permute-start(bf16[128,1024]{1,0:T(8,128)(2,1)S(1)} %get-tuple-element.76), channel_id=1, source_target_pairs={{0,24},{4,28},{8,16},{12,20},{16,8},{20,12},{24,0},{28,4},{1,25},{... | collective-permute-start | bytes 786440 | tf_op jit(solution)/shard_map/ppermute | solution.py:601
  107.7 13.6 %collective-permute-start.19 = (bf16[128,1024]{1,0:T(8,128)(2,1)S(1)}, bf16[128,1024]{1,0:T(8,128)(2,1)S(1)}, u32[]{:S(2)}, u32[]{:S(2)}) collective-permute-start(bf16[128,1024]{1,0:T(8,128)(2,1)S(1)} %get-tuple-element.77), channel_id=1, source_target_pairs={{0,16},{4,20},{8,24},{12,28},{16,0},{20,4},{24,8},{28,12},{1,17},{... | collective-permute-start | bytes 786440 | tf_op jit(solution)/shard_map/ppermute | solution.py:601
  107.7 13.6 %collective-permute-start.18 = (bf16[128,1024]{1,0:T(8,128)(2,1)S(1)}, bf16[128,1024]{1,0:T(8,128)(2,1)S(1)}, u32[]{:S(2)}, u32[]{:S(2)}) collective-permute-start(bf16[128,1024]{1,0:T(8,128)(2,1)S(1)} %get-tuple-element.78), channel_id=1, source_target_pairs={{0,8},{4,12},{8,0},{12,4},{16,24},{20,28},{24,16},{28,20},{1,9},{5... | collective-permute-start | bytes 786440 | tf_op jit(solution)/shard_map/ppermute | solution.py:601
  109.6 1.3 %collective-permute-start.28 = (bf16[128,512]{1,0:T(8,128)(2,1)S(1)}, bf16[128,512]{1,0:T(8,128)(2,1)S(1)}, u32[]{:S(2)}, u32[]{:S(2)}) collective-permute-start(bf16[128,512]{1,0:T(8,128)(2,1)S(1)} %collective-permute-done.27.refs_4_), channel_id=1, source_target_pairs={{0,4},{4,0},{8,12},{12,8},{16,20},{20,16},{24,28},{28,24},{1,5},{5... | collective-permute-start | bytes 393224 | tf_op jit(solution)/shard_map/ppermute | solution.py:429
  109.6 1.5 %collective-permute-start.26 = (bf16[128,512]{1,0:T(8,128)(2,1)S(1)}, bf16[128,512]{1,0:T(8,128)(2,1)S(1)}, u32[]{:S(2)}, u32[]{:S(2)}) collective-permute-start(bf16[128,512]{1,0:T(8,128)(2,1)S(1)} %collective-permute-done.25.refs_2_), channel_id=1, source_target_pairs={{0,4},{4,0},{8,12},{12,8},{16,20},{20,16},{24,28},{28,24},{1,5},{5... | collective-permute-start | bytes 393224 | tf_op jit(solution)/shard_map/ppermute | solution.py:429
  (12 other events, 87.0 us)

commit v2 on v1

v2 whole, which is shorter than its diff:
```python
import functools

import jax
import jax.numpy as jnp
import numpy as np
from jax import lax
from jax.experimental import pallas as pl
from jax.experimental.pallas import tpu as pltpu
from jax.sharding import PartitionSpec as P

HEADS = 8
HEAD_DIM = 64
D = 512
FF = 2048
ROT = 16
HALF = 64
TOK = 128
EPS = 1e-05
F32 = jnp.float32
BF16 = jnp.bfloat16
VMEM_LIMIT = 32 * 1024 * 1024
WIDE_LIMIT = 60 * 1024 * 1024


def mm(left, right, dims):
    return lax.dot_general(left, right, (dims, ((), ())), preferred_element_type=F32)


def mm_nn(left, right):
    return mm(left, right, ((1,), (0,)))


def mm_nt(left, right):
    return mm(left, right, ((1,), (1,)))


def mm_tn(left, right):
    return mm(left, right, ((0,), (0,)))


def vmem_call(body, out_shape, scratch=(), n_smem=0, n_in=0, n_any=0, cost=None, name=None):
    smem = pl.BlockSpec(memory_space=pltpu.SMEM)
    vmem = pl.BlockSpec(memory_space=pltpu.VMEM)
    return pl.pallas_call(
        body,
        out_shape=out_shape,
        in_specs=[smem] * n_smem + [vmem] * n_in + [pl.BlockSpec(memory_space=pl.ANY)] * n_any,
        out_specs=jax.tree.map(lambda _: vmem, out_shape),
        scratch_shapes=list(scratch),
        compiler_params=pltpu.CompilerParams(vmem_limit_bytes=VMEM_LIMIT),
        cost_estimate=cost,
        name=name,
    )


def half_pick(block, odd, to_upper):
    moved = pltpu.roll(block, 64, 1)
    return jnp.where(odd, block if to_upper else moved, moved if to_upper else block)


def low_lanes(shape):
    return lax.broadcasted_iota(jnp.int32, shape, len(shape) - 1) % 128 < 64


def pack_body(nz, place, *refs):
    q_ref, k_ref, v_ref = refs[:3]
    ups = refs[3 : 3 + nz]
    w_down, x, g = refs[3 + nz : 6 + nz]
    vectors = refs[6 + nz : 14 + nz]
    pay, piece, small = refs[14 + nz :]
    odd = (place[0] % 2) == 1
    rows = q_ref.shape[0]
    low = low_lanes((rows, 128))
    small[...] = jnp.zeros_like(small)
    at = 0
    for vector in vectors:
        for r in range(vector.shape[0] // 128):
            small[at : at + 1, :] = vector[r * 128 : (r + 1) * 128].astype(F32).reshape(1, 128)
            at += 1
    few = small[...]
    spare = jnp.concatenate([pltpu.roll(few, 64, 1), few, jnp.zeros((rows - 32, 128), F32)], axis=0)
    q = half_pick(q_ref[...].astype(F32), odd, False)
    k = half_pick(k_ref[...].astype(F32), odd, True)
    v = half_pick(v_ref[...].astype(F32), odd, False)
    pay[:, 0:128] = jnp.where(low, q, k).astype(BF16)
    pay[:, 128:256] = jnp.where(low, v, spare).astype(BF16)
    for z in range(0, nz, 2):
        even = half_pick(ups[z][...].astype(F32), odd, False)
        later = half_pick(ups[z + 1][...].astype(F32), odd, True)
        pay[:, 256 + z * 64 : 256 + z * 64 + 128] = jnp.where(low, even, later).astype(BF16)
    pay[0:64, 512:768] = w_down[:, 0:256]
    pay[64:128, 512:768] = w_down[:, 256:512]
    piece[0:TOK, :] = x[0]
    piece[TOK : 2 * TOK, :] = g[0]


def later_body(place, pay, w_out, after, again, head_w):
    again[...] = pay[...]
    head_w[...] = w_out[...]


def later_call(place, pay, w_out, after):
    outs = [shape(pay.shape, BF16), shape((HEAD_DIM, D), BF16)]
    return pl.pallas_call(
        later_body,
        out_shape=outs,
        grid_spec=pltpu.PrefetchScalarGridSpec(
            num_scalar_prefetch=1,
            grid=(1,),
            in_specs=[
                pl.BlockSpec(pay.shape, lambda i, s: (0, 0)),
                pl.BlockSpec((HEAD_DIM, D), lambda i, s: (s[0] % 2, 0)),
                pl.BlockSpec(memory_space=pl.ANY),
            ],
            out_specs=[pl.BlockSpec(o.shape, lambda i, s: (0, 0)) for o in outs],
        ),
        compiler_params=pltpu.CompilerParams(vmem_limit_bytes=VMEM_LIMIT),
        name="later",
    )(place, pay, w_out, after)


def pack_call(nz, place, w_qkv, w_up, w_down, x, g, vectors):
    span = FF // nz // 128
    rows = D // nz

    def lane_block(first):
        return pl.BlockSpec((rows, 128), lambda i, s: (0, first + s[0] // 2))

    def whole(array):
        rank = array.ndim
        return pl.BlockSpec(array.shape, lambda i, s: (0,) * rank)

    outs = [shape((rows, 768), BF16), shape((2 * TOK, D), BF16)]
    return pl.pallas_call(
        functools.partial(pack_body, nz),
        out_shape=outs,
        grid_spec=pltpu.PrefetchScalarGridSpec(
            num_scalar_prefetch=1,
            grid=(1,),
            in_specs=[lane_block(0), lane_block(D // 128), lane_block(2 * D // 128)]
            + [lane_block(z * span) for z in range(nz)]
            + [
                pl.BlockSpec((64, D), lambda i, s: (s[0], 0)),
                whole(x),
                whole(g),
            ]
            + [whole(v) for v in vectors],
            out_specs=[whole(o) for o in outs],
            scratch_shapes=[pltpu.VMEM((16, 128), F32)],
        ),
        compiler_params=pltpu.CompilerParams(vmem_limit_bytes=WIDE_LIMIT),
        name="pack",
    )(place, w_qkv, w_qkv, w_qkv, *([w_up] * nz), w_down, x, g, *vectors)


def unpack(nz, place, pieces, w_all, w_up, w_down, params, held):
    me, zed = place[0], place[1]
    pair = me // 2
    odd = (me % 2) == 1
    for k in range(nz):
        z = zed ^ k
        tall = pl.ds(pl.multiple_of(z * 128, 128), 128)
        flat = pl.ds(pl.multiple_of(z * 64, 64), 64)
        w_all[tall, 0:128] = pieces[k][:, 0:128]
        third = pieces[k][:, 128:256].astype(F32)
        w_all[tall, 128:256] = jnp.where(low_lanes((128, 128)), third, 0.0).astype(BF16)
        held[z] = jnp.where(low_lanes((16, 128)), pltpu.roll(third[0:16], 64, 1), third[16:32])
        w_up[tall, :] = pieces[k][:, 256:512]
        w_down[flat, 0:256] = pieces[k][0:64, 512:768]
        w_down[flat, 256:512] = pieces[k][64:128, 512:768]
    params[...] = jnp.zeros_like(params)
    for z in range(nz):
        lanes = slice(z * 128, (z + 1) * 128)
        params[0:4, lanes] = held[z, 0:4, :]
        params[4:5, lanes] = held[z, 4:5, :] + held[z, 5:6, :]
    low = low_lanes((1, 128))

    def qkv_row(group):
        index = group * 4 + pair
        z = index // 3
        return held[z, pl.ds(6 + index - 3 * z, 1), :]

    q = half_pick(qkv_row(0), odd, False)
    k = half_pick(qkv_row(1), odd, True)
    v = half_pick(qkv_row(2), odd, False)
    params[5:6, 0:128] = jnp.where(low, q, k)
    params[5:6, 128:256] = jnp.where(low, v, 0.0)
    for z in range(0, nz, 2):
        even = half_pick(held[z, pl.ds(9 + pair, 1), :], odd, False)
        later = half_pick(held[z + 1, pl.ds(9 + pair, 1), :], odd, True)
        params[6:7, z * 64 : z * 64 + 128] = jnp.where(low, even, later)


def normalized(x):
    center = x - jnp.mean(x, axis=-1, keepdims=True)
    spread = jnp.mean(center * center, axis=-1, keepdims=True)
    inv = lax.rsqrt(spread + EPS)
    return center * inv, inv


def fold(values):
    return jnp.sum(values.reshape(values.shape[0] // 8, 8, values.shape[1]), axis=0)


def layer_body(n, nz, fast, place, order, *refs):
    seq = n * TOK
    qblk = min(256, seq)
    pieces = refs[:n]
    n_w = nz if fast else 4
    given = refs[n : n + n_w]
    w_out, cos_t, sin_t = refs[n + n_w : n + n_w + 3]
    outs = refs[n + n_w + 3 :]
    n_pay = nz if fast else 4
    keep_pay, send_pay, g_out, param_out = outs[:4]
    pays = outs[4 : 4 + n_pay]
    scratch = outs[4 + n_pay :]
    (w_all, w_up, w_down, params, held, spare) = scratch[:6]
    (norms, nhats, raw, qs, ks, vs, dms, mixs, dks, dvs, dqs, dqkvs, mixn, dqkvn, gs) = scratch[6:21]
    (norm2s, hiddens, dpres, grad_w, grad_up, grad_down, vec) = scratch[21:]
    width = w_up.shape[1]
    zed = place[1]
    if fast:
        unpack(nz, place, given, w_all, w_up, w_down, params, held)
    else:
        w_all[...] = given[0][...]
        w_up[...] = given[1][...]
        w_down[...] = given[2][...]
        params[...] = given[3][...]
    param_out[...] = params[...]
    gain, shift = params[0:1, :], params[1:2, :]
    gain2, shift2 = params[2:3, :], params[3:4, :]
    bias = params[5:6, 0:256]
    b_up = params[6:7, 0:width]

    def sorted_rows(block):
        return pl.ds(pl.multiple_of(order[block] * HALF, HALF), HALF)

    for p in range(n):
        rows = slice(p * TOK, (p + 1) * TOK)
        nhat, _ = normalized(pieces[p][0:TOK, :].astype(F32))
        g = pieces[p][TOK : 2 * TOK, :]
        norm = (nhat * gain + shift).astype(BF16)
        nhats[rows, :] = nhat
        norms[rows, :] = norm
        norm2s[rows, :] = (nhat * gain2 + shift2).astype(BF16)
        gs[rows, :] = g
        qkv = mm_nn(norm, w_all[...]) + bias
        dmix = mm_nt(g, w_out[...]).astype(BF16)
        for h in range(TOK // HALF):
            here = slice(h * HALF, (h + 1) * HALF)
            where = sorted_rows(p * (TOK // HALF) + h)
            raw[where, :] = qkv[here, :]
            dms[where, :] = dmix[here, :]

    lanes = lax.broadcasted_iota(jnp.int32, (qblk, 128), 1) % 64

    def swapped(t):
        return jnp.where(lanes < ROT // 2, pltpu.roll(t, 128 - ROT // 2, 1), pltpu.roll(t, ROT // 2, 1))

    for i in range(seq // qblk):
        rows = slice(i * qblk, (i + 1) * qblk)
        qk = raw[rows, 0:128]
        turned = (qk * cos_t[rows, :] + swapped(qk) * sin_t[rows, :]).astype(BF16)
        qs[rows, :] = turned[:, 0:64]
        ks[rows, :] = turned[:, 64:128]
        vs[rows, :] = raw[rows, 128:192].astype(BF16)

    dks[...] = jnp.zeros_like(dks)
    dvs[...] = jnp.zeros_like(dvs)
    for i in range(seq // qblk):
        rows = slice(i * qblk, (i + 1) * qblk)
        span = (i + 1) * qblk
        q = qs[rows, :]
        keys = ks[0:span, :]
        values = vs[0:span, :]
        s = mm_nt(q, keys) * 0.125
        q_at = lax.broadcasted_iota(jnp.int32, (qblk, span), 0) + i * qblk
        k_at = lax.broadcasted_iota(jnp.int32, (qblk, span), 1)
        s = jnp.where(q_at >= k_at, s, -1e30)
        top = jnp.max(s, axis=1, keepdims=True)
        e = jnp.exp(s - top)
        prob = e * (1.0 / jnp.sum(e, axis=1, keepdims=True))
        prob_b = prob.astype(BF16)
        mix = mm_nn(prob_b, values)
        mixs[rows, :] = mix.astype(BF16)
        dmix = dms[rows, :]
        delta = jnp.sum(dmix.astype(F32) * mix, axis=1, keepdims=True)
        dprob = mm_nt(dmix, values)
        ds = (prob * (dprob - delta)).astype(BF16)
        dqs[rows, 0:64] = mm_nn(ds, keys) * 0.125
        dks[:, 0:span] += mm_tn(q, ds)
        dvs[:, 0:span] += mm_tn(dmix, prob_b)
    dqs[:, 64:128] = dks[...].T * 0.125
    dqkvs[:, 128:192] = dvs[...].T.astype(BF16)
    dqkvs[:, 192:256] = jnp.zeros((seq, 64), BF16)
    for i in range(seq // qblk):
        rows = slice(i * qblk, (i + 1) * qblk)
        dqk = dqs[rows, :]
        dqkvs[rows, 0:128] = (dqk * cos_t[rows, :] - swapped(dqk) * sin_t[rows, :]).astype(BF16)

    scale = None
    if n > HEADS:
        scale = jnp.where(place[0] % (n // HEADS) == 0, 1.0, 0.0).astype(BF16)
    for b in range(seq // HALF):
        here = slice(b * HALF, (b + 1) * HALF)
        where = sorted_rows(b)
        mix, dqkv = mixs[where, :], dqkvs[where, :]
        if scale is not None:
            mix, dqkv = mix * scale, dqkv * scale
        mixn[here, :] = mix
        dqkvn[here, :] = dqkv

    g_gain = jnp.zeros((8, D), F32)
    g_shift = jnp.zeros((8, D), F32)
    g_bias = jnp.zeros((8, 256), F32)
    g_gain2 = jnp.zeros((8, D), F32)
    g_shift2 = jnp.zeros((8, D), F32)
    g_sum = jnp.zeros((8, D), F32)
    g_bup = jnp.zeros((8, width), F32)
    for p in range(n):
        rows = slice(p * TOK, (p + 1) * TOK)
        g, nhat = gs[rows, :], nhats[rows, :]
        pre = mm_nn(norm2s[rows, :], w_up[...]) + b_up
        cdf = 0.5 * (1.0 + lax.erf(pre * 0.7071067811865476))
        hidden = (pre * cdf).astype(BF16)
        slope = cdf + pre * (0.3989422804014327 * jnp.exp(-0.5 * pre * pre))
        dpre = (mm_nt(g, w_down[...]) * slope).astype(BF16)
        hiddens[rows, :] = hidden
        dpres[rows, :] = dpre
        dqkv = dqkvn[rows, :]
        part_o = mm_nn(hidden, w_down[...]) + mm_nn(mixn[rows, :], w_out[...])
        dnorm2 = mm_nt(dpre, w_up[...])
        dnorm = mm_nt(dqkv, w_all[...])
        g_gain += fold(dnorm * nhat)
        g_shift += fold(dnorm)
        g_bias += fold(dqkv.astype(F32))
        g_gain2 += fold(dnorm2 * nhat)
        g_shift2 += fold(dnorm2)
        g_sum += fold(g.astype(F32))
        g_bup += fold(dpre.astype(F32))
        target = send_pay if p % 2 else keep_pay
        target[p // 2, :, 0:512] = part_o.astype(BF16)
        target[p // 2, :, 512:1024] = (dnorm * gain + dnorm2 * gain2).astype(BF16)
    vec[...] = jnp.zeros_like(vec)
    for row, value in ((0, g_gain), (1, g_shift), (2, g_gain2), (3, g_shift2), (4, g_sum), (5, g_bias), (6, g_bup)):
        vec[row : row + 1, 0 : value.shape[1]] = jnp.sum(value, axis=0, keepdims=True)
    g_out[...] = mm_tn(mixn[...], gs[...]).astype(BF16)
    grad_w[...] = mm_tn(dqkvn[...], norms[...]).T
    grad_up[...] = mm_tn(dpres[...], norm2s[...]).T.astype(BF16)
    grad_down[...] = mm_tn(hiddens[...], gs[...]).astype(BF16)
    if fast:
        spare[...] = jnp.zeros_like(spare)
        for j in range(8):
            lanes_j = vec[:, (j // 2) * 128 : (j // 2) * 128 + 128]
            spare[8 * j : 8 * j + 8, :] = lanes_j if j % 2 else pltpu.roll(lanes_j, 64, 1)
        low = low_lanes((128, 128))
        for k in range(nz):
            z = zed ^ k
            tall = pl.ds(pl.multiple_of(z * 128, 128), 128)
            flat = pl.ds(pl.multiple_of(z * 64, 64), 64)
            pays[k][:, 0:128] = grad_w[tall, 0:128].astype(BF16)
            pays[k][:, 128:256] = jnp.where(low, grad_w[tall, 128:256], spare[...]).astype(BF16)
            pays[k][:, 256:512] = grad_up[tall, :]
            pays[k][0:64, 512:768] = grad_down[flat, 0:256]
            pays[k][64:128, 512:768] = grad_down[flat, 256:512]
    else:
        pays[0][...] = grad_w[...].astype(BF16)
        pays[1][...] = grad_up[...]
        pays[2][...] = grad_down[...]
        pays[3][...] = vec[...]


def close_body(place, x_ref, g_ref, params, *refs):
    parts, out, grad = refs[:-2], refs[-2], refs[-1]
    x = x_ref[...].astype(F32)
    nhat, inv = normalized(x)
    total = parts[0][...].astype(F32)
    for part in parts[1:]:
        total = total + part[...].astype(F32)
    out[...] = (x + total[:, 0:512] + params[4:5, :]).astype(BF16)
    dn = total[:, 512:1024]
    lead = jnp.mean(dn, axis=-1, keepdims=True)
    along = jnp.mean(dn * nhat, axis=-1, keepdims=True)
    grad[...] = g_ref[...].astype(F32) + inv * (dn - lead - nhat * along)


def chip_body(keep, came, *outs):
    for k, out in enumerate(outs):
        out[...] = (keep[k].astype(F32) + came[k].astype(F32)).astype(BF16)


def gate_body(value, after, out):
    out[...] = value[...]


def sum_body(nz, *refs):
    parts, g_out, out = refs[:nz], refs[nz], refs[-1]
    total = parts[0][...].astype(F32)
    for part in parts[1:]:
        total = total + part[...].astype(F32)
    out[:, 0:768] = total.astype(BF16)
    out[0:64, 768:1024] = g_out[:, 0:256]
    out[64:128, 768:1024] = g_out[:, 256:512]


def finish_body(n, nz, place, *refs):
    alls = refs[:n]
    (ln1g, ln1b, gqkv, bqkv, gout, bout, ln2g, ln2b, gup, bup, gdown, bdown) = refs[n : n + 12]
    held_u, held_a, held_v, flat = refs[n + 12 :]
    me, zed = place[0], place[1]
    span = FF // nz
    total = jnp.zeros((8, D), F32)
    wide = low_lanes((8, 128))
    for k in range(n):
        who = me ^ k
        held_a[who] = alls[k][:, 0:256].astype(F32)
        held_u[who] = alls[k][:, 256:512].astype(F32)
        rows = pl.ds(pl.multiple_of(who * 64, 64), 64)
        gdown[rows, 0:256] = alls[k][0:64, 512:768].astype(F32)
        gdown[rows, 256:512] = alls[k][64:128, 512:768].astype(F32)
        spare = alls[k][0:64, 128:256].astype(F32)
        small = []
        for j in range(0, 8, 2):
            small.append(jnp.where(wide, pltpu.roll(spare[8 * j : 8 * j + 8], 64, 1), spare[8 * j + 8 : 8 * j + 16]))
        small = jnp.concatenate(small, axis=1)
        held_v[who] = small
        total = total + small
    for h in range(0, n, 2):
        even, later = held_a[h], held_a[h + 1]
        low = low_lanes((128, 128))
        at = h * 64
        gqkv[:, at : at + 128] = jnp.where(low, even[:, 0:128], pltpu.roll(later[:, 0:128], 64, 1))
        gqkv[:, D + at : D + at + 128] = jnp.where(low, pltpu.roll(even[:, 0:128], 64, 1), later[:, 0:128])
        gqkv[:, 2 * D + at : 2 * D + at + 128] = jnp.where(low, even[:, 128:256], pltpu.roll(later[:, 128:256], 64, 1))
        for z in range(0, nz, 2):
            lanes = slice(z * 64, z * 64 + 128)
            e, l = held_u[h][:, lanes], held_u[h + 1][:, lanes]
            gup[:, z * span + at : z * span + at + 128] = jnp.where(low, e, pltpu.roll(l, 64, 1))
            gup[:, (z + 1) * span + at : (z + 1) * span + at + 128] = jnp.where(low, pltpu.roll(e, 64, 1), l)
        low = low_lanes((1, 128))
        e, l = held_v[h], held_v[h + 1]
        flat[h // 2 : h // 2 + 1, :] = jnp.where(low, e[5:6, 0:128], pltpu.roll(l[5:6, 0:128], 64, 1))
        flat[4 + h // 2 : 5 + h // 2, :] = jnp.where(low, pltpu.roll(e[5:6, 0:128], 64, 1), l[5:6, 0:128])
        flat[8 + h // 2 : 9 + h // 2, :] = jnp.where(low, e[5:6, 128:256], pltpu.roll(l[5:6, 128:256], 64, 1))
        lane = pl.ds(pl.multiple_of((zed // 2) * 128, 128), 128)
        odd = (zed % 2) == 1
        e = half_pick(held_v[h, 6:7, lane], odd, False)
        l = half_pick(held_v[h + 1, 6:7, lane], odd, True)
        bup[:, at : at + 128] = jnp.where(low, e, l)
    mine = pl.multiple_of((me % 2) * 64, 64)
    other = pl.multiple_of((1 - me % 2) * 64, 64)
    for parity, start in ((0, mine), (1, other)):
        acc = alls[parity][:, 768:1024].astype(F32)
        for k in range(parity + 2, n, 2):
            acc = acc + alls[k][:, 768:1024].astype(F32)
        gout[pl.ds(start, 64), 0:256] = acc[0:64]
        gout[pl.ds(start, 64), 256:512] = acc[64:128]
    flat[12:20, :] = jnp.zeros((8, 128), F32)
    for r in range(3):
        bqkv[:, r * 128 : (r + 1) * 128] = flat[pl.ds(zed * 3 + r, 1), :]
    held_v[0] = total
    lane = pl.ds(pl.multiple_of(zed * 128, 128), 128)
    ln1g[...] = held_v[0, 0:1, lane]
    ln1b[...] = held_v[0, 1:2, lane]
    ln2g[...] = held_v[0, 2:3, lane]
    ln2b[...] = held_v[0, 3:4, lane]
    held_v[1] = total * (1.0 / n)
    bout[...] = held_v[1, 4:5, lane]
    bdown[...] = held_v[1, 4:5, lane]


def xor_pairs(size, k):
    return [(i, i ^ k) for i in range(size)]


def gather_ctx(value, n):
    got = {0: value}
    for k in range(2, n, 2):
        got[k] = lax.ppermute(value, "ctx", xor_pairs(n, k))
    for k in range(0, n, 2):
        got[k + 1] = lax.ppermute(got[k], "ctx", xor_pairs(n, 1))
    return [got[k] for k in range(n)]


def gather_fsdp(value, nz):
    return [value] + [lax.ppermute(value, "fsdp", xor_pairs(nz, k)) for k in range(1, nz)]


def swap_fsdp(values, nz):
    return [values[0]] + [lax.ppermute(values[k], "fsdp", xor_pairs(nz, k)) for k in range(1, nz)]


def rotary_tables(seq):
    pos = np.arange(seq, dtype=np.float32)
    inverse = (np.float32(10000.0) ** (-np.arange(ROT // 2, dtype=np.float32) * np.float32(2.0) / np.float32(ROT))).astype(np.float32)
    angles = (pos[:, None] * inverse[None, :]).astype(np.float32).astype(np.float64)
    cos_t = np.ones((seq, 64), np.float32)
    sin_t = np.zeros((seq, 64), np.float32)
    half = ROT // 2
    cos_t[:, 0:half] = np.cos(angles)
    cos_t[:, half:ROT] = np.cos(angles)
    sin_t[:, 0:half] = -np.sin(angles)
    sin_t[:, half:ROT] = np.sin(angles)
    return np.concatenate([cos_t, cos_t], axis=1), np.concatenate([sin_t, sin_t], axis=1)


def shape(dims, dtype=F32):
    return jax.ShapeDtypeStruct(dims, dtype)


def per_device(
    n,
    nz,
    inputs,
    block_order,
    ln1_gain,
    ln1_bias,
    w_qkv,
    b_qkv,
    w_attn_out,
    b_attn_out,
    ln2_gain,
    ln2_bias,
    w_up,
    b_up,
    w_down,
    b_down,
    cotangent,
):
    fast = n == HEADS and nz * 2 == HEADS
    seq = n * TOK
    width = FF // n
    me = lax.axis_index("ctx").astype(jnp.int32)
    zed = lax.axis_index("fsdp").astype(jnp.int32)
    place = jnp.stack([me, zed])
    x, g = inputs[0], cotangent[0]
    blocks = TOK // HALF
    chunk_at = (jnp.arange(n, dtype=jnp.int32) ^ me)[:, None] * blocks + jnp.arange(blocks, dtype=jnp.int32)[None, :]
    pick = chunk_at.reshape(-1)[:, None] == jnp.arange(n * blocks, dtype=jnp.int32)[None, :]
    order = jnp.sum(jnp.where(pick, block_order[None, :], 0), axis=1).astype(jnp.int32)
    cos_t, sin_t = rotary_tables(seq)

    if fast:
        vectors = (ln1_gain, ln1_bias, ln2_gain, ln2_bias, b_attn_out, b_down, b_qkv, b_up)
        pack, piece = pack_call(nz, place, w_qkv, w_up, w_down, inputs, cotangent, vectors)
        pieces = gather_ctx(piece, n)
        near, pack_w = later_call(place, pack, w_attn_out, pieces[2])
        given = swap_fsdp([pack, near, pack, pack], nz)
        pairs = []
        for c in range(n):
            for z in range(nz):
                pairs.append((c * nz + z, (2 * z + c % 2) * nz + c // 2))
        head_w = lax.ppermute(pack_w, ("ctx", "fsdp"), pairs)
    else:
        whole = [
            lax.all_gather(v, "fsdp", axis=0, tiled=True)
            for v in (ln1_gain, ln1_bias, ln2_gain, ln2_bias, b_attn_out, b_down, b_qkv, b_up)
        ]
        whole = [v.astype(F32) for v in whole]
        head = me // (n // HEADS)
        bq = lax.dynamic_index_in_dim(whole[6].reshape(3, HEADS, HEAD_DIM), head, 1, False).reshape(-1)
        bu = lax.dynamic_index_in_dim(whole[7].reshape(n, width), me, 0, False)
        params = jnp.stack(
            [whole[0], whole[1], whole[2], whole[3], whole[4] + whole[5]]
            + [jnp.pad(bq, (0, D - 3 * HEAD_DIM)), jnp.pad(bu, (0, D - width)), jnp.zeros((D,), F32)]
        )
        wq = lax.dynamic_index_in_dim(w_qkv.reshape(-1, 3, HEADS, HEAD_DIM), head, 2, False).reshape(-1, 3 * HEAD_DIM)
        given = [jnp.pad(lax.all_gather(wq, "fsdp", axis=0, tiled=True), ((0, 0), (0, 64)))]
        wu = lax.dynamic_slice_in_dim(w_up, me * width, width, 1)
        wd = lax.all_gather(w_down, "fsdp", axis=0, tiled=True)
        given += [lax.all_gather(wu, "fsdp", axis=0, tiled=True), lax.dynamic_slice_in_dim(wd, me * width, width, 0)]
        wo = lax.all_gather(w_attn_out, "fsdp", axis=0, tiled=True)
        given.append(params)
        pieces = gather_ctx(jnp.concatenate([x, g], axis=0), n)
        head_w = lax.dynamic_slice_in_dim(wo, head * HEAD_DIM, HEAD_DIM, 0)

    if fast:
        pays = [shape((D // nz, 768), BF16)] * nz
    else:
        pays = [shape((D, 256), BF16), shape((D, width), BF16), shape((width, D), BF16), shape((8, D))]
    half = (n // 2, TOK, 2 * D)
    layer_out = vmem_call(
        functools.partial(layer_body, n, nz, fast),
        [shape(half, BF16), shape(half, BF16), shape((HEAD_DIM, D), BF16), shape((8, D))] + pays,
        scratch=[
            pltpu.VMEM((D, 256), BF16),
            pltpu.VMEM((D, width), BF16),
            pltpu.VMEM((width, D), BF16),
            pltpu.VMEM((8, D), F32),
            pltpu.VMEM((nz, 16, 128), F32),
            pltpu.VMEM((128, 128), F32),
            pltpu.VMEM((seq, D), BF16),
            pltpu.VMEM((seq, D), F32),
            pltpu.VMEM((seq, 256), F32),
            pltpu.VMEM((seq, 64), BF16),
            pltpu.VMEM((seq, 64), BF16),
            pltpu.VMEM((seq, 64), BF16),
            pltpu.VMEM((seq, 64), BF16),
            pltpu.VMEM((seq, 64), BF16),
            pltpu.VMEM((64, seq), F32),
            pltpu.VMEM((64, seq), F32),
            pltpu.VMEM((seq, 128), F32),
            pltpu.VMEM((seq, 256), BF16),
            pltpu.VMEM((seq, 64), BF16),
            pltpu.VMEM((seq, 256), BF16),
            pltpu.VMEM((seq, D), BF16),
            pltpu.VMEM((seq, D), BF16),
            pltpu.VMEM((seq, width), BF16),
            pltpu.VMEM((seq, width), BF16),
            pltpu.VMEM((D, 256), F32),
            pltpu.VMEM((D, width), BF16),
            pltpu.VMEM((width, D), BF16),
            pltpu.VMEM((8, D), F32),
        ],
        n_smem=2,
        n_in=n + len(given) + 3,
        cost=pl.CostEstimate(flops=26 * seq * seq * 64, bytes_accessed=12 * seq * D, transcendentals=2 * seq * seq),
        name="layer",
    )(place, order, *pieces, *given, head_w, cos_t, sin_t)
    keep_pay, send_pay, g_out, params = layer_out[:4]
    pay = layer_out[4:]

    came = lax.ppermute(send_pay, "ctx", xor_pairs(n, 1))
    chip_sum = vmem_call(chip_body, [shape((TOK, 2 * D), BF16)] * (n // 2), n_in=2, name="chip_sum")(keep_pay, came)
    parts = [chip_sum[0]] + [lax.ppermute(chip_sum[k // 2], "ctx", xor_pairs(n, k)) for k in range(2, n, 2)]
    output, grad_inputs = vmem_call(
        close_body,
        (shape((TOK, D), BF16), shape((TOK, D))),
        n_smem=1,
        n_in=3 + len(parts),
        name="close",
    )(place, x, g, params, *parts)

    if fast:
        g_out = vmem_call(gate_body, shape(g_out.shape, BF16), n_in=1, n_any=1, name="gate")(g_out, parts[1])
        out_got = lax.ppermute(g_out, ("ctx", "fsdp"), [(b, a) for a, b in pairs])
        got = swap_fsdp(pay, nz)
        share = vmem_call(functools.partial(sum_body, nz), shape((D // nz, 1024), BF16), n_in=nz + 1, n_any=len(parts) - 1, name="sum")(
            *got, out_got, *parts[1:]
        )
        alls = gather_ctx(share, n)
        dz = D // nz
        outs = vmem_call(
            functools.partial(finish_body, n, nz),
            [
                shape((1, dz)),
                shape((1, dz)),
                shape((dz, 3 * D)),
                shape((1, 3 * dz)),
                shape((dz, D)),
                shape((1, dz)),
                shape((1, dz)),
                shape((1, dz)),
                shape((dz, FF)),
                shape((1, FF // nz)),
                shape((FF // nz, D)),
                shape((1, dz)),
            ],
            scratch=[
                pltpu.VMEM((n, 128, 256), F32),
                pltpu.VMEM((n, 128, 256), F32),
                pltpu.VMEM((n, 8, D), F32),
                pltpu.VMEM((24, 128), F32),
            ],
            n_smem=1,
            n_in=n,
            name="finish",
        )(place, *alls)
        outs = [o.reshape(-1) if o.shape[0] == 1 else o for o in outs]
    else:
        everyone = ("ctx", "fsdp")
        head = me // (n // HEADS)
        g_qkv, g_up, g_down, vec = pay

        def own(full, axis=0):
            size = full.shape[axis] // nz
            return lax.dynamic_slice_in_dim(full, zed * size, size, axis)

        def spread(part, dims, index, axis):
            full = jnp.zeros(dims, part.dtype)
            return lax.psum(lax.dynamic_update_index_in_dim(full, part, index, axis), everyone).astype(F32)

        qkv_full = spread(g_qkv[:, 0:192].reshape(D, 3, HEAD_DIM), (D, 3, HEADS, HEAD_DIM), head, 2).reshape(D, 3 * D)
        out_full = spread(g_out, (HEADS, HEAD_DIM, D), head, 0).reshape(D, D)
        up_full = spread(g_up, (D, n, width), me, 1).reshape(D, FF)
        down_full = spread(g_down, (n, width, D), me, 0).reshape(FF, D)
        bq_full = spread(vec[5, 0:192].reshape(3, HEAD_DIM), (3, HEADS, HEAD_DIM), head, 1).reshape(3 * D)
        bu_full = spread(vec[6, 0:width], (n, width), me, 0).reshape(FF)
        flat = lax.psum(vec, everyone)
        b_full = flat[4] * (1.0 / n)
        outs = [own(v) for v in (flat[0], flat[1], qkv_full, bq_full, out_full, b_full)]
        outs += [own(v) for v in (flat[2], flat[3], up_full, bu_full, down_full, b_full)]
    return (output[None], grad_inputs[None], *outs)


def solution(mesh):
    rows, flat, tokens = P("fsdp", None), P("fsdp"), P("fsdp", "ctx", None)
    weights = (flat, flat, rows, flat, rows, flat, flat, flat, rows, flat, rows, flat)
    return jax.shard_map(
        functools.partial(per_device, mesh.shape["ctx"], mesh.shape["fsdp"]),
        mesh=mesh,
        in_specs=(tokens, P(), *weights, tokens),
        out_specs=(tokens, tokens, *weights),
        check_vma=False,
    )
```

time: 123 us -> 100 us (0.81)
  starting transfers between devices: 55.3 us -> 42.4 us
  local copies, waits for them, and re-layouts: 12.8 us -> 3.11 us
    ppermute x10 -> x1, starting transfers between devices: 18.7 us -> 0.66 us  [per_device(): out_got = lax.ppermute(g_out, ('ctx', 'fsdp'), [(b, a) for a, b in pairs])]
    ppermute x6, waiting for transfers between devices: 5.59 us -> 17.1 us  [swap_fsdp(): lax.ppermute(values[k], 'fsdp', xor_pairs(nz, k))]
    unnamed x29 -> x20, local copies, waits for them, and re-layouts: 11.8 us -> 3.03 us
    ppermute x3, starting transfers between devices: 2.71 us -> 10.3 us  [per_device(): lax.ppermute(chip_sum[k // 2], 'ctx', xor_pairs(n, k))]
    ppermute x10 -> x1, waiting for transfers between devices: 6.27 us -> 0.01 us  [per_device(): out_got = lax.ppermute(g_out, ('ctx', 'fsdp'), [(b, a) for a, b in pairs])]
    ppermute x3, waiting for transfers between devices: 6.75 us -> 1.97 us  [per_device(): lax.ppermute(chip_sum[k // 2], 'ctx', xor_pairs(n, k))]
    ppermute x16 -> x8, waiting for transfers between devices: 2.91 us -> 0.02 us  [gather_ctx(): got[k + 1] = lax.ppermute(got[k], 'ctx', xor_pairs(n, 1))]
    ppermute x1, waiting for transfers between devices: 0.01 us -> 2.65 us  [per_device(): came = lax.ppermute(send_pay, 'ctx', xor_pairs(n, 1))]
  transfers between devices with their start and end apart: 49 -> 26, of which waited for: 19 -> 10; matrix products, arithmetic and copies ran while one was open for 7% -> 0% of each run, Pallas kernels for 7% -> 2%
where the time goes in v2:
time: 100 us
  starting transfers between devices  42.4 us (42%)
  waiting for transfers between devices  33.5 us (34%)
  Pallas kernels  18.6 us (19%)
  local copies, waits for them, and re-layouts  3.11 us (3%)
  other arithmetic  1.44 us (1%)
    ppermute x6, starting transfers between devices, swap_fsdp(): lax.ppermute(values[k], 'fsdp', xor_pairs(nz, k))  18.3 us
    ppermute x6, waiting for transfers between devices, swap_fsdp(): lax.ppermute(values[k], 'fsdp', xor_pairs(nz, k))  17.1 us
    ppermute x6, waiting for transfers between devices, gather_ctx(): got[k] = lax.ppermute(value, 'ctx', xor_pairs(n, k))  11.8 us
    ppermute x6, starting transfers between devices, gather_ctx(): got[k] = lax.ppermute(value, 'ctx', xor_pairs(n, k))  11.6 us
    pallas_call x1, Pallas kernels, per_device(): vmem_call(functools.partial(layer_body, n, nz, fast), [shape(half, BF16),...  10.4 us
    ppermute x3, starting transfers between devices, per_device(): lax.ppermute(chip_sum[k // 2], 'ctx', xor_pairs(n, k))  10.3 us
    unnamed x20, local copies, waits for them, and re-layouts  3.03 us
    pallas_call x1, Pallas kernels, per_device(): vmem_call(functools.partial(finish_body, n, nz), [shape((1, dz)), shape((...  2.9 us
  transfers between devices with their start and end apart: 26, of which 10 were waited for; matrix products, arithmetic and copies ran while one was open for 0% of the time, Pallas kernels for 2%

profile of v2, /device:TPU:0, one launch (start us, length us, event | category | flops | bytes accessed | tf_op | source)
XLA Modules:
  0.0 100.0 jit_solution(8760662970617879359)
XLA Ops:
  0.6 0.6 pad_add_fusion.place
  1.2 2.8 %pack.1 = (bf16[128,768]{1,0:T(8,128)(2,1)}, bf16[256,512]{1,0:T(8,128)(2,1)}) custom-call(s32[2]{0:T(128)} %pad_add_fusion.place, bf16[128,1536]{1,0:T(8,128)(2,1)} %refs_2_.1, bf16[128,1536]{1,0:T(8,128)(2,1)} %refs_2_.1, bf16[128,1536]{1,0:T(8,128)(2,1)} %refs_2_.1, bf16[128,2048]{1,0:T(8,128)(2,1)} %refs_6_.1, bf16[128,2048]{1,0:T(8,128)(2,1)} %refs_6_.1, ...), custom_call_target="tpu_custom_call" | custom-call | tf_op jit(solution)/shard_map/pack/pallas_call | solution.py:134
  4.1 2.9 %collective-permute-start.1 = (bf16[256,512]{1,0:T(8,128)(2,1)}, bf16[256,512]{1,0:T(8,128)(2,1)S(1)}, u32[]{:S(2)}, u32[]{:S(2)}) collective-permute-start(bf16[256,512]{1,0:T(8,128)(2,1)} %get-tuple-element.44.refs_0_), channel_id=1, source_target_pairs={{0,8},{4,12},{8,0},{12,4},{16,24},{20,28},{24,16},{28,20},{1,9},{5... | collective-permute-start | bytes 786440 | tf_op jit(solution)/shard_map/ppermute | solution.py:479
  7.0 1.5 %collective-permute-start.5 = (bf16[256,512]{1,0:T(8,128)(2,1)}, bf16[256,512]{1,0:T(8,128)(2,1)S(1)}, u32[]{:S(2)}, u32[]{:S(2)}) collective-permute-start(bf16[256,512]{1,0:T(8,128)(2,1)} %get-tuple-element.44.refs_0_), channel_id=1, source_target_pairs={{0,24},{4,28},{8,16},{12,20},{16,8},{20,12},{24,0},{28,4},{1,25},{... | collective-permute-start | bytes 786440 | tf_op jit(solution)/shard_map/ppermute | solution.py:479
  8.5 0.0 collective-permute-start.3
  8.6 4.1 %collective-permute-start.9 = (bf16[128,768]{1,0:T(8,128)(2,1)}, bf16[128,768]{1,0:T(8,128)(2,1)S(1)}, u32[]{:S(2)}, u32[]{:S(2)}) collective-permute-start(bf16[128,768]{1,0:T(8,128)(2,1)} %get-tuple-element.45.pay.refs_8_), channel_id=1, source_target_pairs={{0,3},{1,2},{2,1},{3,0},{4,7},{5,6},{6,5},{7,4},{8,11},{9,10},{10,... | collective-permute-start | bytes 589832 | tf_op jit(solution)/shard_map/ppermute | solution.py:490
  12.6 1.7 %collective-permute-done.1.after.refs_2_ = bf16[256,512]{1,0:T(8,128)(2,1)S(1)} collective-permute-done((bf16[256,512]{1,0:T(8,128)(2,1)}, bf16[256,512]{1,0:T(8,128)(2,1)S(1)}, u32[]{:S(2)}, u32[]{:S(2)}) %collective-permute-start.1) | collective-permute-done | bytes 262176 | tf_op jit(solution)/shard_map/ppermute | solution.py:479
  14.4 0.0 copy-start.2
  14.4 0.9 copy-done.2
  15.3 0.6 later.1
  15.9 2.8 %collective-permute-done.9.refs_11_ = bf16[128,768]{1,0:T(8,128)(2,1)S(1)} collective-permute-done((bf16[128,768]{1,0:T(8,128)(2,1)}, bf16[128,768]{1,0:T(8,128)(2,1)S(1)}, u32[]{:S(2)}, u32[]{:S(2)}) %collective-permute-start.9) | collective-permute-done | bytes 196640 | tf_op jit(solution)/shard_map/ppermute | solution.py:490
  18.7 7.6 %collective-permute-start.7 = (bf16[128,768]{1,0:T(8,128)(2,1)S(1)}, bf16[128,768]{1,0:T(8,128)(2,1)S(1)}, u32[]{:S(2)}, u32[]{:S(2)}) collective-permute-start(bf16[128,768]{1,0:T(8,128)(2,1)S(1)} %get-tuple-element.46), channel_id=1, source_target_pairs={{0,1},{1,0},{2,3},{3,2},{4,5},{5,4},{6,7},{7,6},{8,9},{9,8},{10,11... | collective-permute-start | bytes 589832 | tf_op jit(solution)/shard_map/ppermute | solution.py:490
  26.3 2.5 %collective-permute-done.8.refs_10_ = bf16[128,768]{1,0:T(8,128)(2,1)S(1)} collective-permute-done((bf16[128,768]{1,0:T(8,128)(2,1)}, bf16[128,768]{1,0:T(8,128)(2,1)S(1)}, u32[]{:S(2)}, u32[]{:S(2)}) %collective-permute-start.8) | collective-permute-done | bytes 196640 | tf_op jit(solution)/shard_map/ppermute | solution.py:490
  28.8 0.5 collective-permute-start.6
  29.3 0.1 collective-permute-start.4
  29.4 0.1 iota_add_fusion
  29.5 0.1 add.23
  29.5 0.8 collective-permute-start.10
  30.4 0.2 select_reduce_fusion.order
  30.5 2.1 %collective-permute-done.7.refs_9_ = bf16[128,768]{1,0:T(8,128)(2,1)S(1)} collective-permute-done((bf16[128,768]{1,0:T(8,128)(2,1)S(1)}, bf16[128,768]{1,0:T(8,128)(2,1)S(1)}, u32[]{:S(2)}, u32[]{:S(2)}) %collective-permute-start.7) | collective-permute-done | bytes 196640 | tf_op jit(solution)/shard_map/ppermute | solution.py:490
  32.7 0.0 copy-start.7
  32.7 1.0 %copy-done.7 = f32[1024,128]{1,0:T(8,128)S(1)} copy-done((f32[1024,128]{1,0:T(8,128)S(1)}, f32[1024,128]{1,0:T(8,128)}, u32[]{:S(2)}) %copy-start.7) | copy-done | bytes 524312
  33.7 1.0 %copy-done.8 = f32[1024,128]{1,0:T(8,128)S(1)} copy-done((f32[1024,128]{1,0:T(8,128)S(1)}, f32[1024,128]{1,0:T(8,128)}, u32[]{:S(2)}) %copy-start.8) | copy-done | bytes 524312
  34.8 10.4 %layer.1 = (bf16[4,128,1024]{2,1,0:T(8,128)(2,1)S(1)}, bf16[4,128,1024]{2,1,0:T(8,128)(2,1)S(1)}, bf16[64,512]{1,0:T(8,128)(2,1)S(1)}, f32[8,512]{1,0:T(8,128)S(...) custom-call(s32[2]{0:T(128)S(1)} %copy-done.5, ...), custom_call_target="tpu_custom_call" | custom-call | flops 1744830464 | bytes 6291456 | tf_op jit(solution)/shard_map/layer/pallas_call | solution.py:582
  45.2 0.1 collective-permute-start.11
  45.3 2.6 %collective-permute-done.11.came = bf16[4,128,1024]{2,1,0:T(8,128)(2,1)S(1)} collective-permute-done((bf16[4,128,1024]{2,1,0:T(8,128)(2,1)S(1)}, bf16[4,128,1024]{2,1,0:T(8,128)(2,1)S(1)}, u32[]{:S(2)}, u32[]{:S(2)}) %collective-permute-start.11) | collective-permute-done | bytes 1048608 | tf_op jit(solution)/shard_map/ppermute | solution.py:623
  47.9 0.2 chip_sum.1
  48.1 8.6 %collective-permute-start.12 = (bf16[128,1024]{1,0:T(8,128)(2,1)S(1)}, bf16[128,1024]{1,0:T(8,128)(2,1)S(1)}, u32[]{:S(2)}, u32[]{:S(2)}) collective-permute-start(bf16[128,1024]{1,0:T(8,128)(2,1)S(1)} %get-tuple-element.52), channel_id=1, source_target_pairs={{0,8},{4,12},{8,0},{12,4},{16,24},{20,28},{24,16},{28,20},{1,9},{5... | collective-permute-start | bytes 786440 | tf_op jit(solution)/shard_map/ppermute | solution.py:625
  56.8 1.4 %collective-permute-start.13 = (bf16[128,1024]{1,0:T(8,128)(2,1)S(1)}, bf16[128,1024]{1,0:T(8,128)(2,1)S(1)}, u32[]{:S(2)}, u32[]{:S(2)}) collective-permute-start(bf16[128,1024]{1,0:T(8,128)(2,1)S(1)} %get-tuple-element.53), channel_id=1, source_target_pairs={{0,16},{4,20},{8,24},{12,28},{16,0},{20,4},{24,8},{28,12},{1,17},{... | collective-permute-start | bytes 786440 | tf_op jit(solution)/shard_map/ppermute | solution.py:625
  58.2 0.2 collective-permute-start.14
  58.4 3.5 %collective-permute-start.16 = (bf16[128,768]{1,0:T(8,128)(2,1)S(1)}, bf16[128,768]{1,0:T(8,128)(2,1)S(1)}, u32[]{:S(2)}, u32[]{:S(2)}) collective-permute-start(bf16[128,768]{1,0:T(8,128)(2,1)S(1)} %get-tuple-element.59), channel_id=1, source_target_pairs={{0,2},{1,3},{2,0},{3,1},{4,6},{5,7},{6,4},{7,5},{8,10},{9,11},{10,... | collective-permute-start | bytes 589832 | tf_op jit(solution)/shard_map/ppermute | solution.py:490
  61.9 2.0 %collective-permute-done.12.refs_1_.after.refs_5_ = bf16[128,1024]{1,0:T(8,128)(2,1)S(1)} collective-permute-done((bf16[128,1024]{1,0:T(8,128)(2,1)S(1)}, bf16[128,1024]{1,0:T(8,128)(2,1)S(1)}, u32[]{:S(2)}, u32[]{:S(2)}) %collective-permute-start.12) | collective-permute-done | bytes 262176 | tf_op jit(solution)/shard_map/ppermute | solution.py:625
  63.9 3.1 %collective-permute-start.17 = (bf16[128,768]{1,0:T(8,128)(2,1)S(1)}, bf16[128,768]{1,0:T(8,128)(2,1)S(1)}, u32[]{:S(2)}, u32[]{:S(2)}) collective-permute-start(bf16[128,768]{1,0:T(8,128)(2,1)S(1)} %get-tuple-element.60), channel_id=1, source_target_pairs={{0,3},{1,2},{2,1},{3,0},{4,7},{5,6},{6,5},{7,4},{8,11},{9,10},{10,... | collective-permute-start | bytes 589832 | tf_op jit(solution)/shard_map/ppermute | solution.py:490
  67.0 0.7 collective-permute-start.18
  67.7 9.7 %collective-permute-done.16.refs_2_ = bf16[128,768]{1,0:T(8,128)(2,1)S(1)} collective-permute-done((bf16[128,768]{1,0:T(8,128)(2,1)S(1)}, bf16[128,768]{1,0:T(8,128)(2,1)S(1)}, u32[]{:S(2)}, u32[]{:S(2)}) %collective-permute-start.16) | collective-permute-done | bytes 196640 | tf_op jit(solution)/shard_map/ppermute | solution.py:490
  77.4 0.0 copy-start
  77.4 0.0 copy-start.1
  77.4 0.1 sum.1.refs_0_
  77.5 0.8 collective-permute-start.24
  78.3 5.0 %collective-permute-start.22 = (bf16[128,1024]{1,0:T(8,128)(2,1)S(1)}, bf16[128,1024]{1,0:T(8,128)(2,1)S(1)}, u32[]{:S(2)}, u32[]{:S(2)}) collective-permute-start(bf16[128,1024]{1,0:T(8,128)(2,1)S(1)} %sum.1.refs_0_), channel_id=1, source_target_pairs={{0,16},{4,20},{8,24},{12,28},{16,0},{20,4},{24,8},{28,12},{1,17},{... | collective-permute-start | bytes 786440 | tf_op jit(solution)/shard_map/ppermute | solution.py:479
  83.2 1.4 %collective-permute-start.20 = (bf16[128,1024]{1,0:T(8,128)(2,1)S(1)}, bf16[128,1024]{1,0:T(8,128)(2,1)S(1)}, u32[]{:S(2)}, u32[]{:S(2)}) collective-permute-start(bf16[128,1024]{1,0:T(8,128)(2,1)S(1)} %sum.1.refs_0_), channel_id=1, source_target_pairs={{0,8},{4,12},{8,0},{12,4},{16,24},{20,28},{24,16},{28,20},{1,9},{5... | collective-permute-start | bytes 786440 | tf_op jit(solution)/shard_map/ppermute | solution.py:479
  84.6 0.3 collective-permute-done.24.refs_6_
  85.0 0.2 collective-permute-start.25
  85.2 7.8 %collective-permute-done.22.refs_4_ = bf16[128,1024]{1,0:T(8,128)(2,1)S(1)} collective-permute-done((bf16[128,1024]{1,0:T(8,128)(2,1)S(1)}, bf16[128,1024]{1,0:T(8,128)(2,1)S(1)}, u32[]{:S(2)}, u32[]{:S(2)}) %collective-permute-start.22) | collective-permute-done | bytes 262176 | tf_op jit(solution)/shard_map/ppermute | solution.py:479
  93.0 1.9 %collective-permute-done.20.refs_2_ = bf16[128,1024]{1,0:T(8,128)(2,1)S(1)} collective-permute-done((bf16[128,1024]{1,0:T(8,128)(2,1)S(1)}, bf16[128,1024]{1,0:T(8,128)(2,1)S(1)}, u32[]{:S(2)}, u32[]{:S(2)}) %collective-permute-start.20) | collective-permute-done | bytes 262176 | tf_op jit(solution)/shard_map/ppermute | solution.py:479
  94.9 1.6 %close.1 = (bf16[128,512]{1,0:T(8,128)(2,1)}, f32[128,512]{1,0:T(8,128)}) custom-call(s32[2]{0:T(128)S(1)} %copy-done.5, bf16[128,512]{1,0:T(8,128)(2,1)S(1)} %bitcast.13, bf16[128,512]{1,0:T(8,128)(2,1)S(1)} %bitcast.14, f32[8,512]{1,0:T(8,128)S(1)} %get-tuple-element.48.params, bf16[128,1024]{1,0:T(8,128)(2,1)S(1)} %get-tuple-element.51.refs_0_, ...), custom_call_target="tpu_custom_call" | custom-call | tf_op jit(solution)/shard_map/close/pallas_call | solution.py:626
  96.5 2.9 %finish.1 = (f32[1,128]{1,0:T(1,128)}, f32[1,128]{1,0:T(1,128)}, f32[128,1536]{1,0:T(8,128)}, f32[1,384]{1,0:T(1,128)S(1)}, f32[128,512]{1,0:T(8,128)}, /*index=...) custom-call(s32[2]{0:T(128)S(1)} %copy-done.5, ...), custom_call_target="tpu_custom_call" | custom-call | tf_op jit(solution)/shard_map/finish/pallas_call | solution.py:643
  99.4 0.6 reduce
  (38 shorter events, 0.1 us)
Async XLA Ops:
  1.2 13.1 %copy-start.4 = (bf16[128,512]{1,0:T(8,128)(2,1)S(1)}, bf16[128,512]{1,0:T(8,128)(2,1)}, u32[]{:S(2)}) copy-start(bf16[128,512]{1,0:T(8,128)(2,1)} %w_out.1) | copy-start | bytes 393220
  4.1 10.3 %collective-permute-start.1 = (bf16[256,512]{1,0:T(8,128)(2,1)}, bf16[256,512]{1,0:T(8,128)(2,1)S(1)}, u32[]{:S(2)}, u32[]{:S(2)}) collective-permute-start(bf16[256,512]{1,0:T(8,128)(2,1)} %get-tuple-element.44.refs_0_), channel_id=1, source_target_pairs={{0,8},{4,12},{8,0},{12,4},{16,24},{20,28},{24,16},{28,20},{1,9},{5... | collective-permute-start | bytes 786440 | tf_op jit(solution)/shard_map/ppermute | solution.py:479
  7.0 21.8 %collective-permute-start.5 = (bf16[256,512]{1,0:T(8,128)(2,1)}, bf16[256,512]{1,0:T(8,128)(2,1)S(1)}, u32[]{:S(2)}, u32[]{:S(2)}) collective-permute-start(bf16[256,512]{1,0:T(8,128)(2,1)} %get-tuple-element.44.refs_0_), channel_id=1, source_target_pairs={{0,24},{4,28},{8,16},{12,20},{16,8},{20,12},{24,0},{28,4},{1,25},{... | collective-permute-start | bytes 786440 | tf_op jit(solution)/shard_map/ppermute | solution.py:479
  8.5 20.8 %collective-permute-start.3 = (bf16[256,512]{1,0:T(8,128)(2,1)}, bf16[256,512]{1,0:T(8,128)(2,1)S(1)}, u32[]{:S(2)}, u32[]{:S(2)}) collective-permute-start(bf16[256,512]{1,0:T(8,128)(2,1)} %get-tuple-element.44.refs_0_), channel_id=1, source_target_pairs={{0,16},{4,20},{8,24},{12,28},{16,0},{20,4},{24,8},{28,12},{1,17},{... | collective-permute-start | bytes 786440 | tf_op jit(solution)/shard_map/ppermute | solution.py:479
  8.6 5.8 %copy-start.5 = (s32[2]{0:T(128)S(1)}, s32[2]{0:T(128)}, u32[]{:S(2)}) copy-start(s32[2]{0:T(128)} %pad_add_fusion.place) | copy-start | bytes 28
  8.6 10.1 %collective-permute-start.9 = (bf16[128,768]{1,0:T(8,128)(2,1)}, bf16[128,768]{1,0:T(8,128)(2,1)S(1)}, u32[]{:S(2)}, u32[]{:S(2)}) collective-permute-start(bf16[128,768]{1,0:T(8,128)(2,1)} %get-tuple-element.45.pay.refs_8_), channel_id=1, source_target_pairs={{0,3},{1,2},{2,1},{3,0},{4,7},{5,6},{6,5},{7,4},{8,11},{9,10},{10,... | collective-permute-start | bytes 589832 | tf_op jit(solution)/shard_map/ppermute | solution.py:490
  12.6 16.2 %collective-permute-start.8 = (bf16[128,768]{1,0:T(8,128)(2,1)}, bf16[128,768]{1,0:T(8,128)(2,1)S(1)}, u32[]{:S(2)}, u32[]{:S(2)}) collective-permute-start(bf16[128,768]{1,0:T(8,128)(2,1)} %get-tuple-element.45.pay.refs_8_), channel_id=1, source_target_pairs={{0,2},{1,3},{2,0},{3,1},{4,6},{5,7},{6,4},{7,5},{8,10},{9,11},{10,... | collective-permute-start | bytes 589832 | tf_op jit(solution)/shard_map/ppermute | solution.py:490
  14.4 15.2 %collective-permute-start = (bf16[256,512]{1,0:T(8,128)(2,1)}, bf16[256,512]{1,0:T(8,128)(2,1)S(1)}, u32[]{:S(2)}, u32[]{:S(2)}) collective-permute-start(bf16[256,512]{1,0:T(8,128)(2,1)} %get-tuple-element.44.refs_0_), channel_id=1, source_target_pairs={{0,4},{4,0},{8,12},{12,8},{16,20},{20,16},{24,28},{28,24},{1,5},{5... | collective-permute-start | bytes 786440 | tf_op jit(solution)/shard_map/ppermute | solution.py:481
  14.4 0.9 copy-start.2
  15.3 17.4 %copy-start.3 = (bf16[128,768]{1,0:T(8,128)(2,1)S(1)}, bf16[128,768]{1,0:T(8,128)(2,1)}, u32[]{:S(2)}) copy-start(bf16[128,768]{1,0:T(8,128)(2,1)} %get-tuple-element.45.pay.refs_8_) | copy-start | bytes 589828
  15.3 17.4 %copy-start.6 = (bf16[256,512]{1,0:T(8,128)(2,1)S(1)}, bf16[256,512]{1,0:T(8,128)(2,1)}, u32[]{:S(2)}) copy-start(bf16[256,512]{1,0:T(8,128)(2,1)} %get-tuple-element.44.refs_0_) | copy-start | bytes 786436
  18.7 13.9 %collective-permute-start.7 = (bf16[128,768]{1,0:T(8,128)(2,1)S(1)}, bf16[128,768]{1,0:T(8,128)(2,1)S(1)}, u32[]{:S(2)}, u32[]{:S(2)}) collective-permute-start(bf16[128,768]{1,0:T(8,128)(2,1)S(1)} %get-tuple-element.46), channel_id=1, source_target_pairs={{0,1},{1,0},{2,3},{3,2},{4,5},{5,4},{6,7},{7,6},{8,9},{9,8},{10,11... | collective-permute-start | bytes 589832 | tf_op jit(solution)/shard_map/ppermute | solution.py:490
  28.8 3.9 %collective-permute-start.2 = (bf16[256,512]{1,0:T(8,128)(2,1)S(1)}, bf16[256,512]{1,0:T(8,128)(2,1)S(1)}, u32[]{:S(2)}, u32[]{:S(2)}) collective-permute-start(bf16[256,512]{1,0:T(8,128)(2,1)S(1)} %collective-permute-done.1.after.refs_2_), channel_id=1, source_target_pairs={{0,4},{4,0},{8,12},{12,8},{16,20},{20,16},{24,28},{28,24},{1,5},{5... | collective-permute-start | bytes 786440 | tf_op jit(solution)/shard_map/ppermute | solution.py:481
  28.8 3.9 %collective-permute-start.6 = (bf16[256,512]{1,0:T(8,128)(2,1)S(1)}, bf16[256,512]{1,0:T(8,128)(2,1)S(1)}, u32[]{:S(2)}, u32[]{:S(2)}) collective-permute-start(bf16[256,512]{1,0:T(8,128)(2,1)S(1)} %collective-permute-done.5.refs_6_), channel_id=1, source_target_pairs={{0,4},{4,0},{8,12},{12,8},{16,20},{20,16},{24,28},{28,24},{1,5},{5... | collective-permute-start | bytes 786440 | tf_op jit(solution)/shard_map/ppermute | solution.py:481
  29.3 3.3 %collective-permute-start.4 = (bf16[256,512]{1,0:T(8,128)(2,1)S(1)}, bf16[256,512]{1,0:T(8,128)(2,1)S(1)}, u32[]{:S(2)}, u32[]{:S(2)}) collective-permute-start(bf16[256,512]{1,0:T(8,128)(2,1)S(1)} %collective-permute-done.3.refs_4_), channel_id=1, source_target_pairs={{0,4},{4,0},{8,12},{12,8},{16,20},{20,16},{24,28},{28,24},{1,5},{5... | collective-permute-start | bytes 786440 | tf_op jit(solution)/shard_map/ppermute | solution.py:481
  29.5 0.8 copy-start.9
  29.5 1.0 collective-permute-start.10
  32.7 1.0 %copy-start.7 = (f32[1024,128]{1,0:T(8,128)S(1)}, f32[1024,128]{1,0:T(8,128)}, u32[]{:S(2)}) copy-start(f32[1024,128]{1,0:T(8,128)} %constant.18.clone.refs_14_) | copy-start | bytes 1572868
  33.7 1.0 %copy-start.8 = (f32[1024,128]{1,0:T(8,128)S(1)}, f32[1024,128]{1,0:T(8,128)}, u32[]{:S(2)}) copy-start(f32[1024,128]{1,0:T(8,128)} %constant.17.clone.refs_13_) | copy-start | bytes 1572868
  45.2 2.7 %collective-permute-start.11 = (bf16[4,128,1024]{2,1,0:T(8,128)(2,1)S(1)}, bf16[4,128,1024]{2,1,0:T(8,128)(2,1)S(1)}, u32[]{:S(2)}, u32[]{:S(2)}) collective-permute-start(bf16[4,128,1024]{2,1,0:T(8,128)(2,1)S(1)} %get-tuple-element.50), channel_id=1, source_target_pairs={{0,4},{4,0},{8,12},{12,8},{16,20},{20,16},{24,28},{28,24},{1,5},{5... | collective-permute-start | bytes 3145736 | tf_op jit(solution)/shard_map/ppermute | solution.py:623
  48.1 15.7 %collective-permute-start.12 = (bf16[128,1024]{1,0:T(8,128)(2,1)S(1)}, bf16[128,1024]{1,0:T(8,128)(2,1)S(1)}, u32[]{:S(2)}, u32[]{:S(2)}) collective-permute-start(bf16[128,1024]{1,0:T(8,128)(2,1)S(1)} %get-tuple-element.52), channel_id=1, source_target_pairs={{0,8},{4,12},{8,0},{12,4},{16,24},{20,28},{24,16},{28,20},{1,9},{5... | collective-permute-start | bytes 786440 | tf_op jit(solution)/shard_map/ppermute | solution.py:625
  56.8 10.2 %collective-permute-start.15 = (bf16[128,768]{1,0:T(8,128)(2,1)S(1)}, bf16[128,768]{1,0:T(8,128)(2,1)S(1)}, u32[]{:S(2)}, u32[]{:S(2)}) collective-permute-start(bf16[128,768]{1,0:T(8,128)(2,1)S(1)} %get-tuple-element.58), channel_id=1, source_target_pairs={{0,1},{1,0},{2,3},{3,2},{4,5},{5,4},{6,7},{7,6},{8,9},{9,8},{10,11... | collective-permute-start | bytes 589832 | tf_op jit(solution)/shard_map/ppermute | solution.py:490
  56.8 20.6 %collective-permute-start.13 = (bf16[128,1024]{1,0:T(8,128)(2,1)S(1)}, bf16[128,1024]{1,0:T(8,128)(2,1)S(1)}, u32[]{:S(2)}, u32[]{:S(2)}) collective-permute-start(bf16[128,1024]{1,0:T(8,128)(2,1)S(1)} %get-tuple-element.53), channel_id=1, source_target_pairs={{0,16},{4,20},{8,24},{12,28},{16,0},{20,4},{24,8},{28,12},{1,17},{... | collective-permute-start | bytes 786440 | tf_op jit(solution)/shard_map/ppermute | solution.py:625
  58.2 19.2 %collective-permute-start.14 = (bf16[128,1024]{1,0:T(8,128)(2,1)S(1)}, bf16[128,1024]{1,0:T(8,128)(2,1)S(1)}, u32[]{:S(2)}, u32[]{:S(2)}) collective-permute-start(bf16[128,1024]{1,0:T(8,128)(2,1)S(1)} %get-tuple-element.54), channel_id=1, source_target_pairs={{0,24},{4,28},{8,16},{12,20},{16,8},{20,12},{24,0},{28,4},{1,25},{... | collective-permute-start | bytes 786440 | tf_op jit(solution)/shard_map/ppermute | solution.py:625
  58.4 18.9 %collective-permute-start.16 = (bf16[128,768]{1,0:T(8,128)(2,1)S(1)}, bf16[128,768]{1,0:T(8,128)(2,1)S(1)}, u32[]{:S(2)}, u32[]{:S(2)}) collective-permute-start(bf16[128,768]{1,0:T(8,128)(2,1)S(1)} %get-tuple-element.59), channel_id=1, source_target_pairs={{0,2},{1,3},{2,0},{3,1},{4,6},{5,7},{6,4},{7,5},{8,10},{9,11},{10,... | collective-permute-start | bytes 589832 | tf_op jit(solution)/shard_map/ppermute | solution.py:490
  63.9 13.5 %collective-permute-start.17 = (bf16[128,768]{1,0:T(8,128)(2,1)S(1)}, bf16[128,768]{1,0:T(8,128)(2,1)S(1)}, u32[]{:S(2)}, u32[]{:S(2)}) collective-permute-start(bf16[128,768]{1,0:T(8,128)(2,1)S(1)} %get-tuple-element.60), channel_id=1, source_target_pairs={{0,3},{1,2},{2,1},{3,0},{4,7},{5,6},{6,5},{7,4},{8,11},{9,10},{10,... | collective-permute-start | bytes 589832 | tf_op jit(solution)/shard_map/ppermute | solution.py:490
  67.0 10.4 %collective-permute-start.18 = (bf16[64,512]{1,0:T(8,128)(2,1)S(1)}, bf16[64,512]{1,0:T(8,128)(2,1)S(1)}, u32[]{:S(2)}, u32[]{:S(2)}) collective-permute-start(bf16[64,512]{1,0:T(8,128)(2,1)S(1)} %gate.1), channel_id=1, source_target_pairs={{0,0},{8,1},{16,2},{24,3},{4,4},{12,5},{20,6},{28,7},{1,8},{9,9},{... | collective-permute-start | bytes 196616 | tf_op jit(solution)/shard_map/ppermute | solution.py:636
  77.4 17.5 %copy-start = (bf16[1,128,512]{2,1,0:T(8,128)(2,1)S(1)}, bf16[1,128,512]{2,1,0:T(8,128)(2,1)}, u32[]{:S(2)}) copy-start(bf16[1,128,512]{2,1,0:T(8,128)(2,1)} %refs_8_.1) | copy-start | bytes 393220
  77.4 17.5 %copy-start.1 = (bf16[1,128,512]{2,1,0:T(8,128)(2,1)S(1)}, bf16[1,128,512]{2,1,0:T(8,128)(2,1)}, u32[]{:S(2)}) copy-start(bf16[1,128,512]{2,1,0:T(8,128)(2,1)} %refs_9_.1) | copy-start | bytes 393220
  77.5 7.4 %collective-permute-start.24 = (bf16[128,1024]{1,0:T(8,128)(2,1)S(1)}, bf16[128,1024]{1,0:T(8,128)(2,1)S(1)}, u32[]{:S(2)}, u32[]{:S(2)}) collective-permute-start(bf16[128,1024]{1,0:T(8,128)(2,1)S(1)} %sum.1.refs_0_), channel_id=1, source_target_pairs={{0,24},{4,28},{8,16},{12,20},{16,8},{20,12},{24,0},{28,4},{1,25},{... | collective-permute-start | bytes 786440 | tf_op jit(solution)/shard_map/ppermute | solution.py:479
  78.3 14.7 %collective-permute-start.22 = (bf16[128,1024]{1,0:T(8,128)(2,1)S(1)}, bf16[128,1024]{1,0:T(8,128)(2,1)S(1)}, u32[]{:S(2)}, u32[]{:S(2)}) collective-permute-start(bf16[128,1024]{1,0:T(8,128)(2,1)S(1)} %sum.1.refs_0_), channel_id=1, source_target_pairs={{0,16},{4,20},{8,24},{12,28},{16,0},{20,4},{24,8},{28,12},{1,17},{... | collective-permute-start | bytes 786440 | tf_op jit(solution)/shard_map/ppermute | solution.py:479
  83.2 11.6 %collective-permute-start.20 = (bf16[128,1024]{1,0:T(8,128)(2,1)S(1)}, bf16[128,1024]{1,0:T(8,128)(2,1)S(1)}, u32[]{:S(2)}, u32[]{:S(2)}) collective-permute-start(bf16[128,1024]{1,0:T(8,128)(2,1)S(1)} %sum.1.refs_0_), channel_id=1, source_target_pairs={{0,8},{4,12},{8,0},{12,4},{16,24},{20,28},{24,16},{28,20},{1,9},{5... | collective-permute-start | bytes 786440 | tf_op jit(solution)/shard_map/ppermute | solution.py:479
  84.6 11.8 %collective-permute-start.19 = (bf16[128,1024]{1,0:T(8,128)(2,1)S(1)}, bf16[128,1024]{1,0:T(8,128)(2,1)S(1)}, u32[]{:S(2)}, u32[]{:S(2)}) collective-permute-start(bf16[128,1024]{1,0:T(8,128)(2,1)S(1)} %sum.1.refs_0_), channel_id=1, source_target_pairs={{0,4},{4,0},{8,12},{12,8},{16,20},{20,16},{24,28},{28,24},{1,5},{5... | collective-permute-start | bytes 786440 | tf_op jit(solution)/shard_map/ppermute | solution.py:481
  85.0 11.5 %collective-permute-start.25 = (bf16[128,1024]{1,0:T(8,128)(2,1)S(1)}, bf16[128,1024]{1,0:T(8,128)(2,1)S(1)}, u32[]{:S(2)}, u32[]{:S(2)}) collective-permute-start(bf16[128,1024]{1,0:T(8,128)(2,1)S(1)} %collective-permute-done.24.refs_6_), channel_id=1, source_target_pairs={{0,4},{4,0},{8,12},{12,8},{16,20},{20,16},{24,28},{28,24},{1,5},{5... | collective-permute-start | bytes 786440 | tf_op jit(solution)/shard_map/ppermute | solution.py:481
  93.0 3.5 %collective-permute-start.23 = (bf16[128,1024]{1,0:T(8,128)(2,1)S(1)}, bf16[128,1024]{1,0:T(8,128)(2,1)S(1)}, u32[]{:S(2)}, u32[]{:S(2)}) collective-permute-start(bf16[128,1024]{1,0:T(8,128)(2,1)S(1)} %collective-permute-done.22.refs_4_), channel_id=1, source_target_pairs={{0,4},{4,0},{8,12},{12,8},{16,20},{20,16},{24,28},{28,24},{1,5},{5... | collective-permute-start | bytes 786440 | tf_op jit(solution)/shard_map/ppermute | solution.py:481
  94.9 1.6 %collective-permute-start.21 = (bf16[128,1024]{1,0:T(8,128)(2,1)S(1)}, bf16[128,1024]{1,0:T(8,128)(2,1)S(1)}, u32[]{:S(2)}, u32[]{:S(2)}) collective-permute-start(bf16[128,1024]{1,0:T(8,128)(2,1)S(1)} %collective-permute-done.20.refs_2_), channel_id=1, source_target_pairs={{0,4},{4,0},{8,12},{12,8},{16,20},{20,16},{24,28},{28,24},{1,5},{5... | collective-permute-start | bytes 786440 | tf_op jit(solution)/shard_map/ppermute | solution.py:481

commit v3 on v2

--- a/solution.py
+++ b/solution.py
@@ -20,6 +20,8 @@
 BF16 = jnp.bfloat16
 VMEM_LIMIT = 32 * 1024 * 1024
 WIDE_LIMIT = 60 * 1024 * 1024
+LONGER = pl.CostEstimate(flops=30_000_000_000, bytes_accessed=0, transcendentals=0)
+LONG = pl.CostEstimate(flops=12_000_000_000, bytes_accessed=0, transcendentals=0)
 
 
 def mm(left, right, dims):
@@ -65,9 +67,9 @@
 def pack_body(nz, place, *refs):
     q_ref, k_ref, v_ref = refs[:3]
     ups = refs[3 : 3 + nz]
-    w_down, x, g = refs[3 + nz : 6 + nz]
-    vectors = refs[6 + nz : 14 + nz]
-    pay, piece, small = refs[14 + nz :]
+    w_down, w_out, x, g = refs[3 + nz : 7 + nz]
+    vectors = refs[7 + nz : 15 + nz]
+    pay, piece, head_w, small = refs[15 + nz :]
     odd = (place[0] % 2) == 1
     rows = q_ref.shape[0]
     low = low_lanes((rows, 128))
@@ -90,36 +92,12 @@
         pay[:, 256 + z * 64 : 256 + z * 64 + 128] = jnp.where(low, even, later).astype(BF16)
     pay[0:64, 512:768] = w_down[:, 0:256]
     pay[64:128, 512:768] = w_down[:, 256:512]
+    head_w[...] = w_out[...]
     piece[0:TOK, :] = x[0]
     piece[TOK : 2 * TOK, :] = g[0]
 
 
-def later_body(place, pay, w_out, after, again, head_w):
-    again[...] = pay[...]
-    head_w[...] = w_out[...]
-
-
-def later_call(place, pay, w_out, after):
-    outs = [shape(pay.shape, BF16), shape((HEAD_DIM, D), BF16)]
-    return pl.pallas_call(
-        later_body,
-        out_shape=outs,
-        grid_spec=pltpu.PrefetchScalarGridSpec(
-            num_scalar_prefetch=1,
-            grid=(1,),
-            in_specs=[
-                pl.BlockSpec(pay.shape, lambda i, s: (0, 0)),
-                pl.BlockSpec((HEAD_DIM, D), lambda i, s: (s[0] % 2, 0)),
-                pl.BlockSpec(memory_space=pl.ANY),
-            ],
-            out_specs=[pl.BlockSpec(o.shape, lambda i, s: (0, 0)) for o in outs],
-        ),
-        compiler_params=pltpu.CompilerParams(vmem_limit_bytes=VMEM_LIMIT),
-        name="later",
-    )(place, pay, w_out, after)
-
-
-def pack_call(nz, place, w_qkv, w_up, w_down, x, g, vectors):
+def pack_call(nz, place, w_qkv, w_up, w_down, w_out, x, g, vectors):
     span = FF // nz // 128
     rows = D // nz
 
@@ -130,7 +108,7 @@
         rank = array.ndim
         return pl.BlockSpec(array.shape, lambda i, s: (0,) * rank)
 
-    outs = [shape((rows, 768), BF16), shape((2 * TOK, D), BF16)]
+    outs = [shape((rows, 768), BF16), shape((2 * TOK, D), BF16), shape((HEAD_DIM, D), BF16)]
     return pl.pallas_call(
         functools.partial(pack_body, nz),
         out_shape=outs,
@@ -141,6 +119,7 @@
             + [lane_block(z * span) for z in range(nz)]
             + [
                 pl.BlockSpec((64, D), lambda i, s: (s[0], 0)),
+                pl.BlockSpec((HEAD_DIM, D), lambda i, s: (s[0] % 2, 0)),
                 whole(x),
                 whole(g),
             ]
@@ -150,10 +129,12 @@
         ),
         compiler_params=pltpu.CompilerParams(vmem_limit_bytes=WIDE_LIMIT),
         name="pack",
-    )(place, w_qkv, w_qkv, w_qkv, *([w_up] * nz), w_down, x, g, *vectors)
-
-
-def unpack(nz, place, pieces, w_all, w_up, w_down, params, held):
+    )(place, w_qkv, w_qkv, w_qkv, *([w_up] * nz), w_down, w_out, x, g, *vectors)
+
+
+def unpack_body(nz, place, *refs):
+    pieces = refs[:nz]
+    w_all, w_up, w_down, params, held = refs[nz:]
     me, zed = place[0], place[1]
     pair = me // 2
     odd = (me % 2) == 1
@@ -206,27 +187,17 @@
     seq = n * TOK
     qblk = min(256, seq)
     pieces = refs[:n]
-    n_w = nz if fast else 4
-    given = refs[n : n + n_w]
-    w_out, cos_t, sin_t = refs[n + n_w : n + n_w + 3]
-    outs = refs[n + n_w + 3 :]
+    w_all, w_up, w_down, params, w_out, turn = refs[n : n + 6]
+    outs = refs[n + 6 :]
     n_pay = nz if fast else 4
-    keep_pay, send_pay, g_out, param_out = outs[:4]
-    pays = outs[4 : 4 + n_pay]
-    scratch = outs[4 + n_pay :]
-    (w_all, w_up, w_down, params, held, spare) = scratch[:6]
-    (norms, nhats, raw, qs, ks, vs, dms, mixs, dks, dvs, dqs, dqkvs, mixn, dqkvn, gs) = scratch[6:21]
-    (norm2s, hiddens, dpres, grad_w, grad_up, grad_down, vec) = scratch[21:]
+    keep_pay, send_pay, g_out = outs[:3]
+    pays = outs[3 : 3 + n_pay]
+    scratch = outs[3 + n_pay :]
+    spare = scratch[0]
+    (norms, nhats, raw, qs, ks, vs, dms, mixs, dks, dvs, dqs, dqkvs, mixn, dqkvn, gs) = scratch[1:16]
+    (norm2s, hiddens, dpres, grad_w, grad_up, grad_down, vec) = scratch[16:]
     width = w_up.shape[1]
     zed = place[1]
-    if fast:
-        unpack(nz, place, given, w_all, w_up, w_down, params, held)
-    else:
-        w_all[...] = given[0][...]
-        w_up[...] = given[1][...]
-        w_down[...] = given[2][...]
-        params[...] = given[3][...]
-    param_out[...] = params[...]
     gain, shift = params[0:1, :], params[1:2, :]
     gain2, shift2 = params[2:3, :], params[3:4, :]
     bias = params[5:6, 0:256]
@@ -254,13 +225,19 @@
 
     lanes = lax.broadcasted_iota(jnp.int32, (qblk, 128), 1) % 64
 
+    def both_heads(t):
+        moved = pltpu.roll(t, 64, 1)
+        low = low_lanes(t.shape)
+        return jnp.where(low, t, moved), jnp.where(low, moved, t)
+
     def swapped(t):
         return jnp.where(lanes < ROT // 2, pltpu.roll(t, 128 - ROT // 2, 1), pltpu.roll(t, ROT // 2, 1))
 
     for i in range(seq // qblk):
         rows = slice(i * qblk, (i + 1) * qblk)
         qk = raw[rows, 0:128]
-        turned = (qk * cos_t[rows, :] + swapped(qk) * sin_t[rows, :]).astype(BF16)
+        cos_t, sin_t = both_heads(turn[rows, :])
+        turned = (qk * cos_t + swapped(qk) * sin_t).astype(BF16)
         qs[rows, :] = turned[:, 0:64]
         ks[rows, :] = turned[:, 64:128]
         vs[rows, :] = raw[rows, 128:192].astype(BF16)
@@ -296,7 +273,8 @@
     for i in range(seq // qblk):
         rows = slice(i * qblk, (i + 1) * qblk)
         dqk = dqs[rows, :]
-        dqkvs[rows, 0:128] = (dqk * cos_t[rows, :] - swapped(dqk) * sin_t[rows, :]).astype(BF16)
+        cos_t, sin_t = both_heads(turn[rows, :])
+        dqkvs[rows, 0:128] = (dqk * cos_t - swapped(dqk) * sin_t).astype(BF16)
 
     scale = None
     if n > HEADS:
@@ -370,35 +348,73 @@
         pays[3][...] = vec[...]
 
 
-def close_body(place, x_ref, g_ref, params, *refs):
+def close_body(fast, place, x_ref, g_ref, params, *refs):
     parts, out, grad = refs[:-2], refs[-2], refs[-1]
     x = x_ref[...].astype(F32)
     nhat, inv = normalized(x)
+    if fast:
+        own, came_a, came_b, last_a, last_b = parts
+        total_o = own[:, 0:D].astype(F32) + came_a[0].astype(F32) + last_a[...].astype(F32)
+        dn = own[:, D : 2 * D].astype(F32) + came_b[0].astype(F32) + last_b[...].astype(F32)
+    else:
+        total = parts[0][...].astype(F32)
+        for part in parts[1:]:
+            total = total + part[...].astype(F32)
+        total_o, dn = total[:, 0:D], total[:, D : 2 * D]
+    out[...] = (x + total_o + params[4:5, :]).astype(BF16)
+    lead = jnp.mean(dn, axis=-1, keepdims=True)
+    along = jnp.mean(dn * nhat, axis=-1, keepdims=True)
+    grad[...] = g_ref[...].astype(F32) + inv * (dn - lead - nhat * along)
+
+
+def chip_body(keep, came, *outs):
+    for k, out in enumerate(outs):
+        out[...] = (keep[k].astype(F32) + came[k].astype(F32)).astype(BF16)
+
+
+def chip_fast_body(n_later, keep, came, *refs):
+    later, (first_a, first_b, own, kept_a, kept_b, *held) = refs[:n_later], refs[n_later:]
+    for value, copy in zip(later, held):
+        copy[...] = value[...]
+
+    def both(k, lanes):
+        return (keep[k, :, lanes].astype(F32) + came[k, :, lanes].astype(F32)).astype(BF16)
+
+    left, right = slice(0, D), slice(D, 2 * D)
+    own[:, left] = both(0, left)
+    own[:, right] = both(0, right)
+    first_a[0] = both(1, left)
+    first_a[1] = both(3, left)
+    first_b[0] = both(2, right)
+    first_b[1] = both(3, right)
+    kept_a[...] = both(2, left)
+    kept_b[...] = both(1, right)
+
+
+def cross_body(n_later, kept_a, kept_b, came_a, came_b, *refs):
+    later, (second_a, second_b, *held) = refs[:n_later], refs[n_later:]
+    for value, copy in zip(later, held):
+        copy[...] = value[...]
+    second_a[...] = (kept_a[...].astype(F32) + came_a[1].astype(F32)).astype(BF16)
+    second_b[...] = (kept_b[...].astype(F32) + came_b[1].astype(F32)).astype(BF16)
+
+
+def gate_body(value, *refs):
+    out = refs[-1]
+    out[...] = value[...]
+
+
+def sum_body(nz, *refs):
+    parts, out = refs[:nz], refs[nz]
     total = parts[0][...].astype(F32)
     for part in parts[1:]:
         total = total + part[...].astype(F32)
-    out[...] = (x + total[:, 0:512] + params[4:5, :]).astype(BF16)
-    dn = total[:, 512:1024]
-    lead = jnp.mean(dn, axis=-1, keepdims=True)
-    along = jnp.mean(dn * nhat, axis=-1, keepdims=True)
-    grad[...] = g_ref[...].astype(F32) + inv * (dn - lead - nhat * along)
-
-
-def chip_body(keep, came, *outs):
-    for k, out in enumerate(outs):
-        out[...] = (keep[k].astype(F32) + came[k].astype(F32)).astype(BF16)
-
-
-def gate_body(value, after, out):
-    out[...] = value[...]
-
-
-def sum_body(nz, *refs):
-    parts, g_out, out = refs[:nz], refs[nz], refs[-1]
-    total = parts[0][...].astype(F32)
-    for part in parts[1:]:
-        total = total + part[...].astype(F32)
-    out[:, 0:768] = total.astype(BF16)
+    out[...] = total.astype(BF16)
+
+
+def share_body(total, g_out, *refs):
+    out = refs[-1]
+    out[:, 0:768] = total[...]
     out[0:64, 768:1024] = g_out[:, 0:256]
     out[64:128, 768:1024] = g_out[:, 256:512]
 
@@ -446,7 +462,7 @@
         odd = (zed % 2) == 1
         e = half_pick(held_v[h, 6:7, lane], odd, False)
         l = half_pick(held_v[h + 1, 6:7, lane], odd, True)
-        bup[:, at : at + 128] = jnp.where(low, e, l)
+        bup[at : at + 128] = jnp.where(low, e, l).reshape(128)
     mine = pl.multiple_of((me % 2) * 64, 64)
     other = pl.multiple_of((1 - me % 2) * 64, 64)
     for parity, start in ((0, mine), (1, other)):
@@ -457,16 +473,16 @@
         gout[pl.ds(start, 64), 256:512] = acc[64:128]
     flat[12:20, :] = jnp.zeros((8, 128), F32)
     for r in range(3):
-        bqkv[:, r * 128 : (r + 1) * 128] = flat[pl.ds(zed * 3 + r, 1), :]
+        bqkv[r * 128 : (r + 1) * 128] = flat[pl.ds(zed * 3 + r, 1), :].reshape(128)
     held_v[0] = total
     lane = pl.ds(pl.multiple_of(zed * 128, 128), 128)
-    ln1g[...] = held_v[0, 0:1, lane]
-    ln1b[...] = held_v[0, 1:2, lane]
-    ln2g[...] = held_v[0, 2:3, lane]
-    ln2b[...] = held_v[0, 3:4, lane]
+    ln1g[...] = held_v[0, 0:1, lane].reshape(128)
+    ln1b[...] = held_v[0, 1:2, lane].reshape(128)
+    ln2g[...] = held_v[0, 2:3, lane].reshape(128)
+    ln2b[...] = held_v[0, 3:4, lane].reshape(128)
     held_v[1] = total * (1.0 / n)
-    bout[...] = held_v[1, 4:5, lane]
-    bdown[...] = held_v[1, 4:5, lane]
+    bout[...] = held_v[1, 4:5, lane].reshape(128)
+    bdown[...] = held_v[1, 4:5, lane].reshape(128)
 
 
 def xor_pairs(size, k):
@@ -484,6 +500,11 @@
 
 def gather_fsdp(value, nz):
     return [value] + [lax.ppermute(value, "fsdp", xor_pairs(nz, k)) for k in range(1, nz)]
+
+
+def relay_fsdp(value, nz):
+    one, two = (lax.ppermute(value, "fsdp", xor_pairs(nz, k)) for k in (1, 2))
+    return [value, one, two, lax.ppermute(two, "fsdp", xor_pairs(nz, 1))]
 
 
 def swap_fsdp(values, nz):
@@ -501,7 +522,7 @@
     cos_t[:, half:ROT] = np.cos(angles)
     sin_t[:, 0:half] = -np.sin(angles)
     sin_t[:, half:ROT] = np.sin(angles)
-    return np.concatenate([cos_t, cos_t], axis=1), np.concatenate([sin_t, sin_t], axis=1)
+    return np.concatenate([cos_t, sin_t], axis=1)
 
 
 def shape(dims, dtype=F32):
@@ -538,18 +559,27 @@
     chunk_at = (jnp.arange(n, dtype=jnp.int32) ^ me)[:, None] * blocks + jnp.arange(blocks, dtype=jnp.int32)[None, :]
     pick = chunk_at.reshape(-1)[:, None] == jnp.arange(n * blocks, dtype=jnp.int32)[None, :]
     order = jnp.sum(jnp.where(pick, block_order[None, :], 0), axis=1).astype(jnp.int32)
-    cos_t, sin_t = rotary_tables(seq)
+    turn = rotary_tables(seq)
 
     if fast:
         vectors = (ln1_gain, ln1_bias, ln2_gain, ln2_bias, b_attn_out, b_down, b_qkv, b_up)
-        pack, piece = pack_call(nz, place, w_qkv, w_up, w_down, inputs, cotangent, vectors)
+        pack, piece, pack_w = pack_call(nz, place, w_qkv, w_up, w_down, w_attn_out, inputs, cotangent, vectors)
         pieces = gather_ctx(piece, n)
-        near, pack_w = later_call(place, pack, w_attn_out, pieces[2])
-        given = swap_fsdp([pack, near, pack, pack], nz)
+        far = relay_fsdp(pack, nz)
+        given = vmem_call(
+            functools.partial(unpack_body, nz),
+            [shape((D, 256), BF16), shape((D, width), BF16), shape((width, D), BF16), shape((8, D))],
+            scratch=[pltpu.VMEM((nz, 16, 128), F32)],
+            n_smem=1,
+            n_in=nz,
+            cost=LONG,
+            name="unpack",
+        )(place, *far)
         pairs = []
         for c in range(n):
             for z in range(nz):
                 pairs.append((c * nz + z, (2 * z + c % 2) * nz + c // 2))
+        pack_w = vmem_call(gate_body, shape(pack_w.shape, BF16), n_in=2, name="gate_w")(pack_w, far[1])
         head_w = lax.ppermute(pack_w, ("ctx", "fsdp"), pairs)
     else:
         whole = [
@@ -581,13 +611,8 @@
     half = (n // 2, TOK, 2 * D)
     layer_out = vmem_call(
         functools.partial(layer_body, n, nz, fast),
-        [shape(half, BF16), shape(half, BF16), shape((HEAD_DIM, D), BF16), shape((8, D))] + pays,
+        [shape(half, BF16), shape(half, BF16), shape((HEAD_DIM, D), BF16)] + pays,
         scratch=[
-            pltpu.VMEM((D, 256), BF16),
-            pltpu.VMEM((D, width), BF16),
-            pltpu.VMEM((width, D), BF16),
-            pltpu.VMEM((8, D), F32),
-            pltpu.VMEM((nz, 16, 128), F32),
             pltpu.VMEM((128, 128), F32),
             pltpu.VMEM((seq, D), BF16),
             pltpu.VMEM((seq, D), F32),
@@ -613,18 +638,43 @@
             pltpu.VMEM((8, D), F32),
         ],
         n_smem=2,
-        n_in=n + len(given) + 3,
+        n_in=n + len(given) + 2,
         cost=pl.CostEstimate(flops=26 * seq * seq * 64, bytes_accessed=12 * seq * D, transcendentals=2 * seq * seq),
         name="layer",
-    )(place, order, *pieces, *given, head_w, cos_t, sin_t)
-    keep_pay, send_pay, g_out, params = layer_out[:4]
-    pay = layer_out[4:]
+    )(place, order, *pieces, *given, head_w, turn)
+    params = given[3]
+    keep_pay, send_pay, g_out = layer_out[:3]
+    pay = layer_out[3:]
 
     came = lax.ppermute(send_pay, "ctx", xor_pairs(n, 1))
-    chip_sum = vmem_call(chip_body, [shape((TOK, 2 * D), BF16)] * (n // 2), n_in=2, name="chip_sum")(keep_pay, came)
-    parts = [chip_sum[0]] + [lax.ppermute(chip_sum[k // 2], "ctx", xor_pairs(n, k)) for k in range(2, n, 2)]
+    pay = list(pay)
+    if fast:
+        chip_out = vmem_call(
+            functools.partial(chip_fast_body, 1),
+            [shape((2, TOK, D), BF16)] * 2 + [shape((TOK, 2 * D), BF16)] + [shape((TOK, D), BF16)] * 2 + [shape(pay[1].shape, BF16)],
+            n_in=2 + 1,
+            cost=LONG,
+            name="chip_sum",
+        )(keep_pay, came, pay[1])
+        first_a, first_b, own_sum, kept_a, kept_b = chip_out[:5]
+        pay[1] = chip_out[5]
+        came_a = lax.ppermute(first_a, "ctx", xor_pairs(n, 2))
+        came_b = lax.ppermute(first_b, "ctx", xor_pairs(n, 4))
+        cross_out = vmem_call(
+            functools.partial(cross_body, 0),
+            [shape((TOK, D), BF16)] * 2 + [],
+            n_in=4 + 0,
+            cost=LONG,
+            name="cross",
+        )(kept_a, kept_b, came_a, came_b)
+        second_a, second_b = cross_out[:2]
+        parts = [own_sum, came_a, came_b]
+        parts += [lax.ppermute(second_a, "ctx", xor_pairs(n, 4)), lax.ppermute(second_b, "ctx", xor_pairs(n, 2))]
+    else:
+        chip_sum = vmem_call(chip_body, [shape((TOK, 2 * D), BF16)] * (n // 2), n_in=2, name="chip_sum")(keep_pay, came)
+        parts = [chip_sum[0]] + [lax.ppermute(chip_sum[k // 2], "ctx", xor_pairs(n, k)) for k in range(2, n, 2)]
     output, grad_inputs = vmem_call(
-        close_body,
+        functools.partial(close_body, fast),
         (shape((TOK, D), BF16), shape((TOK, D))),
         n_smem=1,
         n_in=3 + len(parts),
@@ -632,29 +682,28 @@
     )(place, x, g, params, *parts)
 
     if fast:
-        g_out = vmem_call(gate_body, shape(g_out.shape, BF16), n_in=1, n_any=1, name="gate")(g_out, parts[1])
         out_got = lax.ppermute(g_out, ("ctx", "fsdp"), [(b, a) for a, b in pairs])
         got = swap_fsdp(pay, nz)
-        share = vmem_call(functools.partial(sum_body, nz), shape((D // nz, 1024), BF16), n_in=nz + 1, n_any=len(parts) - 1, name="sum")(
-            *got, out_got, *parts[1:]
-        )
+        out_got = vmem_call(gate_body, shape(out_got.shape, BF16), n_in=1, cost=LONGER, name="gate")(out_got)
+        total = vmem_call(functools.partial(sum_body, nz), shape((D // nz, 768), BF16), n_in=nz, cost=LONGER, name="sum")(*got)
+        share = vmem_call(share_body, shape((D // nz, 1024), BF16), n_in=4, name="share")(total, out_got, *parts[3:])
         alls = gather_ctx(share, n)
         dz = D // nz
         outs = vmem_call(
             functools.partial(finish_body, n, nz),
             [
-                shape((1, dz)),
-                shape((1, dz)),
+                shape((dz,)),
+                shape((dz,)),
                 shape((dz, 3 * D)),
-                shape((1, 3 * dz)),
+                shape((3 * dz,)),
                 shape((dz, D)),
-                shape((1, dz)),
-                shape((1, dz)),
-                shape((1, dz)),
+                shape((dz,)),
+                shape((dz,)),
+                shape((dz,)),
                 shape((dz, FF)),
-                shape((1, FF // nz)),
+                shape((FF // nz,)),
                 shape((FF // nz, D)),
-                shape((1, dz)),
+                shape((dz,)),
             ],
             scratch=[
                 pltpu.VMEM((n, 128, 256), F32),
@@ -666,7 +715,6 @@
             n_in=n,
             name="finish",
         )(place, *alls)
-        outs = [o.reshape(-1) if o.shape[0] == 1 else o for o in outs]
     else:
         everyone = ("ctx", "fsdp")
         head = me // (n // HEADS)

time: 100 us -> 85 us (0.85)
  starting transfers between devices: 42.4 us -> 34.2 us
  waiting for transfers between devices: 33.5 us -> 28.4 us
  local copies, waits for them, and re-layouts: 3.11 us -> 1.52 us
    ppermute x6 -> x3, waiting for transfers between devices: 17.1 us -> 2.85 us  [swap_fsdp(): lax.ppermute(values[k], 'fsdp', xor_pairs(nz, k))]
    ppermute x3 -> x7, waiting for transfers between devices: 1.97 us -> 11.3 us  [the longest x1 4.5 us: per_device(): came_a = lax.ppermute(first_a, 'ctx', xor_pairs(n, 2))]
    ppermute x6 -> x3, starting transfers between devices: 18.3 us -> 12.2 us  [swap_fsdp(): lax.ppermute(values[k], 'fsdp', xor_pairs(nz, k))]
    ppermute x6, starting transfers between devices: 11.6 us -> 7.04 us  [gather_ctx(): got[k] = lax.ppermute(value, 'ctx', xor_pairs(n, k))]
    ppermute x1, waiting for transfers between devices: 2.65 us -> 0.01 us  [per_device(): came = lax.ppermute(send_pay, 'ctx', xor_pairs(n, 1))]
    ppermute x3 -> x7, starting transfers between devices: 10.3 us -> 12.4 us  [the longest x2 5.61 us: relay_fsdp(): one, two = (lax.ppermute(value, 'fsdp', xor_pairs(nz, k)) for k in (1, 2))]
    unnamed x20 -> x16, local copies, waits for them, and re-layouts: 3.03 us -> 1.44 us
    ppermute x6, waiting for transfers between devices: 11.8 us -> 13.3 us  [gather_ctx(): got[k] = lax.ppermute(value, 'ctx', xor_pairs(n, k))]
  transfers between devices with their start and end apart: 26 -> 27, of which waited for: 10 -> 15; matrix products, arithmetic and copies ran while one was open for 0% -> 0% of each run, Pallas kernels for 2% -> 3%
where the time goes in v3:
time: 85 us; the launch traced here: 84.8 us
  starting transfers between devices  34.2 us (40%)
  waiting for transfers between devices  28.4 us (33%)
  Pallas kernels  19 us (22%)
  local copies, waits for them, and re-layouts  1.52 us (2%)
    ppermute x6, waiting for transfers between devices, gather_ctx(): got[k] = lax.ppermute(value, 'ctx', xor_pairs(n, k))  13.3 us
    ppermute x3, starting transfers between devices, swap_fsdp(): lax.ppermute(values[k], 'fsdp', xor_pairs(nz, k))  12.2 us
    pallas_call x1, Pallas kernels, per_device(): vmem_call(functools.partial(layer_body, n, nz, fast), [shape(half, BF16),...  10.6 us
    ppermute x6, starting transfers between devices, gather_ctx(): got[k] = lax.ppermute(value, 'ctx', xor_pairs(n, k))  7.04 us
    ppermute x2, starting transfers between devices, relay_fsdp(): one, two = (lax.ppermute(value, 'fsdp', xor_pairs(nz, k)) for k in (1, 2))  5.61 us
    ppermute x1, waiting for transfers between devices, per_device(): came_a = lax.ppermute(first_a, 'ctx', xor_pairs(n, 2))  4.5 us
    ppermute x2, waiting for transfers between devices, relay_fsdp(): one, two = (lax.ppermute(value, 'fsdp', xor_pairs(nz, k)) for k in (1, 2))  4.36 us
    ppermute x1, starting transfers between devices, per_device(): lax.ppermute(second_a, 'ctx', xor_pairs(n, 4))  3.36 us
  transfers between devices with their start and end apart: 27, of which 15 were waited for; matrix products, arithmetic and copies ran while one was open for 0% of the time, Pallas kernels for 3%

profile of v3, /device:TPU:0, one launch (start us, length us, event | category | flops | bytes accessed | tf_op | source)
XLA Modules:
  0.0 84.8 jit_solution(16538053138323519592)
XLA Ops:
  0.6 0.6 pad_add_fusion.place
  1.2 2.8 %pack.1 = (bf16[128,768]{1,0:T(8,128)(2,1)}, bf16[256,512]{1,0:T(8,128)(2,1)}, bf16[64,512]{1,0:T(8,128)(2,1)}) custom-call(s32[2]{0:T(128)} %pad_add_fusion.place, bf16[128,1536]{1,0:T(8,128)(2,1)} %refs_2_.1, bf16[128,1536]{1,0:T(8,128)(2,1)} %refs_2_.1, bf16[128,1536]{1,0:T(8,128)(2,1)} %refs_2_.1, bf16[128,2048]{1,0:T(8,128)(2,1)} %refs_6_.1, ...), custom_call_target="tpu_custom_call" | custom-call | tf_op jit(solution)/shard_map/pack/pallas_call | solution.py:112
  4.0 4.0 %collective-permute-start.1 = (bf16[128,768]{1,0:T(8,128)(2,1)}, bf16[128,768]{1,0:T(8,128)(2,1)S(1)}, u32[]{:S(2)}, u32[]{:S(2)}) collective-permute-start(bf16[128,768]{1,0:T(8,128)(2,1)} %get-tuple-element.50.refs_0_), channel_id=1, source_target_pairs={{0,2},{1,3},{2,0},{3,1},{4,6},{5,7},{6,4},{7,5},{8,10},{9,11},{10,... | collective-permute-start | bytes 589832 | tf_op jit(solution)/shard_map/ppermute | solution.py:506
  8.0 1.6 %collective-permute-start = (bf16[128,768]{1,0:T(8,128)(2,1)}, bf16[128,768]{1,0:T(8,128)(2,1)S(1)}, u32[]{:S(2)}, u32[]{:S(2)}) collective-permute-start(bf16[128,768]{1,0:T(8,128)(2,1)} %get-tuple-element.50.refs_0_), channel_id=1, source_target_pairs={{0,1},{1,0},{2,3},{3,2},{4,5},{5,4},{6,7},{7,6},{8,9},{9,8},{10,11... | collective-permute-start | bytes 589832 | tf_op jit(solution)/shard_map/ppermute | solution.py:506
  9.6 2.4 %collective-permute-start.8 = (bf16[256,512]{1,0:T(8,128)(2,1)}, bf16[256,512]{1,0:T(8,128)(2,1)S(1)}, u32[]{:S(2)}, u32[]{:S(2)}) collective-permute-start(bf16[256,512]{1,0:T(8,128)(2,1)} %get-tuple-element.52.refs_0_), channel_id=1, source_target_pairs={{0,24},{4,28},{8,16},{12,20},{16,8},{20,12},{24,0},{28,4},{1,25},{... | collective-permute-start | bytes 786440 | tf_op jit(solution)/shard_map/ppermute | solution.py:495
  12.1 0.5 collective-permute-start.6
  12.6 0.5 collective-permute-start.4
  13.1 4.4 %collective-permute-done.1.refs_2_ = bf16[128,768]{1,0:T(8,128)(2,1)S(1)} collective-permute-done((bf16[128,768]{1,0:T(8,128)(2,1)}, bf16[128,768]{1,0:T(8,128)(2,1)S(1)}, u32[]{:S(2)}, u32[]{:S(2)}) %collective-permute-start.1) | collective-permute-done | bytes 196640 | tf_op jit(solution)/shard_map/ppermute | solution.py:506
  17.5 0.7 collective-permute-start.2
  18.3 0.1 add.23
  18.3 0.6 copy-done.7
  18.9 0.2 select_reduce_fusion.order
  19.2 0.8 copy-done.2
  20.1 0.8 collective-permute-start.10
  20.9 3.0 %collective-permute-done.6.refs_4_ = bf16[256,512]{1,0:T(8,128)(2,1)S(1)} collective-permute-done((bf16[256,512]{1,0:T(8,128)(2,1)}, bf16[256,512]{1,0:T(8,128)(2,1)S(1)}, u32[]{:S(2)}, u32[]{:S(2)}) %collective-permute-start.6) | collective-permute-done | bytes 262176 | tf_op jit(solution)/shard_map/ppermute | solution.py:495
  23.8 0.1 collective-permute-done.4.refs_2_
  23.9 0.4 collective-permute-start.7
  24.3 0.1 collective-permute-start.5
  24.4 0.7 unpack.1
  25.2 0.2 collective-permute-done.9.refs_7_
  25.4 0.4 collective-permute-done.7.refs_5_
  25.7 0.4 collective-permute-done.5.refs_3_
  26.1 10.6 %layer.1 = (bf16[4,128,1024]{2,1,0:T(8,128)(2,1)S(1)}, bf16[4,128,1024]{2,1,0:T(8,128)(2,1)S(1)}, bf16[64,512]{1,0:T(8,128)(2,1)S(1)}, bf16[128,768]{1,0:T(8,128...) custom-call(s32[2]{0:T(128)S(1)} %copy-done.3, ...), custom_call_target="tpu_custom_call" | custom-call | flops 1744830464 | bytes 6291456 | tf_op jit(solution)/shard_map/layer/pallas_call | solution.py:612
  36.7 0.2 collective-permute-start.11
  36.9 0.8 collective-permute-start.19
  37.8 7.5 %collective-permute-start.17 = (bf16[128,768]{1,0:T(8,128)(2,1)S(1)}, bf16[128,768]{1,0:T(8,128)(2,1)S(1)}, u32[]{:S(2)}, u32[]{:S(2)}) collective-permute-start(bf16[128,768]{1,0:T(8,128)(2,1)S(1)} %get-tuple-element.71), channel_id=1, source_target_pairs={{0,2},{1,3},{2,0},{3,1},{4,6},{5,7},{6,4},{7,5},{8,10},{9,11},{10,... | collective-permute-start | bytes 589832 | tf_op jit(solution)/shard_map/ppermute | solution.py:511
  45.3 3.6 %collective-permute-start.18 = (bf16[128,768]{1,0:T(8,128)(2,1)S(1)}, bf16[128,768]{1,0:T(8,128)(2,1)S(1)}, u32[]{:S(2)}, u32[]{:S(2)}) collective-permute-start(bf16[128,768]{1,0:T(8,128)(2,1)S(1)} %get-tuple-element.72), channel_id=1, source_target_pairs={{0,3},{1,2},{2,1},{3,0},{4,7},{5,6},{6,5},{7,4},{8,11},{9,10},{10,... | collective-permute-start | bytes 589832 | tf_op jit(solution)/shard_map/ppermute | solution.py:511
  48.9 0.3 chip_sum.1
  49.2 2.5 %collective-permute-start.13 = (bf16[2,128,512]{2,1,0:T(8,128)(2,1)S(1)}, bf16[2,128,512]{2,1,0:T(8,128)(2,1)S(1)}, u32[]{:S(2)}, u32[]{:S(2)}) collective-permute-start(bf16[2,128,512]{2,1,0:T(8,128)(2,1)S(1)} %get-tuple-element.62), channel_id=1, source_target_pairs={{0,16},{4,20},{8,24},{12,28},{16,0},{20,4},{24,8},{28,12},{1,17},{... | collective-permute-start | bytes 786440 | tf_op jit(solution)/shard_map/ppermute | solution.py:662
  51.8 1.1 %collective-permute-start.16 = (bf16[128,768]{1,0:T(8,128)(2,1)S(1)}, bf16[128,768]{1,0:T(8,128)(2,1)S(1)}, u32[]{:S(2)}, u32[]{:S(2)}) collective-permute-start(bf16[128,768]{1,0:T(8,128)(2,1)S(1)} %get-tuple-element.70), channel_id=1, source_target_pairs={{0,1},{1,0},{2,3},{3,2},{4,5},{5,4},{6,7},{7,6},{8,9},{9,8},{10,11... | collective-permute-start | bytes 589832 | tf_op jit(solution)/shard_map/ppermute | solution.py:511
  52.8 4.5 %collective-permute-done.12.came_a.refs_1_ = bf16[2,128,512]{2,1,0:T(8,128)(2,1)S(1)} collective-permute-done((bf16[2,128,512]{2,1,0:T(8,128)(2,1)S(1)}, bf16[2,128,512]{2,1,0:T(8,128)(2,1)S(1)}, u32[]{:S(2)}, u32[]{:S(2)}) %collective-permute-start.12) | collective-permute-done | bytes 262176 | tf_op jit(solution)/shard_map/ppermute | solution.py:661
  57.3 0.5 collective-permute-done.13.came_b.refs_2_
  57.9 3.4 %collective-permute-start.14 = (bf16[128,512]{1,0:T(8,128)(2,1)S(1)}, bf16[128,512]{1,0:T(8,128)(2,1)S(1)}, u32[]{:S(2)}, u32[]{:S(2)}) collective-permute-start(bf16[128,512]{1,0:T(8,128)(2,1)S(1)} %get-tuple-element.65), channel_id=1, source_target_pairs={{0,16},{4,20},{8,24},{12,28},{16,0},{20,4},{24,8},{28,12},{1,17},{... | collective-permute-start | bytes 393224 | tf_op jit(solution)/shard_map/ppermute | solution.py:672
  61.3 0.1 collective-permute-start.15
  61.4 0.6 collective-permute-done.17.refs_2_
  62.0 2.2 %collective-permute-done.16.refs_1_ = bf16[128,768]{1,0:T(8,128)(2,1)S(1)} collective-permute-done((bf16[128,768]{1,0:T(8,128)(2,1)S(1)}, bf16[128,768]{1,0:T(8,128)(2,1)S(1)}, u32[]{:S(2)}, u32[]{:S(2)}) %collective-permute-start.16) | collective-permute-done | bytes 196640 | tf_op jit(solution)/shard_map/ppermute | solution.py:511
  64.3 0.1 sum.1.total
  64.4 0.3 collective-permute-done.14.refs_3_.refs_0_
  64.6 1.6 %collective-permute-done.15.refs_4_.refs_1_ = bf16[128,512]{1,0:T(8,128)(2,1)S(1)} collective-permute-done((bf16[128,512]{1,0:T(8,128)(2,1)S(1)}, bf16[128,512]{1,0:T(8,128)(2,1)S(1)}, u32[]{:S(2)}, u32[]{:S(2)}) %collective-permute-start.15) | collective-permute-done | bytes 131104 | tf_op jit(solution)/shard_map/ppermute | solution.py:672
  66.3 1.9 %collective-permute-start.25 = (bf16[128,1024]{1,0:T(8,128)(2,1)S(1)}, bf16[128,1024]{1,0:T(8,128)(2,1)S(1)}, u32[]{:S(2)}, u32[]{:S(2)}) collective-permute-start(bf16[128,1024]{1,0:T(8,128)(2,1)S(1)} %share.1.refs_0_), channel_id=1, source_target_pairs={{0,24},{4,28},{8,16},{12,20},{16,8},{20,12},{24,0},{28,4},{1,25},{... | collective-permute-start | bytes 786440 | tf_op jit(solution)/shard_map/ppermute | solution.py:495
  68.2 0.2 collective-permute-start.23
  68.4 1.4 %collective-permute-start.21 = (bf16[128,1024]{1,0:T(8,128)(2,1)S(1)}, bf16[128,1024]{1,0:T(8,128)(2,1)S(1)}, u32[]{:S(2)}, u32[]{:S(2)}) collective-permute-start(bf16[128,1024]{1,0:T(8,128)(2,1)S(1)} %share.1.refs_0_), channel_id=1, source_target_pairs={{0,8},{4,12},{8,0},{12,4},{16,24},{20,28},{24,16},{28,20},{1,9},{5... | collective-permute-start | bytes 786440 | tf_op jit(solution)/shard_map/ppermute | solution.py:495
  69.8 6.7 %collective-permute-done.25.refs_6_ = bf16[128,1024]{1,0:T(8,128)(2,1)S(1)} collective-permute-done((bf16[128,1024]{1,0:T(8,128)(2,1)S(1)}, bf16[128,1024]{1,0:T(8,128)(2,1)S(1)}, u32[]{:S(2)}, u32[]{:S(2)}) %collective-permute-start.25) | collective-permute-done | bytes 262176 | tf_op jit(solution)/shard_map/ppermute | solution.py:495
  76.5 3.2 %collective-permute-done.23.refs_4_ = bf16[128,1024]{1,0:T(8,128)(2,1)S(1)} collective-permute-done((bf16[128,1024]{1,0:T(8,128)(2,1)S(1)}, bf16[128,1024]{1,0:T(8,128)(2,1)S(1)}, u32[]{:S(2)}, u32[]{:S(2)}) %collective-permute-start.23) | collective-permute-done | bytes 262176 | tf_op jit(solution)/shard_map/ppermute | solution.py:495
  79.8 0.3 collective-permute-done.21.refs_2_
  80.1 0.2 collective-permute-start.22
  80.3 1.6 %close.1 = (bf16[128,512]{1,0:T(8,128)(2,1)}, f32[128,512]{1,0:T(8,128)}) custom-call(s32[2]{0:T(128)S(1)} %copy-done.3, bf16[128,512]{1,0:T(8,128)(2,1)S(1)} %bitcast.6, bf16[128,512]{1,0:T(8,128)(2,1)S(1)} %bitcast.7, f32[8,512]{1,0:T(8,128)S(1)} %get-tuple-element.51.refs_11_.params, bf16[128,1024]{1,0:T(8,128)(2,1)S(1)} %get-tuple-element.60.refs_0_, ...), custom_call_target="tpu_custom_call" | custom-call | tf_op jit(solution)/shard_map/close/pallas_call | solution.py:676
  81.9 2.9 %finish.1 = (f32[128]{0:T(128)}, f32[128]{0:T(128)}, f32[128,1536]{1,0:T(8,128)}, f32[384]{0:T(512)}, f32[128,512]{1,0:T(8,128)}, /*index=5*/f32[128]{0:T(128)},...) custom-call(s32[2]{0:T(128)S(1)} %copy-done.3, ...), custom_call_target="tpu_custom_call" | custom-call | tf_op jit(solution)/shard_map/finish/pallas_call | solution.py:692
  (38 shorter events, 0.4 us)
Async XLA Ops:
  4.0 13.5 %collective-permute-start.1 = (bf16[128,768]{1,0:T(8,128)(2,1)}, bf16[128,768]{1,0:T(8,128)(2,1)S(1)}, u32[]{:S(2)}, u32[]{:S(2)}) collective-permute-start(bf16[128,768]{1,0:T(8,128)(2,1)} %get-tuple-element.50.refs_0_), channel_id=1, source_target_pairs={{0,2},{1,3},{2,0},{3,1},{4,6},{5,7},{6,4},{7,5},{8,10},{9,11},{10,... | collective-permute-start | bytes 589832 | tf_op jit(solution)/shard_map/ppermute | solution.py:506
  8.0 11.1 %collective-permute-start = (bf16[128,768]{1,0:T(8,128)(2,1)}, bf16[128,768]{1,0:T(8,128)(2,1)S(1)}, u32[]{:S(2)}, u32[]{:S(2)}) collective-permute-start(bf16[128,768]{1,0:T(8,128)(2,1)} %get-tuple-element.50.refs_0_), channel_id=1, source_target_pairs={{0,1},{1,0},{2,3},{3,2},{4,5},{5,4},{6,7},{7,6},{8,9},{9,8},{10,11... | collective-permute-start | bytes 589832 | tf_op jit(solution)/shard_map/ppermute | solution.py:506
  9.6 10.4 %collective-permute-start.8 = (bf16[256,512]{1,0:T(8,128)(2,1)}, bf16[256,512]{1,0:T(8,128)(2,1)S(1)}, u32[]{:S(2)}, u32[]{:S(2)}) collective-permute-start(bf16[256,512]{1,0:T(8,128)(2,1)} %get-tuple-element.52.refs_0_), channel_id=1, source_target_pairs={{0,24},{4,28},{8,16},{12,20},{16,8},{20,12},{24,0},{28,4},{1,25},{... | collective-permute-start | bytes 786440 | tf_op jit(solution)/shard_map/ppermute | solution.py:495
  12.1 11.8 %collective-permute-start.6 = (bf16[256,512]{1,0:T(8,128)(2,1)}, bf16[256,512]{1,0:T(8,128)(2,1)S(1)}, u32[]{:S(2)}, u32[]{:S(2)}) collective-permute-start(bf16[256,512]{1,0:T(8,128)(2,1)} %get-tuple-element.52.refs_0_), channel_id=1, source_target_pairs={{0,16},{4,20},{8,24},{12,28},{16,0},{20,4},{24,8},{28,12},{1,17},{... | collective-permute-start | bytes 786440 | tf_op jit(solution)/shard_map/ppermute | solution.py:495
  12.6 11.4 %collective-permute-start.4 = (bf16[256,512]{1,0:T(8,128)(2,1)}, bf16[256,512]{1,0:T(8,128)(2,1)S(1)}, u32[]{:S(2)}, u32[]{:S(2)}) collective-permute-start(bf16[256,512]{1,0:T(8,128)(2,1)} %get-tuple-element.52.refs_0_), channel_id=1, source_target_pairs={{0,8},{4,12},{8,0},{12,4},{16,24},{20,28},{24,16},{28,20},{1,9},{5... | collective-permute-start | bytes 786440 | tf_op jit(solution)/shard_map/ppermute | solution.py:495
  17.5 6.9 %collective-permute-start.2 = (bf16[128,768]{1,0:T(8,128)(2,1)S(1)}, bf16[128,768]{1,0:T(8,128)(2,1)S(1)}, u32[]{:S(2)}, u32[]{:S(2)}) collective-permute-start(bf16[128,768]{1,0:T(8,128)(2,1)S(1)} %collective-permute-done.1.refs_2_), channel_id=1, source_target_pairs={{0,1},{1,0},{2,3},{3,2},{4,5},{5,4},{6,7},{7,6},{8,9},{9,8},{10,11... | collective-permute-start | bytes 589832 | tf_op jit(solution)/shard_map/ppermute | solution.py:507
  18.3 0.7 copy-start.7
  19.1 6.1 %collective-permute-start.3 = (bf16[256,512]{1,0:T(8,128)(2,1)}, bf16[256,512]{1,0:T(8,128)(2,1)S(1)}, u32[]{:S(2)}, u32[]{:S(2)}) collective-permute-start(bf16[256,512]{1,0:T(8,128)(2,1)} %get-tuple-element.52.refs_0_), channel_id=1, source_target_pairs={{0,4},{4,0},{8,12},{12,8},{16,20},{20,16},{24,28},{28,24},{1,5},{5... | collective-permute-start | bytes 786440 | tf_op jit(solution)/shard_map/ppermute | solution.py:497
  19.2 0.8 copy-start.2
  20.0 4.4 %copy-start.3 = (s32[2]{0:T(128)S(1)}, s32[2]{0:T(128)}, u32[]{:S(2)}) copy-start(s32[2]{0:T(128)} %pad_add_fusion.place) | copy-start | bytes 28
  20.0 4.4 %copy-start.5 = (bf16[128,768]{1,0:T(8,128)(2,1)S(1)}, bf16[128,768]{1,0:T(8,128)(2,1)}, u32[]{:S(2)}) copy-start(bf16[128,768]{1,0:T(8,128)(2,1)} %get-tuple-element.50.refs_0_) | copy-start | bytes 589828
  20.0 6.1 %copy-start.4 = (bf16[256,512]{1,0:T(8,128)(2,1)S(1)}, bf16[256,512]{1,0:T(8,128)(2,1)}, u32[]{:S(2)}) copy-start(bf16[256,512]{1,0:T(8,128)(2,1)} %get-tuple-element.52.refs_0_) | copy-start | bytes 786436
  20.0 6.1 %copy-start.6 = (f32[1024,128]{1,0:T(8,128)S(1)}, f32[1024,128]{1,0:T(8,128)}, u32[]{:S(2)}) copy-start(f32[1024,128]{1,0:T(8,128)} %constant.15.clone.refs_13_) | copy-start | bytes 1572868
  20.1 5.1 %collective-permute-start.10 = (bf16[64,512]{1,0:T(8,128)(2,1)S(1)}, bf16[64,512]{1,0:T(8,128)(2,1)S(1)}, u32[]{:S(2)}, u32[]{:S(2)}) collective-permute-start(bf16[64,512]{1,0:T(8,128)(2,1)S(1)} %gate_w.1), channel_id=1, source_target_pairs={{0,0},{1,8},{2,16},{3,24},{4,4},{5,12},{6,20},{7,28},{8,1},{9,9},{... | collective-permute-start | bytes 196616 | tf_op jit(solution)/shard_map/ppermute | solution.py:583
  23.8 1.5 %collective-permute-start.9 = (bf16[256,512]{1,0:T(8,128)(2,1)S(1)}, bf16[256,512]{1,0:T(8,128)(2,1)S(1)}, u32[]{:S(2)}, u32[]{:S(2)}) collective-permute-start(bf16[256,512]{1,0:T(8,128)(2,1)S(1)} %collective-permute-done.8.refs_6_), channel_id=1, source_target_pairs={{0,4},{4,0},{8,12},{12,8},{16,20},{20,16},{24,28},{28,24},{1,5},{5... | collective-permute-start | bytes 786440 | tf_op jit(solution)/shard_map/ppermute | solution.py:497
  23.9 1.8 %collective-permute-start.7 = (bf16[256,512]{1,0:T(8,128)(2,1)S(1)}, bf16[256,512]{1,0:T(8,128)(2,1)S(1)}, u32[]{:S(2)}, u32[]{:S(2)}) collective-permute-start(bf16[256,512]{1,0:T(8,128)(2,1)S(1)} %collective-permute-done.6.refs_4_), channel_id=1, source_target_pairs={{0,4},{4,0},{8,12},{12,8},{16,20},{20,16},{24,28},{28,24},{1,5},{5... | collective-permute-start | bytes 786440 | tf_op jit(solution)/shard_map/ppermute | solution.py:497
  24.3 1.8 %collective-permute-start.5 = (bf16[256,512]{1,0:T(8,128)(2,1)S(1)}, bf16[256,512]{1,0:T(8,128)(2,1)S(1)}, u32[]{:S(2)}, u32[]{:S(2)}) collective-permute-start(bf16[256,512]{1,0:T(8,128)(2,1)S(1)} %collective-permute-done.4.refs_2_), channel_id=1, source_target_pairs={{0,4},{4,0},{8,12},{12,8},{16,20},{20,16},{24,28},{28,24},{1,5},{5... | collective-permute-start | bytes 786440 | tf_op jit(solution)/shard_map/ppermute | solution.py:497
  36.7 12.1 %collective-permute-start.11 = (bf16[4,128,1024]{2,1,0:T(8,128)(2,1)S(1)}, bf16[4,128,1024]{2,1,0:T(8,128)(2,1)S(1)}, u32[]{:S(2)}, u32[]{:S(2)}) collective-permute-start(bf16[4,128,1024]{2,1,0:T(8,128)(2,1)S(1)} %get-tuple-element.58), channel_id=1, source_target_pairs={{0,4},{4,0},{8,12},{12,8},{16,20},{20,16},{24,28},{28,24},{1,5},{5... | collective-permute-start | bytes 3145736 | tf_op jit(solution)/shard_map/ppermute | solution.py:649
  36.9 14.8 %collective-permute-start.19 = (bf16[64,512]{1,0:T(8,128)(2,1)S(1)}, bf16[64,512]{1,0:T(8,128)(2,1)S(1)}, u32[]{:S(2)}, u32[]{:S(2)}) collective-permute-start(bf16[64,512]{1,0:T(8,128)(2,1)S(1)} %get-tuple-element.73), channel_id=1, source_target_pairs={{0,0},{8,1},{16,2},{24,3},{4,4},{12,5},{20,6},{28,7},{1,8},{9,9},{... | collective-permute-start | bytes 196616 | tf_op jit(solution)/shard_map/ppermute | solution.py:685
  37.8 24.3 %collective-permute-start.17 = (bf16[128,768]{1,0:T(8,128)(2,1)S(1)}, bf16[128,768]{1,0:T(8,128)(2,1)S(1)}, u32[]{:S(2)}, u32[]{:S(2)}) collective-permute-start(bf16[128,768]{1,0:T(8,128)(2,1)S(1)} %get-tuple-element.71), channel_id=1, source_target_pairs={{0,2},{1,3},{2,0},{3,1},{4,6},{5,7},{6,4},{7,5},{8,10},{9,11},{10,... | collective-permute-start | bytes 589832 | tf_op jit(solution)/shard_map/ppermute | solution.py:511
  45.3 16.7 %collective-permute-start.18 = (bf16[128,768]{1,0:T(8,128)(2,1)S(1)}, bf16[128,768]{1,0:T(8,128)(2,1)S(1)}, u32[]{:S(2)}, u32[]{:S(2)}) collective-permute-start(bf16[128,768]{1,0:T(8,128)(2,1)S(1)} %get-tuple-element.72), channel_id=1, source_target_pairs={{0,3},{1,2},{2,1},{3,0},{4,7},{5,6},{6,5},{7,4},{8,11},{9,10},{10,... | collective-permute-start | bytes 589832 | tf_op jit(solution)/shard_map/ppermute | solution.py:511
  49.1 8.2 %collective-permute-start.12 = (bf16[2,128,512]{2,1,0:T(8,128)(2,1)S(1)}, bf16[2,128,512]{2,1,0:T(8,128)(2,1)S(1)}, u32[]{:S(2)}, u32[]{:S(2)}) collective-permute-start(bf16[2,128,512]{2,1,0:T(8,128)(2,1)S(1)} %get-tuple-element.61), channel_id=1, source_target_pairs={{0,8},{4,12},{8,0},{12,4},{16,24},{20,28},{24,16},{28,20},{1,9},{5... | collective-permute-start | bytes 786440 | tf_op jit(solution)/shard_map/ppermute | solution.py:661
  49.2 8.6 %collective-permute-start.13 = (bf16[2,128,512]{2,1,0:T(8,128)(2,1)S(1)}, bf16[2,128,512]{2,1,0:T(8,128)(2,1)S(1)}, u32[]{:S(2)}, u32[]{:S(2)}) collective-permute-start(bf16[2,128,512]{2,1,0:T(8,128)(2,1)S(1)} %get-tuple-element.62), channel_id=1, source_target_pairs={{0,16},{4,20},{8,24},{12,28},{16,0},{20,4},{24,8},{28,12},{1,17},{... | collective-permute-start | bytes 786440 | tf_op jit(solution)/shard_map/ppermute | solution.py:662
  51.8 12.5 %collective-permute-start.16 = (bf16[128,768]{1,0:T(8,128)(2,1)S(1)}, bf16[128,768]{1,0:T(8,128)(2,1)S(1)}, u32[]{:S(2)}, u32[]{:S(2)}) collective-permute-start(bf16[128,768]{1,0:T(8,128)(2,1)S(1)} %get-tuple-element.70), channel_id=1, source_target_pairs={{0,1},{1,0},{2,3},{3,2},{4,5},{5,4},{6,7},{7,6},{8,9},{9,8},{10,11... | collective-permute-start | bytes 589832 | tf_op jit(solution)/shard_map/ppermute | solution.py:511
  57.9 6.7 %collective-permute-start.14 = (bf16[128,512]{1,0:T(8,128)(2,1)S(1)}, bf16[128,512]{1,0:T(8,128)(2,1)S(1)}, u32[]{:S(2)}, u32[]{:S(2)}) collective-permute-start(bf16[128,512]{1,0:T(8,128)(2,1)S(1)} %get-tuple-element.65), channel_id=1, source_target_pairs={{0,16},{4,20},{8,24},{12,28},{16,0},{20,4},{24,8},{28,12},{1,17},{... | collective-permute-start | bytes 393224 | tf_op jit(solution)/shard_map/ppermute | solution.py:672
  61.3 5.0 %collective-permute-start.15 = (bf16[128,512]{1,0:T(8,128)(2,1)S(1)}, bf16[128,512]{1,0:T(8,128)(2,1)S(1)}, u32[]{:S(2)}, u32[]{:S(2)}) collective-permute-start(bf16[128,512]{1,0:T(8,128)(2,1)S(1)} %get-tuple-element.66), channel_id=1, source_target_pairs={{0,8},{4,12},{8,0},{12,4},{16,24},{20,28},{24,16},{28,20},{1,9},{5... | collective-permute-start | bytes 393224 | tf_op jit(solution)/shard_map/ppermute | solution.py:672
  64.4 15.9 %copy-start = (bf16[1,128,512]{2,1,0:T(8,128)(2,1)S(1)}, bf16[1,128,512]{2,1,0:T(8,128)(2,1)}, u32[]{:S(2)}) copy-start(bf16[1,128,512]{2,1,0:T(8,128)(2,1)} %refs_9_.1) | copy-start | bytes 393220
  64.4 15.9 %copy-start.1 = (bf16[1,128,512]{2,1,0:T(8,128)(2,1)S(1)}, bf16[1,128,512]{2,1,0:T(8,128)(2,1)}, u32[]{:S(2)}) copy-start(bf16[1,128,512]{2,1,0:T(8,128)(2,1)} %refs_10_.1) | copy-start | bytes 393220
  66.3 10.2 %collective-permute-start.25 = (bf16[128,1024]{1,0:T(8,128)(2,1)S(1)}, bf16[128,1024]{1,0:T(8,128)(2,1)S(1)}, u32[]{:S(2)}, u32[]{:S(2)}) collective-permute-start(bf16[128,1024]{1,0:T(8,128)(2,1)S(1)} %share.1.refs_0_), channel_id=1, source_target_pairs={{0,24},{4,28},{8,16},{12,20},{16,8},{20,12},{24,0},{28,4},{1,25},{... | collective-permute-start | bytes 786440 | tf_op jit(solution)/shard_map/ppermute | solution.py:495
  68.2 11.6 %collective-permute-start.23 = (bf16[128,1024]{1,0:T(8,128)(2,1)S(1)}, bf16[128,1024]{1,0:T(8,128)(2,1)S(1)}, u32[]{:S(2)}, u32[]{:S(2)}) collective-permute-start(bf16[128,1024]{1,0:T(8,128)(2,1)S(1)} %share.1.refs_0_), channel_id=1, source_target_pairs={{0,16},{4,20},{8,24},{12,28},{16,0},{20,4},{24,8},{28,12},{1,17},{... | collective-permute-start | bytes 786440 | tf_op jit(solution)/shard_map/ppermute | solution.py:495
  68.4 11.7 %collective-permute-start.21 = (bf16[128,1024]{1,0:T(8,128)(2,1)S(1)}, bf16[128,1024]{1,0:T(8,128)(2,1)S(1)}, u32[]{:S(2)}, u32[]{:S(2)}) collective-permute-start(bf16[128,1024]{1,0:T(8,128)(2,1)S(1)} %share.1.refs_0_), channel_id=1, source_target_pairs={{0,8},{4,12},{8,0},{12,4},{16,24},{20,28},{24,16},{28,20},{1,9},{5... | collective-permute-start | bytes 786440 | tf_op jit(solution)/shard_map/ppermute | solution.py:495
  69.8 12.0 %collective-permute-start.20 = (bf16[128,1024]{1,0:T(8,128)(2,1)S(1)}, bf16[128,1024]{1,0:T(8,128)(2,1)S(1)}, u32[]{:S(2)}, u32[]{:S(2)}) collective-permute-start(bf16[128,1024]{1,0:T(8,128)(2,1)S(1)} %share.1.refs_0_), channel_id=1, source_target_pairs={{0,4},{4,0},{8,12},{12,8},{16,20},{20,16},{24,28},{28,24},{1,5},{5... | collective-permute-start | bytes 786440 | tf_op jit(solution)/shard_map/ppermute | solution.py:497
  76.5 5.4 %collective-permute-start.26 = (bf16[128,1024]{1,0:T(8,128)(2,1)S(1)}, bf16[128,1024]{1,0:T(8,128)(2,1)S(1)}, u32[]{:S(2)}, u32[]{:S(2)}) collective-permute-start(bf16[128,1024]{1,0:T(8,128)(2,1)S(1)} %collective-permute-done.25.refs_6_), channel_id=1, source_target_pairs={{0,4},{4,0},{8,12},{12,8},{16,20},{20,16},{24,28},{28,24},{1,5},{5... | collective-permute-start | bytes 786440 | tf_op jit(solution)/shard_map/ppermute | solution.py:497
  79.8 2.1 %collective-permute-start.24 = (bf16[128,1024]{1,0:T(8,128)(2,1)S(1)}, bf16[128,1024]{1,0:T(8,128)(2,1)S(1)}, u32[]{:S(2)}, u32[]{:S(2)}) collective-permute-start(bf16[128,1024]{1,0:T(8,128)(2,1)S(1)} %collective-permute-done.23.refs_4_), channel_id=1, source_target_pairs={{0,4},{4,0},{8,12},{12,8},{16,20},{20,16},{24,28},{28,24},{1,5},{5... | collective-permute-start | bytes 786440 | tf_op jit(solution)/shard_map/ppermute | solution.py:497
  80.1 1.8 %collective-permute-start.22 = (bf16[128,1024]{1,0:T(8,128)(2,1)S(1)}, bf16[128,1024]{1,0:T(8,128)(2,1)S(1)}, u32[]{:S(2)}, u32[]{:S(2)}) collective-permute-start(bf16[128,1024]{1,0:T(8,128)(2,1)S(1)} %collective-permute-done.21.refs_2_), channel_id=1, source_target_pairs={{0,4},{4,0},{8,12},{12,8},{16,20},{20,16},{24,28},{28,24},{1,5},{5... | collective-permute-start | bytes 786440 | tf_op jit(solution)/shard_map/ppermute | solution.py:497

commit v4 on v3

--- a/solution.py
+++ b/solution.py
@@ -183,40 +183,81 @@
     return jnp.sum(values.reshape(values.shape[0] // 8, 8, values.shape[1]), axis=0)
 
 
-def layer_body(n, nz, fast, place, order, *refs):
-    seq = n * TOK
-    qblk = min(256, seq)
+def ff_body(n, nz, fast, place, *refs):
     pieces = refs[:n]
-    w_all, w_up, w_down, params, w_out, turn = refs[n : n + 6]
-    outs = refs[n + 6 :]
-    n_pay = nz if fast else 4
-    keep_pay, send_pay, g_out = outs[:3]
-    pays = outs[3 : 3 + n_pay]
-    scratch = outs[3 + n_pay :]
-    spare = scratch[0]
-    (norms, nhats, raw, qs, ks, vs, dms, mixs, dks, dvs, dqs, dqkvs, mixn, dqkvn, gs) = scratch[1:16]
-    (norm2s, hiddens, dpres, grad_w, grad_up, grad_down, vec) = scratch[16:]
+    w_up, w_down, params = refs[n : n + 3]
+    outs = refs[n + 3 :]
+    n_pay = 3 if fast else 2
+    acc_o, acc_d, vec, norms, nhats = outs[:5]
+    pays = outs[5 : 5 + n_pay]
+    norm2s, hiddens, dpres, gs, grad_up, grad_down = outs[5 + n_pay :]
     width = w_up.shape[1]
     zed = place[1]
     gain, shift = params[0:1, :], params[1:2, :]
     gain2, shift2 = params[2:3, :], params[3:4, :]
-    bias = params[5:6, 0:256]
     b_up = params[6:7, 0:width]
-
-    def sorted_rows(block):
-        return pl.ds(pl.multiple_of(order[block] * HALF, HALF), HALF)
-
+    g_gain = jnp.zeros((8, D), F32)
+    g_shift = jnp.zeros((8, D), F32)
+    g_sum = jnp.zeros((8, D), F32)
+    g_bup = jnp.zeros((8, width), F32)
     for p in range(n):
         rows = slice(p * TOK, (p + 1) * TOK)
         nhat, _ = normalized(pieces[p][0:TOK, :].astype(F32))
         g = pieces[p][TOK : 2 * TOK, :]
-        norm = (nhat * gain + shift).astype(BF16)
-        nhats[rows, :] = nhat
-        norms[rows, :] = norm
-        norm2s[rows, :] = (nhat * gain2 + shift2).astype(BF16)
+        norms[rows, :] = (nhat * gain + shift).astype(BF16)
+        nhats[rows, :] = nhat.astype(BF16)
+        norm2 = (nhat * gain2 + shift2).astype(BF16)
+        pre = mm_nn(norm2, w_up[...]) + b_up
+        cdf = 0.5 * (1.0 + lax.erf(pre * 0.7071067811865476))
+        hidden = (pre * cdf).astype(BF16)
+        slope = cdf + pre * (0.3989422804014327 * jnp.exp(-0.5 * pre * pre))
+        dpre = (mm_nt(g, w_down[...]) * slope).astype(BF16)
+        dnorm = mm_nt(dpre, w_up[...])
+        acc_o[rows, :] = mm_nn(hidden, w_down[...]).astype(BF16)
+        acc_d[rows, :] = (dnorm * gain2).astype(BF16)
+        g_gain += fold(dnorm * nhat)
+        g_shift += fold(dnorm)
+        g_sum += fold(g.astype(F32))
+        g_bup += fold(dpre.astype(F32))
+        norm2s[rows, :] = norm2
+        hiddens[rows, :] = hidden
+        dpres[rows, :] = dpre
         gs[rows, :] = g
-        qkv = mm_nn(norm, w_all[...]) + bias
-        dmix = mm_nt(g, w_out[...]).astype(BF16)
+    vec[...] = jnp.zeros_like(vec)
+    for row, value in ((2, g_gain), (3, g_shift), (4, g_sum), (6, g_bup)):
+        vec[row : row + 1, 0 : value.shape[1]] = jnp.sum(value, axis=0, keepdims=True)
+    grad_up[...] = mm_tn(dpres[...], norm2s[...]).T.astype(BF16)
+    grad_down[...] = mm_tn(hiddens[...], gs[...]).astype(BF16)
+    if fast:
+        own, near, two = pays
+        for k, target in ((0, own), (1, near.at[0]), (2, two), (3, near.at[1])):
+            z = zed ^ k
+            tall = pl.ds(pl.multiple_of(z * 128, 128), 128)
+            flat = pl.ds(pl.multiple_of(z * 64, 64), 64)
+            target[:, 0:256] = grad_up[tall, :]
+            target[0:64, 256:512] = grad_down[flat, 0:256]
+            target[64:128, 256:512] = grad_down[flat, 256:512]
+    else:
+        pays[0][...] = grad_up[...]
+        pays[1][...] = grad_down[...]
+
+
+def attn_body(n, place, order, *refs):
+    seq = n * TOK
+    qblk = min(256, seq)
+    pieces = refs[:n]
+    w_all, params, w_out, turn, norms = refs[n : n + 5]
+    mixn, dqkvn = refs[n + 5 : n + 7]
+    raw, qs, ks, vs, dms, mixs, dks, dvs, dqs, dqkvs = refs[n + 7 :]
+    bias = params[5:6, 0:256]
+
+    def sorted_rows(block):
+        return pl.ds(pl.multiple_of(order[block] * HALF, HALF), HALF)
+
+    for p in range(n):
+        rows = slice(p * TOK, (p + 1) * TOK)
+        qkv = mm_nn(norms[rows, :], w_all[...]) + bias
+        dmix = mm_nt(pieces[p][TOK : 2 * TOK, :], w_out[...]).astype(BF16)
         for h in range(TOK // HALF):
             here = slice(h * HALF, (h + 1) * HALF)
             where = sorted_rows(p * (TOK // HALF) + h)
@@ -288,64 +329,54 @@
         mixn[here, :] = mix
         dqkvn[here, :] = dqkv
 
+
+def ends_body(n, nz, fast, place, *refs):
+    pieces = refs[:n]
+    mixn, dqkvn, norms, nhats, acc_o, acc_d, vec_in, w_all, w_out, params = refs[n : n + 10]
+    at = n + 10
+    if fast:
+        ff_two, ff_came = refs[at : at + 2]
+        at += 2
+    keep_pay, send_pay, g_out = refs[at : at + 3]
+    n_pay = 4 if fast else 2
+    pays = refs[at + 3 : at + 3 + n_pay]
+    spare, gs, grad_w, vec = refs[at + 3 + n_pay :]
+    zed = place[1]
+    gain = params[0:1, :]
     g_gain = jnp.zeros((8, D), F32)
     g_shift = jnp.zeros((8, D), F32)
     g_bias = jnp.zeros((8, 256), F32)
-    g_gain2 = jnp.zeros((8, D), F32)
-    g_shift2 = jnp.zeros((8, D), F32)
-    g_sum = jnp.zeros((8, D), F32)
-    g_bup = jnp.zeros((8, width), F32)
     for p in range(n):
         rows = slice(p * TOK, (p + 1) * TOK)
-        g, nhat = gs[rows, :], nhats[rows, :]
-        pre = mm_nn(norm2s[rows, :], w_up[...]) + b_up
-        cdf = 0.5 * (1.0 + lax.erf(pre * 0.7071067811865476))
-        hidden = (pre * cdf).astype(BF16)
-        slope = cdf + pre * (0.3989422804014327 * jnp.exp(-0.5 * pre * pre))
-        dpre = (mm_nt(g, w_down[...]) * slope).astype(BF16)
-        hiddens[rows, :] = hidden
-        dpres[rows, :] = dpre
+        gs[rows, :] = pieces[p][TOK : 2 * TOK, :]
         dqkv = dqkvn[rows, :]
-        part_o = mm_nn(hidden, w_down[...]) + mm_nn(mixn[rows, :], w_out[...])
-        dnorm2 = mm_nt(dpre, w_up[...])
         dnorm = mm_nt(dqkv, w_all[...])
-        g_gain += fold(dnorm * nhat)
+        g_gain += fold(dnorm * nhats[rows, :].astype(F32))
         g_shift += fold(dnorm)
         g_bias += fold(dqkv.astype(F32))
-        g_gain2 += fold(dnorm2 * nhat)
-        g_shift2 += fold(dnorm2)
-        g_sum += fold(g.astype(F32))
-        g_bup += fold(dpre.astype(F32))
         target = send_pay if p % 2 else keep_pay
-        target[p // 2, :, 0:512] = part_o.astype(BF16)
-        target[p // 2, :, 512:1024] = (dnorm * gain + dnorm2 * gain2).astype(BF16)
-    vec[...] = jnp.zeros_like(vec)
-    for row, value in ((0, g_gain), (1, g_shift), (2, g_gain2), (3, g_shift2), (4, g_sum), (5, g_bias), (6, g_bup)):
+        target[p // 2, :, 0:512] = (mm_nn(mixn[rows, :], w_out[...]) + acc_o[rows, :].astype(F32)).astype(BF16)
+        target[p // 2, :, 512:1024] = (dnorm * gain + acc_d[rows, :].astype(F32)).astype(BF16)
+    vec[...] = vec_in[...]
+    for row, value in ((0, g_gain), (1, g_shift), (5, g_bias)):
         vec[row : row + 1, 0 : value.shape[1]] = jnp.sum(value, axis=0, keepdims=True)
     g_out[...] = mm_tn(mixn[...], gs[...]).astype(BF16)
     grad_w[...] = mm_tn(dqkvn[...], norms[...]).T
-    grad_up[...] = mm_tn(dpres[...], norm2s[...]).T.astype(BF16)
-    grad_down[...] = mm_tn(hiddens[...], gs[...]).astype(BF16)
     if fast:
         spare[...] = jnp.zeros_like(spare)
         for j in range(8):
             lanes_j = vec[:, (j // 2) * 128 : (j // 2) * 128 + 128]
             spare[8 * j : 8 * j + 8, :] = lanes_j if j % 2 else pltpu.roll(lanes_j, 64, 1)
         low = low_lanes((128, 128))
-        for k in range(nz):
-            z = zed ^ k
-            tall = pl.ds(pl.multiple_of(z * 128, 128), 128)
-            flat = pl.ds(pl.multiple_of(z * 64, 64), 64)
-            pays[k][:, 0:128] = grad_w[tall, 0:128].astype(BF16)
-            pays[k][:, 128:256] = jnp.where(low, grad_w[tall, 128:256], spare[...]).astype(BF16)
-            pays[k][:, 256:512] = grad_up[tall, :]
-            pays[k][0:64, 512:768] = grad_down[flat, 0:256]
-            pays[k][64:128, 512:768] = grad_down[flat, 256:512]
+        own, near, two, ff_sum = pays
+        for k, target in ((0, own), (1, near.at[0]), (2, two), (3, near.at[1])):
+            tall = pl.ds(pl.multiple_of((zed ^ k) * 128, 128), 128)
+            target[:, 0:128] = grad_w[tall, 0:128].astype(BF16)
+            target[:, 128:256] = jnp.where(low, grad_w[tall, 128:256], spare[...]).astype(BF16)
+        ff_sum[...] = (ff_two[...].astype(F32) + ff_came[1].astype(F32)).astype(BF16)
     else:
         pays[0][...] = grad_w[...].astype(BF16)
-        pays[1][...] = grad_up[...]
-        pays[2][...] = grad_down[...]
-        pays[3][...] = vec[...]
+        pays[1][...] = vec[...]
 
 
 def close_body(fast, place, x_ref, g_ref, params, *refs):
@@ -404,17 +435,14 @@
     out[...] = value[...]
 
 
-def sum_body(nz, *refs):
-    parts, out = refs[:nz], refs[nz]
-    total = parts[0][...].astype(F32)
-    for part in parts[1:]:
-        total = total + part[...].astype(F32)
-    out[...] = total.astype(BF16)
-
-
-def share_body(total, g_out, *refs):
+def relay_body(two, came, out):
+    out[...] = (two[...].astype(F32) + came[1].astype(F32)).astype(BF16)
+
+
+def share_body(ff_own, ff_near, ff_far, own, near, far, g_out, *refs):
     out = refs[-1]
-    out[:, 0:768] = total[...]
+    out[:, 0:512] = (ff_own[...].astype(F32) + ff_near[0].astype(F32) + ff_far[...].astype(F32)).astype(BF16)
+    out[:, 512:768] = (own[...].astype(F32) + near[0].astype(F32) + far[...].astype(F32)).astype(BF16)
     out[0:64, 768:1024] = g_out[:, 0:256]
     out[64:128, 768:1024] = g_out[:, 256:512]
 
@@ -429,12 +457,12 @@
     wide = low_lanes((8, 128))
     for k in range(n):
         who = me ^ k
-        held_a[who] = alls[k][:, 0:256].astype(F32)
-        held_u[who] = alls[k][:, 256:512].astype(F32)
+        held_a[who] = alls[k][:, 512:768].astype(F32)
+        held_u[who] = alls[k][:, 0:256].astype(F32)
         rows = pl.ds(pl.multiple_of(who * 64, 64), 64)
-        gdown[rows, 0:256] = alls[k][0:64, 512:768].astype(F32)
-        gdown[rows, 256:512] = alls[k][64:128, 512:768].astype(F32)
-        spare = alls[k][0:64, 128:256].astype(F32)
+        gdown[rows, 0:256] = alls[k][0:64, 256:512].astype(F32)
+        gdown[rows, 256:512] = alls[k][64:128, 256:512].astype(F32)
+        spare = alls[k][0:64, 640:768].astype(F32)
         small = []
         for j in range(0, 8, 2):
             small.append(jnp.where(wide, pltpu.roll(spare[8 * j : 8 * j + 8], 64, 1), spare[8 * j + 8 : 8 * j + 16]))
@@ -507,10 +535,6 @@
     return [value, one, two, lax.ppermute(two, "fsdp", xor_pairs(nz, 1))]
 
 
-def swap_fsdp(values, nz):
-    return [values[0]] + [lax.ppermute(values[k], "fsdp", xor_pairs(nz, k)) for k in range(1, nz)]
-
-
 def rotary_tables(seq):
     pos = np.arange(seq, dtype=np.float32)
     inverse = (np.float32(10000.0) ** (-np.arange(ROT // 2, dtype=np.float32) * np.float32(2.0) / np.float32(ROT))).astype(np.float32)
@@ -604,18 +628,42 @@
         pieces = gather_ctx(jnp.concatenate([x, g], axis=0), n)
         head_w = lax.dynamic_slice_in_dim(wo, head * HEAD_DIM, HEAD_DIM, 0)
 
+    w_all, w_up_c, w_down_c, params = given
+    whole_seq = shape((seq, D), BF16)
+    half = (n // 2, TOK, 2 * D)
+    rows = D // nz
     if fast:
-        pays = [shape((D // nz, 768), BF16)] * nz
+        ff_pays = [shape((rows, 512), BF16), shape((2, rows, 512), BF16), shape((rows, 512), BF16)]
+        attn_pays = [shape((rows, 256), BF16), shape((2, rows, 256), BF16), shape((rows, 256), BF16), shape((rows, 512), BF16)]
     else:
-        pays = [shape((D, 256), BF16), shape((D, width), BF16), shape((width, D), BF16), shape((8, D))]
-    half = (n // 2, TOK, 2 * D)
-    layer_out = vmem_call(
-        functools.partial(layer_body, n, nz, fast),
-        [shape(half, BF16), shape(half, BF16), shape((HEAD_DIM, D), BF16)] + pays,
+        ff_pays = [shape((D, width), BF16), shape((width, D), BF16)]
+        attn_pays = [shape((D, 256), BF16), shape((8, D))]
+    ff_out = vmem_call(
+        functools.partial(ff_body, n, nz, fast),
+        [whole_seq, whole_seq, shape((8, D)), whole_seq, whole_seq] + ff_pays,
         scratch=[
-            pltpu.VMEM((128, 128), F32),
             pltpu.VMEM((seq, D), BF16),
-            pltpu.VMEM((seq, D), F32),
+            pltpu.VMEM((seq, width), BF16),
+            pltpu.VMEM((seq, width), BF16),
+            pltpu.VMEM((seq, D), BF16),
+            pltpu.VMEM((D, width), BF16),
+            pltpu.VMEM((width, D), BF16),
+        ],
+        n_smem=1,
+        n_in=n + 3,
+        cost=pl.CostEstimate(flops=4_000_000_000, bytes_accessed=0, transcendentals=0),
+        name="feed_forward",
+    )(place, *pieces, w_up_c, w_down_c, params)
+    acc_o, acc_d, vec_ff, norms, nhats = ff_out[:5]
+    ff_pay = ff_out[5:]
+    from_ff = []
+    if fast:
+        ff_near = lax.ppermute(ff_pay[1], "fsdp", xor_pairs(nz, 1))
+        from_ff = [ff_pay[2], ff_near]
+    mixn, dqkvn = vmem_call(
+        functools.partial(attn_body, n),
+        [shape((seq, 64), BF16), shape((seq, 256), BF16)],
+        scratch=[
             pltpu.VMEM((seq, 256), F32),
             pltpu.VMEM((seq, 64), BF16),
             pltpu.VMEM((seq, 64), BF16),
@@ -626,45 +674,46 @@
             pltpu.VMEM((64, seq), F32),
             pltpu.VMEM((seq, 128), F32),
             pltpu.VMEM((seq, 256), BF16),
-            pltpu.VMEM((seq, 64), BF16),
-            pltpu.VMEM((seq, 256), BF16),
+        ],
+        n_smem=2,
+        n_in=n + 5,
+        cost=pl.CostEstimate(flops=6_000_000_000, bytes_accessed=0, transcendentals=0),
+        name="attention",
+    )(place, order, *pieces, w_all, params, head_w, turn, norms)
+    ends_out = vmem_call(
+        functools.partial(ends_body, n, nz, fast),
+        [shape(half, BF16), shape(half, BF16), shape((HEAD_DIM, D), BF16)] + attn_pays,
+        scratch=[
+            pltpu.VMEM((128, 128), F32),
             pltpu.VMEM((seq, D), BF16),
-            pltpu.VMEM((seq, D), BF16),
-            pltpu.VMEM((seq, width), BF16),
-            pltpu.VMEM((seq, width), BF16),
             pltpu.VMEM((D, 256), F32),
-            pltpu.VMEM((D, width), BF16),
-            pltpu.VMEM((width, D), BF16),
             pltpu.VMEM((8, D), F32),
         ],
-        n_smem=2,
-        n_in=n + len(given) + 2,
-        cost=pl.CostEstimate(flops=26 * seq * seq * 64, bytes_accessed=12 * seq * D, transcendentals=2 * seq * seq),
-        name="layer",
-    )(place, order, *pieces, *given, head_w, turn)
-    params = given[3]
-    keep_pay, send_pay, g_out = layer_out[:3]
-    pay = layer_out[3:]
+        n_smem=1,
+        n_in=n + 10 + len(from_ff),
+        cost=pl.CostEstimate(flops=3_000_000_000, bytes_accessed=0, transcendentals=0),
+        name="ends",
+    )(place, *pieces, mixn, dqkvn, norms, nhats, acc_o, acc_d, vec_ff, w_all, head_w, params, *from_ff)
+    keep_pay, send_pay, g_out = ends_out[:3]
+    attn_pay = ends_out[3:]
 
     came = lax.ppermute(send_pay, "ctx", xor_pairs(n, 1))
-    pay = list(pay)
     if fast:
         chip_out = vmem_call(
-            functools.partial(chip_fast_body, 1),
-            [shape((2, TOK, D), BF16)] * 2 + [shape((TOK, 2 * D), BF16)] + [shape((TOK, D), BF16)] * 2 + [shape(pay[1].shape, BF16)],
-            n_in=2 + 1,
-            cost=LONG,
+            functools.partial(chip_fast_body, 0),
+            [shape((2, TOK, D), BF16)] * 2 + [shape((TOK, 2 * D), BF16)] + [shape((TOK, D), BF16)] * 2 + [],
+            n_in=2 + 0,
+            cost=LONGER,
             name="chip_sum",
-        )(keep_pay, came, pay[1])
+        )(keep_pay, came)
         first_a, first_b, own_sum, kept_a, kept_b = chip_out[:5]
-        pay[1] = chip_out[5]
         came_a = lax.ppermute(first_a, "ctx", xor_pairs(n, 2))
         came_b = lax.ppermute(first_b, "ctx", xor_pairs(n, 4))
         cross_out = vmem_call(
             functools.partial(cross_body, 0),
             [shape((TOK, D), BF16)] * 2 + [],
             n_in=4 + 0,
-            cost=LONG,
+            cost=LONGER,
             name="cross",
         )(kept_a, kept_b, came_a, came_b)
         second_a, second_b = cross_out[:2]
@@ -683,10 +732,14 @@
 
     if fast:
         out_got = lax.ppermute(g_out, ("ctx", "fsdp"), [(b, a) for a, b in pairs])
-        got = swap_fsdp(pay, nz)
+        ff_far = lax.ppermute(attn_pay[3], "fsdp", xor_pairs(nz, 2))
+        attn_near = lax.ppermute(attn_pay[1], "fsdp", xor_pairs(nz, 1))
+        attn_two = vmem_call(relay_body, shape((rows, 256), BF16), n_in=2, cost=LONG, name="relay")(attn_pay[2], attn_near)
+        attn_far = lax.ppermute(attn_two, "fsdp", xor_pairs(nz, 2))
         out_got = vmem_call(gate_body, shape(out_got.shape, BF16), n_in=1, cost=LONGER, name="gate")(out_got)
-        total = vmem_call(functools.partial(sum_body, nz), shape((D // nz, 768), BF16), n_in=nz, cost=LONGER, name="sum")(*got)
-        share = vmem_call(share_body, shape((D // nz, 1024), BF16), n_in=4, name="share")(total, out_got, *parts[3:])
+        share = vmem_call(share_body, shape((rows, 1024), BF16), n_in=7 + 2, name="share")(
+            ff_pay[0], ff_near, ff_far, attn_pay[0], attn_near, attn_far, out_got, parts[3], parts[4]
+        )
         alls = gather_ctx(share, n)
         dz = D // nz
         outs = vmem_call(
@@ -718,7 +771,8 @@
     else:
         everyone = ("ctx", "fsdp")
         head = me // (n // HEADS)
-        g_qkv, g_up, g_down, vec = pay
+        g_up, g_down = ff_pay
+        g_qkv, vec = attn_pay
 
         def own(full, axis=0):
             size = full.shape[axis] // nz

time: 85 us -> 83.4 us (0.981)
  starting transfers between devices: 34.2 us -> 32 us
  Pallas kernels: 19 us -> 21.2 us
  waiting for transfers between devices: 28.4 us -> 26.9 us
    ppermute x1, waiting for transfers between devices: 4.5 us -> 0.23 us  [per_device(): came_a = lax.ppermute(first_a, 'ctx', xor_pairs(n, 2))]
    ppermute x1, starting transfers between devices: 3.36 us -> 0.59 us  [per_device(): lax.ppermute(second_a, 'ctx', xor_pairs(n, 4))]
    ppermute x1, waiting for transfers between devices: 0.25 us -> 2.65 us  [per_device(): lax.ppermute(second_a, 'ctx', xor_pairs(n, 4))]
    ppermute x3 -> x4, waiting for transfers between devices: 2.85 us -> 5.14 us  [the longest x1 4.26 us: per_device(): attn_near = lax.ppermute(attn_pay[1], 'fsdp', xor_pairs(nz, 1))]
    ppermute x1, starting transfers between devices: 2.53 us -> 0.3 us  [per_device(): came_b = lax.ppermute(first_b, 'ctx', xor_pairs(n, 4))]
    pallas_call x4 -> x6, Pallas kernels: 11 us -> 13.2 us  [the longest x1 6.15 us: per_device(): vmem_call(functools.partial(attn_body, n), [shape((seq, 64), BF16), shape...]
    ppermute x1, starting transfers between devices: 0.11 us -> 1.77 us  [per_device(): lax.ppermute(second_b, 'ctx', xor_pairs(n, 2))]
    ppermute x1, waiting for transfers between devices: 1.62 us -> 0.52 us  [per_device(): lax.ppermute(second_b, 'ctx', xor_pairs(n, 2))]
  transfers between devices with their start and end apart: 27 -> 28, of which waited for: 15 -> 14; matrix products, arithmetic and copies ran while one was open for 0% -> 0% of each run, Pallas kernels for 3% -> 16%
where the time goes in v4:
time: 83.4 us; the launch traced here: 83.2 us
  starting transfers between devices  32 us (38%)
  waiting for transfers between devices  26.9 us (32%)
  Pallas kernels  21.2 us (25%)
  local copies, waits for them, and re-layouts  1.51 us (2%)
  other arithmetic  0.84 us (1%)
    ppermute x6, waiting for transfers between devices, gather_ctx(): got[k] = lax.ppermute(value, 'ctx', xor_pairs(n, k))  12.9 us
    ppermute x6, starting transfers between devices, gather_ctx(): got[k] = lax.ppermute(value, 'ctx', xor_pairs(n, k))  7.04 us
    ppermute x1, starting transfers between devices, per_device(): ff_far = lax.ppermute(attn_pay[3], 'fsdp', xor_pairs(nz, 2))  6.84 us
    pallas_call x1, Pallas kernels, per_device(): vmem_call(functools.partial(attn_body, n), [shape((seq, 64), BF16), shape...  6.15 us
    ppermute x2, starting transfers between devices, relay_fsdp(): one, two = (lax.ppermute(value, 'fsdp', xor_pairs(nz, k)) for k in (1, 2))  5.61 us
    ppermute x2, waiting for transfers between devices, relay_fsdp(): one, two = (lax.ppermute(value, 'fsdp', xor_pairs(nz, k)) for k in (1, 2))  4.36 us
    ppermute x1, waiting for transfers between devices, per_device(): attn_near = lax.ppermute(attn_pay[1], 'fsdp', xor_pairs(nz, 1))  4.26 us
    pallas_call x1, Pallas kernels, per_device(): vmem_call(functools.partial(ff_body, n, nz, fast), [whole_seq, whole_seq,...  4.17 us
  transfers between devices with their start and end apart: 28, of which 14 were waited for; matrix products, arithmetic and copies ran while one was open for 0% of the time, Pallas kernels for 16%

profile of v4, /device:TPU:0, one launch (start us, length us, event | category | flops | bytes accessed | tf_op | source)
XLA Modules:
  0.0 83.2 jit_solution(9145726796219054794)
XLA Ops:
  0.6 0.6 pad_add_fusion.place
  1.2 2.8 %pack.1 = (bf16[128,768]{1,0:T(8,128)(2,1)}, bf16[256,512]{1,0:T(8,128)(2,1)}, bf16[64,512]{1,0:T(8,128)(2,1)}) custom-call(s32[2]{0:T(128)} %pad_add_fusion.place, bf16[128,1536]{1,0:T(8,128)(2,1)} %refs_2_.1, bf16[128,1536]{1,0:T(8,128)(2,1)} %refs_2_.1, bf16[128,1536]{1,0:T(8,128)(2,1)} %refs_2_.1, bf16[128,2048]{1,0:T(8,128)(2,1)} %refs_6_.1, ...), custom_call_target="tpu_custom_call" | custom-call | tf_op jit(solution)/shard_map/pack/pallas_call | solution.py:112
  4.0 4.0 %collective-permute-start.1 = (bf16[128,768]{1,0:T(8,128)(2,1)}, bf16[128,768]{1,0:T(8,128)(2,1)S(1)}, u32[]{:S(2)}, u32[]{:S(2)}) collective-permute-start(bf16[128,768]{1,0:T(8,128)(2,1)} %get-tuple-element.59.refs_0_), channel_id=1, source_target_pairs={{0,2},{1,3},{2,0},{3,1},{4,6},{5,7},{6,4},{7,5},{8,10},{9,11},{10,... | collective-permute-start | bytes 589832 | tf_op jit(solution)/shard_map/ppermute | solution.py:534
  8.0 1.6 %collective-permute-start = (bf16[128,768]{1,0:T(8,128)(2,1)}, bf16[128,768]{1,0:T(8,128)(2,1)S(1)}, u32[]{:S(2)}, u32[]{:S(2)}) collective-permute-start(bf16[128,768]{1,0:T(8,128)(2,1)} %get-tuple-element.59.refs_0_), channel_id=1, source_target_pairs={{0,1},{1,0},{2,3},{3,2},{4,5},{5,4},{6,7},{7,6},{8,9},{9,8},{10,11... | collective-permute-start | bytes 589832 | tf_op jit(solution)/shard_map/ppermute | solution.py:534
  9.6 2.4 %collective-permute-start.8 = (bf16[256,512]{1,0:T(8,128)(2,1)}, bf16[256,512]{1,0:T(8,128)(2,1)S(1)}, u32[]{:S(2)}, u32[]{:S(2)}) collective-permute-start(bf16[256,512]{1,0:T(8,128)(2,1)} %get-tuple-element.61.refs_0_), channel_id=1, source_target_pairs={{0,24},{4,28},{8,16},{12,20},{16,8},{20,12},{24,0},{28,4},{1,25},{... | collective-permute-start | bytes 786440 | tf_op jit(solution)/shard_map/ppermute | solution.py:523
  12.1 0.5 collective-permute-start.6
  12.6 0.5 collective-permute-start.4
  13.1 4.4 %collective-permute-done.1.refs_2_ = bf16[128,768]{1,0:T(8,128)(2,1)S(1)} collective-permute-done((bf16[128,768]{1,0:T(8,128)(2,1)}, bf16[128,768]{1,0:T(8,128)(2,1)S(1)}, u32[]{:S(2)}, u32[]{:S(2)}) %collective-permute-start.1) | collective-permute-done | bytes 196640 | tf_op jit(solution)/shard_map/ppermute | solution.py:534
  17.5 0.7 collective-permute-start.2
  18.3 0.1 add.23
  18.3 0.6 copy-done.7
  18.9 0.2 select_reduce_fusion.order
  19.2 0.8 copy-done.2
  20.0 0.8 collective-permute-start.10
  20.9 3.0 %collective-permute-done.6.refs_4_ = bf16[256,512]{1,0:T(8,128)(2,1)S(1)} collective-permute-done((bf16[256,512]{1,0:T(8,128)(2,1)}, bf16[256,512]{1,0:T(8,128)(2,1)S(1)}, u32[]{:S(2)}, u32[]{:S(2)}) %collective-permute-start.6) | collective-permute-done | bytes 262176 | tf_op jit(solution)/shard_map/ppermute | solution.py:523
  23.8 0.1 collective-permute-done.4.refs_2_
  23.9 0.4 collective-permute-start.7
  24.3 0.1 collective-permute-start.5
  24.4 0.7 unpack.1
  25.2 0.2 collective-permute-done.9.refs_7_
  25.4 0.4 collective-permute-done.7.refs_5_
  25.7 0.4 collective-permute-done.5.refs_3_
  26.1 4.2 %feed_forward.1 = (bf16[1024,512]{1,0:T(8,128)(2,1)S(1)}, bf16[1024,512]{1,0:T(8,128)(2,1)S(1)}, f32[8,512]{1,0:T(8,128)S(1)}, bf16[1024,512]{1,0:T(8,128)(2,1)S...) custom-call(s32[2]{0:T(128)S(1)} %copy-done.3, ...), custom_call_target="tpu_custom_call" | custom-call | flops 4000000000 | tf_op jit(solution)/shard_map/feed_forward/pallas_call | solution.py:641
  30.3 1.4 %collective-permute-start.11 = (bf16[2,128,512]{2,1,0:T(8,128)(2,1)S(1)}, bf16[2,128,512]{2,1,0:T(8,128)(2,1)S(1)}, u32[]{:S(2)}, u32[]{:S(2)}) collective-permute-start(bf16[2,128,512]{2,1,0:T(8,128)(2,1)S(1)} %get-tuple-element.74), channel_id=1, source_target_pairs={{0,1},{1,0},{2,3},{3,2},{4,5},{5,4},{6,7},{7,6},{8,9},{9,8},{10,11... | collective-permute-start | bytes 786440 | tf_op jit(solution)/shard_map/ppermute | solution.py:661
  31.7 6.2 %attention.1 = (bf16[1024,64]{1,0:T(8,128)(2,1)S(1)}, bf16[1024,256]{1,0:T(8,128)(2,1)S(1)}) custom-call(s32[2]{0:T(128)S(1)} %copy-done.3, s32[16]{0:T(128)S(1)} %select_reduce_fusion.order, bf16[256,512]{1,0:T(8,128)(2,1)S(1)} %copy-done.4, bf16[256,512]{1,0:T(8,128)(2,1)S(1)} %collective-permute-done.3.refs_1_, ...), custom_call_target="tpu_custom_call" | custom-call | flops 6000000000 | tf_op jit(solution)/shard_map/attention/pallas_call | solution.py:663
  37.8 0.9 %collective-permute-done.11.refs_19_.ff_near = bf16[2,128,512]{2,1,0:T(8,128)(2,1)S(1)} collective-permute-done((bf16[2,128,512]{2,1,0:T(8,128)(2,1)S(1)}, bf16[2,128,512]{2,1,0:T(8,128)(2,1)S(1)}, u32[]{:S(2)}, u32[]{:S(2)}) %collective-permute-start.11) | collective-permute-done | bytes 262176 | tf_op jit(solution)/shard_map/ppermute | solution.py:661
  38.7 2.5 %ends.1 = (bf16[4,128,1024]{2,1,0:T(8,128)(2,1)S(1)}, bf16[4,128,1024]{2,1,0:T(8,128)(2,1)S(1)}, bf16[64,512]{1,0:T(8,128)(2,1)S(1)}, bf16[128,256]{1,0:T(8,128)...) custom-call(s32[2]{0:T(128)S(1)} %copy-done.3, ...), custom_call_target="tpu_custom_call" | custom-call | flops 3000000000 | tf_op jit(solution)/shard_map/ends/pallas_call | solution.py:683
  41.3 0.8 %collective-permute-start.20 = (bf16[64,512]{1,0:T(8,128)(2,1)S(1)}, bf16[64,512]{1,0:T(8,128)(2,1)S(1)}, u32[]{:S(2)}, u32[]{:S(2)}) collective-permute-start(bf16[64,512]{1,0:T(8,128)(2,1)S(1)} %get-tuple-element.91), channel_id=1, source_target_pairs={{0,0},{8,1},{16,2},{24,3},{4,4},{12,5},{20,6},{28,7},{1,8},{9,9},{... | collective-permute-start | bytes 196616 | tf_op jit(solution)/shard_map/ppermute | solution.py:734
  42.2 6.8 %collective-permute-start.17 = (bf16[128,512]{1,0:T(8,128)(2,1)S(1)}, bf16[128,512]{1,0:T(8,128)(2,1)S(1)}, u32[]{:S(2)}, u32[]{:S(2)}) collective-permute-start(bf16[128,512]{1,0:T(8,128)(2,1)S(1)} %get-tuple-element.87), channel_id=1, source_target_pairs={{0,2},{1,3},{2,0},{3,1},{4,6},{5,7},{6,4},{7,5},{8,10},{9,11},{10,... | collective-permute-start | bytes 393224 | tf_op jit(solution)/shard_map/ppermute | solution.py:735
  49.0 1.8 %collective-permute-start.18 = (bf16[2,128,256]{2,1,0:T(8,128)(2,1)S(1)}, bf16[2,128,256]{2,1,0:T(8,128)(2,1)S(1)}, u32[]{:S(2)}, u32[]{:S(2)}) collective-permute-start(bf16[2,128,256]{2,1,0:T(8,128)(2,1)S(1)} %get-tuple-element.89), channel_id=1, source_target_pairs={{0,1},{1,0},{2,3},{3,2},{4,5},{5,4},{6,7},{7,6},{8,9},{9,8},{10,11... | collective-permute-start | bytes 393224 | tf_op jit(solution)/shard_map/ppermute | solution.py:736
  50.8 0.2 chip_sum.1
  51.1 0.3 collective-permute-start.14
  51.4 4.3 %collective-permute-done.18.came.near = bf16[2,128,256]{2,1,0:T(8,128)(2,1)S(1)} collective-permute-done((bf16[2,128,256]{2,1,0:T(8,128)(2,1)S(1)}, bf16[2,128,256]{2,1,0:T(8,128)(2,1)S(1)}, u32[]{:S(2)}, u32[]{:S(2)}) %collective-permute-start.18) | collective-permute-done | bytes 131104 | tf_op jit(solution)/shard_map/ppermute | solution.py:736
  55.7 3.0 %collective-permute-start.19 = (bf16[128,256]{1,0:T(8,128)(2,1)S(1)}, bf16[128,256]{1,0:T(8,128)(2,1)S(1)}, u32[]{:S(2)}, u32[]{:S(2)}) collective-permute-start(bf16[128,256]{1,0:T(8,128)(2,1)S(1)} %relay.1), channel_id=1, source_target_pairs={{0,2},{1,3},{2,0},{3,1},{4,6},{5,7},{6,4},{7,5},{8,10},{9,11},{10,... | collective-permute-start | bytes 196616 | tf_op jit(solution)/shard_map/ppermute | solution.py:738
  58.8 0.2 collective-permute-done.13.came_a.refs_1_
  59.0 0.1 collective-permute-done.14.came_b.refs_2_
  59.1 0.6 collective-permute-start.15
  59.7 1.8 %collective-permute-start.16 = (bf16[128,512]{1,0:T(8,128)(2,1)S(1)}, bf16[128,512]{1,0:T(8,128)(2,1)S(1)}, u32[]{:S(2)}, u32[]{:S(2)}) collective-permute-start(bf16[128,512]{1,0:T(8,128)(2,1)S(1)} %get-tuple-element.83), channel_id=1, source_target_pairs={{0,8},{4,12},{8,0},{12,4},{16,24},{20,28},{24,16},{28,20},{1,9},{5... | collective-permute-start | bytes 393224 | tf_op jit(solution)/shard_map/ppermute | solution.py:721
  61.5 2.6 %collective-permute-done.15.refs_3_.refs_0_ = bf16[128,512]{1,0:T(8,128)(2,1)S(1)} collective-permute-done((bf16[128,512]{1,0:T(8,128)(2,1)S(1)}, bf16[128,512]{1,0:T(8,128)(2,1)S(1)}, u32[]{:S(2)}, u32[]{:S(2)}) %collective-permute-start.15) | collective-permute-done | bytes 131104 | tf_op jit(solution)/shard_map/ppermute | solution.py:721
  64.2 0.5 collective-permute-done.16.refs_4_.refs_1_
  64.8 2.7 %collective-permute-start.26 = (bf16[128,1024]{1,0:T(8,128)(2,1)S(1)}, bf16[128,1024]{1,0:T(8,128)(2,1)S(1)}, u32[]{:S(2)}, u32[]{:S(2)}) collective-permute-start(bf16[128,1024]{1,0:T(8,128)(2,1)S(1)} %share.1.refs_0_), channel_id=1, source_target_pairs={{0,24},{4,28},{8,16},{12,20},{16,8},{20,12},{24,0},{28,4},{1,25},{... | collective-permute-start | bytes 786440 | tf_op jit(solution)/shard_map/ppermute | solution.py:523
  67.4 0.6 collective-permute-start.24
  68.1 0.3 collective-permute-start.22
  68.3 6.7 %collective-permute-done.26.refs_6_ = bf16[128,1024]{1,0:T(8,128)(2,1)S(1)} collective-permute-done((bf16[128,1024]{1,0:T(8,128)(2,1)S(1)}, bf16[128,1024]{1,0:T(8,128)(2,1)S(1)}, u32[]{:S(2)}, u32[]{:S(2)}) %collective-permute-start.26) | collective-permute-done | bytes 262176 | tf_op jit(solution)/shard_map/ppermute | solution.py:523
  75.0 3.2 %collective-permute-done.24.refs_4_ = bf16[128,1024]{1,0:T(8,128)(2,1)S(1)} collective-permute-done((bf16[128,1024]{1,0:T(8,128)(2,1)S(1)}, bf16[128,1024]{1,0:T(8,128)(2,1)S(1)}, u32[]{:S(2)}, u32[]{:S(2)}) %collective-permute-start.24) | collective-permute-done | bytes 262176 | tf_op jit(solution)/shard_map/ppermute | solution.py:523
  78.2 0.5 collective-permute-start.23
  78.7 1.6 %close.1 = (bf16[128,512]{1,0:T(8,128)(2,1)}, f32[128,512]{1,0:T(8,128)}) custom-call(s32[2]{0:T(128)S(1)} %copy-done.3, bf16[128,512]{1,0:T(8,128)(2,1)S(1)} %bitcast.6, bf16[128,512]{1,0:T(8,128)(2,1)S(1)} %bitcast.7, f32[8,512]{1,0:T(8,128)S(1)} %get-tuple-element.60.refs_10_.refs_9_.refs_17_.params, bf16[128,1024]{1,0:T(8,128)(2,1)S(1)} %get-tuple-element.77.refs_0_, ...), custom_call_target="tpu_custom_call" | custom-call | tf_op jit(solution)/shard_map/close/pallas_call | solution.py:725
  80.3 2.9 %finish.1 = (f32[128]{0:T(128)}, f32[128]{0:T(128)}, f32[128,1536]{1,0:T(8,128)}, f32[384]{0:T(512)}, f32[128,512]{1,0:T(8,128)}, /*index=5*/f32[128]{0:T(128)},...) custom-call(s32[2]{0:T(128)S(1)} %copy-done.3, ...), custom_call_target="tpu_custom_call" | custom-call | tf_op jit(solution)/shard_map/finish/pallas_call | solution.py:745
  (42 shorter events, 0.5 us)
Async XLA Ops:
  4.0 13.5 %collective-permute-start.1 = (bf16[128,768]{1,0:T(8,128)(2,1)}, bf16[128,768]{1,0:T(8,128)(2,1)S(1)}, u32[]{:S(2)}, u32[]{:S(2)}) collective-permute-start(bf16[128,768]{1,0:T(8,128)(2,1)} %get-tuple-element.59.refs_0_), channel_id=1, source_target_pairs={{0,2},{1,3},{2,0},{3,1},{4,6},{5,7},{6,4},{7,5},{8,10},{9,11},{10,... | collective-permute-start | bytes 589832 | tf_op jit(solution)/shard_map/ppermute | solution.py:534
  8.0 11.1 %collective-permute-start = (bf16[128,768]{1,0:T(8,128)(2,1)}, bf16[128,768]{1,0:T(8,128)(2,1)S(1)}, u32[]{:S(2)}, u32[]{:S(2)}) collective-permute-start(bf16[128,768]{1,0:T(8,128)(2,1)} %get-tuple-element.59.refs_0_), channel_id=1, source_target_pairs={{0,1},{1,0},{2,3},{3,2},{4,5},{5,4},{6,7},{7,6},{8,9},{9,8},{10,11... | collective-permute-start | bytes 589832 | tf_op jit(solution)/shard_map/ppermute | solution.py:534
  9.6 10.4 %collective-permute-start.8 = (bf16[256,512]{1,0:T(8,128)(2,1)}, bf16[256,512]{1,0:T(8,128)(2,1)S(1)}, u32[]{:S(2)}, u32[]{:S(2)}) collective-permute-start(bf16[256,512]{1,0:T(8,128)(2,1)} %get-tuple-element.61.refs_0_), channel_id=1, source_target_pairs={{0,24},{4,28},{8,16},{12,20},{16,8},{20,12},{24,0},{28,4},{1,25},{... | collective-permute-start | bytes 786440 | tf_op jit(solution)/shard_map/ppermute | solution.py:523
  12.1 11.8 %collective-permute-start.6 = (bf16[256,512]{1,0:T(8,128)(2,1)}, bf16[256,512]{1,0:T(8,128)(2,1)S(1)}, u32[]{:S(2)}, u32[]{:S(2)}) collective-permute-start(bf16[256,512]{1,0:T(8,128)(2,1)} %get-tuple-element.61.refs_0_), channel_id=1, source_target_pairs={{0,16},{4,20},{8,24},{12,28},{16,0},{20,4},{24,8},{28,12},{1,17},{... | collective-permute-start | bytes 786440 | tf_op jit(solution)/shard_map/ppermute | solution.py:523
  12.6 11.4 %collective-permute-start.4 = (bf16[256,512]{1,0:T(8,128)(2,1)}, bf16[256,512]{1,0:T(8,128)(2,1)S(1)}, u32[]{:S(2)}, u32[]{:S(2)}) collective-permute-start(bf16[256,512]{1,0:T(8,128)(2,1)} %get-tuple-element.61.refs_0_), channel_id=1, source_target_pairs={{0,8},{4,12},{8,0},{12,4},{16,24},{20,28},{24,16},{28,20},{1,9},{5... | collective-permute-start | bytes 786440 | tf_op jit(solution)/shard_map/ppermute | solution.py:523
  17.5 6.9 %collective-permute-start.2 = (bf16[128,768]{1,0:T(8,128)(2,1)S(1)}, bf16[128,768]{1,0:T(8,128)(2,1)S(1)}, u32[]{:S(2)}, u32[]{:S(2)}) collective-permute-start(bf16[128,768]{1,0:T(8,128)(2,1)S(1)} %collective-permute-done.1.refs_2_), channel_id=1, source_target_pairs={{0,1},{1,0},{2,3},{3,2},{4,5},{5,4},{6,7},{7,6},{8,9},{9,8},{10,11... | collective-permute-start | bytes 589832 | tf_op jit(solution)/shard_map/ppermute | solution.py:535
  18.3 0.7 copy-start.7
  19.1 6.1 %collective-permute-start.3 = (bf16[256,512]{1,0:T(8,128)(2,1)}, bf16[256,512]{1,0:T(8,128)(2,1)S(1)}, u32[]{:S(2)}, u32[]{:S(2)}) collective-permute-start(bf16[256,512]{1,0:T(8,128)(2,1)} %get-tuple-element.61.refs_0_), channel_id=1, source_target_pairs={{0,4},{4,0},{8,12},{12,8},{16,20},{20,16},{24,28},{28,24},{1,5},{5... | collective-permute-start | bytes 786440 | tf_op jit(solution)/shard_map/ppermute | solution.py:525
  19.2 0.8 %copy-start.2 = (bf16[64,512]{1,0:T(8,128)(2,1)S(1)}, bf16[64,512]{1,0:T(8,128)(2,1)}, u32[]{:S(2)}) copy-start(bf16[64,512]{1,0:T(8,128)(2,1)} %get-tuple-element.63.value) | copy-start | bytes 196612
  20.0 4.4 %copy-start.3 = (s32[2]{0:T(128)S(1)}, s32[2]{0:T(128)}, u32[]{:S(2)}) copy-start(s32[2]{0:T(128)} %pad_add_fusion.place) | copy-start | bytes 28
  20.0 4.4 %copy-start.5 = (bf16[128,768]{1,0:T(8,128)(2,1)S(1)}, bf16[128,768]{1,0:T(8,128)(2,1)}, u32[]{:S(2)}) copy-start(bf16[128,768]{1,0:T(8,128)(2,1)} %get-tuple-element.59.refs_0_) | copy-start | bytes 589828
  20.0 6.1 %copy-start.4 = (bf16[256,512]{1,0:T(8,128)(2,1)S(1)}, bf16[256,512]{1,0:T(8,128)(2,1)}, u32[]{:S(2)}) copy-start(bf16[256,512]{1,0:T(8,128)(2,1)} %get-tuple-element.61.refs_0_) | copy-start | bytes 786436
  20.0 11.6 %collective-permute-start.10 = (bf16[64,512]{1,0:T(8,128)(2,1)S(1)}, bf16[64,512]{1,0:T(8,128)(2,1)S(1)}, u32[]{:S(2)}, u32[]{:S(2)}) collective-permute-start(bf16[64,512]{1,0:T(8,128)(2,1)S(1)} %gate_w.1), channel_id=1, source_target_pairs={{0,0},{1,8},{2,16},{3,24},{4,4},{5,12},{6,20},{7,28},{8,1},{9,9},{... | collective-permute-start | bytes 196616 | tf_op jit(solution)/shard_map/ppermute | solution.py:607
  23.8 1.5 %collective-permute-start.9 = (bf16[256,512]{1,0:T(8,128)(2,1)S(1)}, bf16[256,512]{1,0:T(8,128)(2,1)S(1)}, u32[]{:S(2)}, u32[]{:S(2)}) collective-permute-start(bf16[256,512]{1,0:T(8,128)(2,1)S(1)} %collective-permute-done.8.refs_6_), channel_id=1, source_target_pairs={{0,4},{4,0},{8,12},{12,8},{16,20},{20,16},{24,28},{28,24},{1,5},{5... | collective-permute-start | bytes 786440 | tf_op jit(solution)/shard_map/ppermute | solution.py:525
  23.9 1.8 %collective-permute-start.7 = (bf16[256,512]{1,0:T(8,128)(2,1)S(1)}, bf16[256,512]{1,0:T(8,128)(2,1)S(1)}, u32[]{:S(2)}, u32[]{:S(2)}) collective-permute-start(bf16[256,512]{1,0:T(8,128)(2,1)S(1)} %collective-permute-done.6.refs_4_), channel_id=1, source_target_pairs={{0,4},{4,0},{8,12},{12,8},{16,20},{20,16},{24,28},{28,24},{1,5},{5... | collective-permute-start | bytes 786440 | tf_op jit(solution)/shard_map/ppermute | solution.py:525
  24.3 1.8 %collective-permute-start.5 = (bf16[256,512]{1,0:T(8,128)(2,1)S(1)}, bf16[256,512]{1,0:T(8,128)(2,1)S(1)}, u32[]{:S(2)}, u32[]{:S(2)}) collective-permute-start(bf16[256,512]{1,0:T(8,128)(2,1)S(1)} %collective-permute-done.4.refs_2_), channel_id=1, source_target_pairs={{0,4},{4,0},{8,12},{12,8},{16,20},{20,16},{24,28},{28,24},{1,5},{5... | collective-permute-start | bytes 786440 | tf_op jit(solution)/shard_map/ppermute | solution.py:525
  26.1 5.6 %copy-start.6 = (f32[1024,128]{1,0:T(8,128)S(1)}, f32[1024,128]{1,0:T(8,128)}, u32[]{:S(2)}) copy-start(f32[1024,128]{1,0:T(8,128)} %constant.15.clone.refs_11_) | copy-start | bytes 1572868
  30.3 8.4 %collective-permute-start.11 = (bf16[2,128,512]{2,1,0:T(8,128)(2,1)S(1)}, bf16[2,128,512]{2,1,0:T(8,128)(2,1)S(1)}, u32[]{:S(2)}, u32[]{:S(2)}) collective-permute-start(bf16[2,128,512]{2,1,0:T(8,128)(2,1)S(1)} %get-tuple-element.74), channel_id=1, source_target_pairs={{0,1},{1,0},{2,3},{3,2},{4,5},{5,4},{6,7},{7,6},{8,9},{9,8},{10,11... | collective-permute-start | bytes 786440 | tf_op jit(solution)/shard_map/ppermute | solution.py:661
  41.2 9.6 %collective-permute-start.12 = (bf16[4,128,1024]{2,1,0:T(8,128)(2,1)S(1)}, bf16[4,128,1024]{2,1,0:T(8,128)(2,1)S(1)}, u32[]{:S(2)}, u32[]{:S(2)}) collective-permute-start(bf16[4,128,1024]{2,1,0:T(8,128)(2,1)S(1)} %get-tuple-element.76), channel_id=1, source_target_pairs={{0,4},{4,0},{8,12},{12,8},{16,20},{20,16},{24,28},{28,24},{1,5},{5... | collective-permute-start | bytes 3145736 | tf_op jit(solution)/shard_map/ppermute | solution.py:700
  41.3 20.2 %collective-permute-start.20 = (bf16[64,512]{1,0:T(8,128)(2,1)S(1)}, bf16[64,512]{1,0:T(8,128)(2,1)S(1)}, u32[]{:S(2)}, u32[]{:S(2)}) collective-permute-start(bf16[64,512]{1,0:T(8,128)(2,1)S(1)} %get-tuple-element.91), channel_id=1, source_target_pairs={{0,0},{8,1},{16,2},{24,3},{4,4},{12,5},{20,6},{28,7},{1,8},{9,9},{... | collective-permute-start | bytes 196616 | tf_op jit(solution)/shard_map/ppermute | solution.py:734
  42.2 19.3 %collective-permute-start.17 = (bf16[128,512]{1,0:T(8,128)(2,1)S(1)}, bf16[128,512]{1,0:T(8,128)(2,1)S(1)}, u32[]{:S(2)}, u32[]{:S(2)}) collective-permute-start(bf16[128,512]{1,0:T(8,128)(2,1)S(1)} %get-tuple-element.87), channel_id=1, source_target_pairs={{0,2},{1,3},{2,0},{3,1},{4,6},{5,7},{6,4},{7,5},{8,10},{9,11},{10,... | collective-permute-start | bytes 393224 | tf_op jit(solution)/shard_map/ppermute | solution.py:735
  49.0 6.7 %collective-permute-start.18 = (bf16[2,128,256]{2,1,0:T(8,128)(2,1)S(1)}, bf16[2,128,256]{2,1,0:T(8,128)(2,1)S(1)}, u32[]{:S(2)}, u32[]{:S(2)}) collective-permute-start(bf16[2,128,256]{2,1,0:T(8,128)(2,1)S(1)} %get-tuple-element.89), channel_id=1, source_target_pairs={{0,1},{1,0},{2,3},{3,2},{4,5},{5,4},{6,7},{7,6},{8,9},{9,8},{10,11... | collective-permute-start | bytes 393224 | tf_op jit(solution)/shard_map/ppermute | solution.py:736
  51.1 7.9 %collective-permute-start.13 = (bf16[2,128,512]{2,1,0:T(8,128)(2,1)S(1)}, bf16[2,128,512]{2,1,0:T(8,128)(2,1)S(1)}, u32[]{:S(2)}, u32[]{:S(2)}) collective-permute-start(bf16[2,128,512]{2,1,0:T(8,128)(2,1)S(1)} %get-tuple-element.78), channel_id=1, source_target_pairs={{0,8},{4,12},{8,0},{12,4},{16,24},{20,28},{24,16},{28,20},{1,9},{5... | collective-permute-start | bytes 786440 | tf_op jit(solution)/shard_map/ppermute | solution.py:710
  51.1 7.9 %collective-permute-start.14 = (bf16[2,128,512]{2,1,0:T(8,128)(2,1)S(1)}, bf16[2,128,512]{2,1,0:T(8,128)(2,1)S(1)}, u32[]{:S(2)}, u32[]{:S(2)}) collective-permute-start(bf16[2,128,512]{2,1,0:T(8,128)(2,1)S(1)} %get-tuple-element.79), channel_id=1, source_target_pairs={{0,16},{4,20},{8,24},{12,28},{16,0},{20,4},{24,8},{28,12},{1,17},{... | collective-permute-start | bytes 786440 | tf_op jit(solution)/shard_map/ppermute | solution.py:711
  55.7 5.8 %collective-permute-start.19 = (bf16[128,256]{1,0:T(8,128)(2,1)S(1)}, bf16[128,256]{1,0:T(8,128)(2,1)S(1)}, u32[]{:S(2)}, u32[]{:S(2)}) collective-permute-start(bf16[128,256]{1,0:T(8,128)(2,1)S(1)} %relay.1), channel_id=1, source_target_pairs={{0,2},{1,3},{2,0},{3,1},{4,6},{5,7},{6,4},{7,5},{8,10},{9,11},{10,... | collective-permute-start | bytes 196616 | tf_op jit(solution)/shard_map/ppermute | solution.py:738
  59.1 5.0 %collective-permute-start.15 = (bf16[128,512]{1,0:T(8,128)(2,1)S(1)}, bf16[128,512]{1,0:T(8,128)(2,1)S(1)}, u32[]{:S(2)}, u32[]{:S(2)}) collective-permute-start(bf16[128,512]{1,0:T(8,128)(2,1)S(1)} %get-tuple-element.82), channel_id=1, source_target_pairs={{0,16},{4,20},{8,24},{12,28},{16,0},{20,4},{24,8},{28,12},{1,17},{... | collective-permute-start | bytes 393224 | tf_op jit(solution)/shard_map/ppermute | solution.py:721
  59.7 5.0 %collective-permute-start.16 = (bf16[128,512]{1,0:T(8,128)(2,1)S(1)}, bf16[128,512]{1,0:T(8,128)(2,1)S(1)}, u32[]{:S(2)}, u32[]{:S(2)}) collective-permute-start(bf16[128,512]{1,0:T(8,128)(2,1)S(1)} %get-tuple-element.83), channel_id=1, source_target_pairs={{0,8},{4,12},{8,0},{12,4},{16,24},{20,28},{24,16},{28,20},{1,9},{5... | collective-permute-start | bytes 393224 | tf_op jit(solution)/shard_map/ppermute | solution.py:721
  64.7 14.1 %copy-start = (bf16[1,128,512]{2,1,0:T(8,128)(2,1)S(1)}, bf16[1,128,512]{2,1,0:T(8,128)(2,1)}, u32[]{:S(2)}) copy-start(bf16[1,128,512]{2,1,0:T(8,128)(2,1)} %refs_9_.1) | copy-start | bytes 393220
  64.7 14.1 %copy-start.1 = (bf16[1,128,512]{2,1,0:T(8,128)(2,1)S(1)}, bf16[1,128,512]{2,1,0:T(8,128)(2,1)}, u32[]{:S(2)}) copy-start(bf16[1,128,512]{2,1,0:T(8,128)(2,1)} %refs_10_.1) | copy-start | bytes 393220
  64.8 10.2 %collective-permute-start.26 = (bf16[128,1024]{1,0:T(8,128)(2,1)S(1)}, bf16[128,1024]{1,0:T(8,128)(2,1)S(1)}, u32[]{:S(2)}, u32[]{:S(2)}) collective-permute-start(bf16[128,1024]{1,0:T(8,128)(2,1)S(1)} %share.1.refs_0_), channel_id=1, source_target_pairs={{0,24},{4,28},{8,16},{12,20},{16,8},{20,12},{24,0},{28,4},{1,25},{... | collective-permute-start | bytes 786440 | tf_op jit(solution)/shard_map/ppermute | solution.py:523
  67.4 10.8 %collective-permute-start.24 = (bf16[128,1024]{1,0:T(8,128)(2,1)S(1)}, bf16[128,1024]{1,0:T(8,128)(2,1)S(1)}, u32[]{:S(2)}, u32[]{:S(2)}) collective-permute-start(bf16[128,1024]{1,0:T(8,128)(2,1)S(1)} %share.1.refs_0_), channel_id=1, source_target_pairs={{0,16},{4,20},{8,24},{12,28},{16,0},{20,4},{24,8},{28,12},{1,17},{... | collective-permute-start | bytes 786440 | tf_op jit(solution)/shard_map/ppermute | solution.py:523
  68.1 10.2 %collective-permute-start.22 = (bf16[128,1024]{1,0:T(8,128)(2,1)S(1)}, bf16[128,1024]{1,0:T(8,128)(2,1)S(1)}, u32[]{:S(2)}, u32[]{:S(2)}) collective-permute-start(bf16[128,1024]{1,0:T(8,128)(2,1)S(1)} %share.1.refs_0_), channel_id=1, source_target_pairs={{0,8},{4,12},{8,0},{12,4},{16,24},{20,28},{24,16},{28,20},{1,9},{5... | collective-permute-start | bytes 786440 | tf_op jit(solution)/shard_map/ppermute | solution.py:523
  68.3 12.0 %collective-permute-start.21 = (bf16[128,1024]{1,0:T(8,128)(2,1)S(1)}, bf16[128,1024]{1,0:T(8,128)(2,1)S(1)}, u32[]{:S(2)}, u32[]{:S(2)}) collective-permute-start(bf16[128,1024]{1,0:T(8,128)(2,1)S(1)} %share.1.refs_0_), channel_id=1, source_target_pairs={{0,4},{4,0},{8,12},{12,8},{16,20},{20,16},{24,28},{28,24},{1,5},{5... | collective-permute-start | bytes 786440 | tf_op jit(solution)/shard_map/ppermute | solution.py:525
  75.0 5.3 %collective-permute-start.27 = (bf16[128,1024]{1,0:T(8,128)(2,1)S(1)}, bf16[128,1024]{1,0:T(8,128)(2,1)S(1)}, u32[]{:S(2)}, u32[]{:S(2)}) collective-permute-start(bf16[128,1024]{1,0:T(8,128)(2,1)S(1)} %collective-permute-done.26.refs_6_), channel_id=1, source_target_pairs={{0,4},{4,0},{8,12},{12,8},{16,20},{20,16},{24,28},{28,24},{1,5},{5... | collective-permute-start | bytes 786440 | tf_op jit(solution)/shard_map/ppermute | solution.py:525
  78.2 2.1 %collective-permute-start.25 = (bf16[128,1024]{1,0:T(8,128)(2,1)S(1)}, bf16[128,1024]{1,0:T(8,128)(2,1)S(1)}, u32[]{:S(2)}, u32[]{:S(2)}) collective-permute-start(bf16[128,1024]{1,0:T(8,128)(2,1)S(1)} %collective-permute-done.24.refs_4_), channel_id=1, source_target_pairs={{0,4},{4,0},{8,12},{12,8},{16,20},{20,16},{24,28},{28,24},{1,5},{5... | collective-permute-start | bytes 786440 | tf_op jit(solution)/shard_map/ppermute | solution.py:525
  78.2 2.1 %collective-permute-start.23 = (bf16[128,1024]{1,0:T(8,128)(2,1)S(1)}, bf16[128,1024]{1,0:T(8,128)(2,1)S(1)}, u32[]{:S(2)}, u32[]{:S(2)}) collective-permute-start(bf16[128,1024]{1,0:T(8,128)(2,1)S(1)} %collective-permute-done.22.refs_2_), channel_id=1, source_target_pairs={{0,4},{4,0},{8,12},{12,8},{16,20},{20,16},{24,28},{28,24},{1,5},{5... | collective-permute-start | bytes 786440 | tf_op jit(solution)/shard_map/ppermute | solution.py:525

commit v5 on v4

--- a/solution.py
+++ b/solution.py
@@ -179,6 +179,12 @@
     return center * inv, inv
 
 
+def joined(pieces, first):
+    if len(pieces) == 1:
+        return pieces[0][first : first + TOK, :]
+    return jnp.concatenate([piece[first : first + TOK, :] for piece in pieces], axis=0)
+
+
 def fold(values):
     return jnp.sum(values.reshape(values.shape[0] // 8, 8, values.shape[1]), axis=0)
 
@@ -187,7 +193,7 @@
     pieces = refs[:n]
     w_up, w_down, params = refs[n : n + 3]
     outs = refs[n + 3 :]
-    n_pay = 3 if fast else 2
+    n_pay = nz if fast else 2
     acc_o, acc_d, vec, norms, nhats = outs[:5]
     pays = outs[5 : 5 + n_pay]
     norm2s, hiddens, dpres, gs, grad_up, grad_down = outs[5 + n_pay :]
@@ -200,10 +206,10 @@
     g_shift = jnp.zeros((8, D), F32)
     g_sum = jnp.zeros((8, D), F32)
     g_bup = jnp.zeros((8, width), F32)
-    for p in range(n):
-        rows = slice(p * TOK, (p + 1) * TOK)
-        nhat, _ = normalized(pieces[p][0:TOK, :].astype(F32))
-        g = pieces[p][TOK : 2 * TOK, :]
+    for p in range(0, n, 4):
+        rows = slice(p * TOK, (p + 4) * TOK)
+        nhat, _ = normalized(joined(pieces[p : p + 4], 0).astype(F32))
+        g = joined(pieces[p : p + 4], TOK)
         norms[rows, :] = (nhat * gain + shift).astype(BF16)
         nhats[rows, :] = nhat.astype(BF16)
         norm2 = (nhat * gain2 + shift2).astype(BF16)
@@ -229,8 +235,7 @@
     grad_up[...] = mm_tn(dpres[...], norm2s[...]).T.astype(BF16)
     grad_down[...] = mm_tn(hiddens[...], gs[...]).astype(BF16)
     if fast:
-        own, near, two = pays
-        for k, target in ((0, own), (1, near.at[0]), (2, two), (3, near.at[1])):
+        for k, target in enumerate(pays):
             z = zed ^ k
             tall = pl.ds(pl.multiple_of(z * 128, 128), 128)
             flat = pl.ds(pl.multiple_of(z * 64, 64), 64)
@@ -244,7 +249,7 @@
 
 def attn_body(n, place, order, *refs):
     seq = n * TOK
-    qblk = min(256, seq)
+    qblk = min(512, seq)
     pieces = refs[:n]
     w_all, params, w_out, turn, norms = refs[n : n + 5]
     mixn, dqkvn = refs[n + 5 : n + 7]
@@ -254,11 +259,11 @@
     def sorted_rows(block):
         return pl.ds(pl.multiple_of(order[block] * HALF, HALF), HALF)
 
-    for p in range(n):
-        rows = slice(p * TOK, (p + 1) * TOK)
+    for p in range(0, n, 2):
+        rows = slice(p * TOK, (p + 2) * TOK)
         qkv = mm_nn(norms[rows, :], w_all[...]) + bias
-        dmix = mm_nt(pieces[p][TOK : 2 * TOK, :], w_out[...]).astype(BF16)
-        for h in range(TOK // HALF):
+        dmix = mm_nt(joined(pieces[p : p + 2], TOK), w_out[...]).astype(BF16)
+        for h in range(2 * TOK // HALF):
             here = slice(h * HALF, (h + 1) * HALF)
             where = sorted_rows(p * (TOK // HALF) + h)
             raw[where, :] = qkv[here, :]
@@ -279,10 +284,13 @@
         qk = raw[rows, 0:128]
         cos_t, sin_t = both_heads(turn[rows, :])
         turned = (qk * cos_t + swapped(qk) * sin_t).astype(BF16)
-        qs[rows, :] = turned[:, 0:64]
+        qs[rows, :] = turned[:, 0:64] * jnp.asarray(0.125, BF16)
         ks[rows, :] = turned[:, 64:128]
         vs[rows, :] = raw[rows, 128:192].astype(BF16)
 
+    q_at = lax.broadcasted_iota(jnp.int32, (qblk, qblk), 0)
+    k_at = lax.broadcasted_iota(jnp.int32, (qblk, qblk), 1)
+    causal = q_at >= k_at
     dks[...] = jnp.zeros_like(dks)
     dvs[...] = jnp.zeros_like(dvs)
     for i in range(seq // qblk):
@@ -291,24 +299,22 @@
         q = qs[rows, :]
         keys = ks[0:span, :]
         values = vs[0:span, :]
-        s = mm_nt(q, keys) * 0.125
-        q_at = lax.broadcasted_iota(jnp.int32, (qblk, span), 0) + i * qblk
-        k_at = lax.broadcasted_iota(jnp.int32, (qblk, span), 1)
-        s = jnp.where(q_at >= k_at, s, -1e30)
+        s = jnp.where(causal, mm_nt(q, ks[rows, :]), -1e30)
+        if i:
+            s = jnp.concatenate([mm_nt(q, ks[0 : i * qblk, :]), s], axis=1)
         top = jnp.max(s, axis=1, keepdims=True)
         e = jnp.exp(s - top)
-        prob = e * (1.0 / jnp.sum(e, axis=1, keepdims=True))
-        prob_b = prob.astype(BF16)
-        mix = mm_nn(prob_b, values)
+        inv = 1.0 / jnp.sum(e, axis=1, keepdims=True)
+        e_b = e.astype(BF16)
+        mix = mm_nn(e_b, values) * inv
         mixs[rows, :] = mix.astype(BF16)
-        dmix = dms[rows, :]
+        dmix = (dms[rows, :].astype(F32) * inv).astype(BF16)
         delta = jnp.sum(dmix.astype(F32) * mix, axis=1, keepdims=True)
-        dprob = mm_nt(dmix, values)
-        ds = (prob * (dprob - delta)).astype(BF16)
+        ds = (e * (mm_nt(dmix, values) - delta)).astype(BF16)
         dqs[rows, 0:64] = mm_nn(ds, keys) * 0.125
         dks[:, 0:span] += mm_tn(q, ds)
-        dvs[:, 0:span] += mm_tn(dmix, prob_b)
-    dqs[:, 64:128] = dks[...].T * 0.125
+        dvs[:, 0:span] += mm_tn(dmix, e_b)
+    dqs[:, 64:128] = dks[...].T
     dqkvs[:, 128:192] = dvs[...].T.astype(BF16)
     dqkvs[:, 192:256] = jnp.zeros((seq, 64), BF16)
     for i in range(seq // qblk):
@@ -335,8 +341,8 @@
     mixn, dqkvn, norms, nhats, acc_o, acc_d, vec_in, w_all, w_out, params = refs[n : n + 10]
     at = n + 10
     if fast:
-        ff_two, ff_came = refs[at : at + 2]
-        at += 2
+        ff_one, ff_two, ff_came = refs[at : at + 3]
+        at += 3
     keep_pay, send_pay, g_out = refs[at : at + 3]
     n_pay = 4 if fast else 2
     pays = refs[at + 3 : at + 3 + n_pay]
@@ -346,17 +352,21 @@
     g_gain = jnp.zeros((8, D), F32)
     g_shift = jnp.zeros((8, D), F32)
     g_bias = jnp.zeros((8, 256), F32)
-    for p in range(n):
-        rows = slice(p * TOK, (p + 1) * TOK)
-        gs[rows, :] = pieces[p][TOK : 2 * TOK, :]
+    for p in range(0, n, 2):
+        rows = slice(p * TOK, (p + 2) * TOK)
+        gs[rows, :] = joined(pieces[p : p + 2], TOK)
         dqkv = dqkvn[rows, :]
         dnorm = mm_nt(dqkv, w_all[...])
         g_gain += fold(dnorm * nhats[rows, :].astype(F32))
         g_shift += fold(dnorm)
         g_bias += fold(dqkv.astype(F32))
-        target = send_pay if p % 2 else keep_pay
-        target[p // 2, :, 0:512] = (mm_nn(mixn[rows, :], w_out[...]) + acc_o[rows, :].astype(F32)).astype(BF16)
-        target[p // 2, :, 512:1024] = (dnorm * gain + acc_d[rows, :].astype(F32)).astype(BF16)
+        part_o = (mm_nn(mixn[rows, :], w_out[...]) + acc_o[rows, :].astype(F32)).astype(BF16)
+        part_d = (dnorm * gain + acc_d[rows, :].astype(F32)).astype(BF16)
+        for q in range(2):
+            target = send_pay if (p + q) % 2 else keep_pay
+            here = slice(q * TOK, (q + 1) * TOK)
+            target[(p + q) // 2, :, 0:512] = part_o[here, :]
+            target[(p + q) // 2, :, 512:1024] = part_d[here, :]
     vec[...] = vec_in[...]
     for row, value in ((0, g_gain), (1, g_shift), (5, g_bias)):
         vec[row : row + 1, 0 : value.shape[1]] = jnp.sum(value, axis=0, keepdims=True)
@@ -369,11 +379,13 @@
             spare[8 * j : 8 * j + 8, :] = lanes_j if j % 2 else pltpu.roll(lanes_j, 64, 1)
         low = low_lanes((128, 128))
         own, near, two, ff_sum = pays
-        for k, target in ((0, own), (1, near.at[0]), (2, two), (3, near.at[1])):
+        near[:, 512:1024] = ff_one[...]
+        for k, target in ((0, own), (1, near.at[:, 0:256]), (2, two), (3, near.at[:, 256:512])):
             tall = pl.ds(pl.multiple_of((zed ^ k) * 128, 128), 128)
             target[:, 0:128] = grad_w[tall, 0:128].astype(BF16)
             target[:, 128:256] = jnp.where(low, grad_w[tall, 128:256], spare[...]).astype(BF16)
-        ff_sum[...] = (ff_two[...].astype(F32) + ff_came[1].astype(F32)).astype(BF16)
+        ff_sum[0:128, :] = (ff_two[...].astype(F32) + ff_came[...].astype(F32)).astype(BF16)
+        ff_sum[128:192, :] = g_out[...]
     else:
         pays[0][...] = grad_w[...].astype(BF16)
         pays[1][...] = vec[...]
@@ -436,13 +448,18 @@
 
 
 def relay_body(two, came, out):
-    out[...] = (two[...].astype(F32) + came[1].astype(F32)).astype(BF16)
-
-
-def share_body(ff_own, ff_near, ff_far, own, near, far, g_out, *refs):
+    out[...] = (two[...].astype(F32) + came[:, 256:512].astype(F32)).astype(BF16)
+
+
+def out_body(mine, came, out):
+    out[...] = (mine[...].astype(F32) + came[128:192, :].astype(F32)).astype(BF16)
+
+
+def share_body(ff_own, ff_far, own, near, far, out_half, out_far, *refs):
     out = refs[-1]
-    out[:, 0:512] = (ff_own[...].astype(F32) + ff_near[0].astype(F32) + ff_far[...].astype(F32)).astype(BF16)
-    out[:, 512:768] = (own[...].astype(F32) + near[0].astype(F32) + far[...].astype(F32)).astype(BF16)
+    out[:, 0:512] = (ff_own[...].astype(F32) + near[:, 512:1024].astype(F32) + ff_far[0:128, :].astype(F32)).astype(BF16)
+    out[:, 512:768] = (own[...].astype(F32) + near[:, 0:256].astype(F32) + far[...].astype(F32)).astype(BF16)
+    g_out = (out_half[...].astype(F32) + out_far[...].astype(F32)).astype(BF16)
     out[0:64, 768:1024] = g_out[:, 0:256]
     out[64:128, 768:1024] = g_out[:, 256:512]
 
@@ -491,14 +508,12 @@
         e = half_pick(held_v[h, 6:7, lane], odd, False)
         l = half_pick(held_v[h + 1, 6:7, lane], odd, True)
         bup[at : at + 128] = jnp.where(low, e, l).reshape(128)
-    mine = pl.multiple_of((me % 2) * 64, 64)
-    other = pl.multiple_of((1 - me % 2) * 64, 64)
-    for parity, start in ((0, mine), (1, other)):
-        acc = alls[parity][:, 768:1024].astype(F32)
-        for k in range(parity + 2, n, 2):
-            acc = acc + alls[k][:, 768:1024].astype(F32)
-        gout[pl.ds(start, 64), 0:256] = acc[0:64]
-        gout[pl.ds(start, 64), 256:512] = acc[64:128]
+    for k in range(n):
+        held_a[me ^ k] = alls[k][:, 768:1024].astype(F32)
+    for p in range(2):
+        rows = held_a[2 * zed + p]
+        gout[64 * p : 64 * p + 64, 0:256] = rows[0:64]
+        gout[64 * p : 64 * p + 64, 256:512] = rows[64:128]
     flat[12:20, :] = jnp.zeros((8, 128), F32)
     for r in range(3):
         bqkv[r * 128 : (r + 1) * 128] = flat[pl.ds(zed * 3 + r, 1), :].reshape(128)
@@ -633,8 +648,8 @@
     half = (n // 2, TOK, 2 * D)
     rows = D // nz
     if fast:
-        ff_pays = [shape((rows, 512), BF16), shape((2, rows, 512), BF16), shape((rows, 512), BF16)]
-        attn_pays = [shape((rows, 256), BF16), shape((2, rows, 256), BF16), shape((rows, 256), BF16), shape((rows, 512), BF16)]
+        ff_pays = [shape((rows, 512), BF16)] * nz
+        attn_pays = [shape((rows, 256), BF16), shape((rows, 1024), BF16), shape((rows, 256), BF16), shape((rows + HEAD_DIM, 512), BF16)]
     else:
         ff_pays = [shape((D, width), BF16), shape((width, D), BF16)]
         attn_pays = [shape((D, 256), BF16), shape((8, D))]
@@ -658,8 +673,8 @@
     ff_pay = ff_out[5:]
     from_ff = []
     if fast:
-        ff_near = lax.ppermute(ff_pay[1], "fsdp", xor_pairs(nz, 1))
-        from_ff = [ff_pay[2], ff_near]
+        ff_pass = lax.ppermute(ff_pay[3], "fsdp", xor_pairs(nz, 1))
+        from_ff = [ff_pay[1], ff_pay[2], ff_pass]
     mixn, dqkvn = vmem_call(
         functools.partial(attn_body, n),
         [shape((seq, 64), BF16), shape((seq, 256), BF16)],
@@ -731,14 +746,14 @@
     )(place, x, g, params, *parts)
 
     if fast:
-        out_got = lax.ppermute(g_out, ("ctx", "fsdp"), [(b, a) for a, b in pairs])
         ff_far = lax.ppermute(attn_pay[3], "fsdp", xor_pairs(nz, 2))
+        out_half = vmem_call(out_body, shape((HEAD_DIM, D), BF16), n_in=2, cost=LONG, name="out_half")(g_out, ff_far)
+        out_far = lax.ppermute(out_half, "fsdp", xor_pairs(nz, 1))
         attn_near = lax.ppermute(attn_pay[1], "fsdp", xor_pairs(nz, 1))
         attn_two = vmem_call(relay_body, shape((rows, 256), BF16), n_in=2, cost=LONG, name="relay")(attn_pay[2], attn_near)
         attn_far = lax.ppermute(attn_two, "fsdp", xor_pairs(nz, 2))
-        out_got = vmem_call(gate_body, shape(out_got.shape, BF16), n_in=1, cost=LONGER, name="gate")(out_got)
         share = vmem_call(share_body, shape((rows, 1024), BF16), n_in=7 + 2, name="share")(
-            ff_pay[0], ff_near, ff_far, attn_pay[0], attn_near, attn_far, out_got, parts[3], parts[4]
+            ff_pay[0], ff_far, attn_pay[0], attn_near, attn_far, out_half, out_far, parts[3], parts[4]
         )
         alls = gather_ctx(share, n)
         dz = D // nz

time: 83.4 us -> 78.5 us (0.941)
  starting transfers between devices: 32 us -> 28 us
  Pallas kernels: 21.2 us -> 19.2 us
  waiting for transfers between devices: 26.9 us -> 27.9 us
    ppermute x1, waiting for transfers between devices: 0.01 us -> 6.8 us  [per_device(): ff_far = lax.ppermute(attn_pay[3], 'fsdp', xor_pairs(nz, 2))]
    ppermute x1, waiting for transfers between devices: 4.26 us -> 0.01 us  [per_device(): attn_near = lax.ppermute(attn_pay[1], 'fsdp', xor_pairs(nz, 1))]
    ppermute x1, starting transfers between devices: 6.84 us -> 3.38 us  [per_device(): ff_far = lax.ppermute(attn_pay[3], 'fsdp', xor_pairs(nz, 2))]
    ppermute x1, waiting for transfers between devices: 0.01 us -> 3.22 us  [per_device(): attn_far = lax.ppermute(attn_two, 'fsdp', xor_pairs(nz, 2))]
    ppermute x1, waiting for transfers between devices: 2.65 us -> 0.01 us  [per_device(): lax.ppermute(second_a, 'ctx', xor_pairs(n, 4))]
    ppermute x1, starting transfers between devices: 0.59 us -> 2.71 us  [per_device(): lax.ppermute(second_a, 'ctx', xor_pairs(n, 4))]
    ppermute x1, starting transfers between devices: 1.77 us -> 0.44 us  [per_device(): lax.ppermute(second_b, 'ctx', xor_pairs(n, 2))]
    ppermute x1, starting transfers between devices: 0.3 us -> 1.61 us  [per_device(): came_b = lax.ppermute(first_b, 'ctx', xor_pairs(n, 4))]
  transfers between devices with their start and end apart: 28 -> 28, of which waited for: 14 -> 11; matrix products, arithmetic and copies ran while one was open for 0% -> 0% of each run, Pallas kernels for 16% -> 14%
where the time goes in v5:
time: 78.5 us; the launch traced here: 78.3 us
  starting transfers between devices  28 us (36%)
  waiting for transfers between devices  27.9 us (36%)
  Pallas kernels  19.2 us (24%)
  local copies, waits for them, and re-layouts  1.52 us (2%)
  other arithmetic  0.84 us (1%)
  between operations  0.84 us (1%)
    ppermute x6, waiting for transfers between devices, gather_ctx(): got[k] = lax.ppermute(value, 'ctx', xor_pairs(n, k))  12.6 us
    ppermute x6, starting transfers between devices, gather_ctx(): got[k] = lax.ppermute(value, 'ctx', xor_pairs(n, k))  7.04 us
    ppermute x1, waiting for transfers between devices, per_device(): ff_far = lax.ppermute(attn_pay[3], 'fsdp', xor_pairs(nz, 2))  6.8 us
    ppermute x2, starting transfers between devices, relay_fsdp(): one, two = (lax.ppermute(value, 'fsdp', xor_pairs(nz, k)) for k in (1, 2))  5.61 us
    pallas_call x1, Pallas kernels, per_device(): vmem_call(functools.partial(attn_body, n), [shape((seq, 64), BF16), shape...  5.07 us
    ppermute x2, waiting for transfers between devices, relay_fsdp(): one, two = (lax.ppermute(value, 'fsdp', xor_pairs(nz, k)) for k in (1, 2))  4.36 us
    pallas_call x1, Pallas kernels, per_device(): vmem_call(functools.partial(ff_body, n, nz, fast), [whole_seq, whole_seq,...  3.44 us
    ppermute x1, starting transfers between devices, per_device(): ff_far = lax.ppermute(attn_pay[3], 'fsdp', xor_pairs(nz, 2))  3.38 us
  transfers between devices with their start and end apart: 28, of which 11 were waited for; matrix products, arithmetic and copies ran while one was open for 0% of the time, Pallas kernels for 14%

profile of v5, /device:TPU:0, one launch (start us, length us, event | category | flops | bytes accessed | tf_op | source)
XLA Modules:
  0.0 78.3 jit_solution(14275804770574590050)
XLA Ops:
  0.6 0.6 pad_add_fusion.place
  1.2 2.8 %pack.1 = (bf16[128,768]{1,0:T(8,128)(2,1)}, bf16[256,512]{1,0:T(8,128)(2,1)}, bf16[64,512]{1,0:T(8,128)(2,1)}) custom-call(s32[2]{0:T(128)} %pad_add_fusion.place, bf16[128,1536]{1,0:T(8,128)(2,1)} %refs_2_.1, bf16[128,1536]{1,0:T(8,128)(2,1)} %refs_2_.1, bf16[128,1536]{1,0:T(8,128)(2,1)} %refs_2_.1, bf16[128,2048]{1,0:T(8,128)(2,1)} %refs_6_.1, ...), custom_call_target="tpu_custom_call" | custom-call | tf_op jit(solution)/shard_map/pack/pallas_call | solution.py:112
  4.0 4.0 %collective-permute-start.1 = (bf16[128,768]{1,0:T(8,128)(2,1)}, bf16[128,768]{1,0:T(8,128)(2,1)S(1)}, u32[]{:S(2)}, u32[]{:S(2)}) collective-permute-start(bf16[128,768]{1,0:T(8,128)(2,1)} %get-tuple-element.60.refs_0_), channel_id=1, source_target_pairs={{0,2},{1,3},{2,0},{3,1},{4,6},{5,7},{6,4},{7,5},{8,10},{9,11},{10,... | collective-permute-start | bytes 589832 | tf_op jit(solution)/shard_map/ppermute | solution.py:549
  8.0 1.6 %collective-permute-start = (bf16[128,768]{1,0:T(8,128)(2,1)}, bf16[128,768]{1,0:T(8,128)(2,1)S(1)}, u32[]{:S(2)}, u32[]{:S(2)}) collective-permute-start(bf16[128,768]{1,0:T(8,128)(2,1)} %get-tuple-element.60.refs_0_), channel_id=1, source_target_pairs={{0,1},{1,0},{2,3},{3,2},{4,5},{5,4},{6,7},{7,6},{8,9},{9,8},{10,11... | collective-permute-start | bytes 589832 | tf_op jit(solution)/shard_map/ppermute | solution.py:549
  9.6 2.4 %collective-permute-start.8 = (bf16[256,512]{1,0:T(8,128)(2,1)}, bf16[256,512]{1,0:T(8,128)(2,1)S(1)}, u32[]{:S(2)}, u32[]{:S(2)}) collective-permute-start(bf16[256,512]{1,0:T(8,128)(2,1)} %get-tuple-element.62.refs_0_), channel_id=1, source_target_pairs={{0,24},{4,28},{8,16},{12,20},{16,8},{20,12},{24,0},{28,4},{1,25},{... | collective-permute-start | bytes 786440 | tf_op jit(solution)/shard_map/ppermute | solution.py:538
  12.1 0.5 collective-permute-start.6
  12.6 0.5 collective-permute-start.4
  13.1 4.4 %collective-permute-done.1.refs_2_ = bf16[128,768]{1,0:T(8,128)(2,1)S(1)} collective-permute-done((bf16[128,768]{1,0:T(8,128)(2,1)}, bf16[128,768]{1,0:T(8,128)(2,1)S(1)}, u32[]{:S(2)}, u32[]{:S(2)}) %collective-permute-start.1) | collective-permute-done | bytes 196640 | tf_op jit(solution)/shard_map/ppermute | solution.py:549
  17.5 0.7 collective-permute-start.2
  18.3 0.1 add.23
  18.3 0.6 copy-done.7
  18.9 0.2 select_reduce_fusion.order
  19.2 0.8 %copy-done.2 = bf16[64,512]{1,0:T(8,128)(2,1)S(1)} copy-done((bf16[64,512]{1,0:T(8,128)(2,1)S(1)}, bf16[64,512]{1,0:T(8,128)(2,1)}, u32[]{:S(2)}) %copy-start.2) | copy-done | bytes 65560
  20.0 0.8 %collective-permute-start.10 = (bf16[64,512]{1,0:T(8,128)(2,1)S(1)}, bf16[64,512]{1,0:T(8,128)(2,1)S(1)}, u32[]{:S(2)}, u32[]{:S(2)}) collective-permute-start(bf16[64,512]{1,0:T(8,128)(2,1)S(1)} %gate_w.1), channel_id=1, source_target_pairs={{0,0},{1,8},{2,16},{3,24},{4,4},{5,12},{6,20},{7,28},{8,1},{9,9},{... | collective-permute-start | bytes 196616 | tf_op jit(solution)/shard_map/ppermute | solution.py:622
  20.9 3.0 %collective-permute-done.6.refs_4_ = bf16[256,512]{1,0:T(8,128)(2,1)S(1)} collective-permute-done((bf16[256,512]{1,0:T(8,128)(2,1)}, bf16[256,512]{1,0:T(8,128)(2,1)S(1)}, u32[]{:S(2)}, u32[]{:S(2)}) %collective-permute-start.6) | collective-permute-done | bytes 262176 | tf_op jit(solution)/shard_map/ppermute | solution.py:538
  23.8 0.1 collective-permute-done.4.refs_2_
  23.9 0.4 collective-permute-start.7
  24.3 0.1 collective-permute-start.5
  24.4 0.7 unpack.1
  25.2 0.2 collective-permute-done.9.refs_7_
  25.4 0.4 collective-permute-done.7.refs_5_
  25.7 0.4 collective-permute-done.5.refs_3_
  26.1 3.4 %feed_forward.1 = (bf16[1024,512]{1,0:T(8,128)(2,1)S(1)}, bf16[1024,512]{1,0:T(8,128)(2,1)S(1)}, f32[8,512]{1,0:T(8,128)S(1)}, bf16[1024,512]{1,0:T(8,128)(2,1)S...) custom-call(s32[2]{0:T(128)S(1)} %copy-done.3, ...), custom_call_target="tpu_custom_call" | custom-call | flops 4000000000 | tf_op jit(solution)/shard_map/feed_forward/pallas_call | solution.py:656
  29.6 1.4 %collective-permute-start.11 = (bf16[128,512]{1,0:T(8,128)(2,1)S(1)}, bf16[128,512]{1,0:T(8,128)(2,1)S(1)}, u32[]{:S(2)}, u32[]{:S(2)}) collective-permute-start(bf16[128,512]{1,0:T(8,128)(2,1)S(1)} %get-tuple-element.76), channel_id=1, source_target_pairs={{0,1},{1,0},{2,3},{3,2},{4,5},{5,4},{6,7},{7,6},{8,9},{9,8},{10,11... | collective-permute-start | bytes 393224 | tf_op jit(solution)/shard_map/ppermute | solution.py:676
  30.9 5.1 %attention.1 = (bf16[1024,64]{1,0:T(8,128)(2,1)S(1)}, bf16[1024,256]{1,0:T(8,128)(2,1)S(1)}) custom-call(s32[2]{0:T(128)S(1)} %copy-done.3, s32[16]{0:T(128)S(1)} %select_reduce_fusion.order, bf16[256,512]{1,0:T(8,128)(2,1)S(1)} %copy-done.4, bf16[256,512]{1,0:T(8,128)(2,1)S(1)} %collective-permute-done.3.refs_1_, ...), custom_call_target="tpu_custom_call" | custom-call | flops 6000000000 | tf_op jit(solution)/shard_map/attention/pallas_call | solution.py:678
  36.0 2.3 %ends.1 = (bf16[4,128,1024]{2,1,0:T(8,128)(2,1)S(1)}, bf16[4,128,1024]{2,1,0:T(8,128)(2,1)S(1)}, bf16[64,512]{1,0:T(8,128)(2,1)S(1)}, bf16[128,256]{1,0:T(8,128)...) custom-call(s32[2]{0:T(128)S(1)} %copy-done.3, ...), custom_call_target="tpu_custom_call" | custom-call | flops 3000000000 | tf_op jit(solution)/shard_map/ends/pallas_call | solution.py:698
  38.4 0.1 collective-permute-start.12
  38.4 3.4 %collective-permute-start.17 = (bf16[192,512]{1,0:T(8,128)(2,1)S(1)}, bf16[192,512]{1,0:T(8,128)(2,1)S(1)}, u32[]{:S(2)}, u32[]{:S(2)}) collective-permute-start(bf16[192,512]{1,0:T(8,128)(2,1)S(1)} %get-tuple-element.89), channel_id=1, source_target_pairs={{0,2},{1,3},{2,0},{3,1},{4,6},{5,7},{6,4},{7,5},{8,10},{9,11},{10,... | collective-permute-start | bytes 589832 | tf_op jit(solution)/shard_map/ppermute | solution.py:749
  41.8 0.5 collective-permute-start.18
  42.3 0.3 chip_sum.1
  42.6 0.6 collective-permute-start.13
  43.2 1.6 %collective-permute-start.14 = (bf16[2,128,512]{2,1,0:T(8,128)(2,1)S(1)}, bf16[2,128,512]{2,1,0:T(8,128)(2,1)S(1)}, u32[]{:S(2)}, u32[]{:S(2)}) collective-permute-start(bf16[2,128,512]{2,1,0:T(8,128)(2,1)S(1)} %get-tuple-element.81), channel_id=1, source_target_pairs={{0,16},{4,20},{8,24},{12,28},{16,0},{20,4},{24,8},{28,12},{1,17},{... | collective-permute-start | bytes 786440 | tf_op jit(solution)/shard_map/ppermute | solution.py:726
  44.8 6.8 %collective-permute-done.17.came.ff_far = bf16[192,512]{1,0:T(8,128)(2,1)S(1)} collective-permute-done((bf16[192,512]{1,0:T(8,128)(2,1)S(1)}, bf16[192,512]{1,0:T(8,128)(2,1)S(1)}, u32[]{:S(2)}, u32[]{:S(2)}) %collective-permute-start.17) | collective-permute-done | bytes 196640 | tf_op jit(solution)/shard_map/ppermute | solution.py:749
  51.6 0.1 collective-permute-start.20
  51.8 2.7 %collective-permute-start.15 = (bf16[128,512]{1,0:T(8,128)(2,1)S(1)}, bf16[128,512]{1,0:T(8,128)(2,1)S(1)}, u32[]{:S(2)}, u32[]{:S(2)}) collective-permute-start(bf16[128,512]{1,0:T(8,128)(2,1)S(1)} %get-tuple-element.84), channel_id=1, source_target_pairs={{0,16},{4,20},{8,24},{12,28},{16,0},{20,4},{24,8},{28,12},{1,17},{... | collective-permute-start | bytes 393224 | tf_op jit(solution)/shard_map/ppermute | solution.py:736
  54.5 0.4 collective-permute-start.16
  54.9 2.2 %collective-permute-start.19 = (bf16[128,256]{1,0:T(8,128)(2,1)S(1)}, bf16[128,256]{1,0:T(8,128)(2,1)S(1)}, u32[]{:S(2)}, u32[]{:S(2)}) collective-permute-start(bf16[128,256]{1,0:T(8,128)(2,1)S(1)} %relay.1), channel_id=1, source_target_pairs={{0,2},{1,3},{2,0},{3,1},{4,6},{5,7},{6,4},{7,5},{8,10},{9,11},{10,... | collective-permute-start | bytes 196616 | tf_op jit(solution)/shard_map/ppermute | solution.py:754
  57.1 3.2 %collective-permute-done.19.far = bf16[128,256]{1,0:T(8,128)(2,1)S(1)} collective-permute-done((bf16[128,256]{1,0:T(8,128)(2,1)S(1)}, bf16[128,256]{1,0:T(8,128)(2,1)S(1)}, u32[]{:S(2)}, u32[]{:S(2)}) %collective-permute-start.19) | collective-permute-done | bytes 65568 | tf_op jit(solution)/shard_map/ppermute | solution.py:754
  60.4 0.1 share.1.refs_0_
  60.5 1.6 %collective-permute-start.26 = (bf16[128,1024]{1,0:T(8,128)(2,1)S(1)}, bf16[128,1024]{1,0:T(8,128)(2,1)S(1)}, u32[]{:S(2)}, u32[]{:S(2)}) collective-permute-start(bf16[128,1024]{1,0:T(8,128)(2,1)S(1)} %share.1.refs_0_), channel_id=1, source_target_pairs={{0,24},{4,28},{8,16},{12,20},{16,8},{20,12},{24,0},{28,4},{1,25},{... | collective-permute-start | bytes 786440 | tf_op jit(solution)/shard_map/ppermute | solution.py:538
  62.1 1.7 %collective-permute-start.24 = (bf16[128,1024]{1,0:T(8,128)(2,1)S(1)}, bf16[128,1024]{1,0:T(8,128)(2,1)S(1)}, u32[]{:S(2)}, u32[]{:S(2)}) collective-permute-start(bf16[128,1024]{1,0:T(8,128)(2,1)S(1)} %share.1.refs_0_), channel_id=1, source_target_pairs={{0,16},{4,20},{8,24},{12,28},{16,0},{20,4},{24,8},{28,12},{1,17},{... | collective-permute-start | bytes 786440 | tf_op jit(solution)/shard_map/ppermute | solution.py:538
  63.7 0.3 collective-permute-start.22
  64.0 6.6 %collective-permute-done.26.refs_6_ = bf16[128,1024]{1,0:T(8,128)(2,1)S(1)} collective-permute-done((bf16[128,1024]{1,0:T(8,128)(2,1)S(1)}, bf16[128,1024]{1,0:T(8,128)(2,1)S(1)}, u32[]{:S(2)}, u32[]{:S(2)}) %collective-permute-start.26) | collective-permute-done | bytes 262176 | tf_op jit(solution)/shard_map/ppermute | solution.py:538
  70.6 2.8 %collective-permute-done.24.refs_4_ = bf16[128,1024]{1,0:T(8,128)(2,1)S(1)} collective-permute-done((bf16[128,1024]{1,0:T(8,128)(2,1)S(1)}, bf16[128,1024]{1,0:T(8,128)(2,1)S(1)}, u32[]{:S(2)}, u32[]{:S(2)}) %collective-permute-start.24) | collective-permute-done | bytes 262176 | tf_op jit(solution)/shard_map/ppermute | solution.py:538
  73.3 0.2 collective-permute-done.22.refs_2_
  73.6 0.3 collective-permute-start.23
  73.9 1.6 %close.1 = (bf16[128,512]{1,0:T(8,128)(2,1)}, f32[128,512]{1,0:T(8,128)}) custom-call(s32[2]{0:T(128)S(1)} %copy-done.3, bf16[128,512]{1,0:T(8,128)(2,1)S(1)} %bitcast.6, bf16[128,512]{1,0:T(8,128)(2,1)S(1)} %bitcast.7, f32[8,512]{1,0:T(8,128)S(1)} %get-tuple-element.61.refs_10_.refs_9_.refs_17_.params, bf16[128,1024]{1,0:T(8,128)(2,1)S(1)} %get-tuple-element.79.refs_0_, ...), custom_call_target="tpu_custom_call" | custom-call | tf_op jit(solution)/shard_map/close/pallas_call | solution.py:740
  75.5 2.9 %finish.1 = (f32[128]{0:T(128)}, f32[128]{0:T(128)}, f32[128,1536]{1,0:T(8,128)}, f32[384]{0:T(512)}, f32[128,512]{1,0:T(8,128)}, /*index=5*/f32[128]{0:T(128)},...) custom-call(s32[2]{0:T(128)S(1)} %copy-done.3, ...), custom_call_target="tpu_custom_call" | custom-call | tf_op jit(solution)/shard_map/finish/pallas_call | solution.py:760
  (42 shorter events, 0.4 us)
Async XLA Ops:
  4.0 13.5 %collective-permute-start.1 = (bf16[128,768]{1,0:T(8,128)(2,1)}, bf16[128,768]{1,0:T(8,128)(2,1)S(1)}, u32[]{:S(2)}, u32[]{:S(2)}) collective-permute-start(bf16[128,768]{1,0:T(8,128)(2,1)} %get-tuple-element.60.refs_0_), channel_id=1, source_target_pairs={{0,2},{1,3},{2,0},{3,1},{4,6},{5,7},{6,4},{7,5},{8,10},{9,11},{10,... | collective-permute-start | bytes 589832 | tf_op jit(solution)/shard_map/ppermute | solution.py:549
  8.0 11.1 %collective-permute-start = (bf16[128,768]{1,0:T(8,128)(2,1)}, bf16[128,768]{1,0:T(8,128)(2,1)S(1)}, u32[]{:S(2)}, u32[]{:S(2)}) collective-permute-start(bf16[128,768]{1,0:T(8,128)(2,1)} %get-tuple-element.60.refs_0_), channel_id=1, source_target_pairs={{0,1},{1,0},{2,3},{3,2},{4,5},{5,4},{6,7},{7,6},{8,9},{9,8},{10,11... | collective-permute-start | bytes 589832 | tf_op jit(solution)/shard_map/ppermute | solution.py:549
  9.6 10.4 %collective-permute-start.8 = (bf16[256,512]{1,0:T(8,128)(2,1)}, bf16[256,512]{1,0:T(8,128)(2,1)S(1)}, u32[]{:S(2)}, u32[]{:S(2)}) collective-permute-start(bf16[256,512]{1,0:T(8,128)(2,1)} %get-tuple-element.62.refs_0_), channel_id=1, source_target_pairs={{0,24},{4,28},{8,16},{12,20},{16,8},{20,12},{24,0},{28,4},{1,25},{... | collective-permute-start | bytes 786440 | tf_op jit(solution)/shard_map/ppermute | solution.py:538
  12.1 11.8 %collective-permute-start.6 = (bf16[256,512]{1,0:T(8,128)(2,1)}, bf16[256,512]{1,0:T(8,128)(2,1)S(1)}, u32[]{:S(2)}, u32[]{:S(2)}) collective-permute-start(bf16[256,512]{1,0:T(8,128)(2,1)} %get-tuple-element.62.refs_0_), channel_id=1, source_target_pairs={{0,16},{4,20},{8,24},{12,28},{16,0},{20,4},{24,8},{28,12},{1,17},{... | collective-permute-start | bytes 786440 | tf_op jit(solution)/shard_map/ppermute | solution.py:538
  12.6 11.4 %collective-permute-start.4 = (bf16[256,512]{1,0:T(8,128)(2,1)}, bf16[256,512]{1,0:T(8,128)(2,1)S(1)}, u32[]{:S(2)}, u32[]{:S(2)}) collective-permute-start(bf16[256,512]{1,0:T(8,128)(2,1)} %get-tuple-element.62.refs_0_), channel_id=1, source_target_pairs={{0,8},{4,12},{8,0},{12,4},{16,24},{20,28},{24,16},{28,20},{1,9},{5... | collective-permute-start | bytes 786440 | tf_op jit(solution)/shard_map/ppermute | solution.py:538
  17.5 6.9 %collective-permute-start.2 = (bf16[128,768]{1,0:T(8,128)(2,1)S(1)}, bf16[128,768]{1,0:T(8,128)(2,1)S(1)}, u32[]{:S(2)}, u32[]{:S(2)}) collective-permute-start(bf16[128,768]{1,0:T(8,128)(2,1)S(1)} %collective-permute-done.1.refs_2_), channel_id=1, source_target_pairs={{0,1},{1,0},{2,3},{3,2},{4,5},{5,4},{6,7},{7,6},{8,9},{9,8},{10,11... | collective-permute-start | bytes 589832 | tf_op jit(solution)/shard_map/ppermute | solution.py:550
  18.3 0.7 copy-start.7
  19.1 6.1 %collective-permute-start.3 = (bf16[256,512]{1,0:T(8,128)(2,1)}, bf16[256,512]{1,0:T(8,128)(2,1)S(1)}, u32[]{:S(2)}, u32[]{:S(2)}) collective-permute-start(bf16[256,512]{1,0:T(8,128)(2,1)} %get-tuple-element.62.refs_0_), channel_id=1, source_target_pairs={{0,4},{4,0},{8,12},{12,8},{16,20},{20,16},{24,28},{28,24},{1,5},{5... | collective-permute-start | bytes 786440 | tf_op jit(solution)/shard_map/ppermute | solution.py:540
  19.2 0.8 %copy-start.2 = (bf16[64,512]{1,0:T(8,128)(2,1)S(1)}, bf16[64,512]{1,0:T(8,128)(2,1)}, u32[]{:S(2)}) copy-start(bf16[64,512]{1,0:T(8,128)(2,1)} %get-tuple-element.64.value) | copy-start | bytes 196612
  20.0 4.4 %copy-start.3 = (s32[2]{0:T(128)S(1)}, s32[2]{0:T(128)}, u32[]{:S(2)}) copy-start(s32[2]{0:T(128)} %pad_add_fusion.place) | copy-start | bytes 28
  20.0 4.4 %copy-start.5 = (bf16[128,768]{1,0:T(8,128)(2,1)S(1)}, bf16[128,768]{1,0:T(8,128)(2,1)}, u32[]{:S(2)}) copy-start(bf16[128,768]{1,0:T(8,128)(2,1)} %get-tuple-element.60.refs_0_) | copy-start | bytes 589828
  20.0 6.1 %copy-start.4 = (bf16[256,512]{1,0:T(8,128)(2,1)S(1)}, bf16[256,512]{1,0:T(8,128)(2,1)}, u32[]{:S(2)}) copy-start(bf16[256,512]{1,0:T(8,128)(2,1)} %get-tuple-element.62.refs_0_) | copy-start | bytes 786436
  20.0 10.9 %collective-permute-start.10 = (bf16[64,512]{1,0:T(8,128)(2,1)S(1)}, bf16[64,512]{1,0:T(8,128)(2,1)S(1)}, u32[]{:S(2)}, u32[]{:S(2)}) collective-permute-start(bf16[64,512]{1,0:T(8,128)(2,1)S(1)} %gate_w.1), channel_id=1, source_target_pairs={{0,0},{1,8},{2,16},{3,24},{4,4},{5,12},{6,20},{7,28},{8,1},{9,9},{... | collective-permute-start | bytes 196616 | tf_op jit(solution)/shard_map/ppermute | solution.py:622
  23.8 1.5 %collective-permute-start.9 = (bf16[256,512]{1,0:T(8,128)(2,1)S(1)}, bf16[256,512]{1,0:T(8,128)(2,1)S(1)}, u32[]{:S(2)}, u32[]{:S(2)}) collective-permute-start(bf16[256,512]{1,0:T(8,128)(2,1)S(1)} %collective-permute-done.8.refs_6_), channel_id=1, source_target_pairs={{0,4},{4,0},{8,12},{12,8},{16,20},{20,16},{24,28},{28,24},{1,5},{5... | collective-permute-start | bytes 786440 | tf_op jit(solution)/shard_map/ppermute | solution.py:540
  23.9 1.8 %collective-permute-start.7 = (bf16[256,512]{1,0:T(8,128)(2,1)S(1)}, bf16[256,512]{1,0:T(8,128)(2,1)S(1)}, u32[]{:S(2)}, u32[]{:S(2)}) collective-permute-start(bf16[256,512]{1,0:T(8,128)(2,1)S(1)} %collective-permute-done.6.refs_4_), channel_id=1, source_target_pairs={{0,4},{4,0},{8,12},{12,8},{16,20},{20,16},{24,28},{28,24},{1,5},{5... | collective-permute-start | bytes 786440 | tf_op jit(solution)/shard_map/ppermute | solution.py:540
  24.3 1.8 %collective-permute-start.5 = (bf16[256,512]{1,0:T(8,128)(2,1)S(1)}, bf16[256,512]{1,0:T(8,128)(2,1)S(1)}, u32[]{:S(2)}, u32[]{:S(2)}) collective-permute-start(bf16[256,512]{1,0:T(8,128)(2,1)S(1)} %collective-permute-done.4.refs_2_), channel_id=1, source_target_pairs={{0,4},{4,0},{8,12},{12,8},{16,20},{20,16},{24,28},{28,24},{1,5},{5... | collective-permute-start | bytes 786440 | tf_op jit(solution)/shard_map/ppermute | solution.py:540
  26.1 4.8 %copy-start.6 = (f32[1024,128]{1,0:T(8,128)S(1)}, f32[1024,128]{1,0:T(8,128)}, u32[]{:S(2)}) copy-start(f32[1024,128]{1,0:T(8,128)} %constant.15.clone.refs_11_) | copy-start | bytes 1572868
  29.6 6.5 %collective-permute-start.11 = (bf16[128,512]{1,0:T(8,128)(2,1)S(1)}, bf16[128,512]{1,0:T(8,128)(2,1)S(1)}, u32[]{:S(2)}, u32[]{:S(2)}) collective-permute-start(bf16[128,512]{1,0:T(8,128)(2,1)S(1)} %get-tuple-element.76), channel_id=1, source_target_pairs={{0,1},{1,0},{2,3},{3,2},{4,5},{5,4},{6,7},{7,6},{8,9},{9,8},{10,11... | collective-permute-start | bytes 393224 | tf_op jit(solution)/shard_map/ppermute | solution.py:676
  38.4 4.0 %collective-permute-start.12 = (bf16[4,128,1024]{2,1,0:T(8,128)(2,1)S(1)}, bf16[4,128,1024]{2,1,0:T(8,128)(2,1)S(1)}, u32[]{:S(2)}, u32[]{:S(2)}) collective-permute-start(bf16[4,128,1024]{2,1,0:T(8,128)(2,1)S(1)} %get-tuple-element.78), channel_id=1, source_target_pairs={{0,4},{4,0},{8,12},{12,8},{16,20},{20,16},{24,28},{28,24},{1,5},{5... | collective-permute-start | bytes 3145736 | tf_op jit(solution)/shard_map/ppermute | solution.py:715
  38.4 13.1 %collective-permute-start.17 = (bf16[192,512]{1,0:T(8,128)(2,1)S(1)}, bf16[192,512]{1,0:T(8,128)(2,1)S(1)}, u32[]{:S(2)}, u32[]{:S(2)}) collective-permute-start(bf16[192,512]{1,0:T(8,128)(2,1)S(1)} %get-tuple-element.89), channel_id=1, source_target_pairs={{0,2},{1,3},{2,0},{3,1},{4,6},{5,7},{6,4},{7,5},{8,10},{9,11},{10,... | collective-permute-start | bytes 589832 | tf_op jit(solution)/shard_map/ppermute | solution.py:749
  41.8 13.1 %collective-permute-start.18 = (bf16[128,1024]{1,0:T(8,128)(2,1)S(1)}, bf16[128,1024]{1,0:T(8,128)(2,1)S(1)}, u32[]{:S(2)}, u32[]{:S(2)}) collective-permute-start(bf16[128,1024]{1,0:T(8,128)(2,1)S(1)} %get-tuple-element.91), channel_id=1, source_target_pairs={{0,1},{1,0},{2,3},{3,2},{4,5},{5,4},{6,7},{7,6},{8,9},{9,8},{10,11... | collective-permute-start | bytes 786440 | tf_op jit(solution)/shard_map/ppermute | solution.py:752
  42.6 9.1 %collective-permute-start.13 = (bf16[2,128,512]{2,1,0:T(8,128)(2,1)S(1)}, bf16[2,128,512]{2,1,0:T(8,128)(2,1)S(1)}, u32[]{:S(2)}, u32[]{:S(2)}) collective-permute-start(bf16[2,128,512]{2,1,0:T(8,128)(2,1)S(1)} %get-tuple-element.80), channel_id=1, source_target_pairs={{0,8},{4,12},{8,0},{12,4},{16,24},{20,28},{24,16},{28,20},{1,9},{5... | collective-permute-start | bytes 786440 | tf_op jit(solution)/shard_map/ppermute | solution.py:725
  43.2 8.5 %collective-permute-start.14 = (bf16[2,128,512]{2,1,0:T(8,128)(2,1)S(1)}, bf16[2,128,512]{2,1,0:T(8,128)(2,1)S(1)}, u32[]{:S(2)}, u32[]{:S(2)}) collective-permute-start(bf16[2,128,512]{2,1,0:T(8,128)(2,1)S(1)} %get-tuple-element.81), channel_id=1, source_target_pairs={{0,16},{4,20},{8,24},{12,28},{16,0},{20,4},{24,8},{28,12},{1,17},{... | collective-permute-start | bytes 786440 | tf_op jit(solution)/shard_map/ppermute | solution.py:726
  51.6 5.5 %collective-permute-start.20 = (bf16[64,512]{1,0:T(8,128)(2,1)S(1)}, bf16[64,512]{1,0:T(8,128)(2,1)S(1)}, u32[]{:S(2)}, u32[]{:S(2)}) collective-permute-start(bf16[64,512]{1,0:T(8,128)(2,1)S(1)} %out_half.1), channel_id=1, source_target_pairs={{0,1},{1,0},{2,3},{3,2},{4,5},{5,4},{6,7},{7,6},{8,9},{9,8},{10,11... | collective-permute-start | bytes 196616 | tf_op jit(solution)/shard_map/ppermute | solution.py:751
  51.8 8.6 %collective-permute-start.15 = (bf16[128,512]{1,0:T(8,128)(2,1)S(1)}, bf16[128,512]{1,0:T(8,128)(2,1)S(1)}, u32[]{:S(2)}, u32[]{:S(2)}) collective-permute-start(bf16[128,512]{1,0:T(8,128)(2,1)S(1)} %get-tuple-element.84), channel_id=1, source_target_pairs={{0,16},{4,20},{8,24},{12,28},{16,0},{20,4},{24,8},{28,12},{1,17},{... | collective-permute-start | bytes 393224 | tf_op jit(solution)/shard_map/ppermute | solution.py:736
  54.5 5.9 %collective-permute-start.16 = (bf16[128,512]{1,0:T(8,128)(2,1)S(1)}, bf16[128,512]{1,0:T(8,128)(2,1)S(1)}, u32[]{:S(2)}, u32[]{:S(2)}) collective-permute-start(bf16[128,512]{1,0:T(8,128)(2,1)S(1)} %get-tuple-element.85), channel_id=1, source_target_pairs={{0,8},{4,12},{8,0},{12,4},{16,24},{20,28},{24,16},{28,20},{1,9},{5... | collective-permute-start | bytes 393224 | tf_op jit(solution)/shard_map/ppermute | solution.py:736
  54.9 5.4 %collective-permute-start.19 = (bf16[128,256]{1,0:T(8,128)(2,1)S(1)}, bf16[128,256]{1,0:T(8,128)(2,1)S(1)}, u32[]{:S(2)}, u32[]{:S(2)}) collective-permute-start(bf16[128,256]{1,0:T(8,128)(2,1)S(1)} %relay.1), channel_id=1, source_target_pairs={{0,2},{1,3},{2,0},{3,1},{4,6},{5,7},{6,4},{7,5},{8,10},{9,11},{10,... | collective-permute-start | bytes 196616 | tf_op jit(solution)/shard_map/ppermute | solution.py:754
  60.3 13.5 %copy-start = (bf16[1,128,512]{2,1,0:T(8,128)(2,1)S(1)}, bf16[1,128,512]{2,1,0:T(8,128)(2,1)}, u32[]{:S(2)}) copy-start(bf16[1,128,512]{2,1,0:T(8,128)(2,1)} %refs_9_.1) | copy-start | bytes 393220
  60.4 13.5 %copy-start.1 = (bf16[1,128,512]{2,1,0:T(8,128)(2,1)S(1)}, bf16[1,128,512]{2,1,0:T(8,128)(2,1)}, u32[]{:S(2)}) copy-start(bf16[1,128,512]{2,1,0:T(8,128)(2,1)} %refs_10_.1) | copy-start | bytes 393220
  60.5 10.1 %collective-permute-start.26 = (bf16[128,1024]{1,0:T(8,128)(2,1)S(1)}, bf16[128,1024]{1,0:T(8,128)(2,1)S(1)}, u32[]{:S(2)}, u32[]{:S(2)}) collective-permute-start(bf16[128,1024]{1,0:T(8,128)(2,1)S(1)} %share.1.refs_0_), channel_id=1, source_target_pairs={{0,24},{4,28},{8,16},{12,20},{16,8},{20,12},{24,0},{28,4},{1,25},{... | collective-permute-start | bytes 786440 | tf_op jit(solution)/shard_map/ppermute | solution.py:538
  62.1 11.3 %collective-permute-start.24 = (bf16[128,1024]{1,0:T(8,128)(2,1)S(1)}, bf16[128,1024]{1,0:T(8,128)(2,1)S(1)}, u32[]{:S(2)}, u32[]{:S(2)}) collective-permute-start(bf16[128,1024]{1,0:T(8,128)(2,1)S(1)} %share.1.refs_0_), channel_id=1, source_target_pairs={{0,16},{4,20},{8,24},{12,28},{16,0},{20,4},{24,8},{28,12},{1,17},{... | collective-permute-start | bytes 786440 | tf_op jit(solution)/shard_map/ppermute | solution.py:538
  63.7 9.8 %collective-permute-start.22 = (bf16[128,1024]{1,0:T(8,128)(2,1)S(1)}, bf16[128,1024]{1,0:T(8,128)(2,1)S(1)}, u32[]{:S(2)}, u32[]{:S(2)}) collective-permute-start(bf16[128,1024]{1,0:T(8,128)(2,1)S(1)} %share.1.refs_0_), channel_id=1, source_target_pairs={{0,8},{4,12},{8,0},{12,4},{16,24},{20,28},{24,16},{28,20},{1,9},{5... | collective-permute-start | bytes 786440 | tf_op jit(solution)/shard_map/ppermute | solution.py:538
  64.0 11.4 %collective-permute-start.21 = (bf16[128,1024]{1,0:T(8,128)(2,1)S(1)}, bf16[128,1024]{1,0:T(8,128)(2,1)S(1)}, u32[]{:S(2)}, u32[]{:S(2)}) collective-permute-start(bf16[128,1024]{1,0:T(8,128)(2,1)S(1)} %share.1.refs_0_), channel_id=1, source_target_pairs={{0,4},{4,0},{8,12},{12,8},{16,20},{20,16},{24,28},{28,24},{1,5},{5... | collective-permute-start | bytes 786440 | tf_op jit(solution)/shard_map/ppermute | solution.py:540
  70.6 4.9 %collective-permute-start.27 = (bf16[128,1024]{1,0:T(8,128)(2,1)S(1)}, bf16[128,1024]{1,0:T(8,128)(2,1)S(1)}, u32[]{:S(2)}, u32[]{:S(2)}) collective-permute-start(bf16[128,1024]{1,0:T(8,128)(2,1)S(1)} %collective-permute-done.26.refs_6_), channel_id=1, source_target_pairs={{0,4},{4,0},{8,12},{12,8},{16,20},{20,16},{24,28},{28,24},{1,5},{5... | collective-permute-start | bytes 786440 | tf_op jit(solution)/shard_map/ppermute | solution.py:540
  73.3 2.1 %collective-permute-start.25 = (bf16[128,1024]{1,0:T(8,128)(2,1)S(1)}, bf16[128,1024]{1,0:T(8,128)(2,1)S(1)}, u32[]{:S(2)}, u32[]{:S(2)}) collective-permute-start(bf16[128,1024]{1,0:T(8,128)(2,1)S(1)} %collective-permute-done.24.refs_4_), channel_id=1, source_target_pairs={{0,4},{4,0},{8,12},{12,8},{16,20},{20,16},{24,28},{28,24},{1,5},{5... | collective-permute-start | bytes 786440 | tf_op jit(solution)/shard_map/ppermute | solution.py:540
  73.6 1.9 %collective-permute-start.23 = (bf16[128,1024]{1,0:T(8,128)(2,1)S(1)}, bf16[128,1024]{1,0:T(8,128)(2,1)S(1)}, u32[]{:S(2)}, u32[]{:S(2)}) collective-permute-start(bf16[128,1024]{1,0:T(8,128)(2,1)S(1)} %collective-permute-done.22.refs_2_), channel_id=1, source_target_pairs={{0,4},{4,0},{8,12},{12,8},{16,20},{20,16},{24,28},{28,24},{1,5},{5... | collective-permute-start | bytes 786440 | tf_op jit(solution)/shard_map/ppermute | solution.py:540

commit v6 on v5

--- a/solution.py
+++ b/solution.py
@@ -64,72 +64,68 @@
     return lax.broadcasted_iota(jnp.int32, shape, len(shape) - 1) % 128 < 64
 
 
-def pack_body(nz, place, *refs):
-    q_ref, k_ref, v_ref = refs[:3]
-    ups = refs[3 : 3 + nz]
-    w_down, w_out, x, g = refs[3 + nz : 7 + nz]
-    vectors = refs[7 + nz : 15 + nz]
-    pay, piece, head_w, small = refs[15 + nz :]
-    odd = (place[0] % 2) == 1
-    rows = q_ref.shape[0]
+def pack_body(nz, w_qkv, w_up, w_down, w_out, x, g, *refs):
+    vectors, (pay, piece, head_w) = refs[:8], refs[8:11]
+    qkv, ups, small, sems = refs[11:15]
+    lists = refs[15:]
+    me = lax.axis_index("ctx").astype(jnp.int32)
+    odd = (me % 2) == 1
+    rows = w_qkv.shape[0]
+    span = FF // nz
+
+    def lanes(start):
+        return pl.ds(pl.multiple_of(start + (me // 2) * 128, 128), 128)
+
+    down = pl.ds(pl.multiple_of(me * 64, 64), 64)
+    pairs = [(w_qkv.at[:, lanes(i * D)], qkv.at[i]) for i in range(3)]
+    pairs += [(w_up.at[:, lanes(z * span)], ups.at[z]) for z in range(nz)]
+    pairs += [(w_down.at[down, 0:256], pay.at[0:64, 512:768]), (w_down.at[down, 256:512], pay.at[64:128, 512:768])]
+    pairs += [(x.at[0], piece.at[0:TOK, :]), (g.at[0], piece.at[TOK : 2 * TOK, :])]
+    pairs += [(w_out.at[pl.ds(pl.multiple_of((me % 2) * 64, 64), 64), :], head_w)]
+    pairs += list(zip(vectors, lists))
+    copies = [pltpu.make_async_copy(source, target, sems.at[at]) for at, (source, target) in enumerate(pairs)]
+    for copy in copies:
+        copy.start()
+    for copy in copies:
+        copy.wait()
     low = low_lanes((rows, 128))
     small[...] = jnp.zeros_like(small)
     at = 0
-    for vector in vectors:
+    for vector in lists:
         for r in range(vector.shape[0] // 128):
             small[at : at + 1, :] = vector[r * 128 : (r + 1) * 128].astype(F32).reshape(1, 128)
             at += 1
     few = small[...]
     spare = jnp.concatenate([pltpu.roll(few, 64, 1), few, jnp.zeros((rows - 32, 128), F32)], axis=0)
-    q = half_pick(q_ref[...].astype(F32), odd, False)
-    k = half_pick(k_ref[...].astype(F32), odd, True)
-    v = half_pick(v_ref[...].astype(F32), odd, False)
+    q = half_pick(qkv[0].astype(F32), odd, False)
+    k = half_pick(qkv[1].astype(F32), odd, True)
+    v = half_pick(qkv[2].astype(F32), odd, False)
     pay[:, 0:128] = jnp.where(low, q, k).astype(BF16)
     pay[:, 128:256] = jnp.where(low, v, spare).astype(BF16)
     for z in range(0, nz, 2):
-        even = half_pick(ups[z][...].astype(F32), odd, False)
-        later = half_pick(ups[z + 1][...].astype(F32), odd, True)
+        even = half_pick(ups[z].astype(F32), odd, False)
+        later = half_pick(ups[z + 1].astype(F32), odd, True)
         pay[:, 256 + z * 64 : 256 + z * 64 + 128] = jnp.where(low, even, later).astype(BF16)
-    pay[0:64, 512:768] = w_down[:, 0:256]
-    pay[64:128, 512:768] = w_down[:, 256:512]
-    head_w[...] = w_out[...]
-    piece[0:TOK, :] = x[0]
-    piece[TOK : 2 * TOK, :] = g[0]
-
-
-def pack_call(nz, place, w_qkv, w_up, w_down, w_out, x, g, vectors):
-    span = FF // nz // 128
+
+
+def pack_call(nz, w_qkv, w_up, w_down, w_out, x, g, vectors):
     rows = D // nz
-
-    def lane_block(first):
-        return pl.BlockSpec((rows, 128), lambda i, s: (0, first + s[0] // 2))
-
-    def whole(array):
-        rank = array.ndim
-        return pl.BlockSpec(array.shape, lambda i, s: (0,) * rank)
-
-    outs = [shape((rows, 768), BF16), shape((2 * TOK, D), BF16), shape((HEAD_DIM, D), BF16)]
+    here = pl.BlockSpec(memory_space=pl.ANY)
     return pl.pallas_call(
         functools.partial(pack_body, nz),
-        out_shape=outs,
-        grid_spec=pltpu.PrefetchScalarGridSpec(
-            num_scalar_prefetch=1,
-            grid=(1,),
-            in_specs=[lane_block(0), lane_block(D // 128), lane_block(2 * D // 128)]
-            + [lane_block(z * span) for z in range(nz)]
-            + [
-                pl.BlockSpec((64, D), lambda i, s: (s[0], 0)),
-                pl.BlockSpec((HEAD_DIM, D), lambda i, s: (s[0] % 2, 0)),
-                whole(x),
-                whole(g),
-            ]
-            + [whole(v) for v in vectors],
-            out_specs=[whole(o) for o in outs],
-            scratch_shapes=[pltpu.VMEM((16, 128), F32)],
-        ),
+        out_shape=[shape((rows, 768), BF16), shape((2 * TOK, D), BF16), shape((HEAD_DIM, D), BF16)],
+        in_specs=[here] * (6 + len(vectors)),
+        out_specs=[pl.BlockSpec(memory_space=pltpu.VMEM)] * 3,
+        scratch_shapes=[
+            pltpu.VMEM((3, rows, 128), BF16),
+            pltpu.VMEM((nz, rows, 128), BF16),
+            pltpu.VMEM((16, 128), F32),
+            pltpu.SemaphoreType.DMA((8 + nz + len(vectors),)),
+        ]
+        + [pltpu.VMEM(v.shape, BF16) for v in vectors],
         compiler_params=pltpu.CompilerParams(vmem_limit_bytes=WIDE_LIMIT),
         name="pack",
-    )(place, w_qkv, w_qkv, w_qkv, *([w_up] * nz), w_down, w_out, x, g, *vectors)
+    )(w_qkv, w_up, w_down, w_out, x, g, *vectors)
 
 
 def unpack_body(nz, place, *refs):
@@ -392,7 +388,11 @@
 
 
 def close_body(fast, place, x_ref, g_ref, params, *refs):
-    parts, out, grad = refs[:-2], refs[-2], refs[-1]
+    if fast:
+        parts, (value, out, grad, copy) = refs[:5], refs[5:]
+        copy[...] = value[...]
+    else:
+        parts, out, grad = refs[:-2], refs[-2], refs[-1]
     x = x_ref[...].astype(F32)
     nhat, inv = normalized(x)
     if fast:
@@ -532,12 +532,13 @@
     return [(i, i ^ k) for i in range(size)]
 
 
-def gather_ctx(value, n):
+def gather_ctx(value, n, beside=None):
     got = {0: value}
     for k in range(2, n, 2):
         got[k] = lax.ppermute(value, "ctx", xor_pairs(n, k))
     for k in range(0, n, 2):
-        got[k + 1] = lax.ppermute(got[k], "ctx", xor_pairs(n, 1))
+        source = beside if k == 0 and beside is not None else got[k]
+        got[k + 1] = lax.ppermute(source, "ctx", xor_pairs(n, 1))
     return [got[k] for k in range(n)]
 
 
@@ -602,7 +603,7 @@
 
     if fast:
         vectors = (ln1_gain, ln1_bias, ln2_gain, ln2_bias, b_attn_out, b_down, b_qkv, b_up)
-        pack, piece, pack_w = pack_call(nz, place, w_qkv, w_up, w_down, w_attn_out, inputs, cotangent, vectors)
+        pack, piece, pack_w = pack_call(nz, w_qkv, w_up, w_down, w_attn_out, inputs, cotangent, vectors)
         pieces = gather_ctx(piece, n)
         far = relay_fsdp(pack, nz)
         given = vmem_call(
@@ -737,14 +738,6 @@
     else:
         chip_sum = vmem_call(chip_body, [shape((TOK, 2 * D), BF16)] * (n // 2), n_in=2, name="chip_sum")(keep_pay, came)
         parts = [chip_sum[0]] + [lax.ppermute(chip_sum[k // 2], "ctx", xor_pairs(n, k)) for k in range(2, n, 2)]
-    output, grad_inputs = vmem_call(
-        functools.partial(close_body, fast),
-        (shape((TOK, D), BF16), shape((TOK, D))),
-        n_smem=1,
-        n_in=3 + len(parts),
-        name="close",
-    )(place, x, g, params, *parts)
-
     if fast:
         ff_far = lax.ppermute(attn_pay[3], "fsdp", xor_pairs(nz, 2))
         out_half = vmem_call(out_body, shape((HEAD_DIM, D), BF16), n_in=2, cost=LONG, name="out_half")(g_out, ff_far)
@@ -755,7 +748,20 @@
         share = vmem_call(share_body, shape((rows, 1024), BF16), n_in=7 + 2, name="share")(
             ff_pay[0], ff_far, attn_pay[0], attn_near, attn_far, out_half, out_far, parts[3], parts[4]
         )
-        alls = gather_ctx(share, n)
+        through = [share]
+    else:
+        through = []
+    closed = vmem_call(
+        functools.partial(close_body, fast),
+        [shape((TOK, D), BF16), shape((TOK, D))] + [shape(v.shape, BF16) for v in through],
+        n_smem=1,
+        n_in=3 + len(parts) + len(through),
+        name="close",
+    )(place, x, g, params, *parts, *through)
+
+    output, grad_inputs = closed[:2]
+    if fast:
+        alls = gather_ctx(share, n, closed[2])
         dz = D // nz
         outs = vmem_call(
             functools.partial(finish_body, n, nz),

time: 78.5 us -> 77.1 us (0.982)
    ppermute x6, waiting for transfers between devices: 12.6 us -> 11.1 us  [gather_ctx(): got[k] = lax.ppermute(value, 'ctx', xor_pairs(n, k))]
    ppermute x8, waiting for transfers between devices: 0.96 us -> 2.35 us  [gather_ctx(): got[k + 1] = lax.ppermute(source, 'ctx', xor_pairs(n, 1))]
  transfers between devices with their start and end apart: 28 -> 28, of which waited for: 11 -> 13; matrix products, arithmetic and copies ran while one was open for 0% -> 1% of each run, Pallas kernels for 14% -> 14%
where the time goes in v6:
time: 77.1 us; the launch traced here: 76.9 us
  starting transfers between devices  28 us (36%)
  waiting for transfers between devices  27.6 us (36%)
  Pallas kernels  18.6 us (24%)
  local copies, waits for them, and re-layouts  1.52 us (2%)
  between operations  0.82 us (1%)
    ppermute x6, waiting for transfers between devices, gather_ctx(): got[k] = lax.ppermute(value, 'ctx', xor_pairs(n, k))  11.1 us
    ppermute x6, starting transfers between devices, gather_ctx(): got[k] = lax.ppermute(value, 'ctx', xor_pairs(n, k))  7.04 us
    ppermute x1, waiting for transfers between devices, per_device(): ff_far = lax.ppermute(attn_pay[3], 'fsdp', xor_pairs(nz, 2))  6.83 us
    ppermute x2, starting transfers between devices, relay_fsdp(): one, two = (lax.ppermute(value, 'fsdp', xor_pairs(nz, k)) for k in (1, 2))  5.68 us
    pallas_call x1, Pallas kernels, per_device(): vmem_call(functools.partial(attn_body, n), [shape((seq, 64), BF16), shape...  5.07 us
    ppermute x2, waiting for transfers between devices, relay_fsdp(): one, two = (lax.ppermute(value, 'fsdp', xor_pairs(nz, k)) for k in (1, 2))  4.2 us
    pallas_call x1, Pallas kernels, per_device(): vmem_call(functools.partial(ff_body, n, nz, fast), [whole_seq, whole_seq,...  3.44 us
    ppermute x1, starting transfers between devices, per_device(): ff_far = lax.ppermute(attn_pay[3], 'fsdp', xor_pairs(nz, 2))  3.36 us
  transfers between devices with their start and end apart: 28, of which 13 were waited for; matrix products, arithmetic and copies ran while one was open for 1% of the time, Pallas kernels for 14%

profile of v6, /device:TPU:0, one launch (start us, length us, event | category | flops | bytes accessed | tf_op | source)
XLA Modules:
  0.0 76.9 jit_solution(11100775199188167341)
XLA Ops:
  0.6 2.2 %pack.1 = (bf16[128,768]{1,0:T(8,128)(2,1)}, bf16[256,512]{1,0:T(8,128)(2,1)}, bf16[64,512]{1,0:T(8,128)(2,1)}) custom-call(bf16[128,1536]{1,0:T(8,128)(2,1)} %w_qkv.1, bf16[128,2048]{1,0:T(8,128)(2,1)} %w_up.1, bf16[512,512]{1,0:T(8,128)(2,1)} %w_down.1, bf16[128,512]{1,0:T(8,128)(2,1)} %w_out.1, bf16[1,128,512]{2,1,0:T(8,128)(2,1)} %x.1, ...), custom_call_target="tpu_custom_call" | custom-call | tf_op jit(solution)/shard_map/pack/pallas_call | solution.py:114
  2.8 4.1 %collective-permute-start.1 = (bf16[128,768]{1,0:T(8,128)(2,1)}, bf16[128,768]{1,0:T(8,128)(2,1)S(1)}, u32[]{:S(2)}, u32[]{:S(2)}) collective-permute-start(bf16[128,768]{1,0:T(8,128)(2,1)} %get-tuple-element.61.refs_0_), channel_id=1, source_target_pairs={{0,2},{1,3},{2,0},{3,1},{4,6},{5,7},{6,4},{7,5},{8,10},{9,11},{10,... | collective-permute-start | bytes 589832 | tf_op jit(solution)/shard_map/ppermute | solution.py:550
  6.9 1.6 %collective-permute-start = (bf16[128,768]{1,0:T(8,128)(2,1)}, bf16[128,768]{1,0:T(8,128)(2,1)S(1)}, u32[]{:S(2)}, u32[]{:S(2)}) collective-permute-start(bf16[128,768]{1,0:T(8,128)(2,1)} %get-tuple-element.61.refs_0_), channel_id=1, source_target_pairs={{0,1},{1,0},{2,3},{3,2},{4,5},{5,4},{6,7},{7,6},{8,9},{9,8},{10,11... | collective-permute-start | bytes 589832 | tf_op jit(solution)/shard_map/ppermute | solution.py:550
  8.5 2.4 %collective-permute-start.8 = (bf16[256,512]{1,0:T(8,128)(2,1)}, bf16[256,512]{1,0:T(8,128)(2,1)S(1)}, u32[]{:S(2)}, u32[]{:S(2)}) collective-permute-start(bf16[256,512]{1,0:T(8,128)(2,1)} %get-tuple-element.63.refs_0_), channel_id=1, source_target_pairs={{0,24},{4,28},{8,16},{12,20},{16,8},{20,12},{24,0},{28,4},{1,25},{... | collective-permute-start | bytes 786440 | tf_op jit(solution)/shard_map/ppermute | solution.py:538
  11.0 0.5 collective-permute-start.6
  11.5 0.5 collective-permute-start.4
  12.1 0.1 add.23
  12.2 4.2 %collective-permute-done.1.refs_2_ = bf16[128,768]{1,0:T(8,128)(2,1)S(1)} collective-permute-done((bf16[128,768]{1,0:T(8,128)(2,1)}, bf16[128,768]{1,0:T(8,128)(2,1)S(1)}, u32[]{:S(2)}, u32[]{:S(2)}) %collective-permute-start.1) | collective-permute-done | bytes 196640 | tf_op jit(solution)/shard_map/ppermute | solution.py:550
  16.4 0.7 collective-permute-start.2
  17.1 0.1 pad_add_fusion.place
  17.2 0.6 copy-done.6
  17.7 0.2 select_reduce_fusion.order
  18.0 0.8 %copy-done.2 = bf16[64,512]{1,0:T(8,128)(2,1)S(1)} copy-done((bf16[64,512]{1,0:T(8,128)(2,1)S(1)}, bf16[64,512]{1,0:T(8,128)(2,1)}, u32[]{:S(2)}) %copy-start.2) | copy-done | bytes 65560
  18.9 0.8 %collective-permute-start.10 = (bf16[64,512]{1,0:T(8,128)(2,1)S(1)}, bf16[64,512]{1,0:T(8,128)(2,1)S(1)}, u32[]{:S(2)}, u32[]{:S(2)}) collective-permute-start(bf16[64,512]{1,0:T(8,128)(2,1)S(1)} %gate_w.1), channel_id=1, source_target_pairs={{0,0},{1,8},{2,16},{3,24},{4,4},{5,12},{6,20},{7,28},{8,1},{9,9},{... | collective-permute-start | bytes 196616 | tf_op jit(solution)/shard_map/ppermute | solution.py:623
  19.7 3.0 %collective-permute-done.6.refs_4_ = bf16[256,512]{1,0:T(8,128)(2,1)S(1)} collective-permute-done((bf16[256,512]{1,0:T(8,128)(2,1)}, bf16[256,512]{1,0:T(8,128)(2,1)S(1)}, u32[]{:S(2)}, u32[]{:S(2)}) %collective-permute-start.6) | collective-permute-done | bytes 262176 | tf_op jit(solution)/shard_map/ppermute | solution.py:538
  22.7 0.1 collective-permute-done.4.refs_2_
  22.8 0.4 collective-permute-start.7
  23.2 0.1 collective-permute-start.5
  23.3 0.7 unpack.1
  24.1 0.2 collective-permute-done.9.refs_7_
  24.3 0.4 collective-permute-done.7.refs_5_
  24.6 0.4 collective-permute-done.5.refs_3_
  25.0 3.4 %feed_forward.1 = (bf16[1024,512]{1,0:T(8,128)(2,1)S(1)}, bf16[1024,512]{1,0:T(8,128)(2,1)S(1)}, f32[8,512]{1,0:T(8,128)S(1)}, bf16[1024,512]{1,0:T(8,128)(2,1)S...) custom-call(s32[2]{0:T(128)S(1)} %pad_add_fusion.place, ...), custom_call_target="tpu_custom_call" | custom-call | flops 4000000000 | tf_op jit(solution)/shard_map/feed_forward/pallas_call | solution.py:657
  28.5 1.3 %collective-permute-start.11 = (bf16[128,512]{1,0:T(8,128)(2,1)S(1)}, bf16[128,512]{1,0:T(8,128)(2,1)S(1)}, u32[]{:S(2)}, u32[]{:S(2)}) collective-permute-start(bf16[128,512]{1,0:T(8,128)(2,1)S(1)} %get-tuple-element.77), channel_id=1, source_target_pairs={{0,1},{1,0},{2,3},{3,2},{4,5},{5,4},{6,7},{7,6},{8,9},{9,8},{10,11... | collective-permute-start | bytes 393224 | tf_op jit(solution)/shard_map/ppermute | solution.py:677
  29.8 5.1 %attention.1 = (bf16[1024,64]{1,0:T(8,128)(2,1)S(1)}, bf16[1024,256]{1,0:T(8,128)(2,1)S(1)}) custom-call(s32[2]{0:T(128)S(1)} %pad_add_fusion.place, s32[16]{0:T(128)S(1)} %select_reduce_fusion.order, bf16[256,512]{1,0:T(8,128)(2,1)S(1)} %copy-done.3, bf16[256,512]{1,0:T(8,128)(2,1)S(1)} %collective-permute-done.3.refs_1_, ...), custom_call_target="tpu_custom_call" | custom-call | flops 6000000000 | tf_op jit(solution)/shard_map/attention/pallas_call | solution.py:679
  34.9 2.3 %ends.1 = (bf16[4,128,1024]{2,1,0:T(8,128)(2,1)S(1)}, bf16[4,128,1024]{2,1,0:T(8,128)(2,1)S(1)}, bf16[64,512]{1,0:T(8,128)(2,1)S(1)}, bf16[128,256]{1,0:T(8,128)...) custom-call(s32[2]{0:T(128)S(1)} %pad_add_fusion.place, ...), custom_call_target="tpu_custom_call" | custom-call | flops 3000000000 | tf_op jit(solution)/shard_map/ends/pallas_call | solution.py:699
  37.3 3.4 %collective-permute-start.17 = (bf16[192,512]{1,0:T(8,128)(2,1)S(1)}, bf16[192,512]{1,0:T(8,128)(2,1)S(1)}, u32[]{:S(2)}, u32[]{:S(2)}) collective-permute-start(bf16[192,512]{1,0:T(8,128)(2,1)S(1)} %get-tuple-element.88), channel_id=1, source_target_pairs={{0,2},{1,3},{2,0},{3,1},{4,6},{5,7},{6,4},{7,5},{8,10},{9,11},{10,... | collective-permute-start | bytes 589832 | tf_op jit(solution)/shard_map/ppermute | solution.py:742
  40.6 0.5 collective-permute-start.18
  41.1 0.2 chip_sum.1
  41.4 0.6 collective-permute-start.13
  42.0 1.5 %collective-permute-start.14 = (bf16[2,128,512]{2,1,0:T(8,128)(2,1)S(1)}, bf16[2,128,512]{2,1,0:T(8,128)(2,1)S(1)}, u32[]{:S(2)}, u32[]{:S(2)}) collective-permute-start(bf16[2,128,512]{2,1,0:T(8,128)(2,1)S(1)} %get-tuple-element.82), channel_id=1, source_target_pairs={{0,16},{4,20},{8,24},{12,28},{16,0},{20,4},{24,8},{28,12},{1,17},{... | collective-permute-start | bytes 786440 | tf_op jit(solution)/shard_map/ppermute | solution.py:727
  43.5 6.8 %collective-permute-done.17.came.ff_far = bf16[192,512]{1,0:T(8,128)(2,1)S(1)} collective-permute-done((bf16[192,512]{1,0:T(8,128)(2,1)S(1)}, bf16[192,512]{1,0:T(8,128)(2,1)S(1)}, u32[]{:S(2)}, u32[]{:S(2)}) %collective-permute-start.17) | collective-permute-done | bytes 196640 | tf_op jit(solution)/shard_map/ppermute | solution.py:742
  50.6 2.7 %collective-permute-start.15 = (bf16[128,512]{1,0:T(8,128)(2,1)S(1)}, bf16[128,512]{1,0:T(8,128)(2,1)S(1)}, u32[]{:S(2)}, u32[]{:S(2)}) collective-permute-start(bf16[128,512]{1,0:T(8,128)(2,1)S(1)} %get-tuple-element.85), channel_id=1, source_target_pairs={{0,16},{4,20},{8,24},{12,28},{16,0},{20,4},{24,8},{28,12},{1,17},{... | collective-permute-start | bytes 393224 | tf_op jit(solution)/shard_map/ppermute | solution.py:737
  53.3 0.4 collective-permute-start.16
  53.7 2.3 %collective-permute-start.19 = (bf16[128,256]{1,0:T(8,128)(2,1)S(1)}, bf16[128,256]{1,0:T(8,128)(2,1)S(1)}, u32[]{:S(2)}, u32[]{:S(2)}) collective-permute-start(bf16[128,256]{1,0:T(8,128)(2,1)S(1)} %relay.1), channel_id=1, source_target_pairs={{0,2},{1,3},{2,0},{3,1},{4,6},{5,7},{6,4},{7,5},{8,10},{9,11},{10,... | collective-permute-start | bytes 196616 | tf_op jit(solution)/shard_map/ppermute | solution.py:747
  56.0 3.1 %collective-permute-done.19.far = bf16[128,256]{1,0:T(8,128)(2,1)S(1)} collective-permute-done((bf16[128,256]{1,0:T(8,128)(2,1)S(1)}, bf16[128,256]{1,0:T(8,128)(2,1)S(1)}, u32[]{:S(2)}, u32[]{:S(2)}) %collective-permute-start.19) | collective-permute-done | bytes 65568 | tf_op jit(solution)/shard_map/ppermute | solution.py:747
  59.2 0.1 share.1.refs_5_.refs_0_
  59.3 1.6 %collective-permute-start.26 = (bf16[128,1024]{1,0:T(8,128)(2,1)S(1)}, bf16[128,1024]{1,0:T(8,128)(2,1)S(1)}, u32[]{:S(2)}, u32[]{:S(2)}) collective-permute-start(bf16[128,1024]{1,0:T(8,128)(2,1)S(1)} %share.1.refs_5_.refs_0_), channel_id=1, source_target_pairs={{0,24},{4,28},{8,16},{12,20},{16,8},{20,12},{24,0},{28,4},{1,25},{... | collective-permute-start | bytes 786440 | tf_op jit(solution)/shard_map/ppermute | solution.py:538
  60.9 1.7 %collective-permute-start.24 = (bf16[128,1024]{1,0:T(8,128)(2,1)S(1)}, bf16[128,1024]{1,0:T(8,128)(2,1)S(1)}, u32[]{:S(2)}, u32[]{:S(2)}) collective-permute-start(bf16[128,1024]{1,0:T(8,128)(2,1)S(1)} %share.1.refs_5_.refs_0_), channel_id=1, source_target_pairs={{0,16},{4,20},{8,24},{12,28},{16,0},{20,4},{24,8},{28,12},{1,17},{... | collective-permute-start | bytes 786440 | tf_op jit(solution)/shard_map/ppermute | solution.py:538
  62.5 0.3 collective-permute-start.22
  62.8 1.6 %close.1 = (bf16[128,512]{1,0:T(8,128)(2,1)}, f32[128,512]{1,0:T(8,128)}, bf16[128,1024]{1,0:T(8,128)(2,1)S(1)}) custom-call(s32[2]{0:T(128)S(1)} %pad_add_fusion.place, bf16[128,512]{1,0:T(8,128)(2,1)S(1)} %bitcast.6, bf16[128,512]{1,0:T(8,128)(2,1)S(1)} %bitcast.7, f32[8,512]{1,0:T(8,128)S(1)} %get-tuple-element.62.refs_10_.refs_9_.refs_17_.params, ...), custom_call_target="tpu_custom_call" | custom-call | tf_op jit(solution)/shard_map/close/pallas_call | solution.py:754
  64.4 5.0 %collective-permute-done.26.refs_6_ = bf16[128,1024]{1,0:T(8,128)(2,1)S(1)} collective-permute-done((bf16[128,1024]{1,0:T(8,128)(2,1)S(1)}, bf16[128,1024]{1,0:T(8,128)(2,1)S(1)}, u32[]{:S(2)}, u32[]{:S(2)}) %collective-permute-start.26) | collective-permute-done | bytes 262176 | tf_op jit(solution)/shard_map/ppermute | solution.py:538
  69.4 2.8 %collective-permute-done.24.refs_4_ = bf16[128,1024]{1,0:T(8,128)(2,1)S(1)} collective-permute-done((bf16[128,1024]{1,0:T(8,128)(2,1)S(1)}, bf16[128,1024]{1,0:T(8,128)(2,1)S(1)}, u32[]{:S(2)}, u32[]{:S(2)}) %collective-permute-start.24) | collective-permute-done | bytes 262176 | tf_op jit(solution)/shard_map/ppermute | solution.py:538
  72.1 0.2 collective-permute-done.22.refs_2_
  72.4 0.3 collective-permute-start.23
  72.6 1.0 %collective-permute-done.25.refs_5_ = bf16[128,1024]{1,0:T(8,128)(2,1)S(1)} collective-permute-done((bf16[128,1024]{1,0:T(8,128)(2,1)S(1)}, bf16[128,1024]{1,0:T(8,128)(2,1)S(1)}, u32[]{:S(2)}, u32[]{:S(2)}) %collective-permute-start.25) | collective-permute-done | bytes 262176 | tf_op jit(solution)/shard_map/ppermute | solution.py:541
  73.7 0.4 collective-permute-done.23.refs_3_
  74.0 2.8 %finish.1 = (f32[128]{0:T(128)}, f32[128]{0:T(128)}, f32[128,1536]{1,0:T(8,128)}, f32[384]{0:T(512)}, f32[128,512]{1,0:T(8,128)}, /*index=5*/f32[128]{0:T(128)},...) custom-call(s32[2]{0:T(128)S(1)} %pad_add_fusion.place, ...), custom_call_target="tpu_custom_call" | custom-call | tf_op jit(solution)/shard_map/finish/pallas_call | solution.py:766
  (40 shorter events, 0.5 us)
Async XLA Ops:
  2.8 13.5 %collective-permute-start.1 = (bf16[128,768]{1,0:T(8,128)(2,1)}, bf16[128,768]{1,0:T(8,128)(2,1)S(1)}, u32[]{:S(2)}, u32[]{:S(2)}) collective-permute-start(bf16[128,768]{1,0:T(8,128)(2,1)} %get-tuple-element.61.refs_0_), channel_id=1, source_target_pairs={{0,2},{1,3},{2,0},{3,1},{4,6},{5,7},{6,4},{7,5},{8,10},{9,11},{10,... | collective-permute-start | bytes 589832 | tf_op jit(solution)/shard_map/ppermute | solution.py:550
  6.9 11.0 %collective-permute-start = (bf16[128,768]{1,0:T(8,128)(2,1)}, bf16[128,768]{1,0:T(8,128)(2,1)S(1)}, u32[]{:S(2)}, u32[]{:S(2)}) collective-permute-start(bf16[128,768]{1,0:T(8,128)(2,1)} %get-tuple-element.61.refs_0_), channel_id=1, source_target_pairs={{0,1},{1,0},{2,3},{3,2},{4,5},{5,4},{6,7},{7,6},{8,9},{9,8},{10,11... | collective-permute-start | bytes 589832 | tf_op jit(solution)/shard_map/ppermute | solution.py:550
  8.5 10.4 %collective-permute-start.8 = (bf16[256,512]{1,0:T(8,128)(2,1)}, bf16[256,512]{1,0:T(8,128)(2,1)S(1)}, u32[]{:S(2)}, u32[]{:S(2)}) collective-permute-start(bf16[256,512]{1,0:T(8,128)(2,1)} %get-tuple-element.63.refs_0_), channel_id=1, source_target_pairs={{0,24},{4,28},{8,16},{12,20},{16,8},{20,12},{24,0},{28,4},{1,25},{... | collective-permute-start | bytes 786440 | tf_op jit(solution)/shard_map/ppermute | solution.py:538
  11.0 11.8 %collective-permute-start.6 = (bf16[256,512]{1,0:T(8,128)(2,1)}, bf16[256,512]{1,0:T(8,128)(2,1)S(1)}, u32[]{:S(2)}, u32[]{:S(2)}) collective-permute-start(bf16[256,512]{1,0:T(8,128)(2,1)} %get-tuple-element.63.refs_0_), channel_id=1, source_target_pairs={{0,16},{4,20},{8,24},{12,28},{16,0},{20,4},{24,8},{28,12},{1,17},{... | collective-permute-start | bytes 786440 | tf_op jit(solution)/shard_map/ppermute | solution.py:538
  11.5 11.4 %collective-permute-start.4 = (bf16[256,512]{1,0:T(8,128)(2,1)}, bf16[256,512]{1,0:T(8,128)(2,1)S(1)}, u32[]{:S(2)}, u32[]{:S(2)}) collective-permute-start(bf16[256,512]{1,0:T(8,128)(2,1)} %get-tuple-element.63.refs_0_), channel_id=1, source_target_pairs={{0,8},{4,12},{8,0},{12,4},{16,24},{20,28},{24,16},{28,20},{1,9},{5... | collective-permute-start | bytes 786440 | tf_op jit(solution)/shard_map/ppermute | solution.py:538
  16.4 6.9 %collective-permute-start.2 = (bf16[128,768]{1,0:T(8,128)(2,1)S(1)}, bf16[128,768]{1,0:T(8,128)(2,1)S(1)}, u32[]{:S(2)}, u32[]{:S(2)}) collective-permute-start(bf16[128,768]{1,0:T(8,128)(2,1)S(1)} %collective-permute-done.1.refs_2_), channel_id=1, source_target_pairs={{0,1},{1,0},{2,3},{3,2},{4,5},{5,4},{6,7},{7,6},{8,9},{9,8},{10,11... | collective-permute-start | bytes 589832 | tf_op jit(solution)/shard_map/ppermute | solution.py:551
  17.1 0.7 copy-start.6
  17.9 6.1 %collective-permute-start.3 = (bf16[256,512]{1,0:T(8,128)(2,1)}, bf16[256,512]{1,0:T(8,128)(2,1)S(1)}, u32[]{:S(2)}, u32[]{:S(2)}) collective-permute-start(bf16[256,512]{1,0:T(8,128)(2,1)} %get-tuple-element.63.refs_0_), channel_id=1, source_target_pairs={{0,4},{4,0},{8,12},{12,8},{16,20},{20,16},{24,28},{28,24},{1,5},{5... | collective-permute-start | bytes 786440 | tf_op jit(solution)/shard_map/ppermute | solution.py:541
  18.0 0.8 %copy-start.2 = (bf16[64,512]{1,0:T(8,128)(2,1)S(1)}, bf16[64,512]{1,0:T(8,128)(2,1)}, u32[]{:S(2)}) copy-start(bf16[64,512]{1,0:T(8,128)(2,1)} %get-tuple-element.65.value) | copy-start | bytes 196612
  18.9 4.5 %copy-start.4 = (bf16[128,768]{1,0:T(8,128)(2,1)S(1)}, bf16[128,768]{1,0:T(8,128)(2,1)}, u32[]{:S(2)}) copy-start(bf16[128,768]{1,0:T(8,128)(2,1)} %get-tuple-element.61.refs_0_) | copy-start | bytes 589828
  18.9 6.2 %copy-start.3 = (bf16[256,512]{1,0:T(8,128)(2,1)S(1)}, bf16[256,512]{1,0:T(8,128)(2,1)}, u32[]{:S(2)}) copy-start(bf16[256,512]{1,0:T(8,128)(2,1)} %get-tuple-element.63.refs_0_) | copy-start | bytes 786436
  18.9 10.9 %collective-permute-start.10 = (bf16[64,512]{1,0:T(8,128)(2,1)S(1)}, bf16[64,512]{1,0:T(8,128)(2,1)S(1)}, u32[]{:S(2)}, u32[]{:S(2)}) collective-permute-start(bf16[64,512]{1,0:T(8,128)(2,1)S(1)} %gate_w.1), channel_id=1, source_target_pairs={{0,0},{1,8},{2,16},{3,24},{4,4},{5,12},{6,20},{7,28},{8,1},{9,9},{... | collective-permute-start | bytes 196616 | tf_op jit(solution)/shard_map/ppermute | solution.py:623
  22.7 1.5 %collective-permute-start.9 = (bf16[256,512]{1,0:T(8,128)(2,1)S(1)}, bf16[256,512]{1,0:T(8,128)(2,1)S(1)}, u32[]{:S(2)}, u32[]{:S(2)}) collective-permute-start(bf16[256,512]{1,0:T(8,128)(2,1)S(1)} %collective-permute-done.8.refs_6_), channel_id=1, source_target_pairs={{0,4},{4,0},{8,12},{12,8},{16,20},{20,16},{24,28},{28,24},{1,5},{5... | collective-permute-start | bytes 786440 | tf_op jit(solution)/shard_map/ppermute | solution.py:541
  22.8 1.8 %collective-permute-start.7 = (bf16[256,512]{1,0:T(8,128)(2,1)S(1)}, bf16[256,512]{1,0:T(8,128)(2,1)S(1)}, u32[]{:S(2)}, u32[]{:S(2)}) collective-permute-start(bf16[256,512]{1,0:T(8,128)(2,1)S(1)} %collective-permute-done.6.refs_4_), channel_id=1, source_target_pairs={{0,4},{4,0},{8,12},{12,8},{16,20},{20,16},{24,28},{28,24},{1,5},{5... | collective-permute-start | bytes 786440 | tf_op jit(solution)/shard_map/ppermute | solution.py:541
  23.2 1.8 %collective-permute-start.5 = (bf16[256,512]{1,0:T(8,128)(2,1)S(1)}, bf16[256,512]{1,0:T(8,128)(2,1)S(1)}, u32[]{:S(2)}, u32[]{:S(2)}) collective-permute-start(bf16[256,512]{1,0:T(8,128)(2,1)S(1)} %collective-permute-done.4.refs_2_), channel_id=1, source_target_pairs={{0,4},{4,0},{8,12},{12,8},{16,20},{20,16},{24,28},{28,24},{1,5},{5... | collective-permute-start | bytes 786440 | tf_op jit(solution)/shard_map/ppermute | solution.py:541
  25.0 4.8 %copy-start.5 = (f32[1024,128]{1,0:T(8,128)S(1)}, f32[1024,128]{1,0:T(8,128)}, u32[]{:S(2)}) copy-start(f32[1024,128]{1,0:T(8,128)} %constant.15.clone.refs_11_) | copy-start | bytes 1572868
  28.5 6.4 %collective-permute-start.11 = (bf16[128,512]{1,0:T(8,128)(2,1)S(1)}, bf16[128,512]{1,0:T(8,128)(2,1)S(1)}, u32[]{:S(2)}, u32[]{:S(2)}) collective-permute-start(bf16[128,512]{1,0:T(8,128)(2,1)S(1)} %get-tuple-element.77), channel_id=1, source_target_pairs={{0,1},{1,0},{2,3},{3,2},{4,5},{5,4},{6,7},{7,6},{8,9},{9,8},{10,11... | collective-permute-start | bytes 393224 | tf_op jit(solution)/shard_map/ppermute | solution.py:677
  37.2 3.9 %collective-permute-start.12 = (bf16[4,128,1024]{2,1,0:T(8,128)(2,1)S(1)}, bf16[4,128,1024]{2,1,0:T(8,128)(2,1)S(1)}, u32[]{:S(2)}, u32[]{:S(2)}) collective-permute-start(bf16[4,128,1024]{2,1,0:T(8,128)(2,1)S(1)} %get-tuple-element.79), channel_id=1, source_target_pairs={{0,4},{4,0},{8,12},{12,8},{16,20},{20,16},{24,28},{28,24},{1,5},{5... | collective-permute-start | bytes 3145736 | tf_op jit(solution)/shard_map/ppermute | solution.py:716
  37.3 13.1 %collective-permute-start.17 = (bf16[192,512]{1,0:T(8,128)(2,1)S(1)}, bf16[192,512]{1,0:T(8,128)(2,1)S(1)}, u32[]{:S(2)}, u32[]{:S(2)}) collective-permute-start(bf16[192,512]{1,0:T(8,128)(2,1)S(1)} %get-tuple-element.88), channel_id=1, source_target_pairs={{0,2},{1,3},{2,0},{3,1},{4,6},{5,7},{6,4},{7,5},{8,10},{9,11},{10,... | collective-permute-start | bytes 589832 | tf_op jit(solution)/shard_map/ppermute | solution.py:742
  40.6 13.1 %collective-permute-start.18 = (bf16[128,1024]{1,0:T(8,128)(2,1)S(1)}, bf16[128,1024]{1,0:T(8,128)(2,1)S(1)}, u32[]{:S(2)}, u32[]{:S(2)}) collective-permute-start(bf16[128,1024]{1,0:T(8,128)(2,1)S(1)} %get-tuple-element.90), channel_id=1, source_target_pairs={{0,1},{1,0},{2,3},{3,2},{4,5},{5,4},{6,7},{7,6},{8,9},{9,8},{10,11... | collective-permute-start | bytes 786440 | tf_op jit(solution)/shard_map/ppermute | solution.py:745
  41.4 9.1 %collective-permute-start.13 = (bf16[2,128,512]{2,1,0:T(8,128)(2,1)S(1)}, bf16[2,128,512]{2,1,0:T(8,128)(2,1)S(1)}, u32[]{:S(2)}, u32[]{:S(2)}) collective-permute-start(bf16[2,128,512]{2,1,0:T(8,128)(2,1)S(1)} %get-tuple-element.81), channel_id=1, source_target_pairs={{0,8},{4,12},{8,0},{12,4},{16,24},{20,28},{24,16},{28,20},{1,9},{5... | collective-permute-start | bytes 786440 | tf_op jit(solution)/shard_map/ppermute | solution.py:726
  42.0 8.5 %collective-permute-start.14 = (bf16[2,128,512]{2,1,0:T(8,128)(2,1)S(1)}, bf16[2,128,512]{2,1,0:T(8,128)(2,1)S(1)}, u32[]{:S(2)}, u32[]{:S(2)}) collective-permute-start(bf16[2,128,512]{2,1,0:T(8,128)(2,1)S(1)} %get-tuple-element.82), channel_id=1, source_target_pairs={{0,16},{4,20},{8,24},{12,28},{16,0},{20,4},{24,8},{28,12},{1,17},{... | collective-permute-start | bytes 786440 | tf_op jit(solution)/shard_map/ppermute | solution.py:727
  50.4 5.6 %collective-permute-start.20 = (bf16[64,512]{1,0:T(8,128)(2,1)S(1)}, bf16[64,512]{1,0:T(8,128)(2,1)S(1)}, u32[]{:S(2)}, u32[]{:S(2)}) collective-permute-start(bf16[64,512]{1,0:T(8,128)(2,1)S(1)} %out_half.1), channel_id=1, source_target_pairs={{0,1},{1,0},{2,3},{3,2},{4,5},{5,4},{6,7},{7,6},{8,9},{9,8},{10,11... | collective-permute-start | bytes 196616 | tf_op jit(solution)/shard_map/ppermute | solution.py:744
  50.6 8.6 %collective-permute-start.15 = (bf16[128,512]{1,0:T(8,128)(2,1)S(1)}, bf16[128,512]{1,0:T(8,128)(2,1)S(1)}, u32[]{:S(2)}, u32[]{:S(2)}) collective-permute-start(bf16[128,512]{1,0:T(8,128)(2,1)S(1)} %get-tuple-element.85), channel_id=1, source_target_pairs={{0,16},{4,20},{8,24},{12,28},{16,0},{20,4},{24,8},{28,12},{1,17},{... | collective-permute-start | bytes 393224 | tf_op jit(solution)/shard_map/ppermute | solution.py:737
  53.3 5.9 %collective-permute-start.16 = (bf16[128,512]{1,0:T(8,128)(2,1)S(1)}, bf16[128,512]{1,0:T(8,128)(2,1)S(1)}, u32[]{:S(2)}, u32[]{:S(2)}) collective-permute-start(bf16[128,512]{1,0:T(8,128)(2,1)S(1)} %get-tuple-element.86), channel_id=1, source_target_pairs={{0,8},{4,12},{8,0},{12,4},{16,24},{20,28},{24,16},{28,20},{1,9},{5... | collective-permute-start | bytes 393224 | tf_op jit(solution)/shard_map/ppermute | solution.py:737
  53.7 5.4 %collective-permute-start.19 = (bf16[128,256]{1,0:T(8,128)(2,1)S(1)}, bf16[128,256]{1,0:T(8,128)(2,1)S(1)}, u32[]{:S(2)}, u32[]{:S(2)}) collective-permute-start(bf16[128,256]{1,0:T(8,128)(2,1)S(1)} %relay.1), channel_id=1, source_target_pairs={{0,2},{1,3},{2,0},{3,1},{4,6},{5,7},{6,4},{7,5},{8,10},{9,11},{10,... | collective-permute-start | bytes 196616 | tf_op jit(solution)/shard_map/ppermute | solution.py:747
  59.1 3.7 %copy-start = (bf16[1,128,512]{2,1,0:T(8,128)(2,1)S(1)}, bf16[1,128,512]{2,1,0:T(8,128)(2,1)}, u32[]{:S(2)}) copy-start(bf16[1,128,512]{2,1,0:T(8,128)(2,1)} %x.1) | copy-start | bytes 393220
  59.2 3.7 %copy-start.1 = (bf16[1,128,512]{2,1,0:T(8,128)(2,1)S(1)}, bf16[1,128,512]{2,1,0:T(8,128)(2,1)}, u32[]{:S(2)}) copy-start(bf16[1,128,512]{2,1,0:T(8,128)(2,1)} %g.1) | copy-start | bytes 393220
  59.3 10.1 %collective-permute-start.26 = (bf16[128,1024]{1,0:T(8,128)(2,1)S(1)}, bf16[128,1024]{1,0:T(8,128)(2,1)S(1)}, u32[]{:S(2)}, u32[]{:S(2)}) collective-permute-start(bf16[128,1024]{1,0:T(8,128)(2,1)S(1)} %share.1.refs_5_.refs_0_), channel_id=1, source_target_pairs={{0,24},{4,28},{8,16},{12,20},{16,8},{20,12},{24,0},{28,4},{1,25},{... | collective-permute-start | bytes 786440 | tf_op jit(solution)/shard_map/ppermute | solution.py:538
  60.9 11.3 %collective-permute-start.24 = (bf16[128,1024]{1,0:T(8,128)(2,1)S(1)}, bf16[128,1024]{1,0:T(8,128)(2,1)S(1)}, u32[]{:S(2)}, u32[]{:S(2)}) collective-permute-start(bf16[128,1024]{1,0:T(8,128)(2,1)S(1)} %share.1.refs_5_.refs_0_), channel_id=1, source_target_pairs={{0,16},{4,20},{8,24},{12,28},{16,0},{20,4},{24,8},{28,12},{1,17},{... | collective-permute-start | bytes 786440 | tf_op jit(solution)/shard_map/ppermute | solution.py:538
  62.5 9.8 %collective-permute-start.22 = (bf16[128,1024]{1,0:T(8,128)(2,1)S(1)}, bf16[128,1024]{1,0:T(8,128)(2,1)S(1)}, u32[]{:S(2)}, u32[]{:S(2)}) collective-permute-start(bf16[128,1024]{1,0:T(8,128)(2,1)S(1)} %share.1.refs_5_.refs_0_), channel_id=1, source_target_pairs={{0,8},{4,12},{8,0},{12,4},{16,24},{20,28},{24,16},{28,20},{1,9},{5... | collective-permute-start | bytes 786440 | tf_op jit(solution)/shard_map/ppermute | solution.py:538
  64.4 8.2 %collective-permute-start.21 = (bf16[128,1024]{1,0:T(8,128)(2,1)S(1)}, bf16[128,1024]{1,0:T(8,128)(2,1)S(1)}, u32[]{:S(2)}, u32[]{:S(2)}) collective-permute-start(bf16[128,1024]{1,0:T(8,128)(2,1)S(1)} %get-tuple-element.95), channel_id=1, source_target_pairs={{0,4},{4,0},{8,12},{12,8},{16,20},{20,16},{24,28},{28,24},{1,5},{5... | collective-permute-start | bytes 786440 | tf_op jit(solution)/shard_map/ppermute | solution.py:541
  69.4 3.3 %collective-permute-start.27 = (bf16[128,1024]{1,0:T(8,128)(2,1)S(1)}, bf16[128,1024]{1,0:T(8,128)(2,1)S(1)}, u32[]{:S(2)}, u32[]{:S(2)}) collective-permute-start(bf16[128,1024]{1,0:T(8,128)(2,1)S(1)} %collective-permute-done.26.refs_6_), channel_id=1, source_target_pairs={{0,4},{4,0},{8,12},{12,8},{16,20},{20,16},{24,28},{28,24},{1,5},{5... | collective-permute-start | bytes 786440 | tf_op jit(solution)/shard_map/ppermute | solution.py:541
  72.1 1.5 %collective-permute-start.25 = (bf16[128,1024]{1,0:T(8,128)(2,1)S(1)}, bf16[128,1024]{1,0:T(8,128)(2,1)S(1)}, u32[]{:S(2)}, u32[]{:S(2)}) collective-permute-start(bf16[128,1024]{1,0:T(8,128)(2,1)S(1)} %collective-permute-done.24.refs_4_), channel_id=1, source_target_pairs={{0,4},{4,0},{8,12},{12,8},{16,20},{20,16},{24,28},{28,24},{1,5},{5... | collective-permute-start | bytes 786440 | tf_op jit(solution)/shard_map/ppermute | solution.py:541
  72.4 1.7 %collective-permute-start.23 = (bf16[128,1024]{1,0:T(8,128)(2,1)S(1)}, bf16[128,1024]{1,0:T(8,128)(2,1)S(1)}, u32[]{:S(2)}, u32[]{:S(2)}) collective-permute-start(bf16[128,1024]{1,0:T(8,128)(2,1)S(1)} %collective-permute-done.22.refs_2_), channel_id=1, source_target_pairs={{0,4},{4,0},{8,12},{12,8},{16,20},{20,16},{24,28},{28,24},{1,5},{5... | collective-permute-start | bytes 786440 | tf_op jit(solution)/shard_map/ppermute | solution.py:541

commit v7 on v6

--- a/solution.py
+++ b/solution.py
@@ -348,9 +348,9 @@
     g_gain = jnp.zeros((8, D), F32)
     g_shift = jnp.zeros((8, D), F32)
     g_bias = jnp.zeros((8, 256), F32)
-    for p in range(0, n, 2):
-        rows = slice(p * TOK, (p + 2) * TOK)
-        gs[rows, :] = joined(pieces[p : p + 2], TOK)
+    for p in range(0, n, 8):
+        rows = slice(p * TOK, (p + 8) * TOK)
+        gs[rows, :] = joined(pieces[p : p + 8], TOK)
         dqkv = dqkvn[rows, :]
         dnorm = mm_nt(dqkv, w_all[...])
         g_gain += fold(dnorm * nhats[rows, :].astype(F32))
@@ -358,7 +358,7 @@
         g_bias += fold(dqkv.astype(F32))
         part_o = (mm_nn(mixn[rows, :], w_out[...]) + acc_o[rows, :].astype(F32)).astype(BF16)
         part_d = (dnorm * gain + acc_d[rows, :].astype(F32)).astype(BF16)
-        for q in range(2):
+        for q in range(8):
             target = send_pay if (p + q) % 2 else keep_pay
             here = slice(q * TOK, (q + 1) * TOK)
             target[(p + q) // 2, :, 0:512] = part_o[here, :]
@@ -719,7 +719,7 @@
             functools.partial(chip_fast_body, 0),
             [shape((2, TOK, D), BF16)] * 2 + [shape((TOK, 2 * D), BF16)] + [shape((TOK, D), BF16)] * 2 + [],
             n_in=2 + 0,
-            cost=LONGER,
+
             name="chip_sum",
         )(keep_pay, came)
         first_a, first_b, own_sum, kept_a, kept_b = chip_out[:5]
@@ -729,7 +729,7 @@
             functools.partial(cross_body, 0),
             [shape((TOK, D), BF16)] * 2 + [],
             n_in=4 + 0,
-            cost=LONGER,
+
             name="cross",
         )(kept_a, kept_b, came_a, came_b)
         second_a, second_b = cross_out[:2]

time: 77.1 us -> 77.1 us (level)
  transfers between devices with their start and end apart: 28 -> 28, of which waited for: 13 -> 13; matrix products, arithmetic and copies ran while one was open for 1% -> 1% of each run, Pallas kernels for 14% -> 15%
where the time goes in v7:
time: 77.1 us; the launch traced here: 76.9 us
  starting transfers between devices  28 us (36%)
  waiting for transfers between devices  27.6 us (36%)
  Pallas kernels  18.6 us (24%)
  local copies, waits for them, and re-layouts  1.52 us (2%)
  between operations  0.82 us (1%)
    ppermute x6, waiting for transfers between devices, gather_ctx(): got[k] = lax.ppermute(value, 'ctx', xor_pairs(n, k))  11.1 us
    ppermute x6, starting transfers between devices, gather_ctx(): got[k] = lax.ppermute(value, 'ctx', xor_pairs(n, k))  7.04 us
    ppermute x1, waiting for transfers between devices, per_device(): ff_far = lax.ppermute(attn_pay[3], 'fsdp', xor_pairs(nz, 2))  6.81 us
    ppermute x2, starting transfers between devices, relay_fsdp(): one, two = (lax.ppermute(value, 'fsdp', xor_pairs(nz, k)) for k in (1, 2))  5.68 us
    pallas_call x1, Pallas kernels, per_device(): vmem_call(functools.partial(attn_body, n), [shape((seq, 64), BF16), shape...  5.07 us
    ppermute x2, waiting for transfers between devices, relay_fsdp(): one, two = (lax.ppermute(value, 'fsdp', xor_pairs(nz, k)) for k in (1, 2))  4.2 us
    pallas_call x1, Pallas kernels, per_device(): vmem_call(functools.partial(ff_body, n, nz, fast), [whole_seq, whole_seq,...  3.44 us
    ppermute x1, starting transfers between devices, per_device(): ff_far = lax.ppermute(attn_pay[3], 'fsdp', xor_pairs(nz, 2))  3.36 us
  transfers between devices with their start and end apart: 28, of which 13 were waited for; matrix products, arithmetic and copies ran while one was open for 1% of the time, Pallas kernels for 15%

profile of v7, /device:TPU:0, one launch (start us, length us, event | category | flops | bytes accessed | tf_op | source)
XLA Modules:
  0.0 76.9 jit_solution(1518127160653678166)
XLA Ops:
  0.6 2.2 %pack.1 = (bf16[128,768]{1,0:T(8,128)(2,1)}, bf16[256,512]{1,0:T(8,128)(2,1)}, bf16[64,512]{1,0:T(8,128)(2,1)}) custom-call(bf16[128,1536]{1,0:T(8,128)(2,1)} %w_qkv.1, bf16[128,2048]{1,0:T(8,128)(2,1)} %w_up.1, bf16[512,512]{1,0:T(8,128)(2,1)} %w_down.1, bf16[128,512]{1,0:T(8,128)(2,1)} %w_out.1, bf16[1,128,512]{2,1,0:T(8,128)(2,1)} %x.1, ...), custom_call_target="tpu_custom_call" | custom-call | tf_op jit(solution)/shard_map/pack/pallas_call | solution.py:114
  2.8 4.1 %collective-permute-start.1 = (bf16[128,768]{1,0:T(8,128)(2,1)}, bf16[128,768]{1,0:T(8,128)(2,1)S(1)}, u32[]{:S(2)}, u32[]{:S(2)}) collective-permute-start(bf16[128,768]{1,0:T(8,128)(2,1)} %get-tuple-element.61.refs_0_), channel_id=1, source_target_pairs={{0,2},{1,3},{2,0},{3,1},{4,6},{5,7},{6,4},{7,5},{8,10},{9,11},{10,... | collective-permute-start | bytes 589832 | tf_op jit(solution)/shard_map/ppermute | solution.py:550
  6.9 1.6 %collective-permute-start = (bf16[128,768]{1,0:T(8,128)(2,1)}, bf16[128,768]{1,0:T(8,128)(2,1)S(1)}, u32[]{:S(2)}, u32[]{:S(2)}) collective-permute-start(bf16[128,768]{1,0:T(8,128)(2,1)} %get-tuple-element.61.refs_0_), channel_id=1, source_target_pairs={{0,1},{1,0},{2,3},{3,2},{4,5},{5,4},{6,7},{7,6},{8,9},{9,8},{10,11... | collective-permute-start | bytes 589832 | tf_op jit(solution)/shard_map/ppermute | solution.py:550
  8.5 2.4 %collective-permute-start.8 = (bf16[256,512]{1,0:T(8,128)(2,1)}, bf16[256,512]{1,0:T(8,128)(2,1)S(1)}, u32[]{:S(2)}, u32[]{:S(2)}) collective-permute-start(bf16[256,512]{1,0:T(8,128)(2,1)} %get-tuple-element.63.refs_0_), channel_id=1, source_target_pairs={{0,24},{4,28},{8,16},{12,20},{16,8},{20,12},{24,0},{28,4},{1,25},{... | collective-permute-start | bytes 786440 | tf_op jit(solution)/shard_map/ppermute | solution.py:538
  11.0 0.5 collective-permute-start.6
  11.5 0.5 collective-permute-start.4
  12.1 0.1 add.23
  12.2 4.2 %collective-permute-done.1.refs_2_ = bf16[128,768]{1,0:T(8,128)(2,1)S(1)} collective-permute-done((bf16[128,768]{1,0:T(8,128)(2,1)}, bf16[128,768]{1,0:T(8,128)(2,1)S(1)}, u32[]{:S(2)}, u32[]{:S(2)}) %collective-permute-start.1) | collective-permute-done | bytes 196640 | tf_op jit(solution)/shard_map/ppermute | solution.py:550
  16.4 0.7 collective-permute-start.2
  17.1 0.1 pad_add_fusion.place
  17.2 0.6 copy-done.6
  17.7 0.2 select_reduce_fusion.order
  18.0 0.8 %copy-done.2 = bf16[64,512]{1,0:T(8,128)(2,1)S(1)} copy-done((bf16[64,512]{1,0:T(8,128)(2,1)S(1)}, bf16[64,512]{1,0:T(8,128)(2,1)}, u32[]{:S(2)}) %copy-start.2) | copy-done | bytes 65560
  18.9 0.8 %collective-permute-start.10 = (bf16[64,512]{1,0:T(8,128)(2,1)S(1)}, bf16[64,512]{1,0:T(8,128)(2,1)S(1)}, u32[]{:S(2)}, u32[]{:S(2)}) collective-permute-start(bf16[64,512]{1,0:T(8,128)(2,1)S(1)} %gate_w.1), channel_id=1, source_target_pairs={{0,0},{1,8},{2,16},{3,24},{4,4},{5,12},{6,20},{7,28},{8,1},{9,9},{... | collective-permute-start | bytes 196616 | tf_op jit(solution)/shard_map/ppermute | solution.py:623
  19.7 3.0 %collective-permute-done.6.refs_4_ = bf16[256,512]{1,0:T(8,128)(2,1)S(1)} collective-permute-done((bf16[256,512]{1,0:T(8,128)(2,1)}, bf16[256,512]{1,0:T(8,128)(2,1)S(1)}, u32[]{:S(2)}, u32[]{:S(2)}) %collective-permute-start.6) | collective-permute-done | bytes 262176 | tf_op jit(solution)/shard_map/ppermute | solution.py:538
  22.7 0.1 collective-permute-done.4.refs_2_
  22.8 0.4 collective-permute-start.7
  23.2 0.1 collective-permute-start.5
  23.3 0.7 unpack.1
  24.1 0.2 collective-permute-done.9.refs_7_
  24.3 0.4 collective-permute-done.7.refs_5_
  24.6 0.4 collective-permute-done.5.refs_3_
  25.0 3.4 %feed_forward.1 = (bf16[1024,512]{1,0:T(8,128)(2,1)S(1)}, bf16[1024,512]{1,0:T(8,128)(2,1)S(1)}, f32[8,512]{1,0:T(8,128)S(1)}, bf16[1024,512]{1,0:T(8,128)(2,1)S...) custom-call(s32[2]{0:T(128)S(1)} %pad_add_fusion.place, ...), custom_call_target="tpu_custom_call" | custom-call | flops 4000000000 | tf_op jit(solution)/shard_map/feed_forward/pallas_call | solution.py:657
  28.5 1.3 %collective-permute-start.11 = (bf16[128,512]{1,0:T(8,128)(2,1)S(1)}, bf16[128,512]{1,0:T(8,128)(2,1)S(1)}, u32[]{:S(2)}, u32[]{:S(2)}) collective-permute-start(bf16[128,512]{1,0:T(8,128)(2,1)S(1)} %get-tuple-element.77), channel_id=1, source_target_pairs={{0,1},{1,0},{2,3},{3,2},{4,5},{5,4},{6,7},{7,6},{8,9},{9,8},{10,11... | collective-permute-start | bytes 393224 | tf_op jit(solution)/shard_map/ppermute | solution.py:677
  29.8 5.1 %attention.1 = (bf16[1024,64]{1,0:T(8,128)(2,1)S(1)}, bf16[1024,256]{1,0:T(8,128)(2,1)S(1)}) custom-call(s32[2]{0:T(128)S(1)} %pad_add_fusion.place, s32[16]{0:T(128)S(1)} %select_reduce_fusion.order, bf16[256,512]{1,0:T(8,128)(2,1)S(1)} %copy-done.3, bf16[256,512]{1,0:T(8,128)(2,1)S(1)} %collective-permute-done.3.refs_1_, ...), custom_call_target="tpu_custom_call" | custom-call | flops 6000000000 | tf_op jit(solution)/shard_map/attention/pallas_call | solution.py:679
  34.9 2.3 %ends.1 = (bf16[4,128,1024]{2,1,0:T(8,128)(2,1)S(1)}, bf16[4,128,1024]{2,1,0:T(8,128)(2,1)S(1)}, bf16[64,512]{1,0:T(8,128)(2,1)S(1)}, bf16[128,256]{1,0:T(8,128)...) custom-call(s32[2]{0:T(128)S(1)} %pad_add_fusion.place, ...), custom_call_target="tpu_custom_call" | custom-call | flops 3000000000 | tf_op jit(solution)/shard_map/ends/pallas_call | solution.py:699
  37.2 3.4 %collective-permute-start.17 = (bf16[192,512]{1,0:T(8,128)(2,1)S(1)}, bf16[192,512]{1,0:T(8,128)(2,1)S(1)}, u32[]{:S(2)}, u32[]{:S(2)}) collective-permute-start(bf16[192,512]{1,0:T(8,128)(2,1)S(1)} %get-tuple-element.88), channel_id=1, source_target_pairs={{0,2},{1,3},{2,0},{3,1},{4,6},{5,7},{6,4},{7,5},{8,10},{9,11},{10,... | collective-permute-start | bytes 589832 | tf_op jit(solution)/shard_map/ppermute | solution.py:742
  40.6 0.5 collective-permute-start.18
  41.1 0.3 chip_sum.1
  41.4 0.6 collective-permute-start.13
  42.0 1.5 %collective-permute-start.14 = (bf16[2,128,512]{2,1,0:T(8,128)(2,1)S(1)}, bf16[2,128,512]{2,1,0:T(8,128)(2,1)S(1)}, u32[]{:S(2)}, u32[]{:S(2)}) collective-permute-start(bf16[2,128,512]{2,1,0:T(8,128)(2,1)S(1)} %get-tuple-element.82), channel_id=1, source_target_pairs={{0,16},{4,20},{8,24},{12,28},{16,0},{20,4},{24,8},{28,12},{1,17},{... | collective-permute-start | bytes 786440 | tf_op jit(solution)/shard_map/ppermute | solution.py:727
  43.6 6.8 %collective-permute-done.17.came.ff_far = bf16[192,512]{1,0:T(8,128)(2,1)S(1)} collective-permute-done((bf16[192,512]{1,0:T(8,128)(2,1)S(1)}, bf16[192,512]{1,0:T(8,128)(2,1)S(1)}, u32[]{:S(2)}, u32[]{:S(2)}) %collective-permute-start.17) | collective-permute-done | bytes 196640 | tf_op jit(solution)/shard_map/ppermute | solution.py:742
  50.6 2.7 %collective-permute-start.15 = (bf16[128,512]{1,0:T(8,128)(2,1)S(1)}, bf16[128,512]{1,0:T(8,128)(2,1)S(1)}, u32[]{:S(2)}, u32[]{:S(2)}) collective-permute-start(bf16[128,512]{1,0:T(8,128)(2,1)S(1)} %get-tuple-element.85), channel_id=1, source_target_pairs={{0,16},{4,20},{8,24},{12,28},{16,0},{20,4},{24,8},{28,12},{1,17},{... | collective-permute-start | bytes 393224 | tf_op jit(solution)/shard_map/ppermute | solution.py:737
  53.3 0.5 collective-permute-start.16
  53.7 2.3 %collective-permute-start.19 = (bf16[128,256]{1,0:T(8,128)(2,1)S(1)}, bf16[128,256]{1,0:T(8,128)(2,1)S(1)}, u32[]{:S(2)}, u32[]{:S(2)}) collective-permute-start(bf16[128,256]{1,0:T(8,128)(2,1)S(1)} %relay.1), channel_id=1, source_target_pairs={{0,2},{1,3},{2,0},{3,1},{4,6},{5,7},{6,4},{7,5},{8,10},{9,11},{10,... | collective-permute-start | bytes 196616 | tf_op jit(solution)/shard_map/ppermute | solution.py:747
  56.0 3.1 %collective-permute-done.19.far = bf16[128,256]{1,0:T(8,128)(2,1)S(1)} collective-permute-done((bf16[128,256]{1,0:T(8,128)(2,1)S(1)}, bf16[128,256]{1,0:T(8,128)(2,1)S(1)}, u32[]{:S(2)}, u32[]{:S(2)}) %collective-permute-start.19) | collective-permute-done | bytes 65568 | tf_op jit(solution)/shard_map/ppermute | solution.py:747
  59.1 0.1 share.1.refs_5_.refs_0_
  59.2 1.6 %collective-permute-start.26 = (bf16[128,1024]{1,0:T(8,128)(2,1)S(1)}, bf16[128,1024]{1,0:T(8,128)(2,1)S(1)}, u32[]{:S(2)}, u32[]{:S(2)}) collective-permute-start(bf16[128,1024]{1,0:T(8,128)(2,1)S(1)} %share.1.refs_5_.refs_0_), channel_id=1, source_target_pairs={{0,24},{4,28},{8,16},{12,20},{16,8},{20,12},{24,0},{28,4},{1,25},{... | collective-permute-start | bytes 786440 | tf_op jit(solution)/shard_map/ppermute | solution.py:538
  60.8 1.7 %collective-permute-start.24 = (bf16[128,1024]{1,0:T(8,128)(2,1)S(1)}, bf16[128,1024]{1,0:T(8,128)(2,1)S(1)}, u32[]{:S(2)}, u32[]{:S(2)}) collective-permute-start(bf16[128,1024]{1,0:T(8,128)(2,1)S(1)} %share.1.refs_5_.refs_0_), channel_id=1, source_target_pairs={{0,16},{4,20},{8,24},{12,28},{16,0},{20,4},{24,8},{28,12},{1,17},{... | collective-permute-start | bytes 786440 | tf_op jit(solution)/shard_map/ppermute | solution.py:538
  62.5 0.3 collective-permute-start.22
  62.8 1.6 %close.1 = (bf16[128,512]{1,0:T(8,128)(2,1)}, f32[128,512]{1,0:T(8,128)}, bf16[128,1024]{1,0:T(8,128)(2,1)S(1)}) custom-call(s32[2]{0:T(128)S(1)} %pad_add_fusion.place, bf16[128,512]{1,0:T(8,128)(2,1)S(1)} %bitcast.6, bf16[128,512]{1,0:T(8,128)(2,1)S(1)} %bitcast.7, f32[8,512]{1,0:T(8,128)S(1)} %get-tuple-element.62.refs_10_.refs_9_.refs_17_.params, ...), custom_call_target="tpu_custom_call" | custom-call | tf_op jit(solution)/shard_map/close/pallas_call | solution.py:754
  64.4 5.0 %collective-permute-done.26.refs_6_ = bf16[128,1024]{1,0:T(8,128)(2,1)S(1)} collective-permute-done((bf16[128,1024]{1,0:T(8,128)(2,1)S(1)}, bf16[128,1024]{1,0:T(8,128)(2,1)S(1)}, u32[]{:S(2)}, u32[]{:S(2)}) %collective-permute-start.26) | collective-permute-done | bytes 262176 | tf_op jit(solution)/shard_map/ppermute | solution.py:538
  69.4 2.8 %collective-permute-done.24.refs_4_ = bf16[128,1024]{1,0:T(8,128)(2,1)S(1)} collective-permute-done((bf16[128,1024]{1,0:T(8,128)(2,1)S(1)}, bf16[128,1024]{1,0:T(8,128)(2,1)S(1)}, u32[]{:S(2)}, u32[]{:S(2)}) %collective-permute-start.24) | collective-permute-done | bytes 262176 | tf_op jit(solution)/shard_map/ppermute | solution.py:538
  72.1 0.2 collective-permute-done.22.refs_2_
  72.3 0.3 collective-permute-start.23
  72.6 1.0 %collective-permute-done.25.refs_5_ = bf16[128,1024]{1,0:T(8,128)(2,1)S(1)} collective-permute-done((bf16[128,1024]{1,0:T(8,128)(2,1)S(1)}, bf16[128,1024]{1,0:T(8,128)(2,1)S(1)}, u32[]{:S(2)}, u32[]{:S(2)}) %collective-permute-start.25) | collective-permute-done | bytes 262176 | tf_op jit(solution)/shard_map/ppermute | solution.py:541
  73.6 0.4 collective-permute-done.23.refs_3_
  74.0 2.8 %finish.1 = (f32[128]{0:T(128)}, f32[128]{0:T(128)}, f32[128,1536]{1,0:T(8,128)}, f32[384]{0:T(512)}, f32[128,512]{1,0:T(8,128)}, /*index=5*/f32[128]{0:T(128)},...) custom-call(s32[2]{0:T(128)S(1)} %pad_add_fusion.place, ...), custom_call_target="tpu_custom_call" | custom-call | tf_op jit(solution)/shard_map/finish/pallas_call | solution.py:766
  (40 shorter events, 0.5 us)
Async XLA Ops:
  2.8 13.5 %collective-permute-start.1 = (bf16[128,768]{1,0:T(8,128)(2,1)}, bf16[128,768]{1,0:T(8,128)(2,1)S(1)}, u32[]{:S(2)}, u32[]{:S(2)}) collective-permute-start(bf16[128,768]{1,0:T(8,128)(2,1)} %get-tuple-element.61.refs_0_), channel_id=1, source_target_pairs={{0,2},{1,3},{2,0},{3,1},{4,6},{5,7},{6,4},{7,5},{8,10},{9,11},{10,... | collective-permute-start | bytes 589832 | tf_op jit(solution)/shard_map/ppermute | solution.py:550
  6.9 11.0 %collective-permute-start = (bf16[128,768]{1,0:T(8,128)(2,1)}, bf16[128,768]{1,0:T(8,128)(2,1)S(1)}, u32[]{:S(2)}, u32[]{:S(2)}) collective-permute-start(bf16[128,768]{1,0:T(8,128)(2,1)} %get-tuple-element.61.refs_0_), channel_id=1, source_target_pairs={{0,1},{1,0},{2,3},{3,2},{4,5},{5,4},{6,7},{7,6},{8,9},{9,8},{10,11... | collective-permute-start | bytes 589832 | tf_op jit(solution)/shard_map/ppermute | solution.py:550
  8.5 10.4 %collective-permute-start.8 = (bf16[256,512]{1,0:T(8,128)(2,1)}, bf16[256,512]{1,0:T(8,128)(2,1)S(1)}, u32[]{:S(2)}, u32[]{:S(2)}) collective-permute-start(bf16[256,512]{1,0:T(8,128)(2,1)} %get-tuple-element.63.refs_0_), channel_id=1, source_target_pairs={{0,24},{4,28},{8,16},{12,20},{16,8},{20,12},{24,0},{28,4},{1,25},{... | collective-permute-start | bytes 786440 | tf_op jit(solution)/shard_map/ppermute | solution.py:538
  11.0 11.8 %collective-permute-start.6 = (bf16[256,512]{1,0:T(8,128)(2,1)}, bf16[256,512]{1,0:T(8,128)(2,1)S(1)}, u32[]{:S(2)}, u32[]{:S(2)}) collective-permute-start(bf16[256,512]{1,0:T(8,128)(2,1)} %get-tuple-element.63.refs_0_), channel_id=1, source_target_pairs={{0,16},{4,20},{8,24},{12,28},{16,0},{20,4},{24,8},{28,12},{1,17},{... | collective-permute-start | bytes 786440 | tf_op jit(solution)/shard_map/ppermute | solution.py:538
  11.5 11.4 %collective-permute-start.4 = (bf16[256,512]{1,0:T(8,128)(2,1)}, bf16[256,512]{1,0:T(8,128)(2,1)S(1)}, u32[]{:S(2)}, u32[]{:S(2)}) collective-permute-start(bf16[256,512]{1,0:T(8,128)(2,1)} %get-tuple-element.63.refs_0_), channel_id=1, source_target_pairs={{0,8},{4,12},{8,0},{12,4},{16,24},{20,28},{24,16},{28,20},{1,9},{5... | collective-permute-start | bytes 786440 | tf_op jit(solution)/shard_map/ppermute | solution.py:538
  16.4 6.9 %collective-permute-start.2 = (bf16[128,768]{1,0:T(8,128)(2,1)S(1)}, bf16[128,768]{1,0:T(8,128)(2,1)S(1)}, u32[]{:S(2)}, u32[]{:S(2)}) collective-permute-start(bf16[128,768]{1,0:T(8,128)(2,1)S(1)} %collective-permute-done.1.refs_2_), channel_id=1, source_target_pairs={{0,1},{1,0},{2,3},{3,2},{4,5},{5,4},{6,7},{7,6},{8,9},{9,8},{10,11... | collective-permute-start | bytes 589832 | tf_op jit(solution)/shard_map/ppermute | solution.py:551
  17.1 0.7 copy-start.6
  17.9 6.1 %collective-permute-start.3 = (bf16[256,512]{1,0:T(8,128)(2,1)}, bf16[256,512]{1,0:T(8,128)(2,1)S(1)}, u32[]{:S(2)}, u32[]{:S(2)}) collective-permute-start(bf16[256,512]{1,0:T(8,128)(2,1)} %get-tuple-element.63.refs_0_), channel_id=1, source_target_pairs={{0,4},{4,0},{8,12},{12,8},{16,20},{20,16},{24,28},{28,24},{1,5},{5... | collective-permute-start | bytes 786440 | tf_op jit(solution)/shard_map/ppermute | solution.py:541
  18.0 0.8 %copy-start.2 = (bf16[64,512]{1,0:T(8,128)(2,1)S(1)}, bf16[64,512]{1,0:T(8,128)(2,1)}, u32[]{:S(2)}) copy-start(bf16[64,512]{1,0:T(8,128)(2,1)} %get-tuple-element.65.value) | copy-start | bytes 196612
  18.9 4.5 %copy-start.4 = (bf16[128,768]{1,0:T(8,128)(2,1)S(1)}, bf16[128,768]{1,0:T(8,128)(2,1)}, u32[]{:S(2)}) copy-start(bf16[128,768]{1,0:T(8,128)(2,1)} %get-tuple-element.61.refs_0_) | copy-start | bytes 589828
  18.9 6.2 %copy-start.3 = (bf16[256,512]{1,0:T(8,128)(2,1)S(1)}, bf16[256,512]{1,0:T(8,128)(2,1)}, u32[]{:S(2)}) copy-start(bf16[256,512]{1,0:T(8,128)(2,1)} %get-tuple-element.63.refs_0_) | copy-start | bytes 786436
  18.9 10.9 %collective-permute-start.10 = (bf16[64,512]{1,0:T(8,128)(2,1)S(1)}, bf16[64,512]{1,0:T(8,128)(2,1)S(1)}, u32[]{:S(2)}, u32[]{:S(2)}) collective-permute-start(bf16[64,512]{1,0:T(8,128)(2,1)S(1)} %gate_w.1), channel_id=1, source_target_pairs={{0,0},{1,8},{2,16},{3,24},{4,4},{5,12},{6,20},{7,28},{8,1},{9,9},{... | collective-permute-start | bytes 196616 | tf_op jit(solution)/shard_map/ppermute | solution.py:623
  22.7 1.5 %collective-permute-start.9 = (bf16[256,512]{1,0:T(8,128)(2,1)S(1)}, bf16[256,512]{1,0:T(8,128)(2,1)S(1)}, u32[]{:S(2)}, u32[]{:S(2)}) collective-permute-start(bf16[256,512]{1,0:T(8,128)(2,1)S(1)} %collective-permute-done.8.refs_6_), channel_id=1, source_target_pairs={{0,4},{4,0},{8,12},{12,8},{16,20},{20,16},{24,28},{28,24},{1,5},{5... | collective-permute-start | bytes 786440 | tf_op jit(solution)/shard_map/ppermute | solution.py:541
  22.8 1.8 %collective-permute-start.7 = (bf16[256,512]{1,0:T(8,128)(2,1)S(1)}, bf16[256,512]{1,0:T(8,128)(2,1)S(1)}, u32[]{:S(2)}, u32[]{:S(2)}) collective-permute-start(bf16[256,512]{1,0:T(8,128)(2,1)S(1)} %collective-permute-done.6.refs_4_), channel_id=1, source_target_pairs={{0,4},{4,0},{8,12},{12,8},{16,20},{20,16},{24,28},{28,24},{1,5},{5... | collective-permute-start | bytes 786440 | tf_op jit(solution)/shard_map/ppermute | solution.py:541
  23.2 1.8 %collective-permute-start.5 = (bf16[256,512]{1,0:T(8,128)(2,1)S(1)}, bf16[256,512]{1,0:T(8,128)(2,1)S(1)}, u32[]{:S(2)}, u32[]{:S(2)}) collective-permute-start(bf16[256,512]{1,0:T(8,128)(2,1)S(1)} %collective-permute-done.4.refs_2_), channel_id=1, source_target_pairs={{0,4},{4,0},{8,12},{12,8},{16,20},{20,16},{24,28},{28,24},{1,5},{5... | collective-permute-start | bytes 786440 | tf_op jit(solution)/shard_map/ppermute | solution.py:541
  25.0 4.8 %copy-start.5 = (f32[1024,128]{1,0:T(8,128)S(1)}, f32[1024,128]{1,0:T(8,128)}, u32[]{:S(2)}) copy-start(f32[1024,128]{1,0:T(8,128)} %constant.15.clone.refs_11_) | copy-start | bytes 1572868
  28.5 6.4 %collective-permute-start.11 = (bf16[128,512]{1,0:T(8,128)(2,1)S(1)}, bf16[128,512]{1,0:T(8,128)(2,1)S(1)}, u32[]{:S(2)}, u32[]{:S(2)}) collective-permute-start(bf16[128,512]{1,0:T(8,128)(2,1)S(1)} %get-tuple-element.77), channel_id=1, source_target_pairs={{0,1},{1,0},{2,3},{3,2},{4,5},{5,4},{6,7},{7,6},{8,9},{9,8},{10,11... | collective-permute-start | bytes 393224 | tf_op jit(solution)/shard_map/ppermute | solution.py:677
  37.2 4.0 %collective-permute-start.12 = (bf16[4,128,1024]{2,1,0:T(8,128)(2,1)S(1)}, bf16[4,128,1024]{2,1,0:T(8,128)(2,1)S(1)}, u32[]{:S(2)}, u32[]{:S(2)}) collective-permute-start(bf16[4,128,1024]{2,1,0:T(8,128)(2,1)S(1)} %get-tuple-element.79), channel_id=1, source_target_pairs={{0,4},{4,0},{8,12},{12,8},{16,20},{20,16},{24,28},{28,24},{1,5},{5... | collective-permute-start | bytes 3145736 | tf_op jit(solution)/shard_map/ppermute | solution.py:716
  37.2 13.1 %collective-permute-start.17 = (bf16[192,512]{1,0:T(8,128)(2,1)S(1)}, bf16[192,512]{1,0:T(8,128)(2,1)S(1)}, u32[]{:S(2)}, u32[]{:S(2)}) collective-permute-start(bf16[192,512]{1,0:T(8,128)(2,1)S(1)} %get-tuple-element.88), channel_id=1, source_target_pairs={{0,2},{1,3},{2,0},{3,1},{4,6},{5,7},{6,4},{7,5},{8,10},{9,11},{10,... | collective-permute-start | bytes 589832 | tf_op jit(solution)/shard_map/ppermute | solution.py:742
  40.6 13.1 %collective-permute-start.18 = (bf16[128,1024]{1,0:T(8,128)(2,1)S(1)}, bf16[128,1024]{1,0:T(8,128)(2,1)S(1)}, u32[]{:S(2)}, u32[]{:S(2)}) collective-permute-start(bf16[128,1024]{1,0:T(8,128)(2,1)S(1)} %get-tuple-element.90), channel_id=1, source_target_pairs={{0,1},{1,0},{2,3},{3,2},{4,5},{5,4},{6,7},{7,6},{8,9},{9,8},{10,11... | collective-permute-start | bytes 786440 | tf_op jit(solution)/shard_map/ppermute | solution.py:745
  41.4 9.1 %collective-permute-start.13 = (bf16[2,128,512]{2,1,0:T(8,128)(2,1)S(1)}, bf16[2,128,512]{2,1,0:T(8,128)(2,1)S(1)}, u32[]{:S(2)}, u32[]{:S(2)}) collective-permute-start(bf16[2,128,512]{2,1,0:T(8,128)(2,1)S(1)} %get-tuple-element.81), channel_id=1, source_target_pairs={{0,8},{4,12},{8,0},{12,4},{16,24},{20,28},{24,16},{28,20},{1,9},{5... | collective-permute-start | bytes 786440 | tf_op jit(solution)/shard_map/ppermute | solution.py:726
  42.0 8.4 %collective-permute-start.14 = (bf16[2,128,512]{2,1,0:T(8,128)(2,1)S(1)}, bf16[2,128,512]{2,1,0:T(8,128)(2,1)S(1)}, u32[]{:S(2)}, u32[]{:S(2)}) collective-permute-start(bf16[2,128,512]{2,1,0:T(8,128)(2,1)S(1)} %get-tuple-element.82), channel_id=1, source_target_pairs={{0,16},{4,20},{8,24},{12,28},{16,0},{20,4},{24,8},{28,12},{1,17},{... | collective-permute-start | bytes 786440 | tf_op jit(solution)/shard_map/ppermute | solution.py:727
  50.4 5.6 %collective-permute-start.20 = (bf16[64,512]{1,0:T(8,128)(2,1)S(1)}, bf16[64,512]{1,0:T(8,128)(2,1)S(1)}, u32[]{:S(2)}, u32[]{:S(2)}) collective-permute-start(bf16[64,512]{1,0:T(8,128)(2,1)S(1)} %out_half.1), channel_id=1, source_target_pairs={{0,1},{1,0},{2,3},{3,2},{4,5},{5,4},{6,7},{7,6},{8,9},{9,8},{10,11... | collective-permute-start | bytes 196616 | tf_op jit(solution)/shard_map/ppermute | solution.py:744
  50.6 8.6 %collective-permute-start.15 = (bf16[128,512]{1,0:T(8,128)(2,1)S(1)}, bf16[128,512]{1,0:T(8,128)(2,1)S(1)}, u32[]{:S(2)}, u32[]{:S(2)}) collective-permute-start(bf16[128,512]{1,0:T(8,128)(2,1)S(1)} %get-tuple-element.85), channel_id=1, source_target_pairs={{0,16},{4,20},{8,24},{12,28},{16,0},{20,4},{24,8},{28,12},{1,17},{... | collective-permute-start | bytes 393224 | tf_op jit(solution)/shard_map/ppermute | solution.py:737
  53.3 5.9 %collective-permute-start.16 = (bf16[128,512]{1,0:T(8,128)(2,1)S(1)}, bf16[128,512]{1,0:T(8,128)(2,1)S(1)}, u32[]{:S(2)}, u32[]{:S(2)}) collective-permute-start(bf16[128,512]{1,0:T(8,128)(2,1)S(1)} %get-tuple-element.86), channel_id=1, source_target_pairs={{0,8},{4,12},{8,0},{12,4},{16,24},{20,28},{24,16},{28,20},{1,9},{5... | collective-permute-start | bytes 393224 | tf_op jit(solution)/shard_map/ppermute | solution.py:737
  53.7 5.4 %collective-permute-start.19 = (bf16[128,256]{1,0:T(8,128)(2,1)S(1)}, bf16[128,256]{1,0:T(8,128)(2,1)S(1)}, u32[]{:S(2)}, u32[]{:S(2)}) collective-permute-start(bf16[128,256]{1,0:T(8,128)(2,1)S(1)} %relay.1), channel_id=1, source_target_pairs={{0,2},{1,3},{2,0},{3,1},{4,6},{5,7},{6,4},{7,5},{8,10},{9,11},{10,... | collective-permute-start | bytes 196616 | tf_op jit(solution)/shard_map/ppermute | solution.py:747
  59.1 3.7 %copy-start = (bf16[1,128,512]{2,1,0:T(8,128)(2,1)S(1)}, bf16[1,128,512]{2,1,0:T(8,128)(2,1)}, u32[]{:S(2)}) copy-start(bf16[1,128,512]{2,1,0:T(8,128)(2,1)} %x.1) | copy-start | bytes 393220
  59.1 3.7 %copy-start.1 = (bf16[1,128,512]{2,1,0:T(8,128)(2,1)S(1)}, bf16[1,128,512]{2,1,0:T(8,128)(2,1)}, u32[]{:S(2)}) copy-start(bf16[1,128,512]{2,1,0:T(8,128)(2,1)} %g.1) | copy-start | bytes 393220
  59.2 10.1 %collective-permute-start.26 = (bf16[128,1024]{1,0:T(8,128)(2,1)S(1)}, bf16[128,1024]{1,0:T(8,128)(2,1)S(1)}, u32[]{:S(2)}, u32[]{:S(2)}) collective-permute-start(bf16[128,1024]{1,0:T(8,128)(2,1)S(1)} %share.1.refs_5_.refs_0_), channel_id=1, source_target_pairs={{0,24},{4,28},{8,16},{12,20},{16,8},{20,12},{24,0},{28,4},{1,25},{... | collective-permute-start | bytes 786440 | tf_op jit(solution)/shard_map/ppermute | solution.py:538
  60.8 11.3 %collective-permute-start.24 = (bf16[128,1024]{1,0:T(8,128)(2,1)S(1)}, bf16[128,1024]{1,0:T(8,128)(2,1)S(1)}, u32[]{:S(2)}, u32[]{:S(2)}) collective-permute-start(bf16[128,1024]{1,0:T(8,128)(2,1)S(1)} %share.1.refs_5_.refs_0_), channel_id=1, source_target_pairs={{0,16},{4,20},{8,24},{12,28},{16,0},{20,4},{24,8},{28,12},{1,17},{... | collective-permute-start | bytes 786440 | tf_op jit(solution)/shard_map/ppermute | solution.py:538
  62.5 9.8 %collective-permute-start.22 = (bf16[128,1024]{1,0:T(8,128)(2,1)S(1)}, bf16[128,1024]{1,0:T(8,128)(2,1)S(1)}, u32[]{:S(2)}, u32[]{:S(2)}) collective-permute-start(bf16[128,1024]{1,0:T(8,128)(2,1)S(1)} %share.1.refs_5_.refs_0_), channel_id=1, source_target_pairs={{0,8},{4,12},{8,0},{12,4},{16,24},{20,28},{24,16},{28,20},{1,9},{5... | collective-permute-start | bytes 786440 | tf_op jit(solution)/shard_map/ppermute | solution.py:538
  64.4 8.2 %collective-permute-start.21 = (bf16[128,1024]{1,0:T(8,128)(2,1)S(1)}, bf16[128,1024]{1,0:T(8,128)(2,1)S(1)}, u32[]{:S(2)}, u32[]{:S(2)}) collective-permute-start(bf16[128,1024]{1,0:T(8,128)(2,1)S(1)} %get-tuple-element.95), channel_id=1, source_target_pairs={{0,4},{4,0},{8,12},{12,8},{16,20},{20,16},{24,28},{28,24},{1,5},{5... | collective-permute-start | bytes 786440 | tf_op jit(solution)/shard_map/ppermute | solution.py:541
  69.4 3.3 %collective-permute-start.27 = (bf16[128,1024]{1,0:T(8,128)(2,1)S(1)}, bf16[128,1024]{1,0:T(8,128)(2,1)S(1)}, u32[]{:S(2)}, u32[]{:S(2)}) collective-permute-start(bf16[128,1024]{1,0:T(8,128)(2,1)S(1)} %collective-permute-done.26.refs_6_), channel_id=1, source_target_pairs={{0,4},{4,0},{8,12},{12,8},{16,20},{20,16},{24,28},{28,24},{1,5},{5... | collective-permute-start | bytes 786440 | tf_op jit(solution)/shard_map/ppermute | solution.py:541
  72.1 1.5 %collective-permute-start.25 = (bf16[128,1024]{1,0:T(8,128)(2,1)S(1)}, bf16[128,1024]{1,0:T(8,128)(2,1)S(1)}, u32[]{:S(2)}, u32[]{:S(2)}) collective-permute-start(bf16[128,1024]{1,0:T(8,128)(2,1)S(1)} %collective-permute-done.24.refs_4_), channel_id=1, source_target_pairs={{0,4},{4,0},{8,12},{12,8},{16,20},{20,16},{24,28},{28,24},{1,5},{5... | collective-permute-start | bytes 786440 | tf_op jit(solution)/shard_map/ppermute | solution.py:541
  72.3 1.7 %collective-permute-start.23 = (bf16[128,1024]{1,0:T(8,128)(2,1)S(1)}, bf16[128,1024]{1,0:T(8,128)(2,1)S(1)}, u32[]{:S(2)}, u32[]{:S(2)}) collective-permute-start(bf16[128,1024]{1,0:T(8,128)(2,1)S(1)} %collective-permute-done.22.refs_2_), channel_id=1, source_target_pairs={{0,4},{4,0},{8,12},{12,8},{16,20},{20,16},{24,28},{28,24},{1,5},{5... | collective-permute-start | bytes 786440 | tf_op jit(solution)/shard_map/ppermute | solution.py:541
